TPU v7x, 32 devices: a whole 2x2x4 slice. The times are simulated.
32 devices in a mesh: gx: 4 (over z), gy: 4 (over y, x), gz: 2 (over core).
Axes of the slice: x: 2, y: 2, z: 4, core: 2. Of those that a mesh axis runs over, the one named last changes fastest.
Arguments:
- flow: float32 [4, 32, 64, 256], P(None, 'gx', 'gy', 'gz'), may hold values from -3 to 3
- basis: float32 [127, 3, 8192], P(None, None, ('gx', 'gy', 'gz')), may hold values from -1150 to 1150
- sample: int32 [8192], P(('gx', 'gy', 'gz')), may hold values from 0 to 16383
Outputs:
- flow_next: float32 [4, 32, 64, 256], P(None, 'gx', 'gy', 'gz')
- basis_next: float32 [128, 3, 8192], P(None, None, ('gx', 'gy', 'gz'))
- factor: float32 [128, 128], replicated
All inputs are finite; a program needn't handle non-finite values.
Results may differ from a plain program's by a relative error of at most 0.000065.
Values sent between devices are 32-bit elements; how exact they have to be, the bound alone decides.
No kernel may reach another device: no remote copies, remote signals or barrier semaphores. Data moves between devices by JAX's collectives and lax.ppermute only.
A program may use at most 64 MiB of HBM per device.

v0:
```python
import jax
import jax.numpy as jnp
from jax import lax
from jax.sharding import PartitionSpec as P

DT_STEP = 0.35
VISCOSITY = 0.2
SOUND_SQ = 1.0
DRIVING = 0.5


def padded(block, sides, width, periodic):
    for axis, dim in sides:
        count = lax.axis_size(axis)
        forward = [(i, i + 1) for i in range(count - 1)]
        if periodic:
            forward.append((count - 1, 0))
        backward = [(target, source) for source, target in forward]
        low = lax.ppermute(
            lax.slice_in_dim(block, block.shape[dim] - width, None, axis=dim), axis, forward
        )
        high = lax.ppermute(lax.slice_in_dim(block, 0, width, axis=dim), axis, backward)
        block = jnp.concatenate([low, block, high], axis=dim)
    return block


def rates(ext):
    centre = ext[:, 1:-1, 1:-1, 1:-1]
    x_plus = ext[:, 2:, 1:-1, 1:-1]
    x_minus = ext[:, :-2, 1:-1, 1:-1]
    y_plus = ext[:, 1:-1, 2:, 1:-1]
    y_minus = ext[:, 1:-1, :-2, 1:-1]
    z_plus = ext[:, 1:-1, 1:-1, 2:]
    z_minus = ext[:, 1:-1, 1:-1, :-2]
    slope_x = 0.5 * (x_plus - x_minus)
    slope_y = 0.5 * (y_plus - y_minus)
    slope_z = 0.5 * (z_plus - z_minus)
    laplace = x_plus + x_minus + (y_plus + y_minus) + (z_plus + z_minus) - 6.0 * centre
    advect = centre[0] * slope_x[:3] + centre[1] * slope_y[:3] + centre[2] * slope_z[:3]
    pressure = jnp.stack([slope_x[3], slope_y[3], slope_z[3]])
    forcing = jnp.array([DRIVING, 0.0, 0.0], dtype=jnp.float32).reshape(3, 1, 1, 1)
    velocity = VISCOSITY * laplace[:3] - advect - pressure + forcing
    density = -SOUND_SQ * (slope_x[0] + slope_y[1] + slope_z[2])
    return jnp.concatenate([velocity, density[None]], axis=0)


def extend_one(fields):
    walled = padded(fields, (("gy", 2),), 1, False)
    return padded(walled, (("gx", 1), ("gz", 3)), 1, True)


def local(flow, basis, sample):
    points = basis.shape[2]
    modes = basis.shape[0]
    count = 3.0 * points * lax.axis_size("gx") * lax.axis_size("gy") * lax.axis_size("gz")
    old_modes = basis.reshape(modes, 3 * points)
    old_gram = lax.psum(
        jnp.dot(
            old_modes,
            old_modes.T,
            precision=lax.Precision.HIGHEST,
            preferred_element_type=jnp.float32,
        ),
        ("gx", "gy", "gz"),
    )
    section_one = flow + DT_STEP * rates(extend_one(flow))
    section_two = 0.75 * flow + 0.25 * (section_one + DT_STEP * rates(extend_one(section_one)))
    flow_next = 1.0 / 3.0 * flow + 2.0 / 3.0 * (
        section_two + DT_STEP * rates(extend_one(section_two))
    )
    velocity = flow_next[:3].reshape(3, -1)
    snapshot = jnp.take(velocity, sample, axis=1)
    stacked = jnp.concatenate([basis, snapshot[None]], axis=0).reshape(modes + 1, 3 * points)
    snap_flat = snapshot.reshape(3 * points)
    cross, square = lax.psum(
        (
            jnp.dot(
                old_modes,
                snap_flat,
                precision=lax.Precision.HIGHEST,
                preferred_element_type=jnp.float32,
            ),
            jnp.sum(snap_flat * snap_flat),
        ),
        ("gx", "gy", "gz"),
    )
    upper_rows = jnp.concatenate([old_gram, cross[:, None]], axis=1)
    last_row = jnp.concatenate([cross, square[None]], axis=0)[None]
    gram = jnp.concatenate([upper_rows, last_row], axis=0) / count
    lower = jnp.linalg.cholesky(gram)
    basis_next = jax.scipy.linalg.solve_triangular(lower, stacked, lower=True).reshape(
        modes + 1, 3, points
    )
    return (flow_next, basis_next, lower.T)


def solution(mesh):
    return jax.shard_map(
        local,
        mesh=mesh,
        in_specs=(
            P(None, "gx", "gy", "gz"),
            P(None, None, ("gx", "gy", "gz")),
            P(("gx", "gy", "gz")),
        ),
        out_specs=(P(None, "gx", "gy", "gz"), P(None, None, ("gx", "gy", "gz")), P()),
        check_vma=False,
    )
```

profile of v0, /device:TPU:0, one launch (start us, length us, event | category | flops | bytes accessed | tf_op | source)
XLA Modules:
  0.0 142.7 jit_solution(17457844054715721753)
XLA Ops:
  1.7 4.8 %collective-permute-start = (f32[4,8,1,128]{3,2,1,0:T(1,128)S(1)}, f32[4,8,1,128]{3,2,1,0:T(1,128)S(1)}, u32[]{:S(2)}, u32[]{:S(2)}) collective-permute-start(f32[4,8,1,128]{3,2,1,0:T(1,128)S(1)} %get-tuple-element.72), channel_id=1, source_target_pairs={{0,2},{2,4},{4,6},{1,3},{3,5},{5,7},{8,10},{10,12},{12,14},{9,11},... | collective-permute-start | bytes 49160 | tf_op jit(solution)/shard_map/ppermute | solution.py:19
  6.6 1.3 collective-permute-start.1
  9.5 2.7 %collective-permute-done.1 = f32[4,8,1,128]{3,2,1,0:T(1,128)S(1)} collective-permute-done((f32[4,8,1,128]{3,2,1,0:T(1,128)S(1)}, f32[4,8,1,128]{3,2,1,0:T(1,128)S(1)}, u32[]{:S(2)}, u32[]{:S(2)}) %collective-permute-start.1) | collective-permute-done | bytes 16416 | tf_op jit(solution)/shard_map/ppermute | solution.py:22
  13.0 3.7 %collective-permute-start.2 = (f32[4,1,18,128]{3,2,1,0:T(8,128)S(1)}, f32[4,1,18,128]{3,2,1,0:T(8,128)S(1)}, u32[]{:S(2)}, u32[]{:S(2)}) collective-permute-start(f32[4,1,18,128]{3,2,1,0:T(8,128)S(1)} %get-tuple-element.46), channel_id=1, source_target_pairs={{8,0},{16,8},{24,16},{0,24},{9,1},{17,9},{25,17},{1,25},{10,2},{18... | collective-permute-start | bytes 110600 | tf_op jit(solution)/shard_map/ppermute | solution.py:22
  18.4 4.1 %collective-permute-done.3 = f32[4,1,18,128]{3,2,1,0:T(8,128)S(1)} collective-permute-done((f32[4,1,18,128]{3,2,1,0:T(8,128)S(1)}, f32[4,1,18,128]{3,2,1,0:T(8,128)S(1)}, u32[]{:S(2)}, u32[]{:S(2)}) %collective-permute-start.3) | collective-permute-done | bytes 36896 | tf_op jit(solution)/shard_map/ppermute | solution.py:19
  24.3 1.4 subtract_multiply_fusion.5
  26.4 1.4 subtract_multiply_fusion.4
  27.8 1.3 fusion.21
  29.2 4.3 %collective-permute-start.6 = (f32[4,8,1,128]{3,2,1,0:T(1,128)S(1)}, f32[4,8,1,128]{3,2,1,0:T(1,128)S(1)}, u32[]{:S(2)}, u32[]{:S(2)}) collective-permute-start(f32[4,8,1,128]{3,2,1,0:T(1,128)S(1)} %get-tuple-element.63), channel_id=1, source_target_pairs={{0,2},{2,4},{4,6},{1,3},{3,5},{5,7},{8,10},{10,12},{12,14},{9,11},... | collective-permute-start | bytes 49160 | tf_op jit(solution)/shard_map/ppermute | solution.py:19
  33.5 1.3 collective-permute-start.7
  35.3 3.8 %collective-permute-done.7 = f32[4,8,1,128]{3,2,1,0:T(1,128)S(1)} collective-permute-done((f32[4,8,1,128]{3,2,1,0:T(1,128)S(1)}, f32[4,8,1,128]{3,2,1,0:T(1,128)S(1)}, u32[]{:S(2)}, u32[]{:S(2)}) %collective-permute-start.7) | collective-permute-done | bytes 16416 | tf_op jit(solution)/shard_map/ppermute | solution.py:22
  39.2 2.0 %collective-permute-start.9 = (f32[4,1,18,128]{3,2,1,0:T(8,128)S(1)}, f32[4,1,18,128]{3,2,1,0:T(8,128)S(1)}, u32[]{:S(2)}, u32[]{:S(2)}) collective-permute-start(f32[4,1,18,128]{3,2,1,0:T(8,128)S(1)} %get-tuple-element.42), channel_id=1, source_target_pairs={{0,8},{8,16},{16,24},{24,0},{1,9},{9,17},{17,25},{25,1},{2,10},{10... | collective-permute-start | bytes 110600 | tf_op jit(solution)/shard_map/ppermute | solution.py:19
  41.3 2.2 %collective-permute-done.8 = f32[4,1,18,128]{3,2,1,0:T(8,128)S(1)} collective-permute-done((f32[4,1,18,128]{3,2,1,0:T(8,128)S(1)}, f32[4,1,18,128]{3,2,1,0:T(8,128)S(1)}, u32[]{:S(2)}, u32[]{:S(2)}) %collective-permute-start.8) | collective-permute-done | bytes 36896 | tf_op jit(solution)/shard_map/ppermute | solution.py:22
  43.4 1.7 %collective-permute-done.9 = f32[4,1,18,128]{3,2,1,0:T(8,128)S(1)} collective-permute-done((f32[4,1,18,128]{3,2,1,0:T(8,128)S(1)}, f32[4,1,18,128]{3,2,1,0:T(8,128)S(1)}, u32[]{:S(2)}, u32[]{:S(2)}) %collective-permute-start.9) | collective-permute-done | bytes 36896 | tf_op jit(solution)/shard_map/ppermute | solution.py:19
  48.7 3.4 %collective-permute-start.12 = (f32[4,8,1,128]{3,2,1,0:T(1,128)S(1)}, f32[4,8,1,128]{3,2,1,0:T(1,128)S(1)}, u32[]{:S(2)}, u32[]{:S(2)}) collective-permute-start(f32[4,8,1,128]{3,2,1,0:T(1,128)S(1)} %get-tuple-element.54), channel_id=1, source_target_pairs={{0,2},{2,4},{4,6},{1,3},{3,5},{5,7},{8,10},{10,12},{12,14},{9,11},... | collective-permute-start | bytes 49160 | tf_op jit(solution)/shard_map/ppermute | solution.py:19
  53.6 4.1 %collective-permute-done.13 = f32[4,8,1,128]{3,2,1,0:T(1,128)S(1)} collective-permute-done((f32[4,8,1,128]{3,2,1,0:T(1,128)S(1)}, f32[4,8,1,128]{3,2,1,0:T(1,128)S(1)}, u32[]{:S(2)}, u32[]{:S(2)}) %collective-permute-start.13) | collective-permute-done | bytes 16416 | tf_op jit(solution)/shard_map/ppermute | solution.py:22
  57.9 2.0 %collective-permute-start.15 = (f32[4,1,18,128]{3,2,1,0:T(8,128)S(1)}, f32[4,1,18,128]{3,2,1,0:T(8,128)S(1)}, u32[]{:S(2)}, u32[]{:S(2)}) collective-permute-start(f32[4,1,18,128]{3,2,1,0:T(8,128)S(1)} %get-tuple-element.39), channel_id=1, source_target_pairs={{0,8},{8,16},{16,24},{24,0},{1,9},{9,17},{17,25},{25,1},{2,10},{10... | collective-permute-start | bytes 110600 | tf_op jit(solution)/shard_map/ppermute | solution.py:19
  59.9 2.3 %collective-permute-done.14 = f32[4,1,18,128]{3,2,1,0:T(8,128)S(1)} collective-permute-done((f32[4,1,18,128]{3,2,1,0:T(8,128)S(1)}, f32[4,1,18,128]{3,2,1,0:T(8,128)S(1)}, u32[]{:S(2)}, u32[]{:S(2)}) %collective-permute-start.14) | collective-permute-done | bytes 36896 | tf_op jit(solution)/shard_map/ppermute | solution.py:22
  62.2 1.6 %collective-permute-done.15 = f32[4,1,18,128]{3,2,1,0:T(8,128)S(1)} collective-permute-done((f32[4,1,18,128]{3,2,1,0:T(8,128)S(1)}, f32[4,1,18,128]{3,2,1,0:T(8,128)S(1)}, u32[]{:S(2)}, u32[]{:S(2)}) %collective-permute-start.15) | collective-permute-done | bytes 36896 | tf_op jit(solution)/shard_map/ppermute | solution.py:19
  67.4 4.7 %copy.16 = f32[3,8,16,128]{0,3,2,1:T(8,128)} copy(f32[3,8,16,128]{3,2,1,0:T(8,128)S(1)} %slice.406) | data formatting | bytes 393216 | tf_op jit(solution)/shard_map/slice | solution.py:71
  72.1 4.1 %gather_fusion = f32[256,3]{1,0:T(8,128)S(1)} fusion(f32[3,16384]{0,1:T(8,128)} %bitcast.60, s32[1024]{0:T(1024)S(1)} %pad_clamp_fusion), kind=kCustom, calls=%fused_computation | custom fusion | bytes 7168 | tf_op jit(solution)/shard_map/jit(_take)/gather | solution.py:72
  77.5 38.7 %all-reduce = (f32[1]{0:T(128)}, f32[127]{0:T(128)S(1)}, f32[127,127]{0,1:T(8,128)S(1)}) all-reduce(f32[1]{0:T(128)} %bitcast.15, f32[127]{0:T(128)S(1)} %convolution_bitcast_fusion.1, f32[127,127]{0,1:T(8,128)S(1)} %convolution_bitcast_fusion), channel_id=1, replica_groups=mesh['gx'=4,'gy'=4,'gz'=2] {'gx','gy','gz'}, use_global_device_ids=true, to_apply=%region_3.4 | all-reduce | flops 16257 | bytes 130056 | tf_op jit(solution)/shard_map/psum | solution.py:75
  117.3 11.7 %cholesky.16 = f32[128,128]{1,0:T(8,128)S(1)} custom-call(f32[128,128]{1,0:T(8,128)S(1)} %fusion.54), custom_call_target="Cholesky" | custom-call | tf_op jit(solution)/shard_map/jit(cholesky)/cholesky | solution.py:90
  130.4 9.8 %custom-call.7 = f32[1,128,128]{1,2,0:T(8,128)S(1)} custom-call(f32[1,128,128]{2,1,0:T(8,128)S(1)} %get-tuple-element.75), custom_call_target="InvertDiagBlocksLowerTriangular" | custom-call | tf_op jit(solution)/shard_map/jit(_solve_triangular)/triangular_solve | solution.py:91
  (79 shorter events, 23.1 us)
Async XLA Ops:
  0.6 28.5 %copy-start = (f32[4,8,16,128]{3,2,1,0:T(8,128)S(1)}, f32[4,8,16,128]{3,2,1,0:T(8,128)}, u32[]{:S(2)}) copy-start(f32[4,8,16,128]{3,2,1,0:T(8,128)} %param.6) | copy-start | bytes 786436
  0.6 34.2 %copy-start.1 = (f32[127,3,256]{2,0,1:T(8,128)S(1)}, f32[127,3,256]{2,0,1:T(8,128)}, u32[]{:S(2)}) copy-start(f32[127,3,256]{2,0,1:T(8,128)} %param.7) | copy-start | bytes 1170436
  1.7 7.8 %collective-permute-start = (f32[4,8,1,128]{3,2,1,0:T(1,128)S(1)}, f32[4,8,1,128]{3,2,1,0:T(1,128)S(1)}, u32[]{:S(2)}, u32[]{:S(2)}) collective-permute-start(f32[4,8,1,128]{3,2,1,0:T(1,128)S(1)} %get-tuple-element.72), channel_id=1, source_target_pairs={{0,2},{2,4},{4,6},{1,3},{3,5},{5,7},{8,10},{10,12},{12,14},{9,11},... | collective-permute-start | bytes 49160 | tf_op jit(solution)/shard_map/ppermute | solution.py:19
  6.6 5.6 %collective-permute-start.1 = (f32[4,8,1,128]{3,2,1,0:T(1,128)S(1)}, f32[4,8,1,128]{3,2,1,0:T(1,128)S(1)}, u32[]{:S(2)}, u32[]{:S(2)}) collective-permute-start(f32[4,8,1,128]{3,2,1,0:T(1,128)S(1)} %get-tuple-element.73), channel_id=1, source_target_pairs={{2,0},{4,2},{6,4},{3,1},{5,3},{7,5},{10,8},{12,10},{14,12},{11,9},... | collective-permute-start | bytes 49160 | tf_op jit(solution)/shard_map/ppermute | solution.py:22
  13.0 5.4 %collective-permute-start.2 = (f32[4,1,18,128]{3,2,1,0:T(8,128)S(1)}, f32[4,1,18,128]{3,2,1,0:T(8,128)S(1)}, u32[]{:S(2)}, u32[]{:S(2)}) collective-permute-start(f32[4,1,18,128]{3,2,1,0:T(8,128)S(1)} %get-tuple-element.46), channel_id=1, source_target_pairs={{8,0},{16,8},{24,16},{0,24},{9,1},{17,9},{25,17},{1,25},{10,2},{18... | collective-permute-start | bytes 110600 | tf_op jit(solution)/shard_map/ppermute | solution.py:22
  16.6 5.9 %collective-permute-start.3 = (f32[4,1,18,128]{3,2,1,0:T(8,128)S(1)}, f32[4,1,18,128]{3,2,1,0:T(8,128)S(1)}, u32[]{:S(2)}, u32[]{:S(2)}) collective-permute-start(f32[4,1,18,128]{3,2,1,0:T(8,128)S(1)} %get-tuple-element.45), channel_id=1, source_target_pairs={{0,8},{8,16},{16,24},{24,0},{1,9},{9,17},{17,25},{25,1},{2,10},{10... | collective-permute-start | bytes 110600 | tf_op jit(solution)/shard_map/ppermute | solution.py:19
  23.7 24.7 %copy-start.3 = (f32[3]{0:T(128)S(1)}, f32[3]{0:T(128)}, u32[]{:S(2)}) copy-start(f32[3]{0:T(128)} %constant.81.clone) | copy-start | bytes 40
  23.8 2.0 %collective-permute-start.4 = (f32[4,10,18,1]{3,2,1,0:T(8,128)S(1)}, f32[4,10,18,1]{3,2,1,0:T(8,128)S(1)}, u32[]{:S(2)}, u32[]{:S(2)}) collective-permute-start(f32[4,10,18,1]{3,2,1,0:T(8,128)S(1)} %get-tuple-element.36), channel_id=1, source_target_pairs={{1,0},{0,1},{3,2},{2,3},{5,4},{4,5},{7,6},{6,7},{9,8},{8,9},{11,10... | collective-permute-start | bytes 8648 | tf_op jit(solution)/shard_map/ppermute | solution.py:22
  23.8 2.6 %collective-permute-start.5 = (f32[4,10,18,1]{3,2,1,0:T(8,128)S(1)}, f32[4,10,18,1]{3,2,1,0:T(8,128)S(1)}, u32[]{:S(2)}, u32[]{:S(2)}) collective-permute-start(f32[4,10,18,1]{3,2,1,0:T(8,128)S(1)} %get-tuple-element.37), channel_id=1, source_target_pairs={{0,1},{1,0},{2,3},{3,2},{4,5},{5,4},{6,7},{7,6},{8,9},{9,8},{10,11... | collective-permute-start | bytes 8648 | tf_op jit(solution)/shard_map/ppermute | solution.py:19
  29.2 6.1 %collective-permute-start.6 = (f32[4,8,1,128]{3,2,1,0:T(1,128)S(1)}, f32[4,8,1,128]{3,2,1,0:T(1,128)S(1)}, u32[]{:S(2)}, u32[]{:S(2)}) collective-permute-start(f32[4,8,1,128]{3,2,1,0:T(1,128)S(1)} %get-tuple-element.63), channel_id=1, source_target_pairs={{0,2},{2,4},{4,6},{1,3},{3,5},{5,7},{8,10},{10,12},{12,14},{9,11},... | collective-permute-start | bytes 49160 | tf_op jit(solution)/shard_map/ppermute | solution.py:19
  33.5 5.6 %collective-permute-start.7 = (f32[4,8,1,128]{3,2,1,0:T(1,128)S(1)}, f32[4,8,1,128]{3,2,1,0:T(1,128)S(1)}, u32[]{:S(2)}, u32[]{:S(2)}) collective-permute-start(f32[4,8,1,128]{3,2,1,0:T(1,128)S(1)} %get-tuple-element.64), channel_id=1, source_target_pairs={{2,0},{4,2},{6,4},{3,1},{5,3},{7,5},{10,8},{12,10},{14,12},{11,9},... | collective-permute-start | bytes 49160 | tf_op jit(solution)/shard_map/ppermute | solution.py:22
  39.2 4.3 %collective-permute-start.8 = (f32[4,1,18,128]{3,2,1,0:T(8,128)S(1)}, f32[4,1,18,128]{3,2,1,0:T(8,128)S(1)}, u32[]{:S(2)}, u32[]{:S(2)}) collective-permute-start(f32[4,1,18,128]{3,2,1,0:T(8,128)S(1)} %get-tuple-element.43), channel_id=1, source_target_pairs={{8,0},{16,8},{24,16},{0,24},{9,1},{17,9},{25,17},{1,25},{10,2},{18... | collective-permute-start | bytes 110600 | tf_op jit(solution)/shard_map/ppermute | solution.py:22
  39.2 5.9 %collective-permute-start.9 = (f32[4,1,18,128]{3,2,1,0:T(8,128)S(1)}, f32[4,1,18,128]{3,2,1,0:T(8,128)S(1)}, u32[]{:S(2)}, u32[]{:S(2)}) collective-permute-start(f32[4,1,18,128]{3,2,1,0:T(8,128)S(1)} %get-tuple-element.42), channel_id=1, source_target_pairs={{0,8},{8,16},{16,24},{24,0},{1,9},{9,17},{17,25},{25,1},{2,10},{10... | collective-permute-start | bytes 110600 | tf_op jit(solution)/shard_map/ppermute | solution.py:19
  45.4 1.9 %collective-permute-start.10 = (f32[4,10,18,1]{3,2,1,0:T(8,128)S(1)}, f32[4,10,18,1]{3,2,1,0:T(8,128)S(1)}, u32[]{:S(2)}, u32[]{:S(2)}) collective-permute-start(f32[4,10,18,1]{3,2,1,0:T(8,128)S(1)} %get-tuple-element.34), channel_id=1, source_target_pairs={{1,0},{0,1},{3,2},{2,3},{5,4},{4,5},{7,6},{6,7},{9,8},{8,9},{11,10... | collective-permute-start | bytes 8648 | tf_op jit(solution)/shard_map/ppermute | solution.py:22
  45.5 2.6 %collective-permute-start.11 = (f32[4,10,18,1]{3,2,1,0:T(8,128)S(1)}, f32[4,10,18,1]{3,2,1,0:T(8,128)S(1)}, u32[]{:S(2)}, u32[]{:S(2)}) collective-permute-start(f32[4,10,18,1]{3,2,1,0:T(8,128)S(1)} %get-tuple-element.35), channel_id=1, source_target_pairs={{0,1},{1,0},{2,3},{3,2},{4,5},{5,4},{6,7},{7,6},{8,9},{9,8},{10,11... | collective-permute-start | bytes 8648 | tf_op jit(solution)/shard_map/ppermute | solution.py:19
  48.7 4.9 %collective-permute-start.12 = (f32[4,8,1,128]{3,2,1,0:T(1,128)S(1)}, f32[4,8,1,128]{3,2,1,0:T(1,128)S(1)}, u32[]{:S(2)}, u32[]{:S(2)}) collective-permute-start(f32[4,8,1,128]{3,2,1,0:T(1,128)S(1)} %get-tuple-element.54), channel_id=1, source_target_pairs={{0,2},{2,4},{4,6},{1,3},{3,5},{5,7},{8,10},{10,12},{12,14},{9,11},... | collective-permute-start | bytes 49160 | tf_op jit(solution)/shard_map/ppermute | solution.py:19
  52.2 5.6 %collective-permute-start.13 = (f32[4,8,1,128]{3,2,1,0:T(1,128)S(1)}, f32[4,8,1,128]{3,2,1,0:T(1,128)S(1)}, u32[]{:S(2)}, u32[]{:S(2)}) collective-permute-start(f32[4,8,1,128]{3,2,1,0:T(1,128)S(1)} %get-tuple-element.55), channel_id=1, source_target_pairs={{2,0},{4,2},{6,4},{3,1},{5,3},{7,5},{10,8},{12,10},{14,12},{11,9},... | collective-permute-start | bytes 49160 | tf_op jit(solution)/shard_map/ppermute | solution.py:22
  57.8 4.4 %collective-permute-start.14 = (f32[4,1,18,128]{3,2,1,0:T(8,128)S(1)}, f32[4,1,18,128]{3,2,1,0:T(8,128)S(1)}, u32[]{:S(2)}, u32[]{:S(2)}) collective-permute-start(f32[4,1,18,128]{3,2,1,0:T(8,128)S(1)} %get-tuple-element.40), channel_id=1, source_target_pairs={{8,0},{16,8},{24,16},{0,24},{9,1},{17,9},{25,17},{1,25},{10,2},{18... | collective-permute-start | bytes 110600 | tf_op jit(solution)/shard_map/ppermute | solution.py:22
  57.9 5.9 %collective-permute-start.15 = (f32[4,1,18,128]{3,2,1,0:T(8,128)S(1)}, f32[4,1,18,128]{3,2,1,0:T(8,128)S(1)}, u32[]{:S(2)}, u32[]{:S(2)}) collective-permute-start(f32[4,1,18,128]{3,2,1,0:T(8,128)S(1)} %get-tuple-element.39), channel_id=1, source_target_pairs={{0,8},{8,16},{16,24},{24,0},{1,9},{9,17},{17,25},{25,1},{2,10},{10... | collective-permute-start | bytes 110600 | tf_op jit(solution)/shard_map/ppermute | solution.py:19
  64.1 1.9 %collective-permute-start.16 = (f32[4,10,18,1]{3,2,1,0:T(8,128)S(1)}, f32[4,10,18,1]{3,2,1,0:T(8,128)S(1)}, u32[]{:S(2)}, u32[]{:S(2)}) collective-permute-start(f32[4,10,18,1]{3,2,1,0:T(8,128)S(1)} %get-tuple-element.32), channel_id=1, source_target_pairs={{1,0},{0,1},{3,2},{2,3},{5,4},{4,5},{7,6},{6,7},{9,8},{8,9},{11,10... | collective-permute-start | bytes 8648 | tf_op jit(solution)/shard_map/ppermute | solution.py:22
  64.1 2.6 %collective-permute-start.17 = (f32[4,10,18,1]{3,2,1,0:T(8,128)S(1)}, f32[4,10,18,1]{3,2,1,0:T(8,128)S(1)}, u32[]{:S(2)}, u32[]{:S(2)}) collective-permute-start(f32[4,10,18,1]{3,2,1,0:T(8,128)S(1)} %get-tuple-element.33), channel_id=1, source_target_pairs={{0,1},{1,0},{2,3},{3,2},{4,5},{5,4},{6,7},{7,6},{8,9},{9,8},{10,11... | collective-permute-start | bytes 8648 | tf_op jit(solution)/shard_map/ppermute | solution.py:19
  67.3 75.3 %copy-start.2 = (f32[4,8,16,128]{3,2,1,0:T(8,128)}, f32[4,8,16,128]{3,2,1,0:T(8,128)S(1)}, u32[]{:S(2)}) copy-start(f32[4,8,16,128]{3,2,1,0:T(8,128)S(1)} %fusion.12) | copy-start | bytes 786436
where the time goes:
time: 143 us
  blocking collectives  38.7 us (27%)
  other arithmetic  33.7 us (24%)
  waiting for transfers between devices  28.2 us (20%)
  starting transfers between devices  25.9 us (18%)
  local copies, waits for them, and re-layouts  12.9 us (9%)
  matrix products  2.16 us (2%)
    psum x1, blocking collectives, local(): lax.psum((jnp.dot(old_modes, snap_flat, precision=lax.Precision.HIGHEST,...  38.7 us
    ppermute x9, waiting for transfers between devices, padded(): lax.ppermute(lax.slice_in_dim(block, 0, width, axis=dim), axis, backward)  18.6 us
    ppermute x9, starting transfers between devices, padded(): lax.ppermute(lax.slice_in_dim(block, block.shape[dim] - width, None, axis...  18.1 us
    another operation x3, other arithmetic, local(): lower = jnp.linalg.cholesky(gram)  12.4 us
    another operation x1, other arithmetic, local(): jax.scipy.linalg.solve_triangular(lower, stacked, lower=True)  9.81 us
    ppermute x9, waiting for transfers between devices, padded(): lax.ppermute(lax.slice_in_dim(block, block.shape[dim] - width, None, axis...  9.57 us
    ppermute x9, starting transfers between devices, padded(): lax.ppermute(lax.slice_in_dim(block, 0, width, axis=dim), axis, backward)  7.86 us
    slice x2, local copies, waits for them, and re-layouts, local(): velocity = flow_next[:3].reshape(3, -1)  4.71 us
  transfers between devices with their start and end apart: 18, of which 14 were waited for; matrix products, arithmetic and copies ran while one was open for 3% of the time, Pallas kernels for 0%

commit v1 on v0

v1 whole, which is shorter than its diff:
```python
import functools

import jax
import jax.numpy as jnp
from jax import lax
from jax.experimental import pallas as pl
from jax.experimental.pallas import tpu as pltpu
from jax.sharding import PartitionSpec as P

DT_STEP = 0.35
VISCOSITY = 0.2
SOUND_SQ = 1.0
DRIVING = 0.5

ALL = ("gx", "gy", "gz")
DEPTH = 3
GAP = 2
EXACT = lax.Precision.HIGHEST
VMEM = pl.BlockSpec(memory_space=pltpu.VMEM)
PARAMS = pltpu.CompilerParams(vmem_limit_bytes=40 * 1024 * 1024)


def dot(a, b, dims):
    return lax.dot_general(
        a, b, (dims, ((), ())), precision=EXACT, preferred_element_type=jnp.float32
    )


def neighbours(block_low, block_high, axis, periodic):
    count = lax.axis_size(axis)
    forward = [(i, i + 1) for i in range(count - 1)]
    if periodic:
        forward.append((count - 1, 0))
    backward = [(target, source) for source, target in forward]
    return lax.ppermute(block_high, axis, forward), lax.ppermute(block_low, axis, backward)


def gram_kernel(basis_ref, gram_ref):
    modes = basis_ref.shape[1]
    total = jnp.zeros((modes, modes), jnp.float32)
    for c in range(basis_ref.shape[0]):
        rows = basis_ref[c]
        total = total + dot(rows, rows, ((1,), (1,)))
    gram_ref[...] = jnp.zeros_like(gram_ref)
    gram_ref[0:modes, 0:modes] = total


def slabs(fields, planes):
    return [(f, i) for f in range(fields) for i in range(planes)]


def spread(index, depth):
    per = 128 // (2 * depth)
    return index // per, 2 * depth * (index % per)


def edges_kernel(flow_ref, ylo_ref, yhi_ref, xlo_ref, xhi_ref, ext_ref, packed_ref):
    fields, nx, ny, nz = flow_ref.shape
    rows = ext_ref.shape[2]
    ext_ref[:, 0:DEPTH] = xlo_ref[...]
    ext_ref[:, DEPTH + nx : 2 * DEPTH + nx] = xhi_ref[...]
    gap = jnp.zeros((GAP, nz), jnp.float32)
    for f, i in slabs(fields, nx):
        plane = jnp.concatenate([flow_ref[f, i], yhi_ref[f, i], gap, ylo_ref[f, i]], axis=0)
        ext_ref[f, DEPTH + i] = plane
    lane = lax.broadcasted_iota(jnp.int32, (rows, nz), 1)
    parts = [jnp.zeros((rows, nz), jnp.float32) for _ in range(packed_ref.shape[0])]
    for s, (f, i) in enumerate(slabs(fields, nx + 2 * DEPTH)):
        part, start = spread(s, DEPTH)
        moved = pltpu.roll(ext_ref[f, i], (start + DEPTH) % nz, 1)
        parts[part] = jnp.where((lane >= start) & (lane < start + 2 * DEPTH), moved, parts[part])
    for k, value in enumerate(parts):
        packed_ref[k] = value


def plane_step(read, i, rows, lanes):
    def step(value, by, axis):
        size = value.shape[axis]
        return pltpu.roll(value, (size - by) % size, axis)

    centre = [read(f, i) for f in range(4)]
    x_plus = [read(f, i + 1)[:rows, :lanes] for f in range(4)]
    x_minus = [read(f, i - 1)[:rows, :lanes] for f in range(4)]
    y_plus = [step(v, 1, 0)[:rows, :lanes] for v in centre]
    y_minus = [step(v, -1, 0)[:rows, :lanes] for v in centre]
    z_plus = [step(v[:rows], 1, 1)[:, :lanes] for v in centre]
    z_minus = [step(v[:rows], -1, 1)[:, :lanes] for v in centre]
    centre = [v[:rows, :lanes] for v in centre]
    slope_x = [0.5 * (a - b) for a, b in zip(x_plus, x_minus)]
    slope_y = [0.5 * (a - b) for a, b in zip(y_plus, y_minus)]
    slope_z = [0.5 * (a - b) for a, b in zip(z_plus, z_minus)]
    pressure = [slope_x[3], slope_y[3], slope_z[3]]
    out = []
    for f in range(3):
        laplace = (
            x_plus[f] + x_minus[f] + (y_plus[f] + y_minus[f]) + (z_plus[f] + z_minus[f]) - 6.0 * centre[f]
        )
        advect = centre[0] * slope_x[f] + centre[1] * slope_y[f] + centre[2] * slope_z[f]
        value = VISCOSITY * laplace - advect - pressure[f]
        if f == 0:
            value = value + DRIVING
        out.append(value)
    out.append(-SOUND_SQ * (slope_x[0] + slope_y[1] + slope_z[2]))
    return centre, out


def step_kernel(
    walls_ref, ext_ref, low_ref, high_ref, basis_ref, sample_ref, summed_ref,
    flow_ref, snap_ref, send_ref,
    halo_ref, one_ref, two_ref,
):
    fields, nx, ny, nz = flow_ref.shape
    rows = ext_ref.shape[2]
    modes = basis_ref.shape[1]
    lane = lax.broadcasted_iota(jnp.int32, (rows, nz), 1)
    row = lax.broadcasted_iota(jnp.int32, (rows, 2 * nz), 0)
    below = (row >= ny + DEPTH + GAP) & (walls_ref[0] == 1)
    above = (row >= ny) & (row < ny + DEPTH) & (walls_ref[1] == 1)
    outside = below | above

    around = [
        jnp.where(lane < nz // 2, high_ref[k], low_ref[k]) for k in range(low_ref.shape[0])
    ]
    for s, (f, i) in enumerate(slabs(fields, nx + 2 * DEPTH)):
        part, start = spread(s, DEPTH)
        halo_ref[f, i] = pltpu.roll(around[part], (2 * nz - start - DEPTH) % nz, 1)

    def read_ext(f, i):
        return jnp.concatenate([ext_ref[f, i], halo_ref[f, i]], axis=1)

    def read_one(f, i):
        return one_ref[f, i]

    def read_two(f, i):
        return two_ref[f, i]

    def first(i, carry):
        centre, rate = plane_step(read_ext, i, rows, 2 * nz)
        for f in range(4):
            one_ref[f, i] = jnp.where(outside, 0.0, centre[f] + DT_STEP * rate[f])
        return carry

    def second(i, carry):
        centre, rate = plane_step(read_one, i, rows, 2 * nz)
        for f in range(4):
            value = 0.75 * read_ext(f, i) + 0.25 * (centre[f] + DT_STEP * rate[f])
            two_ref[f, i] = jnp.where(outside, 0.0, value)
        return carry

    def third(i, carry):
        centre, rate = plane_step(read_two, i, ny, nz)
        for f in range(4):
            start = ext_ref[f, i][:ny]
            flow_ref[f, i - DEPTH] = 1.0 / 3.0 * start + 2.0 / 3.0 * (centre[f] + DT_STEP * rate[f])
        return carry

    lax.fori_loop(1, nx + 2 * DEPTH - 1, first, 0)
    lax.fori_loop(2, nx + 2 * DEPTH - 2, second, 0)
    lax.fori_loop(3, nx + 2 * DEPTH - 3, third, 0)

    points = sample_ref.shape[1]
    spot = jnp.broadcast_to(sample_ref[...], (nz, points))
    place = lax.broadcasted_iota(jnp.int32, (nx * ny, points), 0)
    in_row = (place == jnp.broadcast_to(sample_ref[...] // nz, (nx * ny, points))).astype(jnp.bfloat16)
    in_lane = lax.broadcasted_iota(jnp.int32, (nz, points), 0) == spot % nz
    cross = jnp.zeros((8, modes + 1), jnp.float32)
    for c in range(3):
        field = flow_ref[c].reshape(nx * ny, nz)
        high = field.astype(jnp.bfloat16)
        rest = field - high.astype(jnp.float32)
        middle = rest.astype(jnp.bfloat16)
        low = (rest - middle.astype(jnp.float32)).astype(jnp.bfloat16)
        found = sum(
            lax.dot_general(p, in_row, (((0,), (0,)), ((), ())), preferred_element_type=jnp.float32)
            for p in (high, middle, low)
        )
        picked = jnp.sum(jnp.where(in_lane, found, 0.0), axis=0, keepdims=True)
        snap_ref[c] = picked
        stacked = jnp.concatenate([basis_ref[c], picked], axis=0)
        cross = cross + dot(jnp.broadcast_to(picked, (8, points)), stacked, ((1,), (1,)))

    per = send_ref.shape[1] - 4
    summed = jnp.zeros((8, modes + 1), jnp.float32)
    for k in range(summed_ref.shape[0] // 8):
        summed = summed + summed_ref[8 * k : 8 * k + 8]
    summed = summed + pltpu.roll(summed, 4, 0)
    sub = lax.broadcasted_iota(jnp.int32, summed.shape, 0)
    block = jnp.where(sub < per, summed, jnp.where(sub == per, cross, 0.0))
    for d in range(send_ref.shape[0]):
        send_ref[d] = block


def final_kernel(count, got_ref, basis_ref, snap_ref, basis_out_ref, factor_ref, work_ref):
    modes = basis_ref.shape[1]
    size = modes + 1
    per = got_ref.shape[1] - 4
    cross = jnp.zeros((8, size), jnp.float32)
    for d in range(got_ref.shape[0]):
        block = got_ref[d]
        if per * d < size:
            work_ref[per * d : per * d + per, 0:size] = block[0:per] / count
        cross = cross + block
    cross = cross[per : per + 1] / count
    col = lax.broadcasted_iota(jnp.int32, (size, size), 1)
    row = lax.broadcasted_iota(jnp.int32, (size, size), 0)
    work_ref[size - 1 : size, 0:size] = cross
    mark = (lax.broadcasted_iota(jnp.int32, (8, size), 1) == size - 1).astype(jnp.float32)
    top = lax.broadcasted_iota(jnp.int32, (8, size), 0) == 0
    side = dot(jnp.where(top, jnp.broadcast_to(cross, (8, size)), 0.0), mark, ((0,), (0,)))
    work_ref[:, 0:size] = jnp.where(col == size - 1, side, work_ref[:, 0:size])
    work_ref[:, size : 2 * size] = (row == col).astype(jnp.float32)

    tall = 8
    sub = lax.broadcasted_iota(jnp.int32, (tall, 1), 0)
    for p in range(size // tall):
        panel = work_ref[tall * p : tall * p + tall, :]
        for j in range(tall):
            c = tall * p + j
            scale = lax.rsqrt(panel[j : j + 1, c : c + 1])
            scaled = panel[j : j + 1, :] * scale
            times = jnp.where(sub > j, panel[:, c : c + 1] * scale, 0.0)
            panel = jnp.where(sub == j, scaled, panel - times * scaled)
        work_ref[tall * p : tall * p + tall, :] = panel
        if tall * (p + 1) < size:
            change = dot(panel[:, 0:size], panel, ((0,), (0,)))
            work_ref[tall * (p + 1) : size, :] = work_ref[tall * (p + 1) : size, :] - change[tall * (p + 1) : size]
    factor_ref[...] = jnp.where(col >= row, work_ref[:, 0:size], 0.0)
    inverse = work_ref[:, size : 2 * size]
    for c in range(basis_ref.shape[0]):
        stacked = jnp.concatenate([basis_ref[c], snap_ref[c]], axis=0)
        basis_out_ref[c] = dot(inverse, stacked, ((1,), (0,)))


def local(flow, basis, sample):
    fields, nx, ny, nz = flow.shape
    modes, comps, points = basis.shape
    size = modes + 1
    devices = lax.axis_size("gx") * lax.axis_size("gy") * lax.axis_size("gz")
    count = float(comps * points * devices)
    shape = functools.partial(jax.ShapeDtypeStruct, dtype=jnp.float32)
    call = functools.partial(pl.pallas_call, compiler_params=PARAMS)
    bricks = jnp.transpose(basis, (1, 0, 2))

    ylo, yhi = neighbours(flow[:, :, :DEPTH], flow[:, :, ny - DEPTH :], "gy", False)
    gram = call(gram_kernel, out_shape=shape((size, size)), in_specs=[VMEM], out_specs=VMEM)(bricks)

    gap = jnp.zeros((fields, DEPTH, GAP, nz), jnp.float32)

    def face(start):
        part = slice(start, start + DEPTH)
        return jnp.concatenate([flow[:, part], yhi[:, part], gap, ylo[:, part]], axis=2)

    xlo, xhi = neighbours(face(0), face(nx - DEPTH), "gx", True)

    per = 4
    sent = jnp.pad(gram, ((0, per * devices - size), (0, 0))) if per * devices > size else gram
    summed = lax.all_to_all(sent.reshape(devices, per, size), ALL, 0, 0).reshape(devices * per, size)

    rows = ny + 2 * DEPTH + GAP
    planes = nx + 2 * DEPTH
    parts = -(-fields * planes // (nz // (2 * DEPTH)))
    ext, packed = call(
        edges_kernel,
        out_shape=(shape((fields, planes, rows, nz)), shape((parts, rows, nz))),
        in_specs=[VMEM] * 5,
        out_specs=(VMEM, VMEM),
    )(flow, ylo, yhi, xlo, xhi)
    if lax.axis_size("gz") == 2:
        low = high = lax.ppermute(packed, "gz", [(0, 1), (1, 0)])
    else:
        low, high = neighbours(packed, packed, "gz", True)

    place = lax.axis_index("gy")
    walls = jnp.stack([place == 0, place == lax.axis_size("gy") - 1]).astype(jnp.int32)
    wide = pltpu.VMEM((fields, planes, rows, 2 * nz), jnp.float32)
    flow_next, snapshot, send = call(
        step_kernel,
        out_shape=(shape(flow.shape), shape((comps, 1, points)), shape((devices, per + 4, size))),
        in_specs=[pl.BlockSpec(memory_space=pltpu.SMEM)] + [VMEM] * 6,
        out_specs=(VMEM, VMEM, VMEM),
        scratch_shapes=[pltpu.VMEM((fields, planes, rows, nz), jnp.float32), wide, wide],
    )(walls, ext, low, high, bricks, sample.reshape(1, points), summed)

    got = lax.all_to_all(send, ALL, 0, 0)
    basis_next, factor = call(
        functools.partial(final_kernel, count),
        out_shape=(shape((comps, size, points)), shape((size, size))),
        in_specs=[VMEM] * 3,
        out_specs=(VMEM, VMEM),
        scratch_shapes=[pltpu.VMEM((size, 2 * size), jnp.float32)],
    )(got, bricks, snapshot)
    return flow_next, jnp.transpose(basis_next, (1, 0, 2)), factor


def solution(mesh):
    return jax.shard_map(
        local,
        mesh=mesh,
        in_specs=(
            P(None, "gx", "gy", "gz"),
            P(None, None, ("gx", "gy", "gz")),
            P(("gx", "gy", "gz")),
        ),
        out_specs=(P(None, "gx", "gy", "gz"), P(None, None, ("gx", "gy", "gz")), P()),
        check_vma=False,
    )
```

time: 143 us -> 63.3 us (0.44)
  other arithmetic: 33.7 us -> 0.17 us
  blocking collectives: 38.7 us -> 9.92 us
  Pallas kernels: 0 us -> 24.6 us
  waiting for transfers between devices: 28.2 us -> 8.49 us
  local copies, waits for them, and re-layouts: 12.9 us -> 1.83 us
  starting transfers between devices: 25.9 us -> 17.3 us
  matrix products: 2.16 us -> 0 us
    psum x1 -> x0, blocking collectives: 38.7 us -> none  [local(): lax.psum((jnp.dot(old_modes, snap_flat, precision=lax.Precision.HIGHEST,...]
    ppermute x18 -> x5, waiting for transfers between devices: 28.2 us -> 1.76 us  [the longest x2 1.57 us: neighbours(): lax.ppermute(block_high, axis, forward)]
    pallas_call x0 -> x4, Pallas kernels: none -> 24.6 us  [the longest x1 17.2 us: local(): call(functools.partial(final_kernel, count), out_shape=(shape((comps, siz...]
    another operation x4 -> x0, other arithmetic: 22.2 us -> none  [the longest x3 12.4 us: local(): lower = jnp.linalg.cholesky(gram)]
    ppermute x18 -> x5, starting transfers between devices: 25.9 us -> 11.3 us  [the longest x2 7.63 us: neighbours(): lax.ppermute(block_high, axis, forward)]
    all_to_all x0 -> x1, blocking collectives: none -> 9.92 us  [local(): got = lax.all_to_all(send, ALL, 0, 0)]
    all_to_all x0 -> x1, waiting for transfers between devices: none -> 6.73 us  [local(): lax.all_to_all(sent.reshape(devices, per, size), ALL, 0, 0)]
    all_to_all x0 -> x1, starting transfers between devices: none -> 5.94 us  [local(): lax.all_to_all(sent.reshape(devices, per, size), ALL, 0, 0)]
  transfers between devices with their start and end apart: 18 -> 6, of which waited for: 14 -> 3; matrix products, arithmetic and copies ran while one was open for 3% -> 0% of each run, Pallas kernels for 0% -> 2%
where the time goes in v1:
time: 63.3 us; the launch traced here: 63 us
  Pallas kernels  24.6 us (39%)
  starting transfers between devices  17.3 us (27%)
  blocking collectives  9.92 us (16%)
  waiting for transfers between devices  8.49 us (13%)
  local copies, waits for them, and re-layouts  1.83 us (3%)
  between operations  0.74 us (1%)
    pallas_call x1, Pallas kernels, local(): call(functools.partial(final_kernel, count), out_shape=(shape((comps, siz...  17.2 us
    all_to_all x1, blocking collectives, local(): got = lax.all_to_all(send, ALL, 0, 0)  9.92 us
    ppermute x2, starting transfers between devices, neighbours(): lax.ppermute(block_high, axis, forward)  7.63 us
    all_to_all x1, waiting for transfers between devices, local(): lax.all_to_all(sent.reshape(devices, per, size), ALL, 0, 0)  6.73 us
    pallas_call x1, Pallas kernels, local(): call(step_kernel, out_shape=(shape(flow.shape), shape((comps, 1, points))...  6.04 us
    all_to_all x1, starting transfers between devices, local(): lax.all_to_all(sent.reshape(devices, per, size), ALL, 0, 0)  5.94 us
    ppermute x2, starting transfers between devices, neighbours(): lax.ppermute(block_low, axis, backward)  3.38 us
    ppermute x2, waiting for transfers between devices, neighbours(): lax.ppermute(block_high, axis, forward)  1.57 us
  transfers between devices with their start and end apart: 6, of which 3 were waited for; matrix products, arithmetic and copies ran while one was open for 0% of the time, Pallas kernels for 2%

profile of v1, /device:TPU:0, one launch (start us, length us, event | category | flops | bytes accessed | tf_op | source)
XLA Modules:
  0.0 63.0 jit_solution(17723792507258950113)
XLA Ops:
  0.6 0.0 copy-start.1
  0.6 1.0 %fusion.1 = (f32[4,8,3,128]{3,2,1,0:T(4,128)S(1)}, f32[4,8,3,128]{3,2,1,0:T(4,128)S(1)}) fusion(f32[4,8,16,128]{3,2,1,0:T(8,128)} %flow_ref.1), kind=kLoop, calls=%fused_computation.4 | loop fusion | bytes 196608 | tf_op jit(solution)/shard_map/slice | solution.py:244
  1.7 1.3 %collective-permute-start.1 = (f32[4,8,3,128]{3,2,1,0:T(4,128)S(1)}, f32[4,8,3,128]{3,2,1,0:T(4,128)S(1)}, u32[]{:S(2)}, u32[]{:S(2)}) collective-permute-start(f32[4,8,3,128]{3,2,1,0:T(4,128)S(1)} %get-tuple-element.19), channel_id=1, source_target_pairs={{2,0},{4,2},{6,4},{3,1},{5,3},{7,5},{10,8},{12,10},{14,12},{11,9},... | collective-permute-start | bytes 147464 | tf_op jit(solution)/shard_map/ppermute | solution.py:35
  3.0 5.5 %collective-permute-start = (f32[4,8,3,128]{3,2,1,0:T(4,128)S(1)}, f32[4,8,3,128]{3,2,1,0:T(4,128)S(1)}, u32[]{:S(2)}, u32[]{:S(2)}) collective-permute-start(f32[4,8,3,128]{3,2,1,0:T(4,128)S(1)} %get-tuple-element.20), channel_id=1, source_target_pairs={{0,2},{2,4},{4,6},{1,3},{3,5},{5,7},{8,10},{10,12},{12,14},{9,11},... | collective-permute-start | bytes 147464 | tf_op jit(solution)/shard_map/ppermute | solution.py:35
  8.5 0.0 copy-done.1
  8.5 0.1 pad.6.clone
  8.6 0.2 collective-permute-done.1.yhi_ref
  8.8 1.6 %collective-permute-done.ylo_ref = f32[4,8,3,128]{3,2,1,0:T(4,128)S(1)} collective-permute-done((f32[4,8,3,128]{3,2,1,0:T(4,128)S(1)}, f32[4,8,3,128]{3,2,1,0:T(4,128)S(1)}, u32[]{:S(2)}, u32[]{:S(2)}) %collective-permute-start) | collective-permute-done | bytes 49184 | tf_op jit(solution)/shard_map/ppermute | solution.py:35
  10.4 0.1 pad_maximum_fusion.1
  10.5 2.2 %collective-permute-start.2 = (f32[4,3,24,128]{3,2,1,0:T(8,128)S(1)}, f32[4,3,24,128]{3,2,1,0:T(8,128)S(1)}, u32[]{:S(2)}, u32[]{:S(2)}) collective-permute-start(f32[4,3,24,128]{3,2,1,0:T(8,128)S(1)} %get-tuple-element.26), channel_id=1, source_target_pairs={{0,8},{8,16},{16,24},{24,0},{1,9},{9,17},{17,25},{25,1},{2,10},{10... | collective-permute-start | bytes 442376 | tf_op jit(solution)/shard_map/ppermute | solution.py:35
  12.6 2.1 %collective-permute-start.3 = (f32[4,3,24,128]{3,2,1,0:T(8,128)S(1)}, f32[4,3,24,128]{3,2,1,0:T(8,128)S(1)}, u32[]{:S(2)}, u32[]{:S(2)}) collective-permute-start(f32[4,3,24,128]{3,2,1,0:T(8,128)S(1)} %get-tuple-element.25), channel_id=1, source_target_pairs={{8,0},{16,8},{24,16},{0,24},{9,1},{17,9},{25,17},{1,25},{10,2},{18... | collective-permute-start | bytes 442376 | tf_op jit(solution)/shard_map/ppermute | solution.py:35
  14.7 1.1 %shard_map.59 = f32[128,128]{1,0:T(8,128)} custom-call(f32[3,127,256]{2,1,0:T(8,128)S(1)} %bitcast.7), custom_call_target="tpu_custom_call" | custom-call | tf_op jit(solution)/shard_map/pallas_call | solution.py:245
  15.8 5.9 %all-to-all-start = ((f32[32,4,128]{2,1,0:T(4,128)}), f32[32,4,128]{2,1,0:T(4,128)S(1)}, u32[]{:S(2)}, u32[]{:S(2)}) async-start(f32[32,4,128]{2,1,0:T(4,128)} %bitcast.4), calls=%async_computation | async-start | bytes 131072 | tf_op jit(solution)/shard_map/all_to_all | solution.py:257
  21.8 0.0 collective-permute-done.2.xlo_ref
  21.8 0.0 collective-permute-done.3.xhi_ref
  21.8 0.2 shard_map.58
  22.1 0.3 collective-permute-start.4
  22.4 0.1 add_convert_fusion.walls_ref
  22.4 6.7 %all-to-all-done = f32[32,4,128]{2,1,0:T(4,128)S(1)} async-done(((f32[32,4,128]{2,1,0:T(4,128)}), f32[32,4,128]{2,1,0:T(4,128)S(1)}, u32[]{:S(2)}, u32[]{:S(2)}) %all-to-all-start) | async-done | bytes 65568 | tf_op jit(solution)/shard_map/all_to_all | solution.py:257
  29.2 0.0 collective-permute-done.4.low_ref.high_ref
  29.2 0.7 %copy-done.2 = s32[256]{0:T(256)S(1)} copy-done((s32[256]{0:T(256)S(1)}, s32[256]{0:T(256)}, u32[]{:S(2)}) %copy-start.2) | copy-done | bytes 1048
  29.9 6.0 %shard_map.60 = (f32[4,8,16,128]{3,2,1,0:T(8,128)}, f32[3,1,256]{2,1,0:T(1,128)S(1)}, f32[32,8,128]{2,1,0:T(8,128)S(1)}) custom-call(s32[2]{0:T(128)S(1)} %add_convert_fusion.walls_ref, f32[4,14,24,128]{3,2,1,0:T(8,128)S(1)} %get-tuple-element.10.ext_ref, f32[3,24,128]{2,1,0:T(8,128)S(1)} %collective-permute-done.4.low_ref.high_ref, ...), custom_call_target="tpu_custom_call" | custom-call | tf_op jit(solution)/shard_map/pallas_call | solution.py:276
  35.9 9.9 %all_to_all.10.got_ref = f32[32,8,128]{2,1,0:T(8,128)S(1)} all-to-all(f32[32,8,128]{2,1,0:T(8,128)S(1)} %get-tuple-element.13), channel_id=1, replica_groups=mesh['gx'=4,'gy'=4,'gz'=2] {'gx','gy','gz'}, dimensions={0} | all-to-all | bytes 262144 | tf_op jit(solution)/shard_map/all_to_all | solution.py:284
  45.8 17.2 %shard_map.61 = (f32[3,128,256]{2,1,0:T(8,128)}, f32[128,128]{1,0:T(8,128)}) custom-call(f32[32,8,128]{2,1,0:T(8,128)S(1)} %all_to_all.10.got_ref, f32[3,127,256]{2,1,0:T(8,128)S(1)} %bitcast.9, f32[3,1,256]{2,1,0:T(1,128)S(1)} %get-tuple-element.14.snap_ref), custom_call_target="tpu_custom_call" | custom-call | tf_op jit(solution)/shard_map/pallas_call | solution.py:285
  (7 shorter events, 0.0 us)
Async XLA Ops:
  0.6 7.8 %copy-start.1 = (f32[4,8,16,128]{3,2,1,0:T(8,128)S(1)}, f32[4,8,16,128]{3,2,1,0:T(8,128)}, u32[]{:S(2)}) copy-start(f32[4,8,16,128]{3,2,1,0:T(8,128)} %flow_ref.1) | copy-start | bytes 786436
  1.7 7.1 %collective-permute-start.1 = (f32[4,8,3,128]{3,2,1,0:T(4,128)S(1)}, f32[4,8,3,128]{3,2,1,0:T(4,128)S(1)}, u32[]{:S(2)}, u32[]{:S(2)}) collective-permute-start(f32[4,8,3,128]{3,2,1,0:T(4,128)S(1)} %get-tuple-element.19), channel_id=1, source_target_pairs={{2,0},{4,2},{6,4},{3,1},{5,3},{7,5},{10,8},{12,10},{14,12},{11,9},... | collective-permute-start | bytes 147464 | tf_op jit(solution)/shard_map/ppermute | solution.py:35
  3.0 7.4 %collective-permute-start = (f32[4,8,3,128]{3,2,1,0:T(4,128)S(1)}, f32[4,8,3,128]{3,2,1,0:T(4,128)S(1)}, u32[]{:S(2)}, u32[]{:S(2)}) collective-permute-start(f32[4,8,3,128]{3,2,1,0:T(4,128)S(1)} %get-tuple-element.20), channel_id=1, source_target_pairs={{0,2},{2,4},{4,6},{1,3},{3,5},{5,7},{8,10},{10,12},{12,14},{9,11},... | collective-permute-start | bytes 147464 | tf_op jit(solution)/shard_map/ppermute | solution.py:35
  8.6 6.1 %copy-start = (f32[127,3,256]{2,0,1:T(8,128)S(1)}, f32[127,3,256]{2,0,1:T(8,128)}, u32[]{:S(2)}) copy-start(f32[127,3,256]{2,0,1:T(8,128)} %param.4) | copy-start | bytes 1170436
  10.5 11.3 %collective-permute-start.2 = (f32[4,3,24,128]{3,2,1,0:T(8,128)S(1)}, f32[4,3,24,128]{3,2,1,0:T(8,128)S(1)}, u32[]{:S(2)}, u32[]{:S(2)}) collective-permute-start(f32[4,3,24,128]{3,2,1,0:T(8,128)S(1)} %get-tuple-element.26), channel_id=1, source_target_pairs={{0,8},{8,16},{16,24},{24,0},{1,9},{9,17},{17,25},{25,1},{2,10},{10... | collective-permute-start | bytes 442376 | tf_op jit(solution)/shard_map/ppermute | solution.py:35
  12.6 9.2 %collective-permute-start.3 = (f32[4,3,24,128]{3,2,1,0:T(8,128)S(1)}, f32[4,3,24,128]{3,2,1,0:T(8,128)S(1)}, u32[]{:S(2)}, u32[]{:S(2)}) collective-permute-start(f32[4,3,24,128]{3,2,1,0:T(8,128)S(1)} %get-tuple-element.25), channel_id=1, source_target_pairs={{8,0},{16,8},{24,16},{0,24},{9,1},{17,9},{25,17},{1,25},{10,2},{18... | collective-permute-start | bytes 442376 | tf_op jit(solution)/shard_map/ppermute | solution.py:35
  15.8 13.4 %all-to-all-start = ((f32[32,4,128]{2,1,0:T(4,128)}), f32[32,4,128]{2,1,0:T(4,128)S(1)}, u32[]{:S(2)}, u32[]{:S(2)}) async-start(f32[32,4,128]{2,1,0:T(4,128)} %bitcast.4), calls=%async_computation | async-start | bytes 131072 | tf_op jit(solution)/shard_map/all_to_all | solution.py:257
  22.1 7.1 %collective-permute-start.4 = (f32[3,24,128]{2,1,0:T(8,128)S(1)}, f32[3,24,128]{2,1,0:T(8,128)S(1)}, u32[]{:S(2)}, u32[]{:S(2)}) collective-permute-start(f32[3,24,128]{2,1,0:T(8,128)S(1)} %get-tuple-element.11), channel_id=1, source_target_pairs={{0,1},{1,0},{2,3},{3,2},{4,5},{5,4},{6,7},{7,6},{8,9},{9,8},{10,11... | collective-permute-start | bytes 110600 | tf_op jit(solution)/shard_map/ppermute | solution.py:269
  29.2 0.7 %copy-start.2 = (s32[256]{0:T(256)S(1)}, s32[256]{0:T(256)}, u32[]{:S(2)}) copy-start(s32[256]{0:T(256)} %param.5) | copy-start | bytes 3076

commit v2 on v1

--- a/solution.py
+++ b/solution.py
@@ -35,8 +35,12 @@
     return lax.ppermute(block_high, axis, forward), lax.ppermute(block_low, axis, backward)
 
 
-def gram_kernel(basis_ref, gram_ref):
+def first_kernel(basis_ref, flow_ref, sample_ref, gram_ref, bottom_ref, top_ref, cell_ref):
     modes = basis_ref.shape[1]
+    ny = flow_ref.shape[2]
+    bottom_ref[...] = flow_ref[:, :, 0:DEPTH]
+    top_ref[...] = flow_ref[:, :, ny - DEPTH : ny]
+    cell_ref[...] = sample_ref[...]
     total = jnp.zeros((modes, modes), jnp.float32)
     for c in range(basis_ref.shape[0]):
         rows = basis_ref[c]
@@ -190,6 +194,37 @@
         send_ref[d] = block
 
 
+def eliminate(work_ref, tall):
+    size = work_ref.shape[0]
+    blocks = tall // 8
+    sub = lax.broadcasted_iota(jnp.int32, (8, 1), 0)
+    for base in range(0, size, tall):
+        panel = [work_ref[base + 8 * b : base + 8 * b + 8, :] for b in range(blocks)]
+        column = [
+            [jnp.broadcast_to(panel[b][:, base + k : base + k + 1], (8, 128)) for b in range(blocks)]
+            for k in range(tall)
+        ]
+        for j in range(tall):
+            mine, at = divmod(j, 8)
+            scale = lax.rsqrt(column[j][mine][at : at + 1, :])
+            times = {b: column[j][b] * scale for b in range(mine, blocks)}
+            times[mine] = jnp.where(sub > at, times[mine], 0.0)
+            scaled = panel[mine][at : at + 1, :] * jnp.concatenate([scale, scale], axis=1)
+            for b in range(mine, blocks):
+                value = panel[b] - jnp.concatenate([times[b], times[b]], axis=1) * scaled
+                panel[b] = jnp.where(sub == at, scaled, value) if b == mine else value
+            for k in range(j + 1, tall):
+                other, place = divmod(k, 8)
+                for b in range(other, blocks):
+                    column[k][b] = column[k][b] - times[b] * times[other][place : place + 1, :]
+        for b in range(blocks):
+            work_ref[base + 8 * b : base + 8 * b + 8, :] = panel[b]
+        if base + tall < size:
+            done = work_ref[base : base + tall, :]
+            change = dot(done[:, 0:size], done, ((0,), (0,)))
+            work_ref[base + tall : size, :] = work_ref[base + tall : size, :] - change[base + tall : size]
+
+
 def final_kernel(count, got_ref, basis_ref, snap_ref, basis_out_ref, factor_ref, work_ref):
     modes = basis_ref.shape[1]
     size = modes + 1
@@ -210,20 +245,7 @@
     work_ref[:, 0:size] = jnp.where(col == size - 1, side, work_ref[:, 0:size])
     work_ref[:, size : 2 * size] = (row == col).astype(jnp.float32)
 
-    tall = 8
-    sub = lax.broadcasted_iota(jnp.int32, (tall, 1), 0)
-    for p in range(size // tall):
-        panel = work_ref[tall * p : tall * p + tall, :]
-        for j in range(tall):
-            c = tall * p + j
-            scale = lax.rsqrt(panel[j : j + 1, c : c + 1])
-            scaled = panel[j : j + 1, :] * scale
-            times = jnp.where(sub > j, panel[:, c : c + 1] * scale, 0.0)
-            panel = jnp.where(sub == j, scaled, panel - times * scaled)
-        work_ref[tall * p : tall * p + tall, :] = panel
-        if tall * (p + 1) < size:
-            change = dot(panel[:, 0:size], panel, ((0,), (0,)))
-            work_ref[tall * (p + 1) : size, :] = work_ref[tall * (p + 1) : size, :] - change[tall * (p + 1) : size]
+    eliminate(work_ref, 32)
     factor_ref[...] = jnp.where(col >= row, work_ref[:, 0:size], 0.0)
     inverse = work_ref[:, size : 2 * size]
     for c in range(basis_ref.shape[0]):
@@ -241,8 +263,14 @@
     call = functools.partial(pl.pallas_call, compiler_params=PARAMS)
     bricks = jnp.transpose(basis, (1, 0, 2))
 
-    ylo, yhi = neighbours(flow[:, :, :DEPTH], flow[:, :, ny - DEPTH :], "gy", False)
-    gram = call(gram_kernel, out_shape=shape((size, size)), in_specs=[VMEM], out_specs=VMEM)(bricks)
+    strip = shape((fields, nx, DEPTH, nz))
+    gram, bottom, top, cells = call(
+        first_kernel,
+        out_shape=(shape((size, size)), strip, strip, jax.ShapeDtypeStruct((1, points), sample.dtype)),
+        in_specs=[VMEM] * 3,
+        out_specs=(VMEM,) * 4,
+    )(bricks, flow, sample.reshape(1, points))
+    ylo, yhi = neighbours(bottom, top, "gy", False)
 
     gap = jnp.zeros((fields, DEPTH, GAP, nz), jnp.float32)
 
@@ -279,7 +307,7 @@
         in_specs=[pl.BlockSpec(memory_space=pltpu.SMEM)] + [VMEM] * 6,
         out_specs=(VMEM, VMEM, VMEM),
         scratch_shapes=[pltpu.VMEM((fields, planes, rows, nz), jnp.float32), wide, wide],
-    )(walls, ext, low, high, bricks, sample.reshape(1, points), summed)
+    )(walls, ext, low, high, bricks, cells, summed)
 
     got = lax.all_to_all(send, ALL, 0, 0)
     basis_next, factor = call(

time: 63.3 us -> 52 us (0.82)
  Pallas kernels: 24.6 us -> 12.4 us
  local copies, waits for them, and re-layouts: 1.83 us -> 2.74 us
    pallas_call x1, Pallas kernels: 17.2 us -> 4.93 us  [local(): call(functools.partial(final_kernel, count), out_shape=(shape((comps, siz...]
    unnamed x6 -> x10, local copies, waits for them, and re-layouts: 0.69 us -> 2.63 us
    slice x1 -> x0, local copies, waits for them, and re-layouts: 1.04 us -> none  [local(): flow[:, :, :DEPTH]]
  transfers between devices with their start and end apart: 6 -> 6, of which waited for: 3 -> 3; matrix products, arithmetic and copies ran while one was open for 0% -> 0% of each run, Pallas kernels for 2% -> 0%
where the time goes in v2:
time: 52 us; the launch traced here: 51.7 us
  starting transfers between devices  17.3 us (33%)
  Pallas kernels  12.4 us (24%)
  blocking collectives  9.92 us (19%)
  waiting for transfers between devices  8.49 us (16%)
  local copies, waits for them, and re-layouts  2.74 us (5%)
  between operations  0.75 us (1%)
    all_to_all x1, blocking collectives, local(): got = lax.all_to_all(send, ALL, 0, 0)  9.92 us
    ppermute x2, starting transfers between devices, neighbours(): lax.ppermute(block_high, axis, forward)  7.62 us
    all_to_all x1, waiting for transfers between devices, local(): lax.all_to_all(sent.reshape(devices, per, size), ALL, 0, 0)  6.72 us
    pallas_call x1, Pallas kernels, local(): call(step_kernel, out_shape=(shape(flow.shape), shape((comps, 1, points))...  6.04 us
    all_to_all x1, starting transfers between devices, local(): lax.all_to_all(sent.reshape(devices, per, size), ALL, 0, 0)  5.95 us
    pallas_call x1, Pallas kernels, local(): call(functools.partial(final_kernel, count), out_shape=(shape((comps, siz...  4.93 us
    ppermute x2, starting transfers between devices, neighbours(): lax.ppermute(block_low, axis, backward)  3.37 us
    unnamed x10, local copies, waits for them, and re-layouts  2.63 us
  transfers between devices with their start and end apart: 6, of which 3 were waited for; matrix products, arithmetic and copies ran while one was open for 0% of the time, Pallas kernels for 0%

profile of v2, /device:TPU:0, one launch (start us, length us, event | category | flops | bytes accessed | tf_op | source)
XLA Modules:
  0.0 51.7 jit_solution(15313354987670900120)
XLA Ops:
  0.6 0.7 %copy-done.4 = s32[256]{0:T(256)S(1)} copy-done((s32[256]{0:T(256)S(1)}, s32[256]{0:T(256)}, u32[]{:S(2)}) %copy-start.4) | copy-done | bytes 1048
  1.3 1.0 %copy-done = f32[127,3,256]{2,0,1:T(8,128)S(1)} copy-done((f32[127,3,256]{2,0,1:T(8,128)S(1)}, f32[127,3,256]{2,0,1:T(8,128)}, u32[]{:S(2)}) %copy-start) | copy-done | bytes 390168
  2.3 0.9 %copy-done.2 = f32[4,8,16,128]{3,2,1,0:T(8,128)S(1)} copy-done((f32[4,8,16,128]{3,2,1,0:T(8,128)S(1)}, f32[4,8,16,128]{3,2,1,0:T(8,128)}, u32[]{:S(2)}) %copy-start.2) | copy-done | bytes 262168
  3.3 1.1 %shard_map.58 = (f32[128,128]{1,0:T(8,128)}, f32[4,8,3,128]{3,2,1,0:T(4,128)S(1)}, f32[4,8,3,128]{3,2,1,0:T(4,128)S(1)}, s32[1,256]{1,0:T(1,128)S(1)}) custom-call(f32[3,127,256]{2,1,0:T(8,128)S(1)} %bitcast.7, f32[4,8,16,128]{3,2,1,0:T(8,128)S(1)} %copy-done.2, s32[1,256]{1,0:T(1,128)S(1)} %bitcast.11), custom_call_target="tpu_custom_call" | custom-call | tf_op jit(solution)/shard_map/pallas_call | solution.py:267
  4.4 1.3 %collective-permute-start.1 = (f32[4,8,3,128]{3,2,1,0:T(4,128)S(1)}, f32[4,8,3,128]{3,2,1,0:T(4,128)S(1)}, u32[]{:S(2)}, u32[]{:S(2)}) collective-permute-start(f32[4,8,3,128]{3,2,1,0:T(4,128)S(1)} %get-tuple-element.15), channel_id=1, source_target_pairs={{2,0},{4,2},{6,4},{3,1},{5,3},{7,5},{10,8},{12,10},{14,12},{11,9},... | collective-permute-start | bytes 147464 | tf_op jit(solution)/shard_map/ppermute | solution.py:35
  5.7 5.5 %collective-permute-start = (f32[4,8,3,128]{3,2,1,0:T(4,128)S(1)}, f32[4,8,3,128]{3,2,1,0:T(4,128)S(1)}, u32[]{:S(2)}, u32[]{:S(2)}) collective-permute-start(f32[4,8,3,128]{3,2,1,0:T(4,128)S(1)} %get-tuple-element.14), channel_id=1, source_target_pairs={{0,2},{2,4},{4,6},{1,3},{3,5},{5,7},{8,10},{10,12},{12,14},{9,11},... | collective-permute-start | bytes 147464 | tf_op jit(solution)/shard_map/ppermute | solution.py:35
  11.2 0.1 pad.6.clone
  11.3 0.2 collective-permute-done.1.yhi_ref
  11.5 1.6 %collective-permute-done.ylo_ref = f32[4,8,3,128]{3,2,1,0:T(4,128)S(1)} collective-permute-done((f32[4,8,3,128]{3,2,1,0:T(4,128)S(1)}, f32[4,8,3,128]{3,2,1,0:T(4,128)S(1)}, u32[]{:S(2)}, u32[]{:S(2)}) %collective-permute-start) | collective-permute-done | bytes 49184 | tf_op jit(solution)/shard_map/ppermute | solution.py:35
  13.1 0.0 copy-start.3
  13.1 0.1 pad_maximum_fusion.1
  13.2 2.1 %collective-permute-start.2 = (f32[4,3,24,128]{3,2,1,0:T(8,128)S(1)}, f32[4,3,24,128]{3,2,1,0:T(8,128)S(1)}, u32[]{:S(2)}, u32[]{:S(2)}) collective-permute-start(f32[4,3,24,128]{3,2,1,0:T(8,128)S(1)} %get-tuple-element.32), channel_id=1, source_target_pairs={{0,8},{8,16},{16,24},{24,0},{1,9},{9,17},{17,25},{25,1},{2,10},{10... | collective-permute-start | bytes 442376 | tf_op jit(solution)/shard_map/ppermute | solution.py:35
  15.3 2.1 %collective-permute-start.3 = (f32[4,3,24,128]{3,2,1,0:T(8,128)S(1)}, f32[4,3,24,128]{3,2,1,0:T(8,128)S(1)}, u32[]{:S(2)}, u32[]{:S(2)}) collective-permute-start(f32[4,3,24,128]{3,2,1,0:T(8,128)S(1)} %get-tuple-element.31), channel_id=1, source_target_pairs={{8,0},{16,8},{24,16},{0,24},{9,1},{17,9},{25,17},{1,25},{10,2},{18... | collective-permute-start | bytes 442376 | tf_op jit(solution)/shard_map/ppermute | solution.py:35
  17.4 5.9 %all-to-all-start = ((f32[32,4,128]{2,1,0:T(4,128)}), f32[32,4,128]{2,1,0:T(4,128)S(1)}, u32[]{:S(2)}, u32[]{:S(2)}) async-start(f32[32,4,128]{2,1,0:T(4,128)} %bitcast.4), calls=%async_computation | async-start | bytes 131072 | tf_op jit(solution)/shard_map/all_to_all | solution.py:285
  23.4 0.0 collective-permute-done.2.xlo_ref
  23.4 0.0 collective-permute-done.3.xhi_ref
  23.4 0.2 shard_map.59
  23.7 0.3 collective-permute-start.4
  24.0 0.1 add_convert_fusion.walls_ref
  24.1 6.7 %all-to-all-done = f32[32,4,128]{2,1,0:T(4,128)S(1)} async-done(((f32[32,4,128]{2,1,0:T(4,128)}), f32[32,4,128]{2,1,0:T(4,128)S(1)}, u32[]{:S(2)}, u32[]{:S(2)}) %all-to-all-start) | async-done | bytes 65568 | tf_op jit(solution)/shard_map/all_to_all | solution.py:285
  30.8 0.0 collective-permute-done.4.low_ref.high_ref
  30.8 6.0 %shard_map.60 = (f32[4,8,16,128]{3,2,1,0:T(8,128)}, f32[3,1,256]{2,1,0:T(1,128)S(1)}, f32[32,8,128]{2,1,0:T(8,128)S(1)}) custom-call(s32[2]{0:T(128)S(1)} %add_convert_fusion.walls_ref, f32[4,14,24,128]{3,2,1,0:T(8,128)S(1)} %get-tuple-element.16.ext_ref, f32[3,24,128]{2,1,0:T(8,128)S(1)} %collective-permute-done.4.low_ref.high_ref, ...), custom_call_target="tpu_custom_call" | custom-call | tf_op jit(solution)/shard_map/pallas_call | solution.py:304
  36.8 9.9 %all_to_all.10.got_ref = f32[32,8,128]{2,1,0:T(8,128)S(1)} all-to-all(f32[32,8,128]{2,1,0:T(8,128)S(1)} %get-tuple-element.21), channel_id=1, replica_groups=mesh['gx'=4,'gy'=4,'gz'=2] {'gx','gy','gz'}, dimensions={0} | all-to-all | bytes 262144 | tf_op jit(solution)/shard_map/all_to_all | solution.py:312
  46.7 4.9 %shard_map.61 = (f32[3,128,256]{2,1,0:T(8,128)}, f32[128,128]{1,0:T(8,128)}) custom-call(f32[32,8,128]{2,1,0:T(8,128)S(1)} %all_to_all.10.got_ref, f32[3,127,256]{2,1,0:T(8,128)S(1)} %bitcast.9, f32[3,1,256]{2,1,0:T(1,128)S(1)} %get-tuple-element.22.snap_ref), custom_call_target="tpu_custom_call" | custom-call | tf_op jit(solution)/shard_map/pallas_call | solution.py:313
  (10 shorter events, 0.0 us)
Async XLA Ops:
  0.6 0.7 %copy-start.4 = (s32[256]{0:T(256)S(1)}, s32[256]{0:T(256)}, u32[]{:S(2)}) copy-start(s32[256]{0:T(256)} %param.5) | copy-start | bytes 3076
  1.3 1.0 %copy-start = (f32[127,3,256]{2,0,1:T(8,128)S(1)}, f32[127,3,256]{2,0,1:T(8,128)}, u32[]{:S(2)}) copy-start(f32[127,3,256]{2,0,1:T(8,128)} %param.4) | copy-start | bytes 1170436
  2.3 0.9 %copy-start.2 = (f32[4,8,16,128]{3,2,1,0:T(8,128)S(1)}, f32[4,8,16,128]{3,2,1,0:T(8,128)}, u32[]{:S(2)}) copy-start(f32[4,8,16,128]{3,2,1,0:T(8,128)} %flow_ref.3) | copy-start | bytes 786436
  4.4 7.1 %collective-permute-start.1 = (f32[4,8,3,128]{3,2,1,0:T(4,128)S(1)}, f32[4,8,3,128]{3,2,1,0:T(4,128)S(1)}, u32[]{:S(2)}, u32[]{:S(2)}) collective-permute-start(f32[4,8,3,128]{3,2,1,0:T(4,128)S(1)} %get-tuple-element.15), channel_id=1, source_target_pairs={{2,0},{4,2},{6,4},{3,1},{5,3},{7,5},{10,8},{12,10},{14,12},{11,9},... | collective-permute-start | bytes 147464 | tf_op jit(solution)/shard_map/ppermute | solution.py:35
  5.7 7.4 %collective-permute-start = (f32[4,8,3,128]{3,2,1,0:T(4,128)S(1)}, f32[4,8,3,128]{3,2,1,0:T(4,128)S(1)}, u32[]{:S(2)}, u32[]{:S(2)}) collective-permute-start(f32[4,8,3,128]{3,2,1,0:T(4,128)S(1)} %get-tuple-element.14), channel_id=1, source_target_pairs={{0,2},{2,4},{4,6},{1,3},{3,5},{5,7},{8,10},{10,12},{12,14},{9,11},... | collective-permute-start | bytes 147464 | tf_op jit(solution)/shard_map/ppermute | solution.py:35
  13.1 10.3 %copy-start.3 = (f32[4,8,16,128]{3,2,1,0:T(8,128)S(1)}, f32[4,8,16,128]{3,2,1,0:T(8,128)}, u32[]{:S(2)}) copy-start(f32[4,8,16,128]{3,2,1,0:T(8,128)} %flow_ref.3) | copy-start | bytes 786436
  13.2 10.2 %collective-permute-start.2 = (f32[4,3,24,128]{3,2,1,0:T(8,128)S(1)}, f32[4,3,24,128]{3,2,1,0:T(8,128)S(1)}, u32[]{:S(2)}, u32[]{:S(2)}) collective-permute-start(f32[4,3,24,128]{3,2,1,0:T(8,128)S(1)} %get-tuple-element.32), channel_id=1, source_target_pairs={{0,8},{8,16},{16,24},{24,0},{1,9},{9,17},{17,25},{25,1},{2,10},{10... | collective-permute-start | bytes 442376 | tf_op jit(solution)/shard_map/ppermute | solution.py:35
  15.3 8.1 %collective-permute-start.3 = (f32[4,3,24,128]{3,2,1,0:T(8,128)S(1)}, f32[4,3,24,128]{3,2,1,0:T(8,128)S(1)}, u32[]{:S(2)}, u32[]{:S(2)}) collective-permute-start(f32[4,3,24,128]{3,2,1,0:T(8,128)S(1)} %get-tuple-element.31), channel_id=1, source_target_pairs={{8,0},{16,8},{24,16},{0,24},{9,1},{17,9},{25,17},{1,25},{10,2},{18... | collective-permute-start | bytes 442376 | tf_op jit(solution)/shard_map/ppermute | solution.py:35
  17.4 13.4 %copy-start.1 = (f32[127,3,256]{2,0,1:T(8,128)S(1)}, f32[127,3,256]{2,0,1:T(8,128)}, u32[]{:S(2)}) copy-start(f32[127,3,256]{2,0,1:T(8,128)} %param.4) | copy-start | bytes 1170436
  17.4 13.4 %all-to-all-start = ((f32[32,4,128]{2,1,0:T(4,128)}), f32[32,4,128]{2,1,0:T(4,128)S(1)}, u32[]{:S(2)}, u32[]{:S(2)}) async-start(f32[32,4,128]{2,1,0:T(4,128)} %bitcast.4), calls=%async_computation | async-start | bytes 131072 | tf_op jit(solution)/shard_map/all_to_all | solution.py:285
  23.7 7.1 %collective-permute-start.4 = (f32[3,24,128]{2,1,0:T(8,128)S(1)}, f32[3,24,128]{2,1,0:T(8,128)S(1)}, u32[]{:S(2)}, u32[]{:S(2)}) collective-permute-start(f32[3,24,128]{2,1,0:T(8,128)S(1)} %get-tuple-element.17), channel_id=1, source_target_pairs={{0,1},{1,0},{2,3},{3,2},{4,5},{5,4},{6,7},{7,6},{8,9},{9,8},{10,11... | collective-permute-start | bytes 110600 | tf_op jit(solution)/shard_map/ppermute | solution.py:297

commit v3 on v2

--- a/solution.py
+++ b/solution.py
@@ -35,18 +35,23 @@
     return lax.ppermute(block_high, axis, forward), lax.ppermute(block_low, axis, backward)
 
 
-def first_kernel(basis_ref, flow_ref, sample_ref, gram_ref, bottom_ref, top_ref, cell_ref):
+def gram_kernel(basis_ref, gram_ref):
     modes = basis_ref.shape[1]
-    ny = flow_ref.shape[2]
-    bottom_ref[...] = flow_ref[:, :, 0:DEPTH]
-    top_ref[...] = flow_ref[:, :, ny - DEPTH : ny]
-    cell_ref[...] = sample_ref[...]
     total = jnp.zeros((modes, modes), jnp.float32)
     for c in range(basis_ref.shape[0]):
         rows = basis_ref[c]
         total = total + dot(rows, rows, ((1,), (1,)))
     gram_ref[...] = jnp.zeros_like(gram_ref)
     gram_ref[0:modes, 0:modes] = total
+
+
+def strips_kernel(flow_hbm, bottom_ref, top_ref, flow_ref, sem):
+    ny = flow_ref.shape[2]
+    copy = pltpu.make_async_copy(flow_hbm, flow_ref, sem)
+    copy.start()
+    copy.wait()
+    bottom_ref[...] = flow_ref[:, :, 0:DEPTH]
+    top_ref[...] = flow_ref[:, :, ny - DEPTH : ny]
 
 
 def slabs(fields, planes):
@@ -109,8 +114,8 @@
 
 
 def step_kernel(
-    walls_ref, ext_ref, low_ref, high_ref, basis_ref, sample_ref, summed_ref,
-    flow_ref, snap_ref, send_ref,
+    walls_ref, ext_ref, low_ref, high_ref, basis_ref, sample_ref,
+    flow_ref, snap_ref, cross_ref,
     halo_ref, one_ref, two_ref,
 ):
     fields, nx, ny, nz = flow_ref.shape
@@ -183,13 +188,17 @@
         stacked = jnp.concatenate([basis_ref[c], picked], axis=0)
         cross = cross + dot(jnp.broadcast_to(picked, (8, points)), stacked, ((1,), (1,)))
 
+    cross_ref[...] = cross
+
+
+def merge_kernel(summed_ref, cross_ref, send_ref):
     per = send_ref.shape[1] - 4
-    summed = jnp.zeros((8, modes + 1), jnp.float32)
+    summed = jnp.zeros(cross_ref.shape, jnp.float32)
     for k in range(summed_ref.shape[0] // 8):
         summed = summed + summed_ref[8 * k : 8 * k + 8]
     summed = summed + pltpu.roll(summed, 4, 0)
     sub = lax.broadcasted_iota(jnp.int32, summed.shape, 0)
-    block = jnp.where(sub < per, summed, jnp.where(sub == per, cross, 0.0))
+    block = jnp.where(sub < per, summed, jnp.where(sub == per, cross_ref[...], 0.0))
     for d in range(send_ref.shape[0]):
         send_ref[d] = block
 
@@ -264,13 +273,16 @@
     bricks = jnp.transpose(basis, (1, 0, 2))
 
     strip = shape((fields, nx, DEPTH, nz))
-    gram, bottom, top, cells = call(
-        first_kernel,
-        out_shape=(shape((size, size)), strip, strip, jax.ShapeDtypeStruct((1, points), sample.dtype)),
-        in_specs=[VMEM] * 3,
-        out_specs=(VMEM,) * 4,
-    )(bricks, flow, sample.reshape(1, points))
+    bottom, top = call(
+        strips_kernel,
+        out_shape=(strip, strip),
+        in_specs=[pl.BlockSpec(memory_space=pltpu.HBM)],
+        out_specs=(VMEM, VMEM),
+        scratch_shapes=[pltpu.VMEM(flow.shape, jnp.float32), pltpu.SemaphoreType.DMA],
+    )(flow)
     ylo, yhi = neighbours(bottom, top, "gy", False)
+    gram = call(gram_kernel, out_shape=shape((size, size)), in_specs=[VMEM], out_specs=VMEM)(bricks)
+    ylo, yhi, gram = lax.optimization_barrier((ylo, yhi, gram))
 
     gap = jnp.zeros((fields, DEPTH, GAP, nz), jnp.float32)
 
@@ -301,14 +313,17 @@
     place = lax.axis_index("gy")
     walls = jnp.stack([place == 0, place == lax.axis_size("gy") - 1]).astype(jnp.int32)
     wide = pltpu.VMEM((fields, planes, rows, 2 * nz), jnp.float32)
-    flow_next, snapshot, send = call(
+    flow_next, snapshot, cross = call(
         step_kernel,
-        out_shape=(shape(flow.shape), shape((comps, 1, points)), shape((devices, per + 4, size))),
-        in_specs=[pl.BlockSpec(memory_space=pltpu.SMEM)] + [VMEM] * 6,
+        out_shape=(shape(flow.shape), shape((comps, 1, points)), shape((8, size))),
+        in_specs=[pl.BlockSpec(memory_space=pltpu.SMEM)] + [VMEM] * 5,
         out_specs=(VMEM, VMEM, VMEM),
         scratch_shapes=[pltpu.VMEM((fields, planes, rows, nz), jnp.float32), wide, wide],
-    )(walls, ext, low, high, bricks, cells, summed)
-
+    )(walls, ext, low, high, bricks, sample.reshape(1, points))
+
+    send = call(
+        merge_kernel, out_shape=shape((devices, per + 4, size)), in_specs=[VMEM] * 2, out_specs=VMEM
+    )(summed, cross)
     got = lax.all_to_all(send, ALL, 0, 0)
     basis_next, factor = call(
         functools.partial(final_kernel, count),

time: 52 us -> 48.1 us (0.925)
  starting transfers between devices: 17.3 us -> 14.1 us
  blocking collectives: 9.92 us -> 13.1 us
  waiting for transfers between devices: 8.49 us -> 5.53 us
  local copies, waits for them, and re-layouts: 2.74 us -> 1.79 us
    all_to_all x1, waiting for transfers between devices: 6.72 us -> 0.01 us  [local(): lax.all_to_all(sent.reshape(devices, per, size), ALL, 0, 0)]
    ppermute x2, waiting for transfers between devices: 0.2 us -> 4.4 us  [neighbours(): lax.ppermute(block_low, axis, backward)]
    all_to_all x1, blocking collectives: 9.92 us -> 13.1 us  [local(): got = lax.all_to_all(send, ALL, 0, 0)]
    all_to_all x1, starting transfers between devices: 5.95 us -> 4 us  [local(): lax.all_to_all(sent.reshape(devices, per, size), ALL, 0, 0)]
    ppermute x2, waiting for transfers between devices: 1.57 us -> 0.01 us  [neighbours(): lax.ppermute(block_high, axis, forward)]
    ppermute x2, starting transfers between devices: 7.62 us -> 6.47 us  [neighbours(): lax.ppermute(block_high, axis, forward)]
    ppermute x1, waiting for transfers between devices: 0.01 us -> 1.12 us  [local(): low = high = lax.ppermute(packed, 'gz', [(0, 1), (1, 0)])]
    unnamed x10 -> x8, local copies, waits for them, and re-layouts: 2.63 us -> 1.68 us
  transfers between devices with their start and end apart: 6 -> 6, of which waited for: 3 -> 3; matrix products, arithmetic and copies ran while one was open for 0% -> 0% of each run, Pallas kernels for 0% -> 15%
where the time goes in v3:
time: 48.1 us; the launch traced here: 47.9 us
  starting transfers between devices  14.1 us (29%)
  blocking collectives  13.1 us (27%)
  Pallas kernels  12.4 us (26%)
  waiting for transfers between devices  5.53 us (11%)
  local copies, waits for them, and re-layouts  1.79 us (4%)
  between operations  0.75 us (2%)
    all_to_all x1, blocking collectives, local(): got = lax.all_to_all(send, ALL, 0, 0)  13.1 us
    ppermute x2, starting transfers between devices, neighbours(): lax.ppermute(block_high, axis, forward)  6.47 us
    pallas_call x1, Pallas kernels, local(): call(step_kernel, out_shape=(shape(flow.shape), shape((comps, 1, points))...  6.06 us
    pallas_call x1, Pallas kernels, local(): call(functools.partial(final_kernel, count), out_shape=(shape((comps, siz...  4.93 us
    ppermute x2, waiting for transfers between devices, neighbours(): lax.ppermute(block_low, axis, backward)  4.4 us
    all_to_all x1, starting transfers between devices, local(): lax.all_to_all(sent.reshape(devices, per, size), ALL, 0, 0)  4 us
    ppermute x2, starting transfers between devices, neighbours(): lax.ppermute(block_low, axis, backward)  3.54 us
    unnamed x8, local copies, waits for them, and re-layouts  1.68 us
  transfers between devices with their start and end apart: 6, of which 3 were waited for; matrix products, arithmetic and copies ran while one was open for 0% of the time, Pallas kernels for 15%

profile of v3, /device:TPU:0, one launch (start us, length us, event | category | flops | bytes accessed | tf_op | source)
XLA Modules:
  0.0 47.9 jit_solution(3371969796249871310)
XLA Ops:
  0.6 0.0 copy-start.1
  0.7 1.0 %copy-done.1 = f32[4,8,16,128]{3,2,1,0:T(8,128)S(1)} copy-done((f32[4,8,16,128]{3,2,1,0:T(8,128)S(1)}, f32[4,8,16,128]{3,2,1,0:T(8,128)}, u32[]{:S(2)}) %copy-start.1) | copy-done | bytes 262168
  1.6 0.1 shard_map.58
  1.7 4.8 %collective-permute-start = (f32[4,8,3,128]{3,2,1,0:T(4,128)S(1)}, f32[4,8,3,128]{3,2,1,0:T(4,128)S(1)}, u32[]{:S(2)}, u32[]{:S(2)}) collective-permute-start(f32[4,8,3,128]{3,2,1,0:T(4,128)S(1)} %get-tuple-element.15), channel_id=1, source_target_pairs={{0,2},{2,4},{4,6},{1,3},{3,5},{5,7},{8,10},{10,12},{12,14},{9,11},... | collective-permute-start | bytes 147464 | tf_op jit(solution)/shard_map/ppermute | solution.py:35
  6.6 1.3 %collective-permute-start.1 = (f32[4,8,3,128]{3,2,1,0:T(4,128)S(1)}, f32[4,8,3,128]{3,2,1,0:T(4,128)S(1)}, u32[]{:S(2)}, u32[]{:S(2)}) collective-permute-start(f32[4,8,3,128]{3,2,1,0:T(4,128)S(1)} %get-tuple-element.16), channel_id=1, source_target_pairs={{2,0},{4,2},{6,4},{3,1},{5,3},{7,5},{10,8},{12,10},{14,12},{11,9},... | collective-permute-start | bytes 147464 | tf_op jit(solution)/shard_map/ppermute | solution.py:35
  7.9 1.1 %shard_map.59 = f32[128,128]{1,0:T(8,128)} custom-call(f32[3,127,256]{2,1,0:T(8,128)S(1)} %bitcast.7), custom_call_target="tpu_custom_call" | custom-call | tf_op jit(solution)/shard_map/pallas_call | solution.py:284
  9.0 0.1 pad.6.clone
  9.1 0.0 collective-permute-done.ylo_ref
  9.1 3.6 %collective-permute-done.1.yhi_ref = f32[4,8,3,128]{3,2,1,0:T(4,128)S(1)} collective-permute-done((f32[4,8,3,128]{3,2,1,0:T(4,128)S(1)}, f32[4,8,3,128]{3,2,1,0:T(4,128)S(1)}, u32[]{:S(2)}, u32[]{:S(2)}) %collective-permute-start.1) | collective-permute-done | bytes 49184 | tf_op jit(solution)/shard_map/ppermute | solution.py:35
  12.7 0.0 copy-start.2
  12.7 0.1 pad_maximum_fusion.1
  12.8 1.6 %collective-permute-start.2 = (f32[4,3,24,128]{3,2,1,0:T(8,128)S(1)}, f32[4,3,24,128]{3,2,1,0:T(8,128)S(1)}, u32[]{:S(2)}, u32[]{:S(2)}) collective-permute-start(f32[4,3,24,128]{3,2,1,0:T(8,128)S(1)} %get-tuple-element.34), channel_id=1, source_target_pairs={{0,8},{8,16},{16,24},{24,0},{1,9},{9,17},{17,25},{25,1},{2,10},{10... | collective-permute-start | bytes 442376 | tf_op jit(solution)/shard_map/ppermute | solution.py:35
  14.5 2.2 %collective-permute-start.3 = (f32[4,3,24,128]{3,2,1,0:T(8,128)S(1)}, f32[4,3,24,128]{3,2,1,0:T(8,128)S(1)}, u32[]{:S(2)}, u32[]{:S(2)}) collective-permute-start(f32[4,3,24,128]{3,2,1,0:T(8,128)S(1)} %get-tuple-element.33), channel_id=1, source_target_pairs={{8,0},{16,8},{24,16},{0,24},{9,1},{17,9},{25,17},{1,25},{10,2},{18... | collective-permute-start | bytes 442376 | tf_op jit(solution)/shard_map/ppermute | solution.py:35
  16.7 4.0 %all-to-all-start = ((f32[32,4,128]{2,1,0:T(4,128)}), f32[32,4,128]{2,1,0:T(4,128)S(1)}, u32[]{:S(2)}, u32[]{:S(2)}) async-start(f32[32,4,128]{2,1,0:T(4,128)} %bitcast.4), calls=%async_computation | async-start | bytes 131072 | tf_op jit(solution)/shard_map/all_to_all | solution.py:297
  20.7 0.0 collective-permute-done.2.xlo_ref
  20.7 0.8 %collective-permute-done.3.xhi_ref = f32[4,3,24,128]{3,2,1,0:T(8,128)S(1)} collective-permute-done((f32[4,3,24,128]{3,2,1,0:T(8,128)S(1)}, f32[4,3,24,128]{3,2,1,0:T(8,128)S(1)}, u32[]{:S(2)}, u32[]{:S(2)}) %collective-permute-start.3) | collective-permute-done | bytes 147488 | tf_op jit(solution)/shard_map/ppermute | solution.py:35
  21.5 0.2 shard_map.60
  21.8 0.1 collective-permute-start.4
  21.8 0.1 add_convert_fusion.walls_ref
  21.9 1.1 %collective-permute-done.4.low_ref.high_ref = f32[3,24,128]{2,1,0:T(8,128)S(1)} collective-permute-done((f32[3,24,128]{2,1,0:T(8,128)S(1)}, f32[3,24,128]{2,1,0:T(8,128)S(1)}, u32[]{:S(2)}, u32[]{:S(2)}) %collective-permute-start.4) | collective-permute-done | bytes 36896 | tf_op jit(solution)/shard_map/ppermute | solution.py:309
  23.0 0.7 %copy-done.3 = s32[256]{0:T(256)S(1)} copy-done((s32[256]{0:T(256)S(1)}, s32[256]{0:T(256)}, u32[]{:S(2)}) %copy-start.3) | copy-done | bytes 1048
  23.7 6.1 %shard_map.61 = (f32[4,8,16,128]{3,2,1,0:T(8,128)}, f32[3,1,256]{2,1,0:T(1,128)S(1)}, f32[8,128]{1,0:T(8,128)S(1)}) custom-call(s32[2]{0:T(128)S(1)} %add_convert_fusion.walls_ref, f32[4,14,24,128]{3,2,1,0:T(8,128)S(1)} %get-tuple-element.19.ext_ref, f32[3,24,128]{2,1,0:T(8,128)S(1)} %collective-permute-done.4.low_ref.high_ref, ...), custom_call_target="tpu_custom_call" | custom-call | tf_op jit(solution)/shard_map/pallas_call | solution.py:316
  29.8 13.1 %all_to_all.10.got_ref = f32[32,8,128]{2,1,0:T(8,128)S(1)} all-to-all(f32[32,8,128]{2,1,0:T(8,128)S(1)} %shard_map.62), channel_id=1, replica_groups=mesh['gx'=4,'gy'=4,'gz'=2] {'gx','gy','gz'}, dimensions={0} | all-to-all | bytes 262144 | tf_op jit(solution)/shard_map/all_to_all | solution.py:327
  42.9 4.9 %shard_map.63 = (f32[3,128,256]{2,1,0:T(8,128)}, f32[128,128]{1,0:T(8,128)}) custom-call(f32[32,8,128]{2,1,0:T(8,128)S(1)} %all_to_all.10.got_ref, f32[3,127,256]{2,1,0:T(8,128)S(1)} %bitcast.9, f32[3,1,256]{2,1,0:T(1,128)S(1)} %get-tuple-element.24.snap_ref), custom_call_target="tpu_custom_call" | custom-call | tf_op jit(solution)/shard_map/pallas_call | solution.py:328
  (9 shorter events, 0.1 us)
Async XLA Ops:
  0.6 7.3 %copy-start = (f32[127,3,256]{2,0,1:T(8,128)S(1)}, f32[127,3,256]{2,0,1:T(8,128)}, u32[]{:S(2)}) copy-start(f32[127,3,256]{2,0,1:T(8,128)} %param.4) | copy-start | bytes 1170436
  0.6 1.0 %copy-start.1 = (f32[4,8,16,128]{3,2,1,0:T(8,128)S(1)}, f32[4,8,16,128]{3,2,1,0:T(8,128)}, u32[]{:S(2)}) copy-start(f32[4,8,16,128]{3,2,1,0:T(8,128)} %flow_ref.1) | copy-start | bytes 786436
  1.7 7.4 %collective-permute-start = (f32[4,8,3,128]{3,2,1,0:T(4,128)S(1)}, f32[4,8,3,128]{3,2,1,0:T(4,128)S(1)}, u32[]{:S(2)}, u32[]{:S(2)}) collective-permute-start(f32[4,8,3,128]{3,2,1,0:T(4,128)S(1)} %get-tuple-element.15), channel_id=1, source_target_pairs={{0,2},{2,4},{4,6},{1,3},{3,5},{5,7},{8,10},{10,12},{12,14},{9,11},... | collective-permute-start | bytes 147464 | tf_op jit(solution)/shard_map/ppermute | solution.py:35
  6.6 6.2 %collective-permute-start.1 = (f32[4,8,3,128]{3,2,1,0:T(4,128)S(1)}, f32[4,8,3,128]{3,2,1,0:T(4,128)S(1)}, u32[]{:S(2)}, u32[]{:S(2)}) collective-permute-start(f32[4,8,3,128]{3,2,1,0:T(4,128)S(1)} %get-tuple-element.16), channel_id=1, source_target_pairs={{2,0},{4,2},{6,4},{3,1},{5,3},{7,5},{10,8},{12,10},{14,12},{11,9},... | collective-permute-start | bytes 147464 | tf_op jit(solution)/shard_map/ppermute | solution.py:35
  12.7 8.8 %copy-start.2 = (f32[4,8,16,128]{3,2,1,0:T(8,128)S(1)}, f32[4,8,16,128]{3,2,1,0:T(8,128)}, u32[]{:S(2)}) copy-start(f32[4,8,16,128]{3,2,1,0:T(8,128)} %flow_ref.1) | copy-start | bytes 786436
  12.8 7.9 %collective-permute-start.2 = (f32[4,3,24,128]{3,2,1,0:T(8,128)S(1)}, f32[4,3,24,128]{3,2,1,0:T(8,128)S(1)}, u32[]{:S(2)}, u32[]{:S(2)}) collective-permute-start(f32[4,3,24,128]{3,2,1,0:T(8,128)S(1)} %get-tuple-element.34), channel_id=1, source_target_pairs={{0,8},{8,16},{16,24},{24,0},{1,9},{9,17},{17,25},{25,1},{2,10},{10... | collective-permute-start | bytes 442376 | tf_op jit(solution)/shard_map/ppermute | solution.py:35
  14.5 7.0 %collective-permute-start.3 = (f32[4,3,24,128]{3,2,1,0:T(8,128)S(1)}, f32[4,3,24,128]{3,2,1,0:T(8,128)S(1)}, u32[]{:S(2)}, u32[]{:S(2)}) collective-permute-start(f32[4,3,24,128]{3,2,1,0:T(8,128)S(1)} %get-tuple-element.33), channel_id=1, source_target_pairs={{8,0},{16,8},{24,16},{0,24},{9,1},{17,9},{25,17},{1,25},{10,2},{18... | collective-permute-start | bytes 442376 | tf_op jit(solution)/shard_map/ppermute | solution.py:35
  16.7 13.1 %all-to-all-start = ((f32[32,4,128]{2,1,0:T(4,128)}), f32[32,4,128]{2,1,0:T(4,128)S(1)}, u32[]{:S(2)}, u32[]{:S(2)}) async-start(f32[32,4,128]{2,1,0:T(4,128)} %bitcast.4), calls=%async_computation | async-start | bytes 131072 | tf_op jit(solution)/shard_map/all_to_all | solution.py:297
  21.8 1.3 %collective-permute-start.4 = (f32[3,24,128]{2,1,0:T(8,128)S(1)}, f32[3,24,128]{2,1,0:T(8,128)S(1)}, u32[]{:S(2)}, u32[]{:S(2)}) collective-permute-start(f32[3,24,128]{2,1,0:T(8,128)S(1)} %get-tuple-element.20), channel_id=1, source_target_pairs={{0,1},{1,0},{2,3},{3,2},{4,5},{5,4},{6,7},{7,6},{8,9},{9,8},{10,11... | collective-permute-start | bytes 110600 | tf_op jit(solution)/shard_map/ppermute | solution.py:309
  23.0 0.7 %copy-start.3 = (s32[256]{0:T(256)S(1)}, s32[256]{0:T(256)}, u32[]{:S(2)}) copy-start(s32[256]{0:T(256)} %param.5) | copy-start | bytes 3076

commit v4 on v3

v4 whole, which is shorter than its diff:
```python
import functools

import jax
import jax.numpy as jnp
from jax import lax
from jax.experimental import pallas as pl
from jax.experimental.pallas import tpu as pltpu
from jax.sharding import PartitionSpec as P

DT_STEP = 0.35
VISCOSITY = 0.2
SOUND_SQ = 1.0
DRIVING = 0.5

ALL = ("gx", "gy", "gz")
DEPTH = 3
GAP = 2
EXACT = lax.Precision.HIGHEST
VMEM = pl.BlockSpec(memory_space=pltpu.VMEM)
PARAMS = pltpu.CompilerParams(vmem_limit_bytes=40 * 1024 * 1024)


def dot(a, b, dims):
    return lax.dot_general(
        a, b, (dims, ((), ())), precision=EXACT, preferred_element_type=jnp.float32
    )


def neighbours(block_low, block_high, axis):
    count = lax.axis_size(axis)
    forward = [(i, (i + 1) % count) for i in range(count)]
    backward = [(target, source) for source, target in forward]
    return lax.ppermute(block_high, axis, forward), lax.ppermute(block_low, axis, backward)


def gram_kernel(basis_ref, gram_ref):
    modes = basis_ref.shape[1]
    total = jnp.zeros((modes, modes), jnp.float32)
    for c in range(basis_ref.shape[0]):
        rows = basis_ref[c]
        total = total + dot(rows, rows, ((1,), (1,)))
    gram_ref[...] = jnp.zeros_like(gram_ref)
    gram_ref[0:modes, 0:modes] = total


def strips_kernel(flow_hbm, bottom_ref, top_ref, flow_ref, sem):
    ny = flow_ref.shape[2]
    copy = pltpu.make_async_copy(flow_hbm, flow_ref, sem)
    copy.start()
    copy.wait()
    bottom_ref[...] = flow_ref[:, :, 0:DEPTH]
    top_ref[...] = flow_ref[:, :, ny - DEPTH : ny]


def walls_kernel(walls_ref, flow_ref, ylo_ref, yhi_ref, mid_ref, first_ref, last_ref):
    fields, nx, ny, nz = flow_ref.shape
    gap = jnp.zeros((GAP, nz), jnp.float32)
    for f in range(fields):
        for i in range(nx):
            below = jnp.where(walls_ref[0] == 1, 0.0, ylo_ref[f, i])
            above = jnp.where(walls_ref[1] == 1, 0.0, yhi_ref[f, i])
            plane = jnp.concatenate([flow_ref[f, i], above, gap, below], axis=0)
            mid_ref[f, i] = plane
            if i < DEPTH:
                first_ref[f, i] = plane
            if i >= nx - DEPTH:
                last_ref[f, i - nx + DEPTH] = plane


def plane_of(mid_ref, xlo_ref, xhi_ref, f, i):
    nx = mid_ref.shape[1]
    if i < DEPTH:
        return xlo_ref[f, i]
    if i < DEPTH + nx:
        return mid_ref[f, i - DEPTH]
    return xhi_ref[f, i - DEPTH - nx]


GROUP = 8


def pack_kernel(mid_ref, xlo_ref, xhi_ref, packed_ref):
    fields, nx, rows, nz = mid_ref.shape
    lane = lax.broadcasted_iota(jnp.int32, (rows, nz), 1)
    for f in range(fields):
        value = jnp.zeros((rows, nz), jnp.float32)
        for i in range(nx + 2 * DEPTH):
            start = GROUP * i
            moved = pltpu.roll(plane_of(mid_ref, xlo_ref, xhi_ref, f, i), (start + DEPTH) % nz, 1)
            value = jnp.where((lane >= start) & (lane < start + 2 * DEPTH), moved, value)
        packed_ref[f] = value


def step(value, by, axis):
    size = value.shape[axis]
    return pltpu.roll(value, (size - by) % size, axis)


def rates(centre, x_plus, x_minus, y_plus, y_minus, z_plus, z_minus):
    slope_x = [0.5 * (a - b) for a, b in zip(x_plus, x_minus)]
    slope_y = [0.5 * (a - b) for a, b in zip(y_plus, y_minus)]
    slope_z = [0.5 * (a - b) for a, b in zip(z_plus, z_minus)]
    pressure = [slope_x[3], slope_y[3], slope_z[3]]
    out = []
    for f in range(3):
        laplace = (
            x_plus[f] + x_minus[f] + (y_plus[f] + y_minus[f]) + (z_plus[f] + z_minus[f]) - 6.0 * centre[f]
        )
        advect = centre[0] * slope_x[f] + centre[1] * slope_y[f] + centre[2] * slope_z[f]
        value = VISCOSITY * laplace - advect - pressure[f]
        if f == 0:
            value = value + DRIVING
        out.append(value)
    out.append(-SOUND_SQ * (slope_x[0] + slope_y[1] + slope_z[2]))
    return out


def step_kernel(
    walls_ref, mid_ref, xlo_ref, xhi_ref, own_ref, low_ref, high_ref, basis_ref, sample_ref,
    flow_ref, snap_ref, cross_ref,
    one_ref, two_ref,
):
    fields, nx, ny, nz = flow_ref.shape
    rows = mid_ref.shape[2]
    modes = basis_ref.shape[1]
    lane = lax.broadcasted_iota(jnp.int32, (rows, nz), 1)
    row = lax.broadcasted_iota(jnp.int32, (rows, nz), 0)
    below = (row >= ny + DEPTH + GAP) & (walls_ref[0] == 1)
    above = (row >= ny) & (row < ny + DEPTH) & (walls_ref[1] == 1)
    outside = below | above
    every = range(4)

    def start(f, i):
        return plane_of(mid_ref, xlo_ref, xhi_ref, f, i)

    def after_one(value, rate):
        return jnp.where(outside, 0.0, value + DT_STEP * rate)

    def after_two(begin, value, rate):
        return jnp.where(outside, 0.0, 0.75 * begin + 0.25 * (value + DT_STEP * rate))

    left = lane % GROUP < DEPTH

    def window_rates(q):
        return rates(
            q, [step(v, GROUP, 1) for v in q], [step(v, -GROUP, 1) for v in q],
            [step(v, 1, 0) for v in q], [step(v, -1, 0) for v in q],
            [step(v, 1, 1) for v in q], [step(v, -1, 1) for v in q],
        )

    own = [own_ref[f] for f in every]
    other = [jnp.where(left, low_ref[f], high_ref[f]) for f in every]
    ends = [other]
    windows = []
    for parts in ((other, own), (own, other)):
        q0 = [jnp.where(left, a, b) for a, b in zip(*parts)]
        q1 = [after_one(v, r) for v, r in zip(q0, window_rates(q0))]
        q2 = [after_two(s, v, r) for s, v, r in zip(q0, q1, window_rates(q1))]
        windows.append((q1, q2))
    for stage in (0, 1):
        ends.append([jnp.where(left, a, b) for a, b in zip(windows[0][stage], windows[1][stage])])

    def plane_rates(read, beyond, i, rows):
        centre = [read(f, i) for f in every]
        z_plus, z_minus = [], []
        for f in every:
            end = pltpu.roll(beyond[f], (2 * nz - GROUP * i - DEPTH) % nz, 1)[:rows]
            z_plus.append(step(jnp.where(lane[:rows] == 0, end, centre[f][:rows]), 1, 1))
            z_minus.append(step(jnp.where(lane[:rows] == nz - 1, end, centre[f][:rows]), -1, 1))
        y_plus = [step(v, 1, 0)[:rows] for v in centre]
        y_minus = [step(v, -1, 0)[:rows] for v in centre]
        centre = [v[:rows] for v in centre]
        x_plus = [read(f, i + 1)[:rows] for f in every]
        x_minus = [read(f, i - 1)[:rows] for f in every]
        return centre, rates(centre, x_plus, x_minus, y_plus, y_minus, z_plus, z_minus)

    planes = nx + 2 * DEPTH
    for i in range(1, planes - 1):
        centre, rate = plane_rates(start, ends[0], i, rows)
        for f in every:
            one_ref[f, i] = after_one(centre[f], rate[f])
    for i in range(2, planes - 2):
        centre, rate = plane_rates(lambda f, i: one_ref[f, i], ends[1], i, rows)
        for f in every:
            two_ref[f, i] = after_two(start(f, i), centre[f], rate[f])
    for i in range(3, planes - 3):
        centre, rate = plane_rates(lambda f, i: two_ref[f, i], ends[2], i, ny)
        for f in every:
            value = 1.0 / 3.0 * start(f, i)[:ny] + 2.0 / 3.0 * (centre[f] + DT_STEP * rate[f])
            flow_ref[f, i - DEPTH] = value

    points = sample_ref.shape[1]
    spot = jnp.broadcast_to(sample_ref[...], (nz, points))
    place = lax.broadcasted_iota(jnp.int32, (nx * ny, points), 0)
    in_row = (place == jnp.broadcast_to(sample_ref[...] // nz, (nx * ny, points))).astype(jnp.bfloat16)
    in_lane = lax.broadcasted_iota(jnp.int32, (nz, points), 0) == spot % nz
    cross = jnp.zeros((8, modes + 1), jnp.float32)
    for c in range(3):
        field = flow_ref[c].reshape(nx * ny, nz).T
        high = field.astype(jnp.bfloat16)
        rest = field - high.astype(jnp.float32)
        middle = rest.astype(jnp.bfloat16)
        low = (rest - middle.astype(jnp.float32)).astype(jnp.bfloat16)
        found = sum(
            lax.dot_general(p, in_row, (((1,), (0,)), ((), ())), preferred_element_type=jnp.float32)
            for p in (high, middle, low)
        )
        picked = jnp.sum(jnp.where(in_lane, found, 0.0), axis=0, keepdims=True)
        snap_ref[c] = picked
        stacked = jnp.concatenate([basis_ref[c], picked], axis=0)
        cross = cross + dot(jnp.broadcast_to(picked, (8, points)), stacked, ((1,), (1,)))
    cross_ref[...] = cross


def merge_kernel(summed_ref, cross_ref, send_ref):
    per = send_ref.shape[1] - 4
    summed = jnp.zeros(cross_ref.shape, jnp.float32)
    for k in range(summed_ref.shape[0] // 8):
        summed = summed + summed_ref[8 * k : 8 * k + 8]
    summed = summed + pltpu.roll(summed, 4, 0)
    sub = lax.broadcasted_iota(jnp.int32, summed.shape, 0)
    block = jnp.where(sub < per, summed, jnp.where(sub == per, cross_ref[...], 0.0))
    for d in range(send_ref.shape[0]):
        send_ref[d] = block


def eliminate(work_ref, tall):
    size = work_ref.shape[0]
    blocks = tall // 8
    sub = lax.broadcasted_iota(jnp.int32, (8, 1), 0)
    for base in range(0, size, tall):
        panel = [work_ref[base + 8 * b : base + 8 * b + 8, :] for b in range(blocks)]
        column = [
            [jnp.broadcast_to(panel[b][:, base + k : base + k + 1], (8, 128)) for b in range(blocks)]
            for k in range(tall)
        ]
        for j in range(tall):
            mine, at = divmod(j, 8)
            scale = lax.rsqrt(column[j][mine][at : at + 1, :])
            times = {b: column[j][b] * scale for b in range(mine, blocks)}
            times[mine] = jnp.where(sub > at, times[mine], 0.0)
            scaled = panel[mine][at : at + 1, :] * jnp.concatenate([scale, scale], axis=1)
            for b in range(mine, blocks):
                value = panel[b] - jnp.concatenate([times[b], times[b]], axis=1) * scaled
                panel[b] = jnp.where(sub == at, scaled, value) if b == mine else value
            for k in range(j + 1, tall):
                other, place = divmod(k, 8)
                for b in range(other, blocks):
                    column[k][b] = column[k][b] - times[b] * times[other][place : place + 1, :]
        for b in range(blocks):
            work_ref[base + 8 * b : base + 8 * b + 8, :] = panel[b]
        if base + tall < size:
            done = work_ref[base : base + tall, :]
            change = dot(done[:, 0:size], done, ((0,), (0,)))
            work_ref[base + tall : size, :] = work_ref[base + tall : size, :] - change[base + tall : size]


def final_kernel(
    count, got_ref, basis_ref, snap_ref, flow_ref,
    basis_hbm, factor_hbm, flow_hbm,
    work_ref, basis_out_ref, factor_ref, sems,
):
    modes = basis_ref.shape[1]
    size = modes + 1
    per = got_ref.shape[1] - 4
    copies = [pltpu.make_async_copy(flow_ref, flow_hbm, sems.at[0])]
    copies[0].start()
    cross = jnp.zeros((8, size), jnp.float32)
    for d in range(got_ref.shape[0]):
        block = got_ref[d]
        if per * d < size:
            work_ref[per * d : per * d + per, 0:size] = block[0:per] / count
        cross = cross + block
    cross = cross[per : per + 1] / count
    col = lax.broadcasted_iota(jnp.int32, (size, size), 1)
    row = lax.broadcasted_iota(jnp.int32, (size, size), 0)
    work_ref[size - 1 : size, 0:size] = cross
    mark = (lax.broadcasted_iota(jnp.int32, (8, size), 1) == size - 1).astype(jnp.float32)
    top = lax.broadcasted_iota(jnp.int32, (8, size), 0) == 0
    side = dot(jnp.where(top, jnp.broadcast_to(cross, (8, size)), 0.0), mark, ((0,), (0,)))
    work_ref[:, 0:size] = jnp.where(col == size - 1, side, work_ref[:, 0:size])
    work_ref[:, size : 2 * size] = (row == col).astype(jnp.float32)
    eliminate(work_ref, 32)
    factor_ref[...] = jnp.where(col >= row, work_ref[:, 0:size], 0.0)
    copies.append(pltpu.make_async_copy(factor_ref, factor_hbm, sems.at[1]))
    copies[1].start()
    inverse = work_ref[:, size : 2 * size]
    for c in range(basis_ref.shape[0]):
        stacked = jnp.concatenate([basis_ref[c], snap_ref[c]], axis=0)
        basis_out_ref[c] = dot(inverse, stacked, ((1,), (0,)))
        copies.append(pltpu.make_async_copy(basis_out_ref.at[c], basis_hbm.at[c], sems.at[2 + c]))
        copies[-1].start()
    for copy in copies:
        copy.wait()


def local(flow, basis, sample):
    fields, nx, ny, nz = flow.shape
    modes, comps, points = basis.shape
    size = modes + 1
    devices = lax.axis_size("gx") * lax.axis_size("gy") * lax.axis_size("gz")
    count = float(comps * points * devices)
    shape = functools.partial(jax.ShapeDtypeStruct, dtype=jnp.float32)
    call = functools.partial(pl.pallas_call, compiler_params=PARAMS)
    bricks = jnp.transpose(basis, (1, 0, 2))

    strip = shape((fields, nx, DEPTH, nz))
    bottom, top = call(
        strips_kernel,
        out_shape=(strip, strip),
        in_specs=[pl.BlockSpec(memory_space=pltpu.HBM)],
        out_specs=(VMEM, VMEM),
        scratch_shapes=[pltpu.VMEM(flow.shape, jnp.float32), pltpu.SemaphoreType.DMA],
    )(flow)
    ylo, yhi = neighbours(bottom, top, "gy")
    gram = call(gram_kernel, out_shape=shape((size, size)), in_specs=[VMEM], out_specs=VMEM)(bricks)
    ylo, yhi, gram = lax.optimization_barrier((ylo, yhi, gram))

    rows = ny + 2 * DEPTH + GAP
    place = lax.axis_index("gy")
    walls = jnp.stack([place == 0, place == lax.axis_size("gy") - 1]).astype(jnp.int32)
    face = shape((fields, DEPTH, rows, nz))
    mid, first, last = call(
        walls_kernel,
        out_shape=(shape((fields, nx, rows, nz)), face, face),
        in_specs=[pl.BlockSpec(memory_space=pltpu.SMEM)] + [VMEM] * 3,
        out_specs=(VMEM,) * 3,
    )(walls, flow, ylo, yhi)
    xlo, xhi = neighbours(first, last, "gx")

    per = 4
    sent = jnp.pad(gram, ((0, per * devices - size), (0, 0))) if per * devices > size else gram
    summed = lax.all_to_all(sent.reshape(devices, per, size), ALL, 0, 0).reshape(devices * per, size)

    packed = call(
        pack_kernel, out_shape=shape((fields, rows, nz)), in_specs=[VMEM] * 3, out_specs=VMEM
    )(mid, xlo, xhi)
    if lax.axis_size("gz") == 2:
        low = high = lax.ppermute(packed, "gz", [(0, 1), (1, 0)])
    else:
        low, high = neighbours(packed, packed, "gz")

    between = pltpu.VMEM((fields, nx + 2 * DEPTH, rows, nz), jnp.float32)
    flow_new, snapshot, cross = call(
        step_kernel,
        out_shape=(shape(flow.shape), shape((comps, 1, points)), shape((8, size))),
        in_specs=[pl.BlockSpec(memory_space=pltpu.SMEM)] + [VMEM] * 8,
        out_specs=(VMEM, VMEM, VMEM),
        scratch_shapes=[between, between],
    )(walls, mid, xlo, xhi, packed, low, high, bricks, sample.reshape(1, points))

    send = call(
        merge_kernel, out_shape=shape((devices, per + 4, size)), in_specs=[VMEM] * 2, out_specs=VMEM
    )(summed, cross)
    got = lax.all_to_all(send, ALL, 0, 0)
    whole = pl.BlockSpec(memory_space=pltpu.HBM)
    basis_next, factor, flow_next = call(
        functools.partial(final_kernel, count),
        out_shape=(shape((comps, size, points)), shape((size, size)), shape(flow.shape)),
        in_specs=[VMEM] * 4,
        out_specs=(whole,) * 3,
        scratch_shapes=[
            pltpu.VMEM((size, 2 * size), jnp.float32),
            pltpu.VMEM((comps, size, points), jnp.float32),
            pltpu.VMEM((size, size), jnp.float32),
            pltpu.SemaphoreType.DMA((2 + comps,)),
        ],
    )(got, bricks, snapshot, flow_new)
    return flow_next, jnp.transpose(basis_next, (1, 0, 2)), factor


def solution(mesh):
    return jax.shard_map(
        local,
        mesh=mesh,
        in_specs=(
            P(None, "gx", "gy", "gz"),
            P(None, None, ("gx", "gy", "gz")),
            P(("gx", "gy", "gz")),
        ),
        out_specs=(P(None, "gx", "gy", "gz"), P(None, None, ("gx", "gy", "gz")), P()),
        check_vma=False,
    )
```

time: 48.1 us -> 41.5 us (0.86)
  starting transfers between devices: 14.1 us -> 11.5 us
  Pallas kernels: 12.4 us -> 9.96 us
  blocking collectives: 13.1 us -> 11.5 us
    pallas_call x1, Pallas kernels: 6.06 us -> 3.05 us  [local(): call(step_kernel, out_shape=(shape(flow.shape), shape((comps, 1, points))...]
    ppermute x2, waiting for transfers between devices: 4.4 us -> 2.32 us  [neighbours(): lax.ppermute(block_low, axis, backward)]
    ppermute x2, starting transfers between devices: 6.47 us -> 4.62 us  [neighbours(): lax.ppermute(block_high, axis, forward)]
    all_to_all x1, blocking collectives: 13.1 us -> 11.5 us  [local(): got = lax.all_to_all(send, ALL, 0, 0)]
    all_to_all x1, waiting for transfers between devices: 0.01 us -> 1.02 us  [local(): lax.all_to_all(sent.reshape(devices, per, size), ALL, 0, 0)]
    ppermute x2, waiting for transfers between devices: 0.01 us -> 0.95 us  [neighbours(): lax.ppermute(block_high, axis, forward)]
    pallas_call x1 -> x2, Pallas kernels: 0.25 us -> 0.83 us  [the longest x1 0.59 us: local(): call(walls_kernel, out_shape=(shape((fields, nx, rows, nz)), face, face),...]
    unnamed x8 -> x10, local copies, waits for them, and re-layouts: 1.68 us -> 1.95 us
  transfers between devices with their start and end apart: 6 -> 6, of which waited for: 3 -> 6; matrix products, arithmetic and copies ran while one was open for 0% -> 0% of each run, Pallas kernels for 15% -> 11%
where the time goes in v4:
time: 41.5 us; the launch traced here: 41.2 us
  starting transfers between devices  11.5 us (28%)
  blocking collectives  11.5 us (28%)
  Pallas kernels  9.96 us (24%)
  waiting for transfers between devices  5.5 us (13%)
  local copies, waits for them, and re-layouts  1.95 us (5%)
  between operations  0.7 us (2%)
    all_to_all x1, blocking collectives, local(): got = lax.all_to_all(send, ALL, 0, 0)  11.5 us
    pallas_call x1, Pallas kernels, local(): call(functools.partial(final_kernel, count), out_shape=(shape((comps, siz...  4.89 us
    ppermute x2, starting transfers between devices, neighbours(): lax.ppermute(block_high, axis, forward)  4.62 us
    all_to_all x1, starting transfers between devices, local(): lax.all_to_all(sent.reshape(devices, per, size), ALL, 0, 0)  3.56 us
    ppermute x2, starting transfers between devices, neighbours(): lax.ppermute(block_low, axis, backward)  3.27 us
    pallas_call x1, Pallas kernels, local(): call(step_kernel, out_shape=(shape(flow.shape), shape((comps, 1, points))...  3.05 us
    ppermute x2, waiting for transfers between devices, neighbours(): lax.ppermute(block_low, axis, backward)  2.32 us
    unnamed x10, local copies, waits for them, and re-layouts  1.95 us
  transfers between devices with their start and end apart: 6, of which 6 were waited for; matrix products, arithmetic and copies ran while one was open for 0% of the time, Pallas kernels for 11%

profile of v4, /device:TPU:0, one launch (start us, length us, event | category | flops | bytes accessed | tf_op | source)
XLA Modules:
  0.0 41.2 jit_solution(7581753749221550497)
XLA Ops:
  0.6 0.9 %copy-done.2 = f32[4,8,16,128]{3,2,1,0:T(8,128)S(1)} copy-done((f32[4,8,16,128]{3,2,1,0:T(8,128)S(1)}, f32[4,8,16,128]{3,2,1,0:T(8,128)}, u32[]{:S(2)}) %copy-start.2) | copy-done | bytes 262168
  1.6 0.1 shard_map.58
  1.6 3.0 %collective-permute-start = (f32[4,8,3,128]{3,2,1,0:T(4,128)S(1)}, f32[4,8,3,128]{3,2,1,0:T(4,128)S(1)}, u32[]{:S(2)}, u32[]{:S(2)}) collective-permute-start(f32[4,8,3,128]{3,2,1,0:T(4,128)S(1)} %get-tuple-element.17), channel_id=1, source_target_pairs={{0,2},{2,4},{4,6},{6,0},{1,3},{3,5},{5,7},{7,1},{8,10},{10,12},{12... | collective-permute-start | bytes 147464 | tf_op jit(solution)/shard_map/ppermute | solution.py:33
  4.6 1.0 %collective-permute-start.1 = (f32[4,8,3,128]{3,2,1,0:T(4,128)S(1)}, f32[4,8,3,128]{3,2,1,0:T(4,128)S(1)}, u32[]{:S(2)}, u32[]{:S(2)}) collective-permute-start(f32[4,8,3,128]{3,2,1,0:T(4,128)S(1)} %get-tuple-element.18), channel_id=1, source_target_pairs={{2,0},{4,2},{6,4},{0,6},{3,1},{5,3},{7,5},{1,7},{10,8},{12,10},{14... | collective-permute-start | bytes 147464 | tf_op jit(solution)/shard_map/ppermute | solution.py:33
  5.7 0.1 add_convert_fusion.walls_ref
  5.7 1.0 %copy-done = f32[127,3,256]{2,0,1:T(8,128)S(1)} copy-done((f32[127,3,256]{2,0,1:T(8,128)S(1)}, f32[127,3,256]{2,0,1:T(8,128)}, u32[]{:S(2)}) %copy-start) | copy-done | bytes 390168
  6.7 1.1 %shard_map.59 = f32[128,128]{1,0:T(8,128)} custom-call(f32[3,127,256]{2,1,0:T(8,128)S(1)} %bitcast.7), custom_call_target="tpu_custom_call" | custom-call | tf_op jit(solution)/shard_map/pallas_call | solution.py:316
  7.8 0.1 collective-permute-done.ylo_ref
  8.0 1.4 %collective-permute-done.1.yhi_ref = f32[4,8,3,128]{3,2,1,0:T(4,128)S(1)} collective-permute-done((f32[4,8,3,128]{3,2,1,0:T(4,128)S(1)}, f32[4,8,3,128]{3,2,1,0:T(4,128)S(1)}, u32[]{:S(2)}, u32[]{:S(2)}) %collective-permute-start.1) | collective-permute-done | bytes 49184 | tf_op jit(solution)/shard_map/ppermute | solution.py:33
  9.3 0.6 %shard_map.60 = (f32[4,8,24,128]{3,2,1,0:T(8,128)S(1)}, f32[4,3,24,128]{3,2,1,0:T(8,128)S(1)}, f32[4,3,24,128]{3,2,1,0:T(8,128)S(1)}) custom-call(s32[2]{0:T(128)S(1)} %add_convert_fusion.walls_ref, f32[4,8,16,128]{3,2,1,0:T(8,128)S(1)} %copy-done.3, f32[4,8,3,128]{3,2,1,0:T(4,128)S(1)} %collective-permute-done.ylo_ref, ...), custom_call_target="tpu_custom_call" | custom-call | tf_op jit(solution)/shard_map/pallas_call | solution.py:323
  9.9 1.6 %collective-permute-start.2 = (f32[4,3,24,128]{3,2,1,0:T(8,128)S(1)}, f32[4,3,24,128]{3,2,1,0:T(8,128)S(1)}, u32[]{:S(2)}, u32[]{:S(2)}) collective-permute-start(f32[4,3,24,128]{3,2,1,0:T(8,128)S(1)} %get-tuple-element.23), channel_id=1, source_target_pairs={{0,8},{8,16},{16,24},{24,0},{1,9},{9,17},{17,25},{25,1},{2,10},{10... | collective-permute-start | bytes 442376 | tf_op jit(solution)/shard_map/ppermute | solution.py:33
  11.6 2.2 %collective-permute-start.3 = (f32[4,3,24,128]{3,2,1,0:T(8,128)S(1)}, f32[4,3,24,128]{3,2,1,0:T(8,128)S(1)}, u32[]{:S(2)}, u32[]{:S(2)}) collective-permute-start(f32[4,3,24,128]{3,2,1,0:T(8,128)S(1)} %get-tuple-element.24), channel_id=1, source_target_pairs={{8,0},{16,8},{24,16},{0,24},{9,1},{17,9},{25,17},{1,25},{10,2},{18... | collective-permute-start | bytes 442376 | tf_op jit(solution)/shard_map/ppermute | solution.py:33
  13.8 3.6 %all-to-all-start = ((f32[32,4,128]{2,1,0:T(4,128)}), f32[32,4,128]{2,1,0:T(4,128)S(1)}, u32[]{:S(2)}, u32[]{:S(2)}) async-start(f32[32,4,128]{2,1,0:T(4,128)} %bitcast.1), calls=%async_computation | async-start | bytes 131072 | tf_op jit(solution)/shard_map/all_to_all | solution.py:333
  17.4 0.0 copy-start.1
  17.4 0.8 %collective-permute-done.2.xlo_ref = f32[4,3,24,128]{3,2,1,0:T(8,128)S(1)} collective-permute-done((f32[4,3,24,128]{3,2,1,0:T(8,128)S(1)}, f32[4,3,24,128]{3,2,1,0:T(8,128)S(1)}, u32[]{:S(2)}, u32[]{:S(2)}) %collective-permute-start.2) | collective-permute-done | bytes 147488 | tf_op jit(solution)/shard_map/ppermute | solution.py:33
  18.2 1.0 %collective-permute-done.3.xhi_ref = f32[4,3,24,128]{3,2,1,0:T(8,128)S(1)} collective-permute-done((f32[4,3,24,128]{3,2,1,0:T(8,128)S(1)}, f32[4,3,24,128]{3,2,1,0:T(8,128)S(1)}, u32[]{:S(2)}, u32[]{:S(2)}) %collective-permute-start.3) | collective-permute-done | bytes 147488 | tf_op jit(solution)/shard_map/ppermute | solution.py:33
  19.2 0.2 shard_map.61.own_ref
  19.4 0.0 copy-start.4
  19.4 0.1 collective-permute-start.4
  19.5 1.2 %collective-permute-done.4.low_ref.high_ref = f32[4,24,128]{2,1,0:T(8,128)S(1)} collective-permute-done((f32[4,24,128]{2,1,0:T(8,128)S(1)}, f32[4,24,128]{2,1,0:T(8,128)S(1)}, u32[]{:S(2)}, u32[]{:S(2)}) %collective-permute-start.4) | collective-permute-done | bytes 49184 | tf_op jit(solution)/shard_map/ppermute | solution.py:339
  20.7 3.1 %shard_map.62 = (f32[4,8,16,128]{3,2,1,0:T(8,128)S(1)}, f32[3,1,256]{2,1,0:T(1,128)S(1)}, f32[8,128]{1,0:T(8,128)S(1)}) custom-call(s32[2]{0:T(128)S(1)} %add_convert_fusion.walls_ref, f32[4,8,24,128]{3,2,1,0:T(8,128)S(1)} %get-tuple-element.22.mid_ref, f32[4,3,24,128]{3,2,1,0:T(8,128)S(1)} %collective-permute-done.2.xlo_ref, ...), custom_call_target="tpu_custom_call" | custom-call | tf_op jit(solution)/shard_map/pallas_call | solution.py:344
  23.8 1.0 %all-to-all-done = f32[32,4,128]{2,1,0:T(4,128)S(1)} async-done(((f32[32,4,128]{2,1,0:T(4,128)}), f32[32,4,128]{2,1,0:T(4,128)S(1)}, u32[]{:S(2)}, u32[]{:S(2)}) %all-to-all-start) | async-done | bytes 65568 | tf_op jit(solution)/shard_map/all_to_all | solution.py:333
  24.8 11.5 %all_to_all.10.got_ref = f32[32,8,128]{2,1,0:T(8,128)S(1)} all-to-all(f32[32,8,128]{2,1,0:T(8,128)S(1)} %shard_map.63), channel_id=1, replica_groups=mesh['gx'=4,'gy'=4,'gz'=2] {'gx','gy','gz'}, dimensions={0} | all-to-all | bytes 262144 | tf_op jit(solution)/shard_map/all_to_all | solution.py:355
  36.4 4.9 %shard_map.64 = (f32[3,128,256]{2,1,0:T(8,128)}, f32[128,128]{1,0:T(8,128)}, f32[4,8,16,128]{3,2,1,0:T(8,128)}) custom-call(f32[32,8,128]{2,1,0:T(8,128)S(1)} %all_to_all.10.got_ref, f32[3,127,256]{2,1,0:T(8,128)S(1)} %bitcast.9, f32[3,1,256]{2,1,0:T(1,128)S(1)} %get-tuple-element.26.snap_ref, f32[4,8,16,128]{3,2,1,0:T(8,128)S(1)} %get-tuple-element.27.flow_ref), custom_call_target="tpu_custom_call" | custom-call | tf_op jit(solution)/shard_map/pallas_call | solution.py:357
  (7 shorter events, 0.0 us)
Async XLA Ops:
  0.6 1.0 %copy-start.2 = (f32[4,8,16,128]{3,2,1,0:T(8,128)S(1)}, f32[4,8,16,128]{3,2,1,0:T(8,128)}, u32[]{:S(2)}) copy-start(f32[4,8,16,128]{3,2,1,0:T(8,128)} %flow_ref.1) | copy-start | bytes 786436
  1.6 7.8 %copy-start.3 = (f32[4,8,16,128]{3,2,1,0:T(8,128)S(1)}, f32[4,8,16,128]{3,2,1,0:T(8,128)}, u32[]{:S(2)}) copy-start(f32[4,8,16,128]{3,2,1,0:T(8,128)} %flow_ref.1) | copy-start | bytes 786436
  1.6 6.3 %collective-permute-start = (f32[4,8,3,128]{3,2,1,0:T(4,128)S(1)}, f32[4,8,3,128]{3,2,1,0:T(4,128)S(1)}, u32[]{:S(2)}, u32[]{:S(2)}) collective-permute-start(f32[4,8,3,128]{3,2,1,0:T(4,128)S(1)} %get-tuple-element.17), channel_id=1, source_target_pairs={{0,2},{2,4},{4,6},{6,0},{1,3},{3,5},{5,7},{7,1},{8,10},{10,12},{12... | collective-permute-start | bytes 147464 | tf_op jit(solution)/shard_map/ppermute | solution.py:33
  4.6 4.7 %collective-permute-start.1 = (f32[4,8,3,128]{3,2,1,0:T(4,128)S(1)}, f32[4,8,3,128]{3,2,1,0:T(4,128)S(1)}, u32[]{:S(2)}, u32[]{:S(2)}) collective-permute-start(f32[4,8,3,128]{3,2,1,0:T(4,128)S(1)} %get-tuple-element.18), channel_id=1, source_target_pairs={{2,0},{4,2},{6,4},{0,6},{3,1},{5,3},{7,5},{1,7},{10,8},{12,10},{14... | collective-permute-start | bytes 147464 | tf_op jit(solution)/shard_map/ppermute | solution.py:33
  5.7 1.0 %copy-start = (f32[127,3,256]{2,0,1:T(8,128)S(1)}, f32[127,3,256]{2,0,1:T(8,128)}, u32[]{:S(2)}) copy-start(f32[127,3,256]{2,0,1:T(8,128)} %param.4) | copy-start | bytes 1170436
  9.9 8.3 %collective-permute-start.2 = (f32[4,3,24,128]{3,2,1,0:T(8,128)S(1)}, f32[4,3,24,128]{3,2,1,0:T(8,128)S(1)}, u32[]{:S(2)}, u32[]{:S(2)}) collective-permute-start(f32[4,3,24,128]{3,2,1,0:T(8,128)S(1)} %get-tuple-element.23), channel_id=1, source_target_pairs={{0,8},{8,16},{16,24},{24,0},{1,9},{9,17},{17,25},{25,1},{2,10},{10... | collective-permute-start | bytes 442376 | tf_op jit(solution)/shard_map/ppermute | solution.py:33
  11.6 7.6 %collective-permute-start.3 = (f32[4,3,24,128]{3,2,1,0:T(8,128)S(1)}, f32[4,3,24,128]{3,2,1,0:T(8,128)S(1)}, u32[]{:S(2)}, u32[]{:S(2)}) collective-permute-start(f32[4,3,24,128]{3,2,1,0:T(8,128)S(1)} %get-tuple-element.24), channel_id=1, source_target_pairs={{8,0},{16,8},{24,16},{0,24},{9,1},{17,9},{25,17},{1,25},{10,2},{18... | collective-permute-start | bytes 442376 | tf_op jit(solution)/shard_map/ppermute | solution.py:33
  13.8 11.0 %all-to-all-start = ((f32[32,4,128]{2,1,0:T(4,128)}), f32[32,4,128]{2,1,0:T(4,128)S(1)}, u32[]{:S(2)}, u32[]{:S(2)}) async-start(f32[32,4,128]{2,1,0:T(4,128)} %bitcast.1), calls=%async_computation | async-start | bytes 131072 | tf_op jit(solution)/shard_map/all_to_all | solution.py:333
  17.4 3.3 %copy-start.1 = (f32[127,3,256]{2,0,1:T(8,128)S(1)}, f32[127,3,256]{2,0,1:T(8,128)}, u32[]{:S(2)}) copy-start(f32[127,3,256]{2,0,1:T(8,128)} %param.4) | copy-start | bytes 1170436
  19.4 1.3 %copy-start.4 = (s32[256]{0:T(256)S(1)}, s32[256]{0:T(256)}, u32[]{:S(2)}) copy-start(s32[256]{0:T(256)} %param.5) | copy-start | bytes 3076
  19.4 1.3 %collective-permute-start.4 = (f32[4,24,128]{2,1,0:T(8,128)S(1)}, f32[4,24,128]{2,1,0:T(8,128)S(1)}, u32[]{:S(2)}, u32[]{:S(2)}) collective-permute-start(f32[4,24,128]{2,1,0:T(8,128)S(1)} %shard_map.61.own_ref), channel_id=1, source_target_pairs={{0,1},{1,0},{2,3},{3,2},{4,5},{5,4},{6,7},{7,6},{8,9},{9,8},{10,11... | collective-permute-start | bytes 147464 | tf_op jit(solution)/shard_map/ppermute | solution.py:339

commit v5 on v4

v5 whole, which is shorter than its diff:
```python
import functools

import jax
import jax.numpy as jnp
from jax import lax
from jax.experimental import pallas as pl
from jax.experimental.pallas import tpu as pltpu
from jax.sharding import PartitionSpec as P

DT_STEP = 0.35
VISCOSITY = 0.2
SOUND_SQ = 1.0
DRIVING = 0.5

ALL = ("gx", "gy", "gz")
DEPTH = 3
EXACT = lax.Precision.HIGHEST
VMEM = pl.BlockSpec(memory_space=pltpu.VMEM)
PARAMS = pltpu.CompilerParams(vmem_limit_bytes=40 * 1024 * 1024)


def dot(a, b, dims):
    return lax.dot_general(
        a, b, (dims, ((), ())), precision=EXACT, preferred_element_type=jnp.float32
    )


def neighbours(block_low, block_high, axis):
    count = lax.axis_size(axis)
    forward = [(i, (i + 1) % count) for i in range(count)]
    backward = [(target, source) for source, target in forward]
    return lax.ppermute(block_high, axis, forward), lax.ppermute(block_low, axis, backward)


def pack_upper(rows, tall):
    size = rows.shape[1]
    lane = lax.broadcasted_iota(jnp.int32, (tall, size), 1)
    part = [rows[tall * k : tall * k + tall] for k in range(4)]
    return [part[0], jnp.where(lane >= tall, part[1], pltpu.roll(part[3], tall, 1)), part[2]]


def unpack_upper(packed, tall):
    return [packed[0], packed[1], packed[2], pltpu.roll(packed[1], packed[1].shape[1] - tall, 1)]


def gram_kernel(basis_ref, send_ref, gram_ref, packed_ref):
    modes = basis_ref.shape[1]
    tall = gram_ref.shape[0] // 4
    total = jnp.zeros((modes, modes), jnp.float32)
    for c in range(basis_ref.shape[0]):
        rows = basis_ref[c]
        total = total + dot(rows, rows, ((1,), (1,)))
    gram_ref[...] = jnp.zeros_like(gram_ref)
    gram_ref[0:modes, 0:modes] = total
    packed_ref[...] = jnp.zeros_like(packed_ref)
    for k, value in enumerate(pack_upper(gram_ref[...], tall)):
        packed_ref[tall * k : tall * k + tall] = value
    per = send_ref.shape[1]
    for d in range(send_ref.shape[0]):
        send_ref[d] = packed_ref[per * d : per * d + per]


STRIP = 4


def strips_kernel(flow_ref, bottom_ref, top_ref):
    ny = flow_ref.shape[2]
    bottom_ref[...] = flow_ref[:, :, 0:STRIP]
    top_ref[...] = flow_ref[:, :, ny - STRIP : ny]


def walls_kernel(walls_ref, flow_ref, ylo_ref, yhi_ref, mid_ref, first_ref, last_ref):
    fields, nx, ny, nz = flow_ref.shape
    sub = lax.broadcasted_iota(jnp.int32, (2 * STRIP, nz), 0)
    outside = ((sub >= STRIP) & (walls_ref[0] == 1)) | ((sub < STRIP) & (walls_ref[1] == 1))
    for f in range(fields):
        halo = []
        for i in range(nx):
            strips = jnp.concatenate([yhi_ref[f, i], ylo_ref[f, i]], axis=0)
            halo.append(jnp.where(outside, 0.0, strips))
            mid_ref[f, i, 0:ny] = flow_ref[f, i]
            mid_ref[f, i, ny : ny + 2 * STRIP] = halo[i]
        for face_ref, begin, near, next_one in ((first_ref, 0, 0, 1), (last_ref, nx - DEPTH, nx - 1, nx - 2)):
            for k in range(DEPTH):
                face_ref[f, ny * k : ny * k + ny] = flow_ref[f, begin + k]
            face_ref[f, ny * DEPTH : ny * DEPTH + 2 * STRIP] = corner_rows(halo[near], halo[next_one], sub)


def corner_rows(near, next_one, sub):
    tile = jnp.where(sub == 2, pltpu.roll(next_one, 2, 0), pltpu.roll(next_one, 6, 0))
    tile = jnp.where((sub == 2) | (sub == 5), tile, 0.0)
    return jnp.where((sub < 2) | (sub >= 6), near, tile)


def corner_planes(tile, sub):
    near = jnp.where((sub < 2) | (sub >= 6), tile, 0.0)
    next_one = jnp.where(sub == 0, pltpu.roll(tile, 6, 0), pltpu.roll(tile, 2, 0))
    return [near, jnp.where((sub == 0) | (sub == 7), next_one, 0.0), jnp.zeros_like(tile)]


def plane_of(mid_ref, xlo_ref, xhi_ref, f, i):
    nx = mid_ref.shape[1]
    if i < DEPTH:
        return xlo_ref[f, i]
    if i < DEPTH + nx:
        return mid_ref[f, i - DEPTH]
    return xhi_ref[f, i - DEPTH - nx]


GROUP = 8


def pack_kernel(mid_ref, low_face_ref, high_face_ref, packed_ref, xlo_ref, xhi_ref):
    fields, nx, rows, nz = mid_ref.shape
    ny = rows - 2 * STRIP
    lane = lax.broadcasted_iota(jnp.int32, (rows, nz), 1)
    sub = lax.broadcasted_iota(jnp.int32, (2 * STRIP, nz), 0)
    for f in range(fields):
        for face_ref, out_ref, order in ((low_face_ref, xlo_ref, (2, 1, 0)), (high_face_ref, xhi_ref, (0, 1, 2))):
            halo = corner_planes(face_ref[f, ny * DEPTH : ny * DEPTH + 2 * STRIP], sub)
            for k in range(DEPTH):
                out_ref[f, k, 0:ny] = face_ref[f, ny * k : ny * k + ny]
                out_ref[f, k, ny:rows] = halo[order[k]]
        value = jnp.zeros((rows, nz), jnp.float32)
        for i in range(nx + 2 * DEPTH):
            start = GROUP * i
            moved = pltpu.roll(plane_of(mid_ref, xlo_ref, xhi_ref, f, i), (start + DEPTH) % nz, 1)
            value = jnp.where((lane >= start) & (lane < start + 2 * DEPTH), moved, value)
        packed_ref[f] = value


def step(value, by, axis):
    size = value.shape[axis]
    return pltpu.roll(value, (size - by) % size, axis)


def rates(centre, x_plus, x_minus, y_plus, y_minus, z_plus, z_minus):
    slope_x = [0.5 * (a - b) for a, b in zip(x_plus, x_minus)]
    slope_y = [0.5 * (a - b) for a, b in zip(y_plus, y_minus)]
    slope_z = [0.5 * (a - b) for a, b in zip(z_plus, z_minus)]
    pressure = [slope_x[3], slope_y[3], slope_z[3]]
    out = []
    for f in range(3):
        laplace = (
            x_plus[f] + x_minus[f] + (y_plus[f] + y_minus[f]) + (z_plus[f] + z_minus[f]) - 6.0 * centre[f]
        )
        advect = centre[0] * slope_x[f] + centre[1] * slope_y[f] + centre[2] * slope_z[f]
        value = VISCOSITY * laplace - advect - pressure[f]
        if f == 0:
            value = value + DRIVING
        out.append(value)
    out.append(-SOUND_SQ * (slope_x[0] + slope_y[1] + slope_z[2]))
    return out


def beyond_walls(walls_ref, ny, shape):
    row = lax.broadcasted_iota(jnp.int32, shape, 0)
    below = (row >= ny + STRIP) & (walls_ref[0] == 1)
    above = (row >= ny) & (row < ny + STRIP) & (walls_ref[1] == 1)
    return below | above


def plane_rates(read, i, rows, ends=None):
    every = range(4)
    centre = [read(f, i) for f in every]
    x_plus = [read(f, i + 1)[:rows] for f in every]
    x_minus = [read(f, i - 1)[:rows] for f in every]
    y_plus = [step(v, 1, 0)[:rows] for v in centre]
    y_minus = [step(v, -1, 0)[:rows] for v in centre]
    centre = [v[:rows] for v in centre]
    upward, downward = centre, centre
    if ends is not None:
        lane = lax.broadcasted_iota(jnp.int32, centre[0].shape, 1)
        upward = [jnp.where(lane == 0, e[:rows], v) for e, v in zip(ends, centre)]
        downward = [jnp.where(lane == lane.shape[1] - 1, e[:rows], v) for e, v in zip(ends, centre)]
    z_plus = [step(v, 1, 1) for v in upward]
    z_minus = [step(v, -1, 1) for v in downward]
    return centre, rates(centre, x_plus, x_minus, y_plus, y_minus, z_plus, z_minus)


def stage_one(outside, value, rate):
    return jnp.where(outside, 0.0, value + DT_STEP * rate)


def stage_two(outside, begin, value, rate):
    return jnp.where(outside, 0.0, 0.75 * begin + 0.25 * (value + DT_STEP * rate))


def first_kernel(walls_ref, mid_ref, xlo_ref, xhi_ref, one_ref):
    fields, nx, rows, nz = mid_ref.shape
    outside = beyond_walls(walls_ref, rows - 2 * STRIP, (rows, nz))
    for i in range(1, nx + 2 * DEPTH - 1):
        centre, rate = plane_rates(functools.partial(plane_of, mid_ref, xlo_ref, xhi_ref), i, rows)
        for f in range(4):
            one_ref[f, i - 1] = stage_one(outside, centre[f], rate[f])


def step_kernel(
    walls_ref, mid_ref, xlo_ref, xhi_ref, first_ref, own_ref, low_ref, high_ref, basis_ref, sample_ref,
    flow_ref, snap_ref, cross_ref,
    one_ref, two_ref,
):
    fields, nx, ny, nz = flow_ref.shape
    rows = mid_ref.shape[2]
    modes = basis_ref.shape[1]
    planes = nx + 2 * DEPTH
    lane = lax.broadcasted_iota(jnp.int32, (rows, nz), 1)
    outside = beyond_walls(walls_ref, ny, (rows, nz))
    every = range(4)
    start = functools.partial(plane_of, mid_ref, xlo_ref, xhi_ref)

    left = lane % GROUP < DEPTH

    def window_rates(q):
        return rates(
            q, [step(v, GROUP, 1) for v in q], [step(v, -GROUP, 1) for v in q],
            [step(v, 1, 0) for v in q], [step(v, -1, 0) for v in q],
            [step(v, 1, 1) for v in q], [step(v, -1, 1) for v in q],
        )

    own = [own_ref[f] for f in every]
    other = [jnp.where(left, low_ref[f], high_ref[f]) for f in every]
    windows = []
    for parts in ((other, own), (own, other)):
        q0 = [jnp.where(left, a, b) for a, b in zip(*parts)]
        q1 = [stage_one(outside, v, r) for v, r in zip(q0, window_rates(q0))]
        q2 = [stage_two(outside, s, v, r) for s, v, r in zip(q0, q1, window_rates(q1))]
        windows.append((q1, q2))
    (low_one, low_two), (high_one, high_two) = windows
    ends_one = [jnp.where(left, a, b) for a, b in zip(low_one, high_one)]
    ends_two = [jnp.where(left, a, b) for a, b in zip(low_two, high_two)]
    rim_one = [jnp.where(left, b, a) for a, b in zip(low_one, high_one)]

    def at_plane(values, i):
        return [pltpu.roll(v, (2 * nz - GROUP * i - DEPTH) % nz, 1) for v in values]

    rim = (lane == 0) | (lane == nz - 1)
    for i in range(1, planes - 1):
        for f, value in enumerate(at_plane(rim_one, i)):
            one_ref[f, i - 1] = jnp.where(rim, value, first_ref[f, i - 1])
    for i in range(2, planes - 2):
        centre, rate = plane_rates(lambda f, i: one_ref[f, i - 1], i, rows, at_plane(ends_one, i))
        for f in every:
            two_ref[f, i - 2] = stage_two(outside, start(f, i), centre[f], rate[f])
    for i in range(3, planes - 3):
        centre, rate = plane_rates(lambda f, i: two_ref[f, i - 2], i, ny, at_plane(ends_two, i))
        for f in every:
            value = 1.0 / 3.0 * start(f, i)[:ny] + 2.0 / 3.0 * (centre[f] + DT_STEP * rate[f])
            flow_ref[f, i - DEPTH] = value

    points = sample_ref.shape[1]
    spot = jnp.broadcast_to(sample_ref[...], (nz, points))
    place = lax.broadcasted_iota(jnp.int32, (nx * ny, points), 0)
    in_row = (place == jnp.broadcast_to(sample_ref[...] // nz, (nx * ny, points))).astype(jnp.bfloat16)
    in_lane = lax.broadcasted_iota(jnp.int32, (nz, points), 0) == spot % nz
    product = jnp.zeros((modes + 1, points), jnp.float32)
    for c in range(3):
        field = flow_ref[c].reshape(nx * ny, nz).T
        high = field.astype(jnp.bfloat16)
        rest = field - high.astype(jnp.float32)
        middle = rest.astype(jnp.bfloat16)
        low = (rest - middle.astype(jnp.float32)).astype(jnp.bfloat16)
        found = sum(
            lax.dot_general(p, in_row, (((1,), (0,)), ((), ())), preferred_element_type=jnp.float32)
            for p in (high, middle, low)
        )
        picked = jnp.sum(jnp.where(in_lane, found, 0.0), axis=0, keepdims=True)
        snap_ref[c] = picked
        product = product + jnp.concatenate([basis_ref[c], picked], axis=0) * picked
    total = jnp.sum(product, axis=1, keepdims=True)
    size = modes + 1
    diagonal = lax.broadcasted_iota(jnp.int32, (size, size), 0) == lax.broadcasted_iota(jnp.int32, (size, size), 1)
    cross_ref[...] = jnp.sum(jnp.where(diagonal, total, 0.0), axis=0, keepdims=True)


def merge_kernel(parts_ref, cross_ref, send_ref):
    total = parts_ref[0]
    for d in range(1, parts_ref.shape[0]):
        total = total + parts_ref[d]
    block = jnp.concatenate([total, cross_ref[...]], axis=0)
    for d in range(send_ref.shape[0]):
        send_ref[d] = block


def final_kernel(
    count, got_ref, basis_ref, snap_ref, flow_ref,
    basis_hbm, factor_hbm, flow_hbm,
    packed_ref, work_ref, basis_out_ref, factor_ref, sems,
):
    comps, modes, points = basis_ref.shape
    size = modes + 1
    tall = size // 4
    per = got_ref.shape[1] - 1
    copies = [pltpu.make_async_copy(flow_ref, flow_hbm, sems.at[0])]
    copies[0].start()

    total = jnp.zeros((per + 1, size), jnp.float32)
    for d in range(got_ref.shape[0]):
        block = got_ref[d]
        if per * d < packed_ref.shape[0]:
            packed_ref[per * d : per * d + per] = block[0:per]
        total = total + block
    cross = total[per : per + 1] / count
    mark = (lax.broadcasted_iota(jnp.int32, (8, size), 1) == size - 1).astype(jnp.float32)
    top = lax.broadcasted_iota(jnp.int32, (8, size), 0) == 0
    side = dot(jnp.where(top, jnp.broadcast_to(cross, (8, size)), 0.0), mark, ((0,), (0,)))
    lane = lax.broadcasted_iota(jnp.int32, (tall, size), 1)
    row = lax.broadcasted_iota(jnp.int32, (tall, size), 0)
    old = unpack_upper([packed_ref[tall * k : tall * k + tall] / count for k in range(3)], tall)
    for k in range(4):
        value = jnp.where(lane == size - 1, side[tall * k : tall * k + tall], old[k])
        if k == 3:
            value = jnp.where(row == tall - 1, jnp.broadcast_to(cross, value.shape), value)
        work_ref[tall * k : tall * k + tall, 0:size] = value
        work_ref[tall * k : tall * k + tall, size : 2 * size] = (lane == row + tall * k).astype(jnp.float32)

    stacked = [jnp.concatenate([basis_ref[c], snap_ref[c]], axis=0) for c in range(comps)]
    for k in range(4):
        base = tall * k
        eliminate(work_ref, base, tall)
        done = work_ref[base : base + tall, :]
        if k < 3:
            change = dot(done[:, 0:size], done, ((0,), (0,)))
            work_ref[base + tall : size, :] = work_ref[base + tall : size, :] - change[base + tall : size]
        factor_ref[base : base + tall, :] = jnp.where(lane >= row + base, done[:, 0:size], 0.0)
        for c in range(comps):
            basis_out_ref[c, base : base + tall, :] = dot(done[:, size : 2 * size], stacked[c], ((1,), (0,)))
        rows = (slice(None), pl.ds(base, tall), slice(None))
        copies.append(pltpu.make_async_copy(basis_out_ref.at[rows], basis_hbm.at[rows], sems.at[2 + k]))
        copies[-1].start()
    copies.append(pltpu.make_async_copy(factor_ref, factor_hbm, sems.at[1]))
    copies[-1].start()
    for copy in copies:
        copy.wait()


def eliminate(work_ref, base, tall):
    blocks = tall // 8
    sub = lax.broadcasted_iota(jnp.int32, (8, 128), 0)
    panel = [work_ref[base + 8 * b : base + 8 * b + 8, :] for b in range(blocks)]
    column = [
        [jnp.broadcast_to(panel[b][:, base + k : base + k + 1], (8, 128)) for b in range(blocks)] for k in range(tall)
    ]
    scale = [jnp.zeros((8, 128), jnp.float32) for _ in range(blocks)]
    for j in range(tall):
        mine, at = divmod(j, 8)
        pivot = column[j][mine][at : at + 1, :]
        inverse = 1.0 / pivot
        for k in range(j + 1, tall):
            other, place = divmod(k, 8)
            times = column[j][other][place : place + 1, :]
            for b in range(other, blocks):
                if k == j + 1:
                    column[k][b] = column[k][b] - (column[j][b] * times) * inverse
                else:
                    column[k][b] = column[k][b] - column[j][b] * (times * inverse)
        scale[mine] = jnp.where(sub == at, lax.rsqrt(pivot), scale[mine])
        pivot_row = panel[mine][at : at + 1, :] * jnp.concatenate([inverse, inverse], axis=1)
        for b in range(mine, blocks):
            times = jnp.where(sub > at, column[j][b], 0.0) if b == mine else column[j][b]
            panel[b] = panel[b] - jnp.concatenate([times, times], axis=1) * pivot_row
    for b in range(blocks):
        work_ref[base + 8 * b : base + 8 * b + 8, :] = panel[b] * jnp.concatenate([scale[b], scale[b]], axis=1)


def local(flow, basis, sample):
    fields, nx, ny, nz = flow.shape
    modes, comps, points = basis.shape
    size = modes + 1
    devices = lax.axis_size("gx") * lax.axis_size("gy") * lax.axis_size("gz")
    count = float(comps * points * devices)
    shape = functools.partial(jax.ShapeDtypeStruct, dtype=jnp.float32)
    call = functools.partial(pl.pallas_call, compiler_params=PARAMS)
    bricks = jnp.transpose(basis, (1, 0, 2))

    smem = pl.BlockSpec(memory_space=pltpu.SMEM)
    quarter = size // 4
    per = -(-3 * quarter // devices)

    strip = shape((fields, nx, STRIP, nz))
    bottom, top = call(strips_kernel, out_shape=(strip, strip), in_specs=[VMEM], out_specs=(VMEM, VMEM))(flow)
    ylo, yhi = neighbours(bottom, top, "gy")
    gram = call(
        gram_kernel,
        out_shape=shape((devices, per, size)),
        in_specs=[VMEM],
        out_specs=VMEM,
        scratch_shapes=[pltpu.VMEM((size, size), jnp.float32), pltpu.VMEM((devices * per, size), jnp.float32)],
    )(bricks)
    ylo, yhi, gram = lax.optimization_barrier((ylo, yhi, gram))

    rows = ny + 2 * STRIP
    place = lax.axis_index("gy")
    walls = jnp.stack([place == 0, place == lax.axis_size("gy") - 1]).astype(jnp.int32)
    face = shape((fields, DEPTH * ny + 2 * STRIP, nz))
    mid, first, last = call(
        walls_kernel,
        out_shape=(shape((fields, nx, rows, nz)), face, face),
        in_specs=[smem] + [VMEM] * 3,
        out_specs=(VMEM,) * 3,
    )(walls, flow, ylo, yhi)
    low_face, high_face = neighbours(first, last, "gx")
    parts = lax.all_to_all(gram, ALL, 0, 0)

    beside = shape((fields, DEPTH, rows, nz))
    packed, xlo, xhi = call(
        pack_kernel,
        out_shape=(shape((fields, rows, nz)), beside, beside),
        in_specs=[VMEM] * 3,
        out_specs=(VMEM,) * 3,
    )(mid, low_face, high_face)
    if lax.axis_size("gz") == 2:
        low = high = lax.ppermute(packed, "gz", [(0, 1), (1, 0)])
    else:
        low, high = neighbours(packed, packed, "gz")
    begun = call(
        first_kernel,
        out_shape=shape((fields, nx + 2 * DEPTH - 2, rows, nz)),
        in_specs=[smem] + [VMEM] * 3,
        out_specs=VMEM,
    )(walls, mid, xlo, xhi)
    flow_new, snapshot, cross = call(
        step_kernel,
        out_shape=(shape(flow.shape), shape((comps, 1, points)), shape((1, size))),
        in_specs=[smem] + [VMEM] * 9,
        out_specs=(VMEM, VMEM, VMEM),
        scratch_shapes=[
            pltpu.VMEM((fields, nx + 2 * DEPTH - 2, rows, nz), jnp.float32),
            pltpu.VMEM((fields, nx + 2 * DEPTH - 4, rows, nz), jnp.float32),
        ],
    )(walls, mid, xlo, xhi, begun, packed, low, high, bricks, sample.reshape(1, points))

    send = call(
        merge_kernel, out_shape=shape((devices, per + 1, size)), in_specs=[VMEM] * 2, out_specs=VMEM
    )(parts, cross)
    got = lax.all_to_all(send, ALL, 0, 0)
    whole = pl.BlockSpec(memory_space=pltpu.HBM)
    basis_next, factor, flow_next = call(
        functools.partial(final_kernel, count),
        out_shape=(shape((comps, size, points)), shape((size, size)), shape(flow.shape)),
        in_specs=[VMEM] * 4,
        out_specs=(whole,) * 3,
        scratch_shapes=[
            pltpu.VMEM((3 * quarter, size), jnp.float32),
            pltpu.VMEM((size, 2 * size), jnp.float32),
            pltpu.VMEM((comps, size, points), jnp.float32),
            pltpu.VMEM((size, size), jnp.float32),
            pltpu.SemaphoreType.DMA((6,)),
        ],
    )(got, bricks, snapshot, flow_new)
    return flow_next, jnp.transpose(basis_next, (1, 0, 2)), factor


def solution(mesh):
    return jax.shard_map(
        local,
        mesh=mesh,
        in_specs=(
            P(None, "gx", "gy", "gz"),
            P(None, None, ("gx", "gy", "gz")),
            P(("gx", "gy", "gz")),
        ),
        out_specs=(P(None, "gx", "gy", "gz"), P(None, None, ("gx", "gy", "gz")), P()),
        check_vma=False,
    )
```

time: 41.5 us -> 40.5 us (0.976)
  blocking collectives: 11.5 us -> 10.3 us
  waiting for transfers between devices: 5.5 us -> 4.43 us
  Pallas kernels: 9.96 us -> 10.6 us
  local copies, waits for them, and re-layouts: 1.95 us -> 2.49 us
    all_to_all x1, waiting for transfers between devices: 1.02 us -> 2.53 us  [local(): parts = lax.all_to_all(gram, ALL, 0, 0)]
    all_to_all x1, blocking collectives: 11.5 us -> 10.3 us  [local(): got = lax.all_to_all(send, ALL, 0, 0)]
    pallas_call x4 -> x5, Pallas kernels: 1.43 us -> 2.57 us  [the longest x1 1.2 us: local(): call(gram_kernel, out_shape=shape((devices, per, size)), in_specs=[VMEM],...]
    ppermute x1, waiting for transfers between devices: 1.22 us -> 0.13 us  [local(): low = high = lax.ppermute(packed, 'gz', [(0, 1), (1, 0)])]
    ppermute x2, waiting for transfers between devices: 0.95 us -> 0.05 us  [neighbours(): lax.ppermute(block_high, axis, forward)]
    pallas_call x1, Pallas kernels: 3.05 us -> 2.41 us  [local(): call(step_kernel, out_shape=(shape(flow.shape), shape((comps, 1, points))...]
    ppermute x2, waiting for transfers between devices: 2.32 us -> 1.72 us  [neighbours(): lax.ppermute(block_low, axis, backward)]
    unnamed x10, local copies, waits for them, and re-layouts: 1.95 us -> 2.49 us
  transfers between devices with their start and end apart: 6 -> 6, of which waited for: 6 -> 5; matrix products, arithmetic and copies ran while one was open for 0% -> 0% of each run, Pallas kernels for 11% -> 12%
where the time goes in v5:
time: 40.5 us; the launch traced here: 40.2 us
  starting transfers between devices  11.5 us (28%)
  Pallas kernels  10.6 us (26%)
  blocking collectives  10.3 us (25%)
  waiting for transfers between devices  4.43 us (11%)
  local copies, waits for them, and re-layouts  2.49 us (6%)
  between operations  0.72 us (2%)
    all_to_all x1, blocking collectives, local(): got = lax.all_to_all(send, ALL, 0, 0)  10.3 us
    pallas_call x1, Pallas kernels, local(): call(functools.partial(final_kernel, count), out_shape=(shape((comps, siz...  5.08 us
    ppermute x2, starting transfers between devices, neighbours(): lax.ppermute(block_high, axis, forward)  4.62 us
    all_to_all x1, starting transfers between devices, local(): parts = lax.all_to_all(gram, ALL, 0, 0)  3.56 us
    ppermute x2, starting transfers between devices, neighbours(): lax.ppermute(block_low, axis, backward)  3.27 us
    all_to_all x1, waiting for transfers between devices, local(): parts = lax.all_to_all(gram, ALL, 0, 0)  2.53 us
    unnamed x10, local copies, waits for them, and re-layouts  2.49 us
    pallas_call x1, Pallas kernels, local(): call(step_kernel, out_shape=(shape(flow.shape), shape((comps, 1, points))...  2.41 us
  transfers between devices with their start and end apart: 6, of which 5 were waited for; matrix products, arithmetic and copies ran while one was open for 0% of the time, Pallas kernels for 12%

profile of v5, /device:TPU:0, one launch (start us, length us, event | category | flops | bytes accessed | tf_op | source)
XLA Modules:
  0.0 40.2 jit_solution(11925454475531294154)
XLA Ops:
  0.6 0.9 %copy-done.2 = f32[4,8,16,128]{3,2,1,0:T(8,128)S(1)} copy-done((f32[4,8,16,128]{3,2,1,0:T(8,128)S(1)}, f32[4,8,16,128]{3,2,1,0:T(8,128)}, u32[]{:S(2)}) %copy-start.2) | copy-done | bytes 262168
  1.6 3.0 %collective-permute-start = (f32[4,8,4,128]{3,2,1,0:T(4,128)S(1)}, f32[4,8,4,128]{3,2,1,0:T(4,128)S(1)}, u32[]{:S(2)}, u32[]{:S(2)}) collective-permute-start(f32[4,8,4,128]{3,2,1,0:T(4,128)S(1)} %get-tuple-element.20), channel_id=1, source_target_pairs={{0,2},{2,4},{4,6},{6,0},{1,3},{3,5},{5,7},{7,1},{8,10},{10,12},{12... | collective-permute-start | bytes 196616 | tf_op jit(solution)/shard_map/ppermute | solution.py:32
  4.6 1.0 %collective-permute-start.1 = (f32[4,8,4,128]{3,2,1,0:T(4,128)S(1)}, f32[4,8,4,128]{3,2,1,0:T(4,128)S(1)}, u32[]{:S(2)}, u32[]{:S(2)}) collective-permute-start(f32[4,8,4,128]{3,2,1,0:T(4,128)S(1)} %get-tuple-element.21), channel_id=1, source_target_pairs={{2,0},{4,2},{6,4},{0,6},{3,1},{5,3},{7,5},{1,7},{10,8},{12,10},{14... | collective-permute-start | bytes 196616 | tf_op jit(solution)/shard_map/ppermute | solution.py:32
  5.6 1.0 %copy-done = f32[127,3,256]{2,0,1:T(8,128)S(1)} copy-done((f32[127,3,256]{2,0,1:T(8,128)S(1)}, f32[127,3,256]{2,0,1:T(8,128)}, u32[]{:S(2)}) %copy-start) | copy-done | bytes 390168
  6.6 1.2 %shard_map.59 = f32[32,3,128]{2,1,0:T(4,128)} custom-call(f32[3,127,256]{2,1,0:T(8,128)S(1)} %bitcast.5), custom_call_target="tpu_custom_call" | custom-call | tf_op jit(solution)/shard_map/pallas_call | solution.py:383
  7.8 0.1 add_convert_fusion.walls_ref
  7.9 0.1 collective-permute-done.ylo_ref
  7.9 1.4 %collective-permute-done.1.yhi_ref = f32[4,8,4,128]{3,2,1,0:T(4,128)S(1)} collective-permute-done((f32[4,8,4,128]{3,2,1,0:T(4,128)S(1)}, f32[4,8,4,128]{3,2,1,0:T(4,128)S(1)}, u32[]{:S(2)}, u32[]{:S(2)}) %collective-permute-start.1) | collective-permute-done | bytes 65568 | tf_op jit(solution)/shard_map/ppermute | solution.py:32
  9.3 0.6 %shard_map.60 = (f32[4,8,24,128]{3,2,1,0:T(8,128)S(1)}, f32[4,56,128]{2,1,0:T(8,128)S(1)}, f32[4,56,128]{2,1,0:T(8,128)S(1)}) custom-call(s32[2]{0:T(128)S(1)} %add_convert_fusion.walls_ref, f32[4,8,16,128]{3,2,1,0:T(8,128)S(1)} %copy-done.3, f32[4,8,4,128]{3,2,1,0:T(4,128)S(1)} %collective-permute-done.ylo_ref, ...), custom_call_target="tpu_custom_call" | custom-call | tf_op jit(solution)/shard_map/pallas_call | solution.py:396
  9.9 1.6 %collective-permute-start.2 = (f32[4,56,128]{2,1,0:T(8,128)S(1)}, f32[4,56,128]{2,1,0:T(8,128)S(1)}, u32[]{:S(2)}, u32[]{:S(2)}) collective-permute-start(f32[4,56,128]{2,1,0:T(8,128)S(1)} %get-tuple-element.26), channel_id=1, source_target_pairs={{0,8},{8,16},{16,24},{24,0},{1,9},{9,17},{17,25},{25,1},{2,10},{10... | collective-permute-start | bytes 344072 | tf_op jit(solution)/shard_map/ppermute | solution.py:32
  11.5 2.2 %collective-permute-start.3 = (f32[4,56,128]{2,1,0:T(8,128)S(1)}, f32[4,56,128]{2,1,0:T(8,128)S(1)}, u32[]{:S(2)}, u32[]{:S(2)}) collective-permute-start(f32[4,56,128]{2,1,0:T(8,128)S(1)} %get-tuple-element.27), channel_id=1, source_target_pairs={{8,0},{16,8},{24,16},{0,24},{9,1},{17,9},{25,17},{1,25},{10,2},{18... | collective-permute-start | bytes 344072 | tf_op jit(solution)/shard_map/ppermute | solution.py:32
  13.8 3.6 %all-to-all-start = ((f32[32,3,128]{2,1,0:T(4,128)}), f32[32,3,128]{2,1,0:T(4,128)S(1)}, u32[]{:S(2)}, u32[]{:S(2)}) async-start(f32[32,3,128]{2,1,0:T(4,128)} %shard_map.59), calls=%async_computation | async-start | bytes 131072 | tf_op jit(solution)/shard_map/all_to_all | solution.py:403
  17.4 0.4 collective-permute-done.3.high_face_ref
  17.7 0.2 shard_map.61
  18.0 0.1 collective-permute-start.4
  18.0 0.0 copy-start.1
  18.1 1.1 %shard_map.62.first_ref = f32[4,12,24,128]{3,2,1,0:T(8,128)S(1)} custom-call(s32[2]{0:T(128)S(1)} %add_convert_fusion.walls_ref, f32[4,8,24,128]{3,2,1,0:T(8,128)S(1)} %get-tuple-element.25.mid_ref, f32[4,3,24,128]{3,2,1,0:T(8,128)S(1)} %get-tuple-element.28.xlo_ref, f32[4,3,24,128]{3,2,1,0:T(8,128)S(1)} %get-tuple-element.29.xhi_ref), custom_call_target="tpu_custom_call" | custom-call | tf_op jit(solution)/shard_map/pallas_call | solution.py:416
  19.1 0.0 copy-start.4
  19.1 0.1 collective-permute-done.4.low_ref.high_ref
  19.3 0.5 %copy-done.4 = s32[256]{0:T(256)S(1)} copy-done((s32[256]{0:T(256)S(1)}, s32[256]{0:T(256)}, u32[]{:S(2)}) %copy-start.4) | copy-done | bytes 1048
  19.8 2.4 %shard_map.63 = (f32[4,8,16,128]{3,2,1,0:T(8,128)S(1)}, f32[3,1,256]{2,1,0:T(1,128)S(1)}, f32[1,128]{1,0:T(1,128)S(1)}) custom-call(s32[2]{0:T(128)S(1)} %add_convert_fusion.walls_ref, f32[4,8,24,128]{3,2,1,0:T(8,128)S(1)} %get-tuple-element.25.mid_ref, f32[4,3,24,128]{3,2,1,0:T(8,128)S(1)} %get-tuple-element.28.xlo_ref, ...), custom_call_target="tpu_custom_call" | custom-call | tf_op jit(solution)/shard_map/pallas_call | solution.py:422
  22.2 2.5 %all-to-all-done.parts_ref = f32[32,3,128]{2,1,0:T(4,128)S(1)} async-done(((f32[32,3,128]{2,1,0:T(4,128)}), f32[32,3,128]{2,1,0:T(4,128)S(1)}, u32[]{:S(2)}, u32[]{:S(2)}) %all-to-all-start) | async-done | bytes 49184 | tf_op jit(solution)/shard_map/all_to_all | solution.py:403
  24.8 10.3 %all_to_all.10.got_ref = f32[32,4,128]{2,1,0:T(4,128)S(1)} all-to-all(f32[32,4,128]{2,1,0:T(4,128)S(1)} %shard_map.64), channel_id=1, replica_groups=mesh['gx'=4,'gy'=4,'gz'=2] {'gx','gy','gz'}, dimensions={0} | all-to-all | bytes 131072 | tf_op jit(solution)/shard_map/all_to_all | solution.py:436
  35.1 5.1 %shard_map.65 = (f32[3,128,256]{2,1,0:T(8,128)}, f32[128,128]{1,0:T(8,128)}, f32[4,8,16,128]{3,2,1,0:T(8,128)}) custom-call(f32[32,4,128]{2,1,0:T(4,128)S(1)} %all_to_all.10.got_ref, f32[3,127,256]{2,1,0:T(8,128)S(1)} %bitcast.7, f32[3,1,256]{2,1,0:T(1,128)S(1)} %get-tuple-element.32.snap_ref, f32[4,8,16,128]{3,2,1,0:T(8,128)S(1)} %get-tuple-element.33.flow_ref), custom_call_target="tpu_custom_call" | custom-call | tf_op jit(solution)/shard_map/pallas_call | solution.py:438
  (8 shorter events, 0.1 us)
Async XLA Ops:
  0.6 1.0 %copy-start.2 = (f32[4,8,16,128]{3,2,1,0:T(8,128)S(1)}, f32[4,8,16,128]{3,2,1,0:T(8,128)}, u32[]{:S(2)}) copy-start(f32[4,8,16,128]{3,2,1,0:T(8,128)} %flow_ref.3) | copy-start | bytes 786436
  1.6 7.7 %copy-start.3 = (f32[4,8,16,128]{3,2,1,0:T(8,128)S(1)}, f32[4,8,16,128]{3,2,1,0:T(8,128)}, u32[]{:S(2)}) copy-start(f32[4,8,16,128]{3,2,1,0:T(8,128)} %flow_ref.3) | copy-start | bytes 786436
  1.6 6.3 %collective-permute-start = (f32[4,8,4,128]{3,2,1,0:T(4,128)S(1)}, f32[4,8,4,128]{3,2,1,0:T(4,128)S(1)}, u32[]{:S(2)}, u32[]{:S(2)}) collective-permute-start(f32[4,8,4,128]{3,2,1,0:T(4,128)S(1)} %get-tuple-element.20), channel_id=1, source_target_pairs={{0,2},{2,4},{4,6},{6,0},{1,3},{3,5},{5,7},{7,1},{8,10},{10,12},{12... | collective-permute-start | bytes 196616 | tf_op jit(solution)/shard_map/ppermute | solution.py:32
  4.6 4.7 %collective-permute-start.1 = (f32[4,8,4,128]{3,2,1,0:T(4,128)S(1)}, f32[4,8,4,128]{3,2,1,0:T(4,128)S(1)}, u32[]{:S(2)}, u32[]{:S(2)}) collective-permute-start(f32[4,8,4,128]{3,2,1,0:T(4,128)S(1)} %get-tuple-element.21), channel_id=1, source_target_pairs={{2,0},{4,2},{6,4},{0,6},{3,1},{5,3},{7,5},{1,7},{10,8},{12,10},{14... | collective-permute-start | bytes 196616 | tf_op jit(solution)/shard_map/ppermute | solution.py:32
  5.6 1.0 %copy-start = (f32[127,3,256]{2,0,1:T(8,128)S(1)}, f32[127,3,256]{2,0,1:T(8,128)}, u32[]{:S(2)}) copy-start(f32[127,3,256]{2,0,1:T(8,128)} %param.4) | copy-start | bytes 1170436
  9.9 7.4 %collective-permute-start.2 = (f32[4,56,128]{2,1,0:T(8,128)S(1)}, f32[4,56,128]{2,1,0:T(8,128)S(1)}, u32[]{:S(2)}, u32[]{:S(2)}) collective-permute-start(f32[4,56,128]{2,1,0:T(8,128)S(1)} %get-tuple-element.26), channel_id=1, source_target_pairs={{0,8},{8,16},{16,24},{24,0},{1,9},{9,17},{17,25},{25,1},{2,10},{10... | collective-permute-start | bytes 344072 | tf_op jit(solution)/shard_map/ppermute | solution.py:32
  11.5 6.2 %collective-permute-start.3 = (f32[4,56,128]{2,1,0:T(8,128)S(1)}, f32[4,56,128]{2,1,0:T(8,128)S(1)}, u32[]{:S(2)}, u32[]{:S(2)}) collective-permute-start(f32[4,56,128]{2,1,0:T(8,128)S(1)} %get-tuple-element.27), channel_id=1, source_target_pairs={{8,0},{16,8},{24,16},{0,24},{9,1},{17,9},{25,17},{1,25},{10,2},{18... | collective-permute-start | bytes 344072 | tf_op jit(solution)/shard_map/ppermute | solution.py:32
  13.8 11.0 %all-to-all-start = ((f32[32,3,128]{2,1,0:T(4,128)}), f32[32,3,128]{2,1,0:T(4,128)S(1)}, u32[]{:S(2)}, u32[]{:S(2)}) async-start(f32[32,3,128]{2,1,0:T(4,128)} %shard_map.59), calls=%async_computation | async-start | bytes 131072 | tf_op jit(solution)/shard_map/all_to_all | solution.py:403
  18.0 1.3 %collective-permute-start.4 = (f32[4,24,128]{2,1,0:T(8,128)S(1)}, f32[4,24,128]{2,1,0:T(8,128)S(1)}, u32[]{:S(2)}, u32[]{:S(2)}) collective-permute-start(f32[4,24,128]{2,1,0:T(8,128)S(1)} %get-tuple-element.30.own_ref), channel_id=1, source_target_pairs={{0,1},{1,0},{2,3},{3,2},{4,5},{5,4},{6,7},{7,6},{8,9},{9,8},{10,11... | collective-permute-start | bytes 147464 | tf_op jit(solution)/shard_map/ppermute | solution.py:413
  18.0 1.2 %copy-start.1 = (f32[127,3,256]{2,0,1:T(8,128)S(1)}, f32[127,3,256]{2,0,1:T(8,128)}, u32[]{:S(2)}) copy-start(f32[127,3,256]{2,0,1:T(8,128)} %param.4) | copy-start | bytes 1170436
  19.1 0.7 %copy-start.4 = (s32[256]{0:T(256)S(1)}, s32[256]{0:T(256)}, u32[]{:S(2)}) copy-start(s32[256]{0:T(256)} %param.5) | copy-start | bytes 3076

commit v6 on v5

--- a/solution.py
+++ b/solution.py
@@ -60,30 +60,43 @@
         send_ref[d] = packed_ref[per * d : per * d + per]
 
 
-STRIP = 4
-
-
-def strips_kernel(flow_ref, bottom_ref, top_ref):
-    ny = flow_ref.shape[2]
-    bottom_ref[...] = flow_ref[:, :, 0:STRIP]
-    top_ref[...] = flow_ref[:, :, ny - STRIP : ny]
-
-
-def walls_kernel(walls_ref, flow_ref, ylo_ref, yhi_ref, mid_ref, first_ref, last_ref):
-    fields, nx, ny, nz = flow_ref.shape
-    sub = lax.broadcasted_iota(jnp.int32, (2 * STRIP, nz), 0)
-    outside = ((sub >= STRIP) & (walls_ref[0] == 1)) | ((sub < STRIP) & (walls_ref[1] == 1))
+GAP = 2
+HALO = 2 * DEPTH + GAP
+
+
+def strips_kernel(planes, flow_ref, bottom_ref, top_ref):
+    ny = flow_ref.shape[1] // planes
+    for f in range(flow_ref.shape[0]):
+        for j in range(DEPTH):
+            bottom_ref[f, planes * j : planes * j + planes] = flow_ref[f, pl.ds(j, planes, stride=ny), :]
+            top_ref[f, planes * j : planes * j + planes] = flow_ref[f, pl.ds(ny - DEPTH + j, planes, stride=ny), :]
+
+
+def walls_kernel(planes, walls_ref, flow_ref, ylo_ref, yhi_ref, mid_ref, first_ref, last_ref):
+    fields, cells, nz = flow_ref.shape
+    ny = cells // planes
+    rows = ny + HALO
+    sub = lax.broadcasted_iota(jnp.int32, (HALO, nz), 0)
+    empty = jnp.zeros((planes, nz), jnp.float32)
     for f in range(fields):
-        halo = []
-        for i in range(nx):
-            strips = jnp.concatenate([yhi_ref[f, i], ylo_ref[f, i]], axis=0)
-            halo.append(jnp.where(outside, 0.0, strips))
-            mid_ref[f, i, 0:ny] = flow_ref[f, i]
-            mid_ref[f, i, ny : ny + 2 * STRIP] = halo[i]
-        for face_ref, begin, near, next_one in ((first_ref, 0, 0, 1), (last_ref, nx - DEPTH, nx - 1, nx - 2)):
+        for i in range(planes):
+            mid_ref[f, rows * i : rows * i + ny] = flow_ref[f, ny * i : ny * i + ny]
+        for j in range(HALO):
+            if j < DEPTH:
+                value = jnp.where(walls_ref[1] == 1, 0.0, yhi_ref[f, planes * j : planes * j + planes])
+            elif j < DEPTH + GAP:
+                value = empty
+            else:
+                k = j - DEPTH - GAP
+                value = jnp.where(walls_ref[0] == 1, 0.0, ylo_ref[f, planes * k : planes * k + planes])
+            mid_ref[f, pl.ds(ny + j, planes, stride=rows), :] = value
+        for face_ref, begin, near, next_one in (
+            (first_ref, 0, 0, 1), (last_ref, planes - DEPTH, planes - 1, planes - 2)
+        ):
             for k in range(DEPTH):
-                face_ref[f, ny * k : ny * k + ny] = flow_ref[f, begin + k]
-            face_ref[f, ny * DEPTH : ny * DEPTH + 2 * STRIP] = corner_rows(halo[near], halo[next_one], sub)
+                face_ref[f, ny * k : ny * k + ny] = flow_ref[f, ny * (begin + k) : ny * (begin + k) + ny]
+            halos = [mid_ref[f, rows * i + ny : rows * i + rows] for i in (near, next_one)]
+            face_ref[f, ny * DEPTH : ny * DEPTH + HALO] = corner_rows(*halos, sub)
 
 
 def corner_rows(near, next_one, sub):
@@ -112,12 +125,12 @@
 
 def pack_kernel(mid_ref, low_face_ref, high_face_ref, packed_ref, xlo_ref, xhi_ref):
     fields, nx, rows, nz = mid_ref.shape
-    ny = rows - 2 * STRIP
+    ny = rows - HALO
     lane = lax.broadcasted_iota(jnp.int32, (rows, nz), 1)
-    sub = lax.broadcasted_iota(jnp.int32, (2 * STRIP, nz), 0)
+    sub = lax.broadcasted_iota(jnp.int32, (HALO, nz), 0)
     for f in range(fields):
         for face_ref, out_ref, order in ((low_face_ref, xlo_ref, (2, 1, 0)), (high_face_ref, xhi_ref, (0, 1, 2))):
-            halo = corner_planes(face_ref[f, ny * DEPTH : ny * DEPTH + 2 * STRIP], sub)
+            halo = corner_planes(face_ref[f, ny * DEPTH : ny * DEPTH + HALO], sub)
             for k in range(DEPTH):
                 out_ref[f, k, 0:ny] = face_ref[f, ny * k : ny * k + ny]
                 out_ref[f, k, ny:rows] = halo[order[k]]
@@ -155,8 +168,8 @@
 
 def beyond_walls(walls_ref, ny, shape):
     row = lax.broadcasted_iota(jnp.int32, shape, 0)
-    below = (row >= ny + STRIP) & (walls_ref[0] == 1)
-    above = (row >= ny) & (row < ny + STRIP) & (walls_ref[1] == 1)
+    below = (row >= ny + DEPTH + GAP) & (walls_ref[0] == 1)
+    above = (row >= ny) & (row < ny + DEPTH) & (walls_ref[1] == 1)
     return below | above
 
 
@@ -186,13 +199,16 @@
     return jnp.where(outside, 0.0, 0.75 * begin + 0.25 * (value + DT_STEP * rate))
 
 
-def first_kernel(walls_ref, mid_ref, xlo_ref, xhi_ref, one_ref):
+def first_kernel(walls_ref, sample_hbm, mid_ref, xlo_ref, xhi_ref, one_ref, sample_ref, sem):
+    copy = pltpu.make_async_copy(sample_hbm, sample_ref, sem)
+    copy.start()
     fields, nx, rows, nz = mid_ref.shape
-    outside = beyond_walls(walls_ref, rows - 2 * STRIP, (rows, nz))
+    outside = beyond_walls(walls_ref, rows - HALO, (rows, nz))
     for i in range(1, nx + 2 * DEPTH - 1):
         centre, rate = plane_rates(functools.partial(plane_of, mid_ref, xlo_ref, xhi_ref), i, rows)
         for f in range(4):
             one_ref[f, i - 1] = stage_one(outside, centre[f], rate[f])
+    copy.wait()
 
 
 def step_kernel(
@@ -301,14 +317,12 @@
             packed_ref[per * d : per * d + per] = block[0:per]
         total = total + block
     cross = total[per : per + 1] / count
-    mark = (lax.broadcasted_iota(jnp.int32, (8, size), 1) == size - 1).astype(jnp.float32)
-    top = lax.broadcasted_iota(jnp.int32, (8, size), 0) == 0
-    side = dot(jnp.where(top, jnp.broadcast_to(cross, (8, size)), 0.0), mark, ((0,), (0,)))
     lane = lax.broadcasted_iota(jnp.int32, (tall, size), 1)
     row = lax.broadcasted_iota(jnp.int32, (tall, size), 0)
     old = unpack_upper([packed_ref[tall * k : tall * k + tall] / count for k in range(3)], tall)
     for k in range(4):
-        value = jnp.where(lane == size - 1, side[tall * k : tall * k + tall], old[k])
+        side = jnp.sum(jnp.where(lane == row + tall * k, cross, 0.0), axis=1, keepdims=True)
+        value = jnp.where(lane == size - 1, side, old[k])
         if k == 3:
             value = jnp.where(row == tall - 1, jnp.broadcast_to(cross, value.shape), value)
         work_ref[tall * k : tall * k + tall, 0:size] = value
@@ -374,11 +388,15 @@
     bricks = jnp.transpose(basis, (1, 0, 2))
 
     smem = pl.BlockSpec(memory_space=pltpu.SMEM)
+    whole = pl.BlockSpec(memory_space=pltpu.HBM)
+    flat = flow.reshape(fields, nx * ny, nz)
     quarter = size // 4
     per = -(-3 * quarter // devices)
 
-    strip = shape((fields, nx, STRIP, nz))
-    bottom, top = call(strips_kernel, out_shape=(strip, strip), in_specs=[VMEM], out_specs=(VMEM, VMEM))(flow)
+    strip = shape((fields, nx * DEPTH, nz))
+    bottom, top = call(
+        functools.partial(strips_kernel, nx), out_shape=(strip, strip), in_specs=[VMEM], out_specs=(VMEM, VMEM)
+    )(flat)
     ylo, yhi = neighbours(bottom, top, "gy")
     gram = call(
         gram_kernel,
@@ -389,16 +407,17 @@
     )(bricks)
     ylo, yhi, gram = lax.optimization_barrier((ylo, yhi, gram))
 
-    rows = ny + 2 * STRIP
+    rows = ny + HALO
     place = lax.axis_index("gy")
     walls = jnp.stack([place == 0, place == lax.axis_size("gy") - 1]).astype(jnp.int32)
-    face = shape((fields, DEPTH * ny + 2 * STRIP, nz))
+    face = shape((fields, DEPTH * ny + HALO, nz))
     mid, first, last = call(
-        walls_kernel,
-        out_shape=(shape((fields, nx, rows, nz)), face, face),
+        functools.partial(walls_kernel, nx),
+        out_shape=(shape((fields, nx * rows, nz)), face, face),
         in_specs=[smem] + [VMEM] * 3,
         out_specs=(VMEM,) * 3,
-    )(walls, flow, ylo, yhi)
+    )(walls, flat, ylo, yhi)
+    mid = mid.reshape(fields, nx, rows, nz)
     low_face, high_face = neighbours(first, last, "gx")
     parts = lax.all_to_all(gram, ALL, 0, 0)
 
@@ -413,12 +432,16 @@
         low = high = lax.ppermute(packed, "gz", [(0, 1), (1, 0)])
     else:
         low, high = neighbours(packed, packed, "gz")
-    begun = call(
+    begun, cells = call(
         first_kernel,
-        out_shape=shape((fields, nx + 2 * DEPTH - 2, rows, nz)),
-        in_specs=[smem] + [VMEM] * 3,
-        out_specs=VMEM,
-    )(walls, mid, xlo, xhi)
+        out_shape=(
+            shape((fields, nx + 2 * DEPTH - 2, rows, nz)),
+            jax.ShapeDtypeStruct((1, points), sample.dtype),
+        ),
+        in_specs=[smem, whole] + [VMEM] * 3,
+        out_specs=(VMEM, VMEM),
+        scratch_shapes=[pltpu.SemaphoreType.DMA],
+    )(walls, sample.reshape(1, points), mid, xlo, xhi)
     flow_new, snapshot, cross = call(
         step_kernel,
         out_shape=(shape(flow.shape), shape((comps, 1, points)), shape((1, size))),
@@ -428,13 +451,12 @@
             pltpu.VMEM((fields, nx + 2 * DEPTH - 2, rows, nz), jnp.float32),
             pltpu.VMEM((fields, nx + 2 * DEPTH - 4, rows, nz), jnp.float32),
         ],
-    )(walls, mid, xlo, xhi, begun, packed, low, high, bricks, sample.reshape(1, points))
+    )(walls, mid, xlo, xhi, begun, packed, low, high, bricks, cells)
 
     send = call(
         merge_kernel, out_shape=shape((devices, per + 1, size)), in_specs=[VMEM] * 2, out_specs=VMEM
     )(parts, cross)
     got = lax.all_to_all(send, ALL, 0, 0)
-    whole = pl.BlockSpec(memory_space=pltpu.HBM)
     basis_next, factor, flow_next = call(
         functools.partial(final_kernel, count),
         out_shape=(shape((comps, size, points)), shape((size, size)), shape(flow.shape)),

time: 40.5 us -> 39.9 us (0.985)
  starting transfers between devices: 11.5 us -> 12.2 us
  waiting for transfers between devices: 4.43 us -> 3.98 us
  local copies, waits for them, and re-layouts: 2.49 us -> 2.05 us
  blocking collectives: 10.3 us -> 9.88 us
    ppermute x2, waiting for transfers between devices: 1.72 us -> 0.79 us  [neighbours(): lax.ppermute(block_low, axis, backward)]
    all_to_all x1, waiting for transfers between devices: 2.53 us -> 3.18 us  [local(): parts = lax.all_to_all(gram, ALL, 0, 0)]
    unnamed x10, local copies, waits for them, and re-layouts: 2.49 us -> 2.05 us
    all_to_all x1, blocking collectives: 10.3 us -> 9.88 us  [local(): got = lax.all_to_all(send, ALL, 0, 0)]
    all_to_all x1, starting transfers between devices: 3.56 us -> 4 us  [local(): parts = lax.all_to_all(gram, ALL, 0, 0)]
  transfers between devices with their start and end apart: 6 -> 6, of which waited for: 5 -> 2; matrix products, arithmetic and copies ran while one was open for 0% -> 0% of each run, Pallas kernels for 12% -> 12%
where the time goes in v6:
time: 39.9 us; the launch traced here: 39.7 us
  starting transfers between devices  12.2 us (31%)
  Pallas kernels  10.8 us (27%)
  blocking collectives  9.88 us (25%)
  waiting for transfers between devices  3.98 us (10%)
  local copies, waits for them, and re-layouts  2.05 us (5%)
  between operations  0.73 us (2%)
    all_to_all x1, blocking collectives, local(): got = lax.all_to_all(send, ALL, 0, 0)  9.88 us
    pallas_call x1, Pallas kernels, local(): call(functools.partial(final_kernel, count), out_shape=(shape((comps, siz...  5.16 us
    ppermute x2, starting transfers between devices, neighbours(): lax.ppermute(block_high, axis, forward)  4.63 us
    all_to_all x1, starting transfers between devices, local(): parts = lax.all_to_all(gram, ALL, 0, 0)  4 us
    ppermute x2, starting transfers between devices, neighbours(): lax.ppermute(block_low, axis, backward)  3.25 us
    all_to_all x1, waiting for transfers between devices, local(): parts = lax.all_to_all(gram, ALL, 0, 0)  3.18 us
    pallas_call x1, Pallas kernels, local(): call(step_kernel, out_shape=(shape(flow.shape), shape((comps, 1, points))...  2.42 us
    unnamed x10, local copies, waits for them, and re-layouts  2.05 us
  transfers between devices with their start and end apart: 6, of which 2 were waited for; matrix products, arithmetic and copies ran while one was open for 0% of the time, Pallas kernels for 12%

profile of v6, /device:TPU:0, one launch (start us, length us, event | category | flops | bytes accessed | tf_op | source)
XLA Modules:
  0.0 39.7 jit_solution(2431380776256029259)
XLA Ops:
  0.6 0.9 %copy-done.2 = f32[4,8,16,128]{3,2,1,0:T(8,128)S(1)} copy-done((f32[4,8,16,128]{3,2,1,0:T(8,128)S(1)}, f32[4,8,16,128]{3,2,1,0:T(8,128)}, u32[]{:S(2)}) %copy-start.2) | copy-done | bytes 262168
  1.6 3.0 %collective-permute-start = (f32[4,24,128]{2,1,0:T(8,128)S(1)}, f32[4,24,128]{2,1,0:T(8,128)S(1)}, u32[]{:S(2)}, u32[]{:S(2)}) collective-permute-start(f32[4,24,128]{2,1,0:T(8,128)S(1)} %get-tuple-element.22), channel_id=1, source_target_pairs={{0,2},{2,4},{4,6},{6,0},{1,3},{3,5},{5,7},{7,1},{8,10},{10,12},{12... | collective-permute-start | bytes 147464 | tf_op jit(solution)/shard_map/ppermute | solution.py:32
  4.6 1.0 %collective-permute-start.1 = (f32[4,24,128]{2,1,0:T(8,128)S(1)}, f32[4,24,128]{2,1,0:T(8,128)S(1)}, u32[]{:S(2)}, u32[]{:S(2)}) collective-permute-start(f32[4,24,128]{2,1,0:T(8,128)S(1)} %get-tuple-element.23), channel_id=1, source_target_pairs={{2,0},{4,2},{6,4},{0,6},{3,1},{5,3},{7,5},{1,7},{10,8},{12,10},{14... | collective-permute-start | bytes 147464 | tf_op jit(solution)/shard_map/ppermute | solution.py:32
  5.6 0.1 add_convert_fusion.walls_ref
  5.7 1.0 %copy-done = f32[127,3,256]{2,0,1:T(8,128)S(1)} copy-done((f32[127,3,256]{2,0,1:T(8,128)S(1)}, f32[127,3,256]{2,0,1:T(8,128)}, u32[]{:S(2)}) %copy-start) | copy-done | bytes 390168
  6.7 1.2 %shard_map.59 = f32[32,3,128]{2,1,0:T(4,128)} custom-call(f32[3,127,256]{2,1,0:T(8,128)S(1)} %bitcast.10), custom_call_target="tpu_custom_call" | custom-call | tf_op jit(solution)/shard_map/pallas_call | solution.py:401
  7.9 0.0 collective-permute-done.ylo_ref
  7.9 0.8 %collective-permute-done.1.yhi_ref = f32[4,24,128]{2,1,0:T(8,128)S(1)} collective-permute-done((f32[4,24,128]{2,1,0:T(8,128)S(1)}, f32[4,24,128]{2,1,0:T(8,128)S(1)}, u32[]{:S(2)}, u32[]{:S(2)}) %collective-permute-start.1) | collective-permute-done | bytes 49184 | tf_op jit(solution)/shard_map/ppermute | solution.py:32
  8.7 0.6 %shard_map.60 = (f32[4,192,128]{2,1,0:T(8,128)S(1)}, f32[4,56,128]{2,1,0:T(8,128)S(1)}, f32[4,56,128]{2,1,0:T(8,128)S(1)}) custom-call(s32[2]{0:T(128)S(1)} %add_convert_fusion.walls_ref, f32[4,128,128]{2,1,0:T(8,128)S(1)} %bitcast.14, f32[4,24,128]{2,1,0:T(8,128)S(1)} %collective-permute-done.ylo_ref, f32[4,24,128]{2,1,0:T(8,128)S(1)} %collective-permute-done.1.yhi_ref), custom_call_target="tpu_custom_call" | custom-call | tf_op jit(solution)/shard_map/pallas_call | solution.py:414
  9.3 1.6 %collective-permute-start.2 = (f32[4,56,128]{2,1,0:T(8,128)S(1)}, f32[4,56,128]{2,1,0:T(8,128)S(1)}, u32[]{:S(2)}, u32[]{:S(2)}) collective-permute-start(f32[4,56,128]{2,1,0:T(8,128)S(1)} %get-tuple-element.28), channel_id=1, source_target_pairs={{0,8},{8,16},{16,24},{24,0},{1,9},{9,17},{17,25},{25,1},{2,10},{10... | collective-permute-start | bytes 344072 | tf_op jit(solution)/shard_map/ppermute | solution.py:32
  11.0 2.2 %collective-permute-start.3 = (f32[4,56,128]{2,1,0:T(8,128)S(1)}, f32[4,56,128]{2,1,0:T(8,128)S(1)}, u32[]{:S(2)}, u32[]{:S(2)}) collective-permute-start(f32[4,56,128]{2,1,0:T(8,128)S(1)} %get-tuple-element.29), channel_id=1, source_target_pairs={{8,0},{16,8},{24,16},{0,24},{9,1},{17,9},{25,17},{1,25},{10,2},{18... | collective-permute-start | bytes 344072 | tf_op jit(solution)/shard_map/ppermute | solution.py:32
  13.2 4.0 %all-to-all-start = ((f32[32,3,128]{2,1,0:T(4,128)}), f32[32,3,128]{2,1,0:T(4,128)S(1)}, u32[]{:S(2)}, u32[]{:S(2)}) async-start(f32[32,3,128]{2,1,0:T(4,128)} %shard_map.59), calls=%async_computation | async-start | bytes 131072 | tf_op jit(solution)/shard_map/all_to_all | solution.py:422
  17.2 0.0 collective-permute-done.2.low_face_ref
  17.2 0.0 collective-permute-done.3.high_face_ref
  17.2 0.0 copy-start.4
  17.2 0.2 shard_map.61
  17.5 0.0 copy-start.1
  17.5 0.3 collective-permute-start.4
  17.8 0.1 copy-done.4
  17.9 1.1 %shard_map.62 = (f32[4,12,24,128]{3,2,1,0:T(8,128)S(1)}, s32[1,256]{1,0:T(1,128)S(1)}) custom-call(s32[2]{0:T(128)S(1)} %add_convert_fusion.walls_ref, s32[1,256]{1,0:T(1,128)S(1)} %bitcast.15, f32[4,8,24,128]{3,2,1,0:T(8,128)S(1)} %bitcast.8, f32[4,3,24,128]{3,2,1,0:T(8,128)S(1)} %get-tuple-element.30.xlo_ref, f32[4,3,24,128]{3,2,1,0:T(8,128)S(1)} %get-tuple-element.31.xhi_ref), custom_call_target="tpu_custom_call" | custom-call | tf_op jit(solution)/shard_map/pallas_call | solution.py:435
  19.0 2.4 %shard_map.63 = (f32[4,8,16,128]{3,2,1,0:T(8,128)S(1)}, f32[3,1,256]{2,1,0:T(1,128)S(1)}, f32[1,128]{1,0:T(1,128)S(1)}) custom-call(s32[2]{0:T(128)S(1)} %add_convert_fusion.walls_ref, f32[4,8,24,128]{3,2,1,0:T(8,128)S(1)} %bitcast.9, f32[4,3,24,128]{3,2,1,0:T(8,128)S(1)} %get-tuple-element.30.xlo_ref, f32[4,3,24,128]{3,2,1,0:T(8,128)S(1)} %get-tuple-element.31.xhi_ref, ...), custom_call_target="tpu_custom_call" | custom-call | tf_op jit(solution)/shard_map/pallas_call | solution.py:445
  21.4 3.2 %all-to-all-done.parts_ref = f32[32,3,128]{2,1,0:T(4,128)S(1)} async-done(((f32[32,3,128]{2,1,0:T(4,128)}), f32[32,3,128]{2,1,0:T(4,128)S(1)}, u32[]{:S(2)}, u32[]{:S(2)}) %all-to-all-start) | async-done | bytes 49184 | tf_op jit(solution)/shard_map/all_to_all | solution.py:422
  24.6 9.9 %all_to_all.10.got_ref = f32[32,4,128]{2,1,0:T(4,128)S(1)} all-to-all(f32[32,4,128]{2,1,0:T(4,128)S(1)} %shard_map.64), channel_id=1, replica_groups=mesh['gx'=4,'gy'=4,'gz'=2] {'gx','gy','gz'}, dimensions={0} | all-to-all | bytes 131072 | tf_op jit(solution)/shard_map/all_to_all | solution.py:459
  34.5 5.2 %shard_map.65 = (f32[3,128,256]{2,1,0:T(8,128)}, f32[128,128]{1,0:T(8,128)}, f32[4,8,16,128]{3,2,1,0:T(8,128)}) custom-call(f32[32,4,128]{2,1,0:T(4,128)S(1)} %all_to_all.10.got_ref, f32[3,127,256]{2,1,0:T(8,128)S(1)} %bitcast.12, f32[3,1,256]{2,1,0:T(1,128)S(1)} %get-tuple-element.36.snap_ref, f32[4,8,16,128]{3,2,1,0:T(8,128)S(1)} %get-tuple-element.37.flow_ref), custom_call_target="tpu_custom_call" | custom-call | tf_op jit(solution)/shard_map/pallas_call | solution.py:460
  (8 shorter events, 0.1 us)
Async XLA Ops:
  0.6 1.0 %copy-start.2 = (f32[4,8,16,128]{3,2,1,0:T(8,128)S(1)}, f32[4,8,16,128]{3,2,1,0:T(8,128)}, u32[]{:S(2)}) copy-start(f32[4,8,16,128]{3,2,1,0:T(8,128)} %param.3) | copy-start | bytes 786436
  1.6 7.1 %copy-start.3 = (f32[4,8,16,128]{3,2,1,0:T(8,128)S(1)}, f32[4,8,16,128]{3,2,1,0:T(8,128)}, u32[]{:S(2)}) copy-start(f32[4,8,16,128]{3,2,1,0:T(8,128)} %param.3) | copy-start | bytes 786436
  1.6 6.3 %collective-permute-start = (f32[4,24,128]{2,1,0:T(8,128)S(1)}, f32[4,24,128]{2,1,0:T(8,128)S(1)}, u32[]{:S(2)}, u32[]{:S(2)}) collective-permute-start(f32[4,24,128]{2,1,0:T(8,128)S(1)} %get-tuple-element.22), channel_id=1, source_target_pairs={{0,2},{2,4},{4,6},{6,0},{1,3},{3,5},{5,7},{7,1},{8,10},{10,12},{12... | collective-permute-start | bytes 147464 | tf_op jit(solution)/shard_map/ppermute | solution.py:32
  4.6 4.1 %collective-permute-start.1 = (f32[4,24,128]{2,1,0:T(8,128)S(1)}, f32[4,24,128]{2,1,0:T(8,128)S(1)}, u32[]{:S(2)}, u32[]{:S(2)}) collective-permute-start(f32[4,24,128]{2,1,0:T(8,128)S(1)} %get-tuple-element.23), channel_id=1, source_target_pairs={{2,0},{4,2},{6,4},{0,6},{3,1},{5,3},{7,5},{1,7},{10,8},{12,10},{14... | collective-permute-start | bytes 147464 | tf_op jit(solution)/shard_map/ppermute | solution.py:32
  5.7 1.0 %copy-start = (f32[127,3,256]{2,0,1:T(8,128)S(1)}, f32[127,3,256]{2,0,1:T(8,128)}, u32[]{:S(2)}) copy-start(f32[127,3,256]{2,0,1:T(8,128)} %param.4) | copy-start | bytes 1170436
  9.3 7.9 %collective-permute-start.2 = (f32[4,56,128]{2,1,0:T(8,128)S(1)}, f32[4,56,128]{2,1,0:T(8,128)S(1)}, u32[]{:S(2)}, u32[]{:S(2)}) collective-permute-start(f32[4,56,128]{2,1,0:T(8,128)S(1)} %get-tuple-element.28), channel_id=1, source_target_pairs={{0,8},{8,16},{16,24},{24,0},{1,9},{9,17},{17,25},{25,1},{2,10},{10... | collective-permute-start | bytes 344072 | tf_op jit(solution)/shard_map/ppermute | solution.py:32
  11.0 6.2 %collective-permute-start.3 = (f32[4,56,128]{2,1,0:T(8,128)S(1)}, f32[4,56,128]{2,1,0:T(8,128)S(1)}, u32[]{:S(2)}, u32[]{:S(2)}) collective-permute-start(f32[4,56,128]{2,1,0:T(8,128)S(1)} %get-tuple-element.29), channel_id=1, source_target_pairs={{8,0},{16,8},{24,16},{0,24},{9,1},{17,9},{25,17},{1,25},{10,2},{18... | collective-permute-start | bytes 344072 | tf_op jit(solution)/shard_map/ppermute | solution.py:32
  13.2 11.4 %all-to-all-start = ((f32[32,3,128]{2,1,0:T(4,128)}), f32[32,3,128]{2,1,0:T(4,128)S(1)}, u32[]{:S(2)}, u32[]{:S(2)}) async-start(f32[32,3,128]{2,1,0:T(4,128)} %shard_map.59), calls=%async_computation | async-start | bytes 131072 | tf_op jit(solution)/shard_map/all_to_all | solution.py:422
  17.2 0.7 %copy-start.4 = (s32[256]{0:T(256)S(1)}, s32[256]{0:T(256)}, u32[]{:S(2)}) copy-start(s32[256]{0:T(256)} %param.5) | copy-start | bytes 3076
  17.5 1.5 %copy-start.1 = (f32[127,3,256]{2,0,1:T(8,128)S(1)}, f32[127,3,256]{2,0,1:T(8,128)}, u32[]{:S(2)}) copy-start(f32[127,3,256]{2,0,1:T(8,128)} %param.4) | copy-start | bytes 1170436
  17.5 1.5 %collective-permute-start.4 = (f32[4,24,128]{2,1,0:T(8,128)S(1)}, f32[4,24,128]{2,1,0:T(8,128)S(1)}, u32[]{:S(2)}, u32[]{:S(2)}) collective-permute-start(f32[4,24,128]{2,1,0:T(8,128)S(1)} %get-tuple-element.33.own_ref), channel_id=1, source_target_pairs={{0,1},{1,0},{2,3},{3,2},{4,5},{5,4},{6,7},{7,6},{8,9},{9,8},{10,11... | collective-permute-start | bytes 147464 | tf_op jit(solution)/shard_map/ppermute | solution.py:432

commit v7 on v6

--- a/solution.py
+++ b/solution.py
@@ -83,12 +83,12 @@
             mid_ref[f, rows * i : rows * i + ny] = flow_ref[f, ny * i : ny * i + ny]
         for j in range(HALO):
             if j < DEPTH:
-                value = jnp.where(walls_ref[1] == 1, 0.0, yhi_ref[f, planes * j : planes * j + planes])
+                value = jnp.where(walls_ref[1:2] == 1, 0.0, yhi_ref[f, planes * j : planes * j + planes])
             elif j < DEPTH + GAP:
                 value = empty
             else:
                 k = j - DEPTH - GAP
-                value = jnp.where(walls_ref[0] == 1, 0.0, ylo_ref[f, planes * k : planes * k + planes])
+                value = jnp.where(walls_ref[0:1] == 1, 0.0, ylo_ref[f, planes * k : planes * k + planes])
             mid_ref[f, pl.ds(ny + j, planes, stride=rows), :] = value
         for face_ref, begin, near, next_one in (
             (first_ref, 0, 0, 1), (last_ref, planes - DEPTH, planes - 1, planes - 2)
@@ -168,8 +168,8 @@
 
 def beyond_walls(walls_ref, ny, shape):
     row = lax.broadcasted_iota(jnp.int32, shape, 0)
-    below = (row >= ny + DEPTH + GAP) & (walls_ref[0] == 1)
-    above = (row >= ny) & (row < ny + DEPTH) & (walls_ref[1] == 1)
+    below = (row >= ny + DEPTH + GAP) & (walls_ref[0:1] == 1)
+    above = (row >= ny) & (row < ny + DEPTH) & (walls_ref[1:2] == 1)
     return below | above
 
 
@@ -387,7 +387,6 @@
     call = functools.partial(pl.pallas_call, compiler_params=PARAMS)
     bricks = jnp.transpose(basis, (1, 0, 2))
 
-    smem = pl.BlockSpec(memory_space=pltpu.SMEM)
     whole = pl.BlockSpec(memory_space=pltpu.HBM)
     flat = flow.reshape(fields, nx * ny, nz)
     quarter = size // 4
@@ -410,11 +409,12 @@
     rows = ny + HALO
     place = lax.axis_index("gy")
     walls = jnp.stack([place == 0, place == lax.axis_size("gy") - 1]).astype(jnp.int32)
+    walls = jnp.broadcast_to(walls[:, None], (2, nz))
     face = shape((fields, DEPTH * ny + HALO, nz))
     mid, first, last = call(
         functools.partial(walls_kernel, nx),
         out_shape=(shape((fields, nx * rows, nz)), face, face),
-        in_specs=[smem] + [VMEM] * 3,
+        in_specs=[VMEM] * 4,
         out_specs=(VMEM,) * 3,
     )(walls, flat, ylo, yhi)
     mid = mid.reshape(fields, nx, rows, nz)
@@ -438,14 +438,14 @@
             shape((fields, nx + 2 * DEPTH - 2, rows, nz)),
             jax.ShapeDtypeStruct((1, points), sample.dtype),
         ),
-        in_specs=[smem, whole] + [VMEM] * 3,
+        in_specs=[VMEM, whole] + [VMEM] * 3,
         out_specs=(VMEM, VMEM),
         scratch_shapes=[pltpu.SemaphoreType.DMA],
     )(walls, sample.reshape(1, points), mid, xlo, xhi)
     flow_new, snapshot, cross = call(
         step_kernel,
         out_shape=(shape(flow.shape), shape((comps, 1, points)), shape((1, size))),
-        in_specs=[smem] + [VMEM] * 9,
+        in_specs=[VMEM] * 10,
         out_specs=(VMEM, VMEM, VMEM),
         scratch_shapes=[
             pltpu.VMEM((fields, nx + 2 * DEPTH - 2, rows, nz), jnp.float32),

time: 39.9 us -> 38.7 us (0.970)
  Pallas kernels: 10.8 us -> 9.14 us
  waiting for transfers between devices: 3.98 us -> 5.09 us
  blocking collectives: 9.88 us -> 9.12 us
    all_to_all x1, waiting for transfers between devices: 3.18 us -> 3.95 us  [local(): parts = lax.all_to_all(gram, ALL, 0, 0)]
    all_to_all x1, blocking collectives: 9.88 us -> 9.12 us  [local(): got = lax.all_to_all(send, ALL, 0, 0)]
    pallas_call x1, Pallas kernels: 2.42 us -> 1.86 us  [local(): call(step_kernel, out_shape=(shape(flow.shape), shape((comps, 1, points))...]
    pallas_call x1, Pallas kernels: 1.07 us -> 0.53 us  [local(): call(first_kernel, out_shape=(shape((fields, nx + 2 * DEPTH - 2, rows, nz...]
    pallas_call x1, Pallas kernels: 0.6 us -> 0.06 us  [local(): call(functools.partial(walls_kernel, nx), out_shape=(shape((fields, nx *...]
  transfers between devices with their start and end apart: 6 -> 6, of which waited for: 2 -> 3; matrix products, arithmetic and copies ran while one was open for 0% -> 0% of each run, Pallas kernels for 12% -> 10%
where the time goes in v7:
time: 38.7 us; the launch traced here: 38.5 us
  starting transfers between devices  12.2 us (32%)
  Pallas kernels  9.14 us (24%)
  blocking collectives  9.12 us (24%)
  waiting for transfers between devices  5.09 us (13%)
  local copies, waits for them, and re-layouts  2.12 us (5%)
  between operations  0.72 us (2%)
    all_to_all x1, blocking collectives, local(): got = lax.all_to_all(send, ALL, 0, 0)  9.12 us
    pallas_call x1, Pallas kernels, local(): call(functools.partial(final_kernel, count), out_shape=(shape((comps, siz...  5.16 us
    ppermute x2, starting transfers between devices, neighbours(): lax.ppermute(block_high, axis, forward)  4.63 us
    all_to_all x1, starting transfers between devices, local(): parts = lax.all_to_all(gram, ALL, 0, 0)  4 us
    all_to_all x1, waiting for transfers between devices, local(): parts = lax.all_to_all(gram, ALL, 0, 0)  3.95 us
    ppermute x2, starting transfers between devices, neighbours(): lax.ppermute(block_low, axis, backward)  3.25 us
    unnamed x10, local copies, waits for them, and re-layouts  2.05 us
    pallas_call x1, Pallas kernels, local(): call(step_kernel, out_shape=(shape(flow.shape), shape((comps, 1, points))...  1.86 us
  transfers between devices with their start and end apart: 6, of which 3 were waited for; matrix products, arithmetic and copies ran while one was open for 0% of the time, Pallas kernels for 10%

profile of v7, /device:TPU:0, one launch (start us, length us, event | category | flops | bytes accessed | tf_op | source)
XLA Modules:
  0.0 38.5 jit_solution(8273964368084235597)
XLA Ops:
  0.6 0.9 %copy-done.2 = f32[4,8,16,128]{3,2,1,0:T(8,128)S(1)} copy-done((f32[4,8,16,128]{3,2,1,0:T(8,128)S(1)}, f32[4,8,16,128]{3,2,1,0:T(8,128)}, u32[]{:S(2)}) %copy-start.2) | copy-done | bytes 262168
  1.6 3.0 %collective-permute-start = (f32[4,24,128]{2,1,0:T(8,128)S(1)}, f32[4,24,128]{2,1,0:T(8,128)S(1)}, u32[]{:S(2)}, u32[]{:S(2)}) collective-permute-start(f32[4,24,128]{2,1,0:T(8,128)S(1)} %get-tuple-element.22), channel_id=1, source_target_pairs={{0,2},{2,4},{4,6},{6,0},{1,3},{3,5},{5,7},{7,1},{8,10},{10,12},{12... | collective-permute-start | bytes 147464 | tf_op jit(solution)/shard_map/ppermute | solution.py:32
  4.6 1.0 %collective-permute-start.1 = (f32[4,24,128]{2,1,0:T(8,128)S(1)}, f32[4,24,128]{2,1,0:T(8,128)S(1)}, u32[]{:S(2)}, u32[]{:S(2)}) collective-permute-start(f32[4,24,128]{2,1,0:T(8,128)S(1)} %get-tuple-element.23), channel_id=1, source_target_pairs={{2,0},{4,2},{6,4},{0,6},{3,1},{5,3},{7,5},{1,7},{10,8},{12,10},{14... | collective-permute-start | bytes 147464 | tf_op jit(solution)/shard_map/ppermute | solution.py:32
  5.6 0.1 add_convert_fusion
  5.7 1.0 %copy-done = f32[127,3,256]{2,0,1:T(8,128)S(1)} copy-done((f32[127,3,256]{2,0,1:T(8,128)S(1)}, f32[127,3,256]{2,0,1:T(8,128)}, u32[]{:S(2)}) %copy-start) | copy-done | bytes 390168
  6.7 1.2 %shard_map.59 = f32[32,3,128]{2,1,0:T(4,128)} custom-call(f32[3,127,256]{2,1,0:T(8,128)S(1)} %bitcast.7), custom_call_target="tpu_custom_call" | custom-call | tf_op jit(solution)/shard_map/pallas_call | solution.py:400
  7.9 0.8 %collective-permute-done.1.yhi_ref = f32[4,24,128]{2,1,0:T(8,128)S(1)} collective-permute-done((f32[4,24,128]{2,1,0:T(8,128)S(1)}, f32[4,24,128]{2,1,0:T(8,128)S(1)}, u32[]{:S(2)}, u32[]{:S(2)}) %collective-permute-start.1) | collective-permute-done | bytes 49184 | tf_op jit(solution)/shard_map/ppermute | solution.py:32
  8.7 0.1 broadcast_in_dim.2.walls_ref
  8.8 0.1 shard_map.60
  8.8 1.6 %collective-permute-start.2 = (f32[4,56,128]{2,1,0:T(8,128)S(1)}, f32[4,56,128]{2,1,0:T(8,128)S(1)}, u32[]{:S(2)}, u32[]{:S(2)}) collective-permute-start(f32[4,56,128]{2,1,0:T(8,128)S(1)} %get-tuple-element.28), channel_id=1, source_target_pairs={{0,8},{8,16},{16,24},{24,0},{1,9},{9,17},{17,25},{25,1},{2,10},{10... | collective-permute-start | bytes 344072 | tf_op jit(solution)/shard_map/ppermute | solution.py:32
  10.5 2.2 %collective-permute-start.3 = (f32[4,56,128]{2,1,0:T(8,128)S(1)}, f32[4,56,128]{2,1,0:T(8,128)S(1)}, u32[]{:S(2)}, u32[]{:S(2)}) collective-permute-start(f32[4,56,128]{2,1,0:T(8,128)S(1)} %get-tuple-element.29), channel_id=1, source_target_pairs={{8,0},{16,8},{24,16},{0,24},{9,1},{17,9},{25,17},{1,25},{10,2},{18... | collective-permute-start | bytes 344072 | tf_op jit(solution)/shard_map/ppermute | solution.py:32
  12.7 4.0 %all-to-all-start = ((f32[32,3,128]{2,1,0:T(4,128)}), f32[32,3,128]{2,1,0:T(4,128)S(1)}, u32[]{:S(2)}, u32[]{:S(2)}) async-start(f32[32,3,128]{2,1,0:T(4,128)} %shard_map.59), calls=%async_computation | async-start | bytes 131072 | tf_op jit(solution)/shard_map/all_to_all | solution.py:422
  16.7 0.0 collective-permute-done.2.low_face_ref
  16.7 0.0 copy-start.4
  16.8 0.2 shard_map.61
  17.0 0.0 copy-start.1
  17.0 0.3 collective-permute-start.4
  17.3 0.1 copy-done.4
  17.4 0.5 %shard_map.62 = (f32[4,12,24,128]{3,2,1,0:T(8,128)S(1)}, s32[1,256]{1,0:T(1,128)S(1)}) custom-call(s32[2,128]{1,0:T(2,128)S(1)} %broadcast_in_dim.2.walls_ref, s32[1,256]{1,0:T(1,128)S(1)} %bitcast.15, f32[4,8,24,128]{3,2,1,0:T(8,128)S(1)} %bitcast.11, f32[4,3,24,128]{3,2,1,0:T(8,128)S(1)} %get-tuple-element.30.xlo_ref, ...), custom_call_target="tpu_custom_call" | custom-call | tf_op jit(solution)/shard_map/pallas_call | solution.py:435
  18.0 0.3 collective-permute-done.4.low_ref.high_ref
  18.3 1.9 %shard_map.63 = (f32[4,8,16,128]{3,2,1,0:T(8,128)S(1)}, f32[3,1,256]{2,1,0:T(1,128)S(1)}, f32[1,128]{1,0:T(1,128)S(1)}) custom-call(s32[2,128]{1,0:T(2,128)S(1)} %broadcast_in_dim.2.walls_ref, f32[4,8,24,128]{3,2,1,0:T(8,128)S(1)} %bitcast.12, f32[4,3,24,128]{3,2,1,0:T(8,128)S(1)} %get-tuple-element.30.xlo_ref, ...), custom_call_target="tpu_custom_call" | custom-call | tf_op jit(solution)/shard_map/pallas_call | solution.py:445
  20.2 3.9 %all-to-all-done.parts_ref = f32[32,3,128]{2,1,0:T(4,128)S(1)} async-done(((f32[32,3,128]{2,1,0:T(4,128)}), f32[32,3,128]{2,1,0:T(4,128)S(1)}, u32[]{:S(2)}, u32[]{:S(2)}) %all-to-all-start) | async-done | bytes 49184 | tf_op jit(solution)/shard_map/all_to_all | solution.py:422
  24.2 9.1 %all_to_all.10.got_ref = f32[32,4,128]{2,1,0:T(4,128)S(1)} all-to-all(f32[32,4,128]{2,1,0:T(4,128)S(1)} %shard_map.64), channel_id=1, replica_groups=mesh['gx'=4,'gy'=4,'gz'=2] {'gx','gy','gz'}, dimensions={0} | all-to-all | bytes 131072 | tf_op jit(solution)/shard_map/all_to_all | solution.py:459
  33.3 5.2 %shard_map.65 = (f32[3,128,256]{2,1,0:T(8,128)}, f32[128,128]{1,0:T(8,128)}, f32[4,8,16,128]{3,2,1,0:T(8,128)}) custom-call(f32[32,4,128]{2,1,0:T(4,128)S(1)} %all_to_all.10.got_ref, f32[3,127,256]{2,1,0:T(8,128)S(1)} %bitcast.9, f32[3,1,256]{2,1,0:T(1,128)S(1)} %get-tuple-element.36.snap_ref, f32[4,8,16,128]{3,2,1,0:T(8,128)S(1)} %get-tuple-element.37.flow_ref), custom_call_target="tpu_custom_call" | custom-call | tf_op jit(solution)/shard_map/pallas_call | solution.py:460
  (9 shorter events, 0.1 us)
Async XLA Ops:
  0.6 1.0 %copy-start.2 = (f32[4,8,16,128]{3,2,1,0:T(8,128)S(1)}, f32[4,8,16,128]{3,2,1,0:T(8,128)}, u32[]{:S(2)}) copy-start(f32[4,8,16,128]{3,2,1,0:T(8,128)} %param.3) | copy-start | bytes 786436
  1.6 7.2 %copy-start.3 = (f32[4,8,16,128]{3,2,1,0:T(8,128)S(1)}, f32[4,8,16,128]{3,2,1,0:T(8,128)}, u32[]{:S(2)}) copy-start(f32[4,8,16,128]{3,2,1,0:T(8,128)} %param.3) | copy-start | bytes 786436
  1.6 6.3 %collective-permute-start = (f32[4,24,128]{2,1,0:T(8,128)S(1)}, f32[4,24,128]{2,1,0:T(8,128)S(1)}, u32[]{:S(2)}, u32[]{:S(2)}) collective-permute-start(f32[4,24,128]{2,1,0:T(8,128)S(1)} %get-tuple-element.22), channel_id=1, source_target_pairs={{0,2},{2,4},{4,6},{6,0},{1,3},{3,5},{5,7},{7,1},{8,10},{10,12},{12... | collective-permute-start | bytes 147464 | tf_op jit(solution)/shard_map/ppermute | solution.py:32
  4.6 4.1 %collective-permute-start.1 = (f32[4,24,128]{2,1,0:T(8,128)S(1)}, f32[4,24,128]{2,1,0:T(8,128)S(1)}, u32[]{:S(2)}, u32[]{:S(2)}) collective-permute-start(f32[4,24,128]{2,1,0:T(8,128)S(1)} %get-tuple-element.23), channel_id=1, source_target_pairs={{2,0},{4,2},{6,4},{0,6},{3,1},{5,3},{7,5},{1,7},{10,8},{12,10},{14... | collective-permute-start | bytes 147464 | tf_op jit(solution)/shard_map/ppermute | solution.py:32
  5.7 1.0 %copy-start = (f32[127,3,256]{2,0,1:T(8,128)S(1)}, f32[127,3,256]{2,0,1:T(8,128)}, u32[]{:S(2)}) copy-start(f32[127,3,256]{2,0,1:T(8,128)} %param.4) | copy-start | bytes 1170436
  8.8 7.9 %collective-permute-start.2 = (f32[4,56,128]{2,1,0:T(8,128)S(1)}, f32[4,56,128]{2,1,0:T(8,128)S(1)}, u32[]{:S(2)}, u32[]{:S(2)}) collective-permute-start(f32[4,56,128]{2,1,0:T(8,128)S(1)} %get-tuple-element.28), channel_id=1, source_target_pairs={{0,8},{8,16},{16,24},{24,0},{1,9},{9,17},{17,25},{25,1},{2,10},{10... | collective-permute-start | bytes 344072 | tf_op jit(solution)/shard_map/ppermute | solution.py:32
  10.5 6.2 %collective-permute-start.3 = (f32[4,56,128]{2,1,0:T(8,128)S(1)}, f32[4,56,128]{2,1,0:T(8,128)S(1)}, u32[]{:S(2)}, u32[]{:S(2)}) collective-permute-start(f32[4,56,128]{2,1,0:T(8,128)S(1)} %get-tuple-element.29), channel_id=1, source_target_pairs={{8,0},{16,8},{24,16},{0,24},{9,1},{17,9},{25,17},{1,25},{10,2},{18... | collective-permute-start | bytes 344072 | tf_op jit(solution)/shard_map/ppermute | solution.py:32
  12.7 11.4 %all-to-all-start = ((f32[32,3,128]{2,1,0:T(4,128)}), f32[32,3,128]{2,1,0:T(4,128)S(1)}, u32[]{:S(2)}, u32[]{:S(2)}) async-start(f32[32,3,128]{2,1,0:T(4,128)} %shard_map.59), calls=%async_computation | async-start | bytes 131072 | tf_op jit(solution)/shard_map/all_to_all | solution.py:422
  16.7 0.7 %copy-start.4 = (s32[256]{0:T(256)S(1)}, s32[256]{0:T(256)}, u32[]{:S(2)}) copy-start(s32[256]{0:T(256)} %param.5) | copy-start | bytes 3076
  17.0 1.3 %copy-start.1 = (f32[127,3,256]{2,0,1:T(8,128)S(1)}, f32[127,3,256]{2,0,1:T(8,128)}, u32[]{:S(2)}) copy-start(f32[127,3,256]{2,0,1:T(8,128)} %param.4) | copy-start | bytes 1170436
  17.0 1.3 %collective-permute-start.4 = (f32[4,24,128]{2,1,0:T(8,128)S(1)}, f32[4,24,128]{2,1,0:T(8,128)S(1)}, u32[]{:S(2)}, u32[]{:S(2)}) collective-permute-start(f32[4,24,128]{2,1,0:T(8,128)S(1)} %get-tuple-element.33.own_ref), channel_id=1, source_target_pairs={{0,1},{1,0},{2,3},{3,2},{4,5},{5,4},{6,7},{7,6},{8,9},{9,8},{10,11... | collective-permute-start | bytes 147464 | tf_op jit(solution)/shard_map/ppermute | solution.py:432

commit v8 on v7

--- a/solution.py
+++ b/solution.py
@@ -30,6 +30,20 @@
     forward = [(i, (i + 1) % count) for i in range(count)]
     backward = [(target, source) for source, target in forward]
     return lax.ppermute(block_high, axis, forward), lax.ppermute(block_low, axis, backward)
+
+
+def pairs(block_even, block_odd, axis):
+    count = lax.axis_size(axis)
+    even = [(i, i + 1 - 2 * (i % 2)) for i in range(count)]
+    odd = [(i, (i - 1 + 2 * (i % 2)) % count) for i in range(count)]
+    return lax.ppermute(block_even, axis, even), lax.ppermute(block_odd, axis, odd)
+
+
+LOWER_WALL, UPPER_WALL, ODD_Y, ODD_X = range(4)
+
+
+def flag(flags_ref, which):
+    return flags_ref[which : which + 1] == 1
 
 
 def pack_upper(rows, tall):
@@ -64,16 +78,20 @@
 HALO = 2 * DEPTH + GAP
 
 
-def strips_kernel(planes, flow_ref, bottom_ref, top_ref):
+def strips_kernel(planes, flags_ref, flow_ref, even_ref, odd_ref):
     ny = flow_ref.shape[1] // planes
+    odd = flag(flags_ref, ODD_Y)
     for f in range(flow_ref.shape[0]):
         for j in range(DEPTH):
-            bottom_ref[f, planes * j : planes * j + planes] = flow_ref[f, pl.ds(j, planes, stride=ny), :]
-            top_ref[f, planes * j : planes * j + planes] = flow_ref[f, pl.ds(ny - DEPTH + j, planes, stride=ny), :]
-
-
-def walls_kernel(planes, walls_ref, flow_ref, ylo_ref, yhi_ref, mid_ref, first_ref, last_ref):
+            bottom = flow_ref[f, pl.ds(j, planes, stride=ny), :]
+            top = flow_ref[f, pl.ds(ny - DEPTH + j, planes, stride=ny), :]
+            even_ref[f, planes * j : planes * j + planes] = jnp.where(odd, bottom, top)
+            odd_ref[f, planes * j : planes * j + planes] = jnp.where(odd, top, bottom)
+
+
+def walls_kernel(planes, flags_ref, flow_ref, even_ref, odd_ref, mid_ref, face_even_ref, face_odd_ref):
     fields, cells, nz = flow_ref.shape
+    odd_y, odd_x = flag(flags_ref, ODD_Y), flag(flags_ref, ODD_X)
     ny = cells // planes
     rows = ny + HALO
     sub = lax.broadcasted_iota(jnp.int32, (HALO, nz), 0)
@@ -82,21 +100,25 @@
         for i in range(planes):
             mid_ref[f, rows * i : rows * i + ny] = flow_ref[f, ny * i : ny * i + ny]
         for j in range(HALO):
+            k = j if j < DEPTH else j - DEPTH - GAP
+            part = slice(planes * k, planes * k + planes)
             if j < DEPTH:
-                value = jnp.where(walls_ref[1:2] == 1, 0.0, yhi_ref[f, planes * j : planes * j + planes])
+                value = jnp.where(odd_y, odd_ref[f, part], even_ref[f, part])
+                value = jnp.where(flag(flags_ref, UPPER_WALL), 0.0, value)
             elif j < DEPTH + GAP:
                 value = empty
             else:
-                k = j - DEPTH - GAP
-                value = jnp.where(walls_ref[0:1] == 1, 0.0, ylo_ref[f, planes * k : planes * k + planes])
+                value = jnp.where(odd_y, even_ref[f, part], odd_ref[f, part])
+                value = jnp.where(flag(flags_ref, LOWER_WALL), 0.0, value)
             mid_ref[f, pl.ds(ny + j, planes, stride=rows), :] = value
-        for face_ref, begin, near, next_one in (
-            (first_ref, 0, 0, 1), (last_ref, planes - DEPTH, planes - 1, planes - 2)
-        ):
-            for k in range(DEPTH):
-                face_ref[f, ny * k : ny * k + ny] = flow_ref[f, ny * (begin + k) : ny * (begin + k) + ny]
+        faces = []
+        for begin, near, next_one in ((0, 0, 1), (planes - DEPTH, planes - 1, planes - 2)):
             halos = [mid_ref[f, rows * i + ny : rows * i + rows] for i in (near, next_one)]
-            face_ref[f, ny * DEPTH : ny * DEPTH + HALO] = corner_rows(*halos, sub)
+            faces.append([flow_ref[f, ny * i : ny * i + ny] for i in range(begin, begin + DEPTH)] + [corner_rows(*halos, sub)])
+        for k, (first, last) in enumerate(zip(*faces)):
+            part = slice(ny * k, ny * k + first.shape[0])
+            face_even_ref[f, part] = jnp.where(odd_x, first, last)
+            face_odd_ref[f, part] = jnp.where(odd_x, last, first)
 
 
 def corner_rows(near, next_one, sub):
@@ -123,16 +145,20 @@
 GROUP = 8
 
 
-def pack_kernel(mid_ref, low_face_ref, high_face_ref, packed_ref, xlo_ref, xhi_ref):
+def pack_kernel(flags_ref, mid_ref, even_ref, odd_ref, packed_ref, xlo_ref, xhi_ref):
     fields, nx, rows, nz = mid_ref.shape
     ny = rows - HALO
+    odd = flag(flags_ref, ODD_X)
     lane = lax.broadcasted_iota(jnp.int32, (rows, nz), 1)
     sub = lax.broadcasted_iota(jnp.int32, (HALO, nz), 0)
     for f in range(fields):
-        for face_ref, out_ref, order in ((low_face_ref, xlo_ref, (2, 1, 0)), (high_face_ref, xhi_ref, (0, 1, 2))):
-            halo = corner_planes(face_ref[f, ny * DEPTH : ny * DEPTH + HALO], sub)
+        for one_ref, other_ref, out_ref, order in (
+            (even_ref, odd_ref, xlo_ref, (2, 1, 0)), (odd_ref, even_ref, xhi_ref, (0, 1, 2))
+        ):
+            face = jnp.where(odd, one_ref[f], other_ref[f])
+            halo = corner_planes(face[ny * DEPTH :], sub)
             for k in range(DEPTH):
-                out_ref[f, k, 0:ny] = face_ref[f, ny * k : ny * k + ny]
+                out_ref[f, k, 0:ny] = face[ny * k : ny * k + ny]
                 out_ref[f, k, ny:rows] = halo[order[k]]
         value = jnp.zeros((rows, nz), jnp.float32)
         for i in range(nx + 2 * DEPTH):
@@ -166,10 +192,10 @@
     return out
 
 
-def beyond_walls(walls_ref, ny, shape):
+def beyond_walls(flags_ref, ny, shape):
     row = lax.broadcasted_iota(jnp.int32, shape, 0)
-    below = (row >= ny + DEPTH + GAP) & (walls_ref[0:1] == 1)
-    above = (row >= ny) & (row < ny + DEPTH) & (walls_ref[1:2] == 1)
+    below = (row >= ny + DEPTH + GAP) & flag(flags_ref, LOWER_WALL)
+    above = (row >= ny) & (row < ny + DEPTH) & flag(flags_ref, UPPER_WALL)
     return below | above
 
 
@@ -199,11 +225,11 @@
     return jnp.where(outside, 0.0, 0.75 * begin + 0.25 * (value + DT_STEP * rate))
 
 
-def first_kernel(walls_ref, sample_hbm, mid_ref, xlo_ref, xhi_ref, one_ref, sample_ref, sem):
+def first_kernel(flags_ref, sample_hbm, mid_ref, xlo_ref, xhi_ref, one_ref, sample_ref, sem):
     copy = pltpu.make_async_copy(sample_hbm, sample_ref, sem)
     copy.start()
     fields, nx, rows, nz = mid_ref.shape
-    outside = beyond_walls(walls_ref, rows - HALO, (rows, nz))
+    outside = beyond_walls(flags_ref, rows - HALO, (rows, nz))
     for i in range(1, nx + 2 * DEPTH - 1):
         centre, rate = plane_rates(functools.partial(plane_of, mid_ref, xlo_ref, xhi_ref), i, rows)
         for f in range(4):
@@ -212,7 +238,7 @@
 
 
 def step_kernel(
-    walls_ref, mid_ref, xlo_ref, xhi_ref, first_ref, own_ref, low_ref, high_ref, basis_ref, sample_ref,
+    flags_ref, mid_ref, xlo_ref, xhi_ref, first_ref, own_ref, low_ref, high_ref, basis_ref, sample_ref,
     flow_ref, snap_ref, cross_ref,
     one_ref, two_ref,
 ):
@@ -221,7 +247,7 @@
     modes = basis_ref.shape[1]
     planes = nx + 2 * DEPTH
     lane = lax.broadcasted_iota(jnp.int32, (rows, nz), 1)
-    outside = beyond_walls(walls_ref, ny, (rows, nz))
+    outside = beyond_walls(flags_ref, ny, (rows, nz))
     every = range(4)
     start = functools.partial(plane_of, mid_ref, xlo_ref, xhi_ref)
 
@@ -317,12 +343,14 @@
             packed_ref[per * d : per * d + per] = block[0:per]
         total = total + block
     cross = total[per : per + 1] / count
+    mark = (lax.broadcasted_iota(jnp.int32, (8, size), 1) == size - 1).astype(jnp.float32)
+    top = lax.broadcasted_iota(jnp.int32, (8, size), 0) == 0
+    side = dot(jnp.where(top, jnp.broadcast_to(cross, (8, size)), 0.0), mark, ((0,), (0,)))
     lane = lax.broadcasted_iota(jnp.int32, (tall, size), 1)
     row = lax.broadcasted_iota(jnp.int32, (tall, size), 0)
     old = unpack_upper([packed_ref[tall * k : tall * k + tall] / count for k in range(3)], tall)
     for k in range(4):
-        side = jnp.sum(jnp.where(lane == row + tall * k, cross, 0.0), axis=1, keepdims=True)
-        value = jnp.where(lane == size - 1, side, old[k])
+        value = jnp.where(lane == size - 1, side[tall * k : tall * k + tall], old[k])
         if k == 3:
             value = jnp.where(row == tall - 1, jnp.broadcast_to(cross, value.shape), value)
         work_ref[tall * k : tall * k + tall, 0:size] = value
@@ -360,14 +388,12 @@
         mine, at = divmod(j, 8)
         pivot = column[j][mine][at : at + 1, :]
         inverse = 1.0 / pivot
+        scaled = {b: column[j][b] * inverse for b in range(mine, blocks)}
         for k in range(j + 1, tall):
             other, place = divmod(k, 8)
-            times = column[j][other][place : place + 1, :]
+            times = scaled[other][place : place + 1, :]
             for b in range(other, blocks):
-                if k == j + 1:
-                    column[k][b] = column[k][b] - (column[j][b] * times) * inverse
-                else:
-                    column[k][b] = column[k][b] - column[j][b] * (times * inverse)
+                column[k][b] = column[k][b] - column[j][b] * times
         scale[mine] = jnp.where(sub == at, lax.rsqrt(pivot), scale[mine])
         pivot_row = panel[mine][at : at + 1, :] * jnp.concatenate([inverse, inverse], axis=1)
         for b in range(mine, blocks):
@@ -392,11 +418,14 @@
     quarter = size // 4
     per = -(-3 * quarter // devices)
 
+    place = lax.axis_index("gy")
+    flags = [place == 0, place == lax.axis_size("gy") - 1, place % 2 == 1, lax.axis_index("gx") % 2 == 1]
+    flags = jnp.broadcast_to(jnp.stack(flags).astype(jnp.int32)[:, None], (len(flags), nz))
     strip = shape((fields, nx * DEPTH, nz))
-    bottom, top = call(
-        functools.partial(strips_kernel, nx), out_shape=(strip, strip), in_specs=[VMEM], out_specs=(VMEM, VMEM)
-    )(flat)
-    ylo, yhi = neighbours(bottom, top, "gy")
+    strips = call(
+        functools.partial(strips_kernel, nx), out_shape=(strip, strip), in_specs=[VMEM] * 2, out_specs=(VMEM, VMEM)
+    )(flags, flat)
+    y_even, y_odd = pairs(*strips, "gy")
     gram = call(
         gram_kernel,
         out_shape=shape((devices, per, size)),
@@ -404,30 +433,27 @@
         out_specs=VMEM,
         scratch_shapes=[pltpu.VMEM((size, size), jnp.float32), pltpu.VMEM((devices * per, size), jnp.float32)],
     )(bricks)
-    ylo, yhi, gram = lax.optimization_barrier((ylo, yhi, gram))
+    y_even, y_odd, gram = lax.optimization_barrier((y_even, y_odd, gram))
 
     rows = ny + HALO
-    place = lax.axis_index("gy")
-    walls = jnp.stack([place == 0, place == lax.axis_size("gy") - 1]).astype(jnp.int32)
-    walls = jnp.broadcast_to(walls[:, None], (2, nz))
     face = shape((fields, DEPTH * ny + HALO, nz))
-    mid, first, last = call(
+    mid, *faces = call(
         functools.partial(walls_kernel, nx),
         out_shape=(shape((fields, nx * rows, nz)), face, face),
         in_specs=[VMEM] * 4,
         out_specs=(VMEM,) * 3,
-    )(walls, flat, ylo, yhi)
+    )(flags, flat, y_even, y_odd)
     mid = mid.reshape(fields, nx, rows, nz)
-    low_face, high_face = neighbours(first, last, "gx")
+    x_even, x_odd = pairs(*faces, "gx")
     parts = lax.all_to_all(gram, ALL, 0, 0)
 
     beside = shape((fields, DEPTH, rows, nz))
     packed, xlo, xhi = call(
         pack_kernel,
         out_shape=(shape((fields, rows, nz)), beside, beside),
-        in_specs=[VMEM] * 3,
+        in_specs=[VMEM] * 4,
         out_specs=(VMEM,) * 3,
-    )(mid, low_face, high_face)
+    )(flags, mid, x_even, x_odd)
     if lax.axis_size("gz") == 2:
         low = high = lax.ppermute(packed, "gz", [(0, 1), (1, 0)])
     else:
@@ -441,7 +467,7 @@
         in_specs=[VMEM, whole] + [VMEM] * 3,
         out_specs=(VMEM, VMEM),
         scratch_shapes=[pltpu.SemaphoreType.DMA],
-    )(walls, sample.reshape(1, points), mid, xlo, xhi)
+    )(flags, sample.reshape(1, points), mid, xlo, xhi)
     flow_new, snapshot, cross = call(
         step_kernel,
         out_shape=(shape(flow.shape), shape((comps, 1, points)), shape((1, size))),
@@ -451,7 +477,7 @@
             pltpu.VMEM((fields, nx + 2 * DEPTH - 2, rows, nz), jnp.float32),
             pltpu.VMEM((fields, nx + 2 * DEPTH - 4, rows, nz), jnp.float32),
         ],
-    )(walls, mid, xlo, xhi, begun, packed, low, high, bricks, cells)
+    )(flags, mid, xlo, xhi, begun, packed, low, high, bricks, cells)
 
     send = call(
         merge_kernel, out_shape=shape((devices, per + 1, size)), in_specs=[VMEM] * 2, out_specs=VMEM

time: 38.7 us -> 38.3 us (0.990)
  starting transfers between devices: 12.2 us -> 11.4 us
  waiting for transfers between devices: 5.09 us -> 5.61 us
    ppermute x4, waiting for transfers between devices: 0.8 us -> 3.12 us  [the longest x2 3.11 us: pairs(): lax.ppermute(block_odd, axis, odd)]
    all_to_all x1, waiting for transfers between devices: 3.95 us -> 2.15 us  [local(): parts = lax.all_to_all(gram, ALL, 0, 0)]
    all_to_all x1, starting transfers between devices: 4 us -> 2.67 us  [local(): parts = lax.all_to_all(gram, ALL, 0, 0)]
    ppermute x4, starting transfers between devices: 7.89 us -> 8.61 us  [the longest x2 4.65 us: pairs(): lax.ppermute(block_even, axis, even)]
  transfers between devices with their start and end apart: 6 -> 6, of which waited for: 3 -> 4; matrix products, arithmetic and copies ran while one was open for 0% -> 0% of each run, Pallas kernels for 10% -> 10%
where the time goes in v8:
time: 38.3 us; the launch traced here: 38.1 us
  starting transfers between devices  11.4 us (30%)
  blocking collectives  9.12 us (24%)
  Pallas kernels  8.81 us (23%)
  waiting for transfers between devices  5.61 us (15%)
  local copies, waits for them, and re-layouts  2.37 us (6%)
  between operations  0.73 us (2%)
    all_to_all x1, blocking collectives, local(): got = lax.all_to_all(send, ALL, 0, 0)  9.12 us
    pallas_call x1, Pallas kernels, local(): call(functools.partial(final_kernel, count), out_shape=(shape((comps, siz...  4.84 us
    ppermute x2, starting transfers between devices, pairs(): lax.ppermute(block_even, axis, even)  4.65 us
    ppermute x2, starting transfers between devices, pairs(): lax.ppermute(block_odd, axis, odd)  3.97 us
    ppermute x2, waiting for transfers between devices, pairs(): lax.ppermute(block_odd, axis, odd)  3.11 us
    all_to_all x1, starting transfers between devices, local(): parts = lax.all_to_all(gram, ALL, 0, 0)  2.67 us
    unnamed x10, local copies, waits for them, and re-layouts  2.3 us
    all_to_all x1, waiting for transfers between devices, local(): parts = lax.all_to_all(gram, ALL, 0, 0)  2.15 us
  transfers between devices with their start and end apart: 6, of which 4 were waited for; matrix products, arithmetic and copies ran while one was open for 0% of the time, Pallas kernels for 10%

profile of v8, /device:TPU:0, one launch (start us, length us, event | category | flops | bytes accessed | tf_op | source)
XLA Modules:
  0.0 38.1 jit_solution(14779582088934323910)
XLA Ops:
  0.7 0.1 add_convert_fusion
  0.7 0.1 broadcast_in_dim.2.flags_ref
  0.8 0.9 %copy-done.2 = f32[4,8,16,128]{3,2,1,0:T(8,128)S(1)} copy-done((f32[4,8,16,128]{3,2,1,0:T(8,128)S(1)}, f32[4,8,16,128]{3,2,1,0:T(8,128)}, u32[]{:S(2)}) %copy-start.2) | copy-done | bytes 262168
  1.8 3.0 %collective-permute-start = (f32[4,24,128]{2,1,0:T(8,128)S(1)}, f32[4,24,128]{2,1,0:T(8,128)S(1)}, u32[]{:S(2)}, u32[]{:S(2)}) collective-permute-start(f32[4,24,128]{2,1,0:T(8,128)S(1)} %get-tuple-element.22), channel_id=1, source_target_pairs={{0,2},{2,0},{4,6},{6,4},{1,3},{3,1},{5,7},{7,5},{8,10},{10,8},{12,... | collective-permute-start | bytes 147464 | tf_op jit(solution)/shard_map/ppermute | solution.py:39
  4.8 1.5 %collective-permute-start.1 = (f32[4,24,128]{2,1,0:T(8,128)S(1)}, f32[4,24,128]{2,1,0:T(8,128)S(1)}, u32[]{:S(2)}, u32[]{:S(2)}) collective-permute-start(f32[4,24,128]{2,1,0:T(8,128)S(1)} %get-tuple-element.23), channel_id=1, source_target_pairs={{0,6},{2,4},{4,2},{6,0},{1,7},{3,5},{5,3},{7,1},{8,14},{10,12},{12... | collective-permute-start | bytes 147464 | tf_op jit(solution)/shard_map/ppermute | solution.py:39
  6.3 1.0 %copy-done = f32[127,3,256]{2,0,1:T(8,128)S(1)} copy-done((f32[127,3,256]{2,0,1:T(8,128)S(1)}, f32[127,3,256]{2,0,1:T(8,128)}, u32[]{:S(2)}) %copy-start) | copy-done | bytes 390168
  7.3 1.2 %shard_map.59 = f32[32,3,128]{2,1,0:T(4,128)} custom-call(f32[3,127,256]{2,1,0:T(8,128)S(1)} %bitcast.9), custom_call_target="tpu_custom_call" | custom-call | tf_op jit(solution)/shard_map/pallas_call | solution.py:429
  8.5 0.0 collective-permute-done.even_ref
  8.5 1.3 %collective-permute-done.1.odd_ref = f32[4,24,128]{2,1,0:T(8,128)S(1)} collective-permute-done((f32[4,24,128]{2,1,0:T(8,128)S(1)}, f32[4,24,128]{2,1,0:T(8,128)S(1)}, u32[]{:S(2)}, u32[]{:S(2)}) %collective-permute-start.1) | collective-permute-done | bytes 49184 | tf_op jit(solution)/shard_map/ppermute | solution.py:39
  9.8 0.1 shard_map.60
  9.9 1.6 %collective-permute-start.2 = (f32[4,56,128]{2,1,0:T(8,128)S(1)}, f32[4,56,128]{2,1,0:T(8,128)S(1)}, u32[]{:S(2)}, u32[]{:S(2)}) collective-permute-start(f32[4,56,128]{2,1,0:T(8,128)S(1)} %get-tuple-element.28), channel_id=1, source_target_pairs={{0,8},{8,0},{16,24},{24,16},{1,9},{9,1},{17,25},{25,17},{2,10},{10... | collective-permute-start | bytes 344072 | tf_op jit(solution)/shard_map/ppermute | solution.py:39
  11.5 2.5 %collective-permute-start.3 = (f32[4,56,128]{2,1,0:T(8,128)S(1)}, f32[4,56,128]{2,1,0:T(8,128)S(1)}, u32[]{:S(2)}, u32[]{:S(2)}) collective-permute-start(f32[4,56,128]{2,1,0:T(8,128)S(1)} %get-tuple-element.29), channel_id=1, source_target_pairs={{0,24},{8,16},{16,8},{24,0},{1,25},{9,17},{17,9},{25,1},{2,26},{10... | collective-permute-start | bytes 344072 | tf_op jit(solution)/shard_map/ppermute | solution.py:39
  14.0 2.7 %all-to-all-start = ((f32[32,3,128]{2,1,0:T(4,128)}), f32[32,3,128]{2,1,0:T(4,128)S(1)}, u32[]{:S(2)}, u32[]{:S(2)}) async-start(f32[32,3,128]{2,1,0:T(4,128)} %shard_map.59), calls=%async_computation | async-start | bytes 131072 | tf_op jit(solution)/shard_map/all_to_all | solution.py:448
  16.7 1.8 %collective-permute-done.3.odd_ref = f32[4,56,128]{2,1,0:T(8,128)S(1)} collective-permute-done((f32[4,56,128]{2,1,0:T(8,128)S(1)}, f32[4,56,128]{2,1,0:T(8,128)S(1)}, u32[]{:S(2)}, u32[]{:S(2)}) %collective-permute-start.3) | collective-permute-done | bytes 114720 | tf_op jit(solution)/shard_map/ppermute | solution.py:39
  18.5 0.2 shard_map.61
  18.7 0.0 copy-start.1
  18.7 0.1 collective-permute-start.4
  18.8 0.3 copy-done.4
  19.2 0.5 %shard_map.62 = (f32[4,12,24,128]{3,2,1,0:T(8,128)S(1)}, s32[1,256]{1,0:T(1,128)S(1)}) custom-call(s32[4,128]{1,0:T(4,128)S(1)} %broadcast_in_dim.2.flags_ref, s32[1,256]{1,0:T(1,128)S(1)} %bitcast.17, f32[4,8,24,128]{3,2,1,0:T(8,128)S(1)} %bitcast.13, f32[4,3,24,128]{3,2,1,0:T(8,128)S(1)} %get-tuple-element.30.xlo_ref, ...), custom_call_target="tpu_custom_call" | custom-call | tf_op jit(solution)/shard_map/pallas_call | solution.py:461
  19.7 0.3 collective-permute-done.4.low_ref.high_ref
  20.0 1.9 %shard_map.63 = (f32[4,8,16,128]{3,2,1,0:T(8,128)S(1)}, f32[3,1,256]{2,1,0:T(1,128)S(1)}, f32[1,128]{1,0:T(1,128)S(1)}) custom-call(s32[4,128]{1,0:T(4,128)S(1)} %broadcast_in_dim.2.flags_ref, f32[4,8,24,128]{3,2,1,0:T(8,128)S(1)} %bitcast.14, f32[4,3,24,128]{3,2,1,0:T(8,128)S(1)} %get-tuple-element.30.xlo_ref, ...), custom_call_target="tpu_custom_call" | custom-call | tf_op jit(solution)/shard_map/pallas_call | solution.py:471
  21.9 2.1 %all-to-all-done.parts_ref = f32[32,3,128]{2,1,0:T(4,128)S(1)} async-done(((f32[32,3,128]{2,1,0:T(4,128)}), f32[32,3,128]{2,1,0:T(4,128)S(1)}, u32[]{:S(2)}, u32[]{:S(2)}) %all-to-all-start) | async-done | bytes 49184 | tf_op jit(solution)/shard_map/all_to_all | solution.py:448
  24.1 9.1 %all_to_all.10.got_ref = f32[32,4,128]{2,1,0:T(4,128)S(1)} all-to-all(f32[32,4,128]{2,1,0:T(4,128)S(1)} %shard_map.64), channel_id=1, replica_groups=mesh['gx'=4,'gy'=4,'gz'=2] {'gx','gy','gz'}, dimensions={0} | all-to-all | bytes 131072 | tf_op jit(solution)/shard_map/all_to_all | solution.py:485
  33.2 4.8 %shard_map.65 = (f32[3,128,256]{2,1,0:T(8,128)}, f32[128,128]{1,0:T(8,128)}, f32[4,8,16,128]{3,2,1,0:T(8,128)}) custom-call(f32[32,4,128]{2,1,0:T(4,128)S(1)} %all_to_all.10.got_ref, f32[3,127,256]{2,1,0:T(8,128)S(1)} %bitcast.11, f32[3,1,256]{2,1,0:T(1,128)S(1)} %get-tuple-element.36.snap_ref, f32[4,8,16,128]{3,2,1,0:T(8,128)S(1)} %get-tuple-element.37.flow_ref), custom_call_target="tpu_custom_call" | custom-call | tf_op jit(solution)/shard_map/pallas_call | solution.py:486
  (9 shorter events, 0.1 us)
Async XLA Ops:
  0.8 1.0 %copy-start.2 = (f32[4,8,16,128]{3,2,1,0:T(8,128)S(1)}, f32[4,8,16,128]{3,2,1,0:T(8,128)}, u32[]{:S(2)}) copy-start(f32[4,8,16,128]{3,2,1,0:T(8,128)} %param.3) | copy-start | bytes 786436
  1.8 8.0 %copy-start.3 = (f32[4,8,16,128]{3,2,1,0:T(8,128)S(1)}, f32[4,8,16,128]{3,2,1,0:T(8,128)}, u32[]{:S(2)}) copy-start(f32[4,8,16,128]{3,2,1,0:T(8,128)} %param.3) | copy-start | bytes 786436
  1.8 6.7 %collective-permute-start = (f32[4,24,128]{2,1,0:T(8,128)S(1)}, f32[4,24,128]{2,1,0:T(8,128)S(1)}, u32[]{:S(2)}, u32[]{:S(2)}) collective-permute-start(f32[4,24,128]{2,1,0:T(8,128)S(1)} %get-tuple-element.22), channel_id=1, source_target_pairs={{0,2},{2,0},{4,6},{6,4},{1,3},{3,1},{5,7},{7,5},{8,10},{10,8},{12,... | collective-permute-start | bytes 147464 | tf_op jit(solution)/shard_map/ppermute | solution.py:39
  4.8 5.0 %collective-permute-start.1 = (f32[4,24,128]{2,1,0:T(8,128)S(1)}, f32[4,24,128]{2,1,0:T(8,128)S(1)}, u32[]{:S(2)}, u32[]{:S(2)}) collective-permute-start(f32[4,24,128]{2,1,0:T(8,128)S(1)} %get-tuple-element.23), channel_id=1, source_target_pairs={{0,6},{2,4},{4,2},{6,0},{1,7},{3,5},{5,3},{7,1},{8,14},{10,12},{12... | collective-permute-start | bytes 147464 | tf_op jit(solution)/shard_map/ppermute | solution.py:39
  6.3 1.0 %copy-start = (f32[127,3,256]{2,0,1:T(8,128)S(1)}, f32[127,3,256]{2,0,1:T(8,128)}, u32[]{:S(2)}) copy-start(f32[127,3,256]{2,0,1:T(8,128)} %param.4) | copy-start | bytes 1170436
  9.9 6.8 %collective-permute-start.2 = (f32[4,56,128]{2,1,0:T(8,128)S(1)}, f32[4,56,128]{2,1,0:T(8,128)S(1)}, u32[]{:S(2)}, u32[]{:S(2)}) collective-permute-start(f32[4,56,128]{2,1,0:T(8,128)S(1)} %get-tuple-element.28), channel_id=1, source_target_pairs={{0,8},{8,0},{16,24},{24,16},{1,9},{9,1},{17,25},{25,17},{2,10},{10... | collective-permute-start | bytes 344072 | tf_op jit(solution)/shard_map/ppermute | solution.py:39
  11.5 7.0 %collective-permute-start.3 = (f32[4,56,128]{2,1,0:T(8,128)S(1)}, f32[4,56,128]{2,1,0:T(8,128)S(1)}, u32[]{:S(2)}, u32[]{:S(2)}) collective-permute-start(f32[4,56,128]{2,1,0:T(8,128)S(1)} %get-tuple-element.29), channel_id=1, source_target_pairs={{0,24},{8,16},{16,8},{24,0},{1,25},{9,17},{17,9},{25,1},{2,26},{10... | collective-permute-start | bytes 344072 | tf_op jit(solution)/shard_map/ppermute | solution.py:39
  14.0 10.1 %all-to-all-start = ((f32[32,3,128]{2,1,0:T(4,128)}), f32[32,3,128]{2,1,0:T(4,128)S(1)}, u32[]{:S(2)}, u32[]{:S(2)}) async-start(f32[32,3,128]{2,1,0:T(4,128)} %shard_map.59), calls=%async_computation | async-start | bytes 131072 | tf_op jit(solution)/shard_map/all_to_all | solution.py:448
  18.5 0.7 %copy-start.4 = (s32[256]{0:T(256)S(1)}, s32[256]{0:T(256)}, u32[]{:S(2)}) copy-start(s32[256]{0:T(256)} %param.5) | copy-start | bytes 3076
  18.7 1.3 %copy-start.1 = (f32[127,3,256]{2,0,1:T(8,128)S(1)}, f32[127,3,256]{2,0,1:T(8,128)}, u32[]{:S(2)}) copy-start(f32[127,3,256]{2,0,1:T(8,128)} %param.4) | copy-start | bytes 1170436
  18.7 1.3 %collective-permute-start.4 = (f32[4,24,128]{2,1,0:T(8,128)S(1)}, f32[4,24,128]{2,1,0:T(8,128)S(1)}, u32[]{:S(2)}, u32[]{:S(2)}) collective-permute-start(f32[4,24,128]{2,1,0:T(8,128)S(1)} %get-tuple-element.33.own_ref), channel_id=1, source_target_pairs={{0,1},{1,0},{2,3},{3,2},{4,5},{5,4},{6,7},{7,6},{8,9},{9,8},{10,11... | collective-permute-start | bytes 147464 | tf_op jit(solution)/shard_map/ppermute | solution.py:458

commit v9 on v8

--- a/solution.py
+++ b/solution.py
@@ -32,11 +32,14 @@
     return lax.ppermute(block_high, axis, forward), lax.ppermute(block_low, axis, backward)
 
 
-def pairs(block_even, block_odd, axis):
+def pairs(block_even, block_odd, axis, periodic):
     count = lax.axis_size(axis)
     even = [(i, i + 1 - 2 * (i % 2)) for i in range(count)]
     odd = [(i, (i - 1 + 2 * (i % 2)) % count) for i in range(count)]
-    return lax.ppermute(block_even, axis, even), lax.ppermute(block_odd, axis, odd)
+    if not periodic:
+        odd[0], odd[-1] = (0, 0), (count - 1, count - 1)
+    from_odd = lax.ppermute(block_odd, axis, odd)
+    return lax.ppermute(block_even, axis, even), from_odd
 
 
 LOWER_WALL, UPPER_WALL, ODD_Y, ODD_X = range(4)
@@ -425,7 +428,7 @@
     strips = call(
         functools.partial(strips_kernel, nx), out_shape=(strip, strip), in_specs=[VMEM] * 2, out_specs=(VMEM, VMEM)
     )(flags, flat)
-    y_even, y_odd = pairs(*strips, "gy")
+    y_even, y_odd = pairs(*strips, "gy", False)
     gram = call(
         gram_kernel,
         out_shape=shape((devices, per, size)),
@@ -444,7 +447,7 @@
         out_specs=(VMEM,) * 3,
     )(flags, flat, y_even, y_odd)
     mid = mid.reshape(fields, nx, rows, nz)
-    x_even, x_odd = pairs(*faces, "gx")
+    x_even, x_odd = pairs(*faces, "gx", True)
     parts = lax.all_to_all(gram, ALL, 0, 0)
 
     beside = shape((fields, DEPTH, rows, nz))

time: 38.3 us -> 40.2 us (1.050)
  starting transfers between devices: 11.4 us -> 14.8 us
  waiting for transfers between devices: 5.61 us -> 4.3 us
    all_to_all x1, starting transfers between devices: 2.67 us -> 6.67 us  [local(): parts = lax.all_to_all(gram, ALL, 0, 0)]
    ppermute x4, waiting for transfers between devices: 3.12 us -> 0.01 us  [the longest x2 0.01 us: pairs(): from_odd = lax.ppermute(block_odd, axis, odd)]
    all_to_all x1, waiting for transfers between devices: 2.15 us -> 3.94 us  [local(): parts = lax.all_to_all(gram, ALL, 0, 0)]
    ppermute x4, starting transfers between devices: 8.61 us -> 7.77 us  [the longest x2 4.64 us: pairs(): return (lax.ppermute(block_even, axis, even), from_odd)]
  transfers between devices with their start and end apart: 6 -> 6, of which waited for: 4 -> 2; matrix products, arithmetic and copies ran while one was open for 0% -> 0% of each run, Pallas kernels for 10% -> 10%
where the time goes in v9:
time: 40.2 us; the launch traced here: 39.9 us
  starting transfers between devices  14.8 us (37%)
  blocking collectives  9.12 us (23%)
  Pallas kernels  8.82 us (22%)
  waiting for transfers between devices  4.3 us (11%)
  local copies, waits for them, and re-layouts  2.12 us (5%)
  between operations  0.75 us (2%)
    all_to_all x1, blocking collectives, local(): got = lax.all_to_all(send, ALL, 0, 0)  9.12 us
    all_to_all x1, starting transfers between devices, local(): parts = lax.all_to_all(gram, ALL, 0, 0)  6.67 us
    pallas_call x1, Pallas kernels, local(): call(functools.partial(final_kernel, count), out_shape=(shape((comps, siz...  4.84 us
    ppermute x2, starting transfers between devices, pairs(): return (lax.ppermute(block_even, axis, even), from_odd)  4.64 us
    all_to_all x1, waiting for transfers between devices, local(): parts = lax.all_to_all(gram, ALL, 0, 0)  3.94 us
    ppermute x2, starting transfers between devices, pairs(): from_odd = lax.ppermute(block_odd, axis, odd)  3.13 us
    unnamed x10, local copies, waits for them, and re-layouts  2.05 us
    pallas_call x1, Pallas kernels, local(): call(step_kernel, out_shape=(shape(flow.shape), shape((comps, 1, points))...  1.87 us
  transfers between devices with their start and end apart: 6, of which 2 were waited for; matrix products, arithmetic and copies ran while one was open for 0% of the time, Pallas kernels for 10%

profile of v9, /device:TPU:0, one launch (start us, length us, event | category | flops | bytes accessed | tf_op | source)
XLA Modules:
  0.0 39.9 jit_solution(10431127269348557298)
XLA Ops:
  0.7 0.1 add_convert_fusion
  0.7 0.1 broadcast_in_dim.2.flags_ref
  0.8 0.9 %copy-done.2 = f32[4,8,16,128]{3,2,1,0:T(8,128)S(1)} copy-done((f32[4,8,16,128]{3,2,1,0:T(8,128)S(1)}, f32[4,8,16,128]{3,2,1,0:T(8,128)}, u32[]{:S(2)}) %copy-start.2) | copy-done | bytes 262168
  1.8 3.0 %collective-permute-start = (f32[4,24,128]{2,1,0:T(8,128)S(1)}, f32[4,24,128]{2,1,0:T(8,128)S(1)}, u32[]{:S(2)}, u32[]{:S(2)}) collective-permute-start(f32[4,24,128]{2,1,0:T(8,128)S(1)} %get-tuple-element.22), channel_id=1, source_target_pairs={{0,2},{2,0},{4,6},{6,4},{1,3},{3,1},{5,7},{7,5},{8,10},{10,8},{12,... | collective-permute-start | bytes 147464 | tf_op jit(solution)/shard_map/ppermute | solution.py:42
  4.8 0.7 %collective-permute-start.1 = (f32[4,24,128]{2,1,0:T(8,128)S(1)}, f32[4,24,128]{2,1,0:T(8,128)S(1)}, u32[]{:S(2)}, u32[]{:S(2)}) collective-permute-start(f32[4,24,128]{2,1,0:T(8,128)S(1)} %get-tuple-element.23), channel_id=1, source_target_pairs={{0,0},{2,4},{4,2},{6,6},{1,1},{3,5},{5,3},{7,7},{8,8},{10,12},{12,... | collective-permute-start | bytes 147464 | tf_op jit(solution)/shard_map/ppermute | solution.py:41
  5.5 0.0 copy-start
  5.5 1.0 %copy-done = f32[127,3,256]{2,0,1:T(8,128)S(1)} copy-done((f32[127,3,256]{2,0,1:T(8,128)S(1)}, f32[127,3,256]{2,0,1:T(8,128)}, u32[]{:S(2)}) %copy-start) | copy-done | bytes 390168
  6.5 1.2 %shard_map.59 = f32[32,3,128]{2,1,0:T(4,128)} custom-call(f32[3,127,256]{2,1,0:T(8,128)S(1)} %bitcast.9), custom_call_target="tpu_custom_call" | custom-call | tf_op jit(solution)/shard_map/pallas_call | solution.py:432
  7.7 0.0 collective-permute-done.even_ref
  7.7 0.1 shard_map.60
  7.7 1.6 %collective-permute-start.2 = (f32[4,56,128]{2,1,0:T(8,128)S(1)}, f32[4,56,128]{2,1,0:T(8,128)S(1)}, u32[]{:S(2)}, u32[]{:S(2)}) collective-permute-start(f32[4,56,128]{2,1,0:T(8,128)S(1)} %get-tuple-element.28), channel_id=1, source_target_pairs={{0,8},{8,0},{16,24},{24,16},{1,9},{9,1},{17,25},{25,17},{2,10},{10... | collective-permute-start | bytes 344072 | tf_op jit(solution)/shard_map/ppermute | solution.py:42
  9.4 2.5 %collective-permute-start.3 = (f32[4,56,128]{2,1,0:T(8,128)S(1)}, f32[4,56,128]{2,1,0:T(8,128)S(1)}, u32[]{:S(2)}, u32[]{:S(2)}) collective-permute-start(f32[4,56,128]{2,1,0:T(8,128)S(1)} %get-tuple-element.29), channel_id=1, source_target_pairs={{0,24},{8,16},{16,8},{24,0},{1,25},{9,17},{17,9},{25,1},{2,26},{10... | collective-permute-start | bytes 344072 | tf_op jit(solution)/shard_map/ppermute | solution.py:41
  11.9 6.7 %all-to-all-start = ((f32[32,3,128]{2,1,0:T(4,128)}), f32[32,3,128]{2,1,0:T(4,128)S(1)}, u32[]{:S(2)}, u32[]{:S(2)}) async-start(f32[32,3,128]{2,1,0:T(4,128)} %shard_map.59), calls=%async_computation | async-start | bytes 131072 | tf_op jit(solution)/shard_map/all_to_all | solution.py:451
  18.6 0.0 copy-start.4
  18.6 0.2 shard_map.61
  18.8 0.0 copy-start.1
  18.8 0.3 collective-permute-start.4
  19.1 0.1 copy-done.4
  19.2 0.5 %shard_map.62 = (f32[4,12,24,128]{3,2,1,0:T(8,128)S(1)}, s32[1,256]{1,0:T(1,128)S(1)}) custom-call(s32[4,128]{1,0:T(4,128)S(1)} %broadcast_in_dim.2.flags_ref, s32[1,256]{1,0:T(1,128)S(1)} %bitcast.17, f32[4,8,24,128]{3,2,1,0:T(8,128)S(1)} %bitcast.13, f32[4,3,24,128]{3,2,1,0:T(8,128)S(1)} %get-tuple-element.30.xlo_ref, ...), custom_call_target="tpu_custom_call" | custom-call | tf_op jit(solution)/shard_map/pallas_call | solution.py:464
  19.8 0.3 collective-permute-done.4.low_ref.high_ref
  20.1 1.9 %shard_map.63 = (f32[4,8,16,128]{3,2,1,0:T(8,128)S(1)}, f32[3,1,256]{2,1,0:T(1,128)S(1)}, f32[1,128]{1,0:T(1,128)S(1)}) custom-call(s32[4,128]{1,0:T(4,128)S(1)} %broadcast_in_dim.2.flags_ref, f32[4,8,24,128]{3,2,1,0:T(8,128)S(1)} %bitcast.14, f32[4,3,24,128]{3,2,1,0:T(8,128)S(1)} %get-tuple-element.30.xlo_ref, ...), custom_call_target="tpu_custom_call" | custom-call | tf_op jit(solution)/shard_map/pallas_call | solution.py:474
  22.0 3.9 %all-to-all-done.parts_ref = f32[32,3,128]{2,1,0:T(4,128)S(1)} async-done(((f32[32,3,128]{2,1,0:T(4,128)}), f32[32,3,128]{2,1,0:T(4,128)S(1)}, u32[]{:S(2)}, u32[]{:S(2)}) %all-to-all-start) | async-done | bytes 49184 | tf_op jit(solution)/shard_map/all_to_all | solution.py:451
  26.0 9.1 %all_to_all.10.got_ref = f32[32,4,128]{2,1,0:T(4,128)S(1)} all-to-all(f32[32,4,128]{2,1,0:T(4,128)S(1)} %shard_map.64), channel_id=1, replica_groups=mesh['gx'=4,'gy'=4,'gz'=2] {'gx','gy','gz'}, dimensions={0} | all-to-all | bytes 131072 | tf_op jit(solution)/shard_map/all_to_all | solution.py:488
  35.1 4.8 %shard_map.65 = (f32[3,128,256]{2,1,0:T(8,128)}, f32[128,128]{1,0:T(8,128)}, f32[4,8,16,128]{3,2,1,0:T(8,128)}) custom-call(f32[32,4,128]{2,1,0:T(4,128)S(1)} %all_to_all.10.got_ref, f32[3,127,256]{2,1,0:T(8,128)S(1)} %bitcast.11, f32[3,1,256]{2,1,0:T(1,128)S(1)} %get-tuple-element.36.snap_ref, f32[4,8,16,128]{3,2,1,0:T(8,128)S(1)} %get-tuple-element.37.flow_ref), custom_call_target="tpu_custom_call" | custom-call | tf_op jit(solution)/shard_map/pallas_call | solution.py:489
  (9 shorter events, 0.1 us)
Async XLA Ops:
  0.8 1.0 %copy-start.2 = (f32[4,8,16,128]{3,2,1,0:T(8,128)S(1)}, f32[4,8,16,128]{3,2,1,0:T(8,128)}, u32[]{:S(2)}) copy-start(f32[4,8,16,128]{3,2,1,0:T(8,128)} %param.3) | copy-start | bytes 786436
  1.8 5.9 %copy-start.3 = (f32[4,8,16,128]{3,2,1,0:T(8,128)S(1)}, f32[4,8,16,128]{3,2,1,0:T(8,128)}, u32[]{:S(2)}) copy-start(f32[4,8,16,128]{3,2,1,0:T(8,128)} %param.3) | copy-start | bytes 786436
  1.8 5.9 %collective-permute-start = (f32[4,24,128]{2,1,0:T(8,128)S(1)}, f32[4,24,128]{2,1,0:T(8,128)S(1)}, u32[]{:S(2)}, u32[]{:S(2)}) collective-permute-start(f32[4,24,128]{2,1,0:T(8,128)S(1)} %get-tuple-element.22), channel_id=1, source_target_pairs={{0,2},{2,0},{4,6},{6,4},{1,3},{3,1},{5,7},{7,5},{8,10},{10,8},{12,... | collective-permute-start | bytes 147464 | tf_op jit(solution)/shard_map/ppermute | solution.py:42
  4.8 2.9 %collective-permute-start.1 = (f32[4,24,128]{2,1,0:T(8,128)S(1)}, f32[4,24,128]{2,1,0:T(8,128)S(1)}, u32[]{:S(2)}, u32[]{:S(2)}) collective-permute-start(f32[4,24,128]{2,1,0:T(8,128)S(1)} %get-tuple-element.23), channel_id=1, source_target_pairs={{0,0},{2,4},{4,2},{6,6},{1,1},{3,5},{5,3},{7,7},{8,8},{10,12},{12,... | collective-permute-start | bytes 147464 | tf_op jit(solution)/shard_map/ppermute | solution.py:41
  5.5 1.0 %copy-start = (f32[127,3,256]{2,0,1:T(8,128)S(1)}, f32[127,3,256]{2,0,1:T(8,128)}, u32[]{:S(2)}) copy-start(f32[127,3,256]{2,0,1:T(8,128)} %param.4) | copy-start | bytes 1170436
  7.7 10.8 %collective-permute-start.2 = (f32[4,56,128]{2,1,0:T(8,128)S(1)}, f32[4,56,128]{2,1,0:T(8,128)S(1)}, u32[]{:S(2)}, u32[]{:S(2)}) collective-permute-start(f32[4,56,128]{2,1,0:T(8,128)S(1)} %get-tuple-element.28), channel_id=1, source_target_pairs={{0,8},{8,0},{16,24},{24,16},{1,9},{9,1},{17,25},{25,17},{2,10},{10... | collective-permute-start | bytes 344072 | tf_op jit(solution)/shard_map/ppermute | solution.py:42
  9.4 9.2 %collective-permute-start.3 = (f32[4,56,128]{2,1,0:T(8,128)S(1)}, f32[4,56,128]{2,1,0:T(8,128)S(1)}, u32[]{:S(2)}, u32[]{:S(2)}) collective-permute-start(f32[4,56,128]{2,1,0:T(8,128)S(1)} %get-tuple-element.29), channel_id=1, source_target_pairs={{0,24},{8,16},{16,8},{24,0},{1,25},{9,17},{17,9},{25,1},{2,26},{10... | collective-permute-start | bytes 344072 | tf_op jit(solution)/shard_map/ppermute | solution.py:41
  11.9 14.1 %all-to-all-start = ((f32[32,3,128]{2,1,0:T(4,128)}), f32[32,3,128]{2,1,0:T(4,128)S(1)}, u32[]{:S(2)}, u32[]{:S(2)}) async-start(f32[32,3,128]{2,1,0:T(4,128)} %shard_map.59), calls=%async_computation | async-start | bytes 131072 | tf_op jit(solution)/shard_map/all_to_all | solution.py:451
  18.6 0.7 %copy-start.4 = (s32[256]{0:T(256)S(1)}, s32[256]{0:T(256)}, u32[]{:S(2)}) copy-start(s32[256]{0:T(256)} %param.5) | copy-start | bytes 3076
  18.8 1.3 %copy-start.1 = (f32[127,3,256]{2,0,1:T(8,128)S(1)}, f32[127,3,256]{2,0,1:T(8,128)}, u32[]{:S(2)}) copy-start(f32[127,3,256]{2,0,1:T(8,128)} %param.4) | copy-start | bytes 1170436
  18.8 1.3 %collective-permute-start.4 = (f32[4,24,128]{2,1,0:T(8,128)S(1)}, f32[4,24,128]{2,1,0:T(8,128)S(1)}, u32[]{:S(2)}, u32[]{:S(2)}) collective-permute-start(f32[4,24,128]{2,1,0:T(8,128)S(1)} %get-tuple-element.33.own_ref), channel_id=1, source_target_pairs={{0,1},{1,0},{2,3},{3,2},{4,5},{5,4},{6,7},{7,6},{8,9},{9,8},{10,11... | collective-permute-start | bytes 147464 | tf_op jit(solution)/shard_map/ppermute | solution.py:461

commit v10 on v8

--- a/solution.py
+++ b/solution.py
@@ -25,6 +25,24 @@
     )
 
 
+def three_parts(value):
+    high = value.astype(jnp.bfloat16)
+    rest = value - high.astype(jnp.float32)
+    middle = rest.astype(jnp.bfloat16)
+    return high, middle, (rest - middle.astype(jnp.float32)).astype(jnp.bfloat16)
+
+
+def dot_parts(a, b, dims):
+    return lax.dot_general(a, b, (dims, ((), ())), preferred_element_type=jnp.float32)
+
+
+def dot_stacked(a, b):
+    (a1, a2, a3), (b1, b2, b3) = three_parts(a), three_parts(b)
+    first = jnp.concatenate([a1, a1, a2, a2, a1, a3], axis=0)
+    second = jnp.concatenate([b1, b2, b1, b2, b3, b1], axis=0)
+    return dot_parts(first, second, ((0,), (0,)))
+
+
 def neighbours(block_low, block_high, axis):
     count = lax.axis_size(axis)
     forward = [(i, (i + 1) % count) for i in range(count)]
@@ -57,13 +75,16 @@
     return [packed[0], packed[1], packed[2], pltpu.roll(packed[1], packed[1].shape[1] - tall, 1)]
 
 
-def gram_kernel(basis_ref, send_ref, gram_ref, packed_ref):
+def gram_kernel(basis_ref, send_ref, parts_ref, gram_ref, packed_ref):
     modes = basis_ref.shape[1]
     tall = gram_ref.shape[0] // 4
     total = jnp.zeros((modes, modes), jnp.float32)
     for c in range(basis_ref.shape[0]):
         rows = basis_ref[c]
         total = total + dot(rows, rows, ((1,), (1,)))
+        filled = jnp.concatenate([rows, jnp.zeros((1, rows.shape[1]), jnp.float32)], axis=0)
+        for k, part in enumerate(three_parts(filled)):
+            parts_ref[k, c] = part
     gram_ref[...] = jnp.zeros_like(gram_ref)
     gram_ref[0:modes, 0:modes] = total
     packed_ref[...] = jnp.zeros_like(packed_ref)
@@ -298,14 +319,7 @@
     product = jnp.zeros((modes + 1, points), jnp.float32)
     for c in range(3):
         field = flow_ref[c].reshape(nx * ny, nz).T
-        high = field.astype(jnp.bfloat16)
-        rest = field - high.astype(jnp.float32)
-        middle = rest.astype(jnp.bfloat16)
-        low = (rest - middle.astype(jnp.float32)).astype(jnp.bfloat16)
-        found = sum(
-            lax.dot_general(p, in_row, (((1,), (0,)), ((), ())), preferred_element_type=jnp.float32)
-            for p in (high, middle, low)
-        )
+        found = sum(dot_parts(part, in_row, ((1,), (0,))) for part in three_parts(field))
         picked = jnp.sum(jnp.where(in_lane, found, 0.0), axis=0, keepdims=True)
         snap_ref[c] = picked
         product = product + jnp.concatenate([basis_ref[c], picked], axis=0) * picked
@@ -325,12 +339,11 @@
 
 
 def final_kernel(
-    count, got_ref, basis_ref, snap_ref, flow_ref,
+    count, got_ref, parts_ref, snap_ref, flow_ref,
     basis_hbm, factor_hbm, flow_hbm,
     packed_ref, work_ref, basis_out_ref, factor_ref, sems,
 ):
-    comps, modes, points = basis_ref.shape
-    size = modes + 1
+    _, comps, size, points = parts_ref.shape
     tall = size // 4
     per = got_ref.shape[1] - 1
     copies = [pltpu.make_async_copy(flow_ref, flow_hbm, sems.at[0])]
@@ -343,9 +356,12 @@
             packed_ref[per * d : per * d + per] = block[0:per]
         total = total + block
     cross = total[per : per + 1] / count
-    mark = (lax.broadcasted_iota(jnp.int32, (8, size), 1) == size - 1).astype(jnp.float32)
-    top = lax.broadcasted_iota(jnp.int32, (8, size), 0) == 0
-    side = dot(jnp.where(top, jnp.broadcast_to(cross, (8, size)), 0.0), mark, ((0,), (0,)))
+    top = lax.broadcasted_iota(jnp.int32, (16, size), 0)
+    mark = (lax.broadcasted_iota(jnp.int32, (16, size), 1) == size - 1) & (top < 3)
+    thirds = jnp.zeros((16, size), jnp.float32)
+    for k, part in enumerate(three_parts(cross)):
+        thirds = jnp.where(top == k, part.astype(jnp.float32), thirds)
+    side = dot_parts(thirds.astype(jnp.bfloat16), mark.astype(jnp.bfloat16), ((0,), (0,)))
     lane = lax.broadcasted_iota(jnp.int32, (tall, size), 1)
     row = lax.broadcasted_iota(jnp.int32, (tall, size), 0)
     old = unpack_upper([packed_ref[tall * k : tall * k + tall] / count for k in range(3)], tall)
@@ -356,19 +372,30 @@
         work_ref[tall * k : tall * k + tall, 0:size] = value
         work_ref[tall * k : tall * k + tall, size : 2 * size] = (lane == row + tall * k).astype(jnp.float32)
 
-    stacked = [jnp.concatenate([basis_ref[c], snap_ref[c]], axis=0) for c in range(comps)]
     for k in range(4):
         base = tall * k
         eliminate(work_ref, base, tall)
         done = work_ref[base : base + tall, :]
         if k < 3:
-            change = dot(done[:, 0:size], done, ((0,), (0,)))
+            change = dot_stacked(done[:, 0:size], done)
             work_ref[base + tall : size, :] = work_ref[base + tall : size, :] - change[base + tall : size]
         factor_ref[base : base + tall, :] = jnp.where(lane >= row + base, done[:, 0:size], 0.0)
+        if k < 2:
+            continue
+        begin, count_rows = (0, base + tall) if k == 2 else (base, tall)
+        inverse = work_ref[begin : base + tall, size : 2 * size]
+        pieces = jnp.concatenate(three_parts(inverse), axis=0)
         for c in range(comps):
-            basis_out_ref[c, base : base + tall, :] = dot(done[:, size : 2 * size], stacked[c], ((1,), (0,)))
-        rows = (slice(None), pl.ds(base, tall), slice(None))
-        copies.append(pltpu.make_async_copy(basis_out_ref.at[rows], basis_hbm.at[rows], sems.at[2 + k]))
+            value = jnp.zeros((count_rows, points), jnp.float32)
+            for n in (2, 1, 0):
+                products = dot_parts(pieces[: count_rows * (3 - n)], parts_ref[n, c], ((1,), (0,)))
+                for m in range(2 - n, -1, -1):
+                    value = value + products[count_rows * m : count_rows * m + count_rows]
+            if k == 3:
+                value = value + inverse[:, size - 1 : size] * snap_ref[c]
+            basis_out_ref[c, begin : base + tall, :] = value
+        rows = (slice(None), pl.ds(begin, count_rows), slice(None))
+        copies.append(pltpu.make_async_copy(basis_out_ref.at[rows], basis_hbm.at[rows], sems.at[k]))
         copies[-1].start()
     copies.append(pltpu.make_async_copy(factor_ref, factor_hbm, sems.at[1]))
     copies[-1].start()
@@ -426,11 +453,11 @@
         functools.partial(strips_kernel, nx), out_shape=(strip, strip), in_specs=[VMEM] * 2, out_specs=(VMEM, VMEM)
     )(flags, flat)
     y_even, y_odd = pairs(*strips, "gy")
-    gram = call(
+    gram, basis_parts = call(
         gram_kernel,
-        out_shape=shape((devices, per, size)),
+        out_shape=(shape((devices, per, size)), jax.ShapeDtypeStruct((3, comps, size, points), jnp.bfloat16)),
         in_specs=[VMEM],
-        out_specs=VMEM,
+        out_specs=(VMEM, VMEM),
         scratch_shapes=[pltpu.VMEM((size, size), jnp.float32), pltpu.VMEM((devices * per, size), jnp.float32)],
     )(bricks)
     y_even, y_odd, gram = lax.optimization_barrier((y_even, y_odd, gram))
@@ -493,9 +520,9 @@
             pltpu.VMEM((size, 2 * size), jnp.float32),
             pltpu.VMEM((comps, size, points), jnp.float32),
             pltpu.VMEM((size, size), jnp.float32),
-            pltpu.SemaphoreType.DMA((6,)),
+            pltpu.SemaphoreType.DMA((4,)),
         ],
-    )(got, bricks, snapshot, flow_new)
+    )(got, basis_parts, snapshot, flow_new)
     return flow_next, jnp.transpose(basis_next, (1, 0, 2)), factor
 
 

time: 38.3 us -> 37.6 us (0.982)
  Pallas kernels: 8.81 us -> 8.14 us
    pallas_call x1, Pallas kernels: 4.84 us -> 4.13 us  [local(): call(functools.partial(final_kernel, count), out_shape=(shape((comps, siz...]
where the time goes in v10:
time: 37.6 us; the launch traced here: 37.4 us
  starting transfers between devices  11.4 us (30%)
  blocking collectives  9.12 us (24%)
  Pallas kernels  8.14 us (22%)
  waiting for transfers between devices  5.57 us (15%)
  local copies, waits for them, and re-layouts  2.37 us (6%)
  between operations  0.73 us (2%)
    all_to_all x1, blocking collectives, local(): got = lax.all_to_all(send, ALL, 0, 0)  9.12 us
    ppermute x2, starting transfers between devices, pairs(): lax.ppermute(block_even, axis, even)  4.65 us
    pallas_call x1, Pallas kernels, local(): call(functools.partial(final_kernel, count), out_shape=(shape((comps, siz...  4.13 us
    ppermute x2, starting transfers between devices, pairs(): lax.ppermute(block_odd, axis, odd)  3.97 us
    ppermute x2, waiting for transfers between devices, pairs(): lax.ppermute(block_odd, axis, odd)  3.07 us
    all_to_all x1, starting transfers between devices, local(): parts = lax.all_to_all(gram, ALL, 0, 0)  2.67 us
    unnamed x10, local copies, waits for them, and re-layouts  2.3 us
    all_to_all x1, waiting for transfers between devices, local(): parts = lax.all_to_all(gram, ALL, 0, 0)  2.15 us
  transfers between devices with their start and end apart: 6, of which 4 were waited for; matrix products, arithmetic and copies ran while one was open for 0% of the time, Pallas kernels for 10%

profile of v10, /device:TPU:0, one launch (start us, length us, event | category | flops | bytes accessed | tf_op | source)
XLA Modules:
  0.0 37.4 jit_solution(15850815390295004740)
XLA Ops:
  0.7 0.1 add_convert_fusion
  0.7 0.1 broadcast_in_dim.2.flags_ref
  0.8 0.9 %copy-done.2 = f32[4,8,16,128]{3,2,1,0:T(8,128)S(1)} copy-done((f32[4,8,16,128]{3,2,1,0:T(8,128)S(1)}, f32[4,8,16,128]{3,2,1,0:T(8,128)}, u32[]{:S(2)}) %copy-start.2) | copy-done | bytes 262168
  1.8 3.0 %collective-permute-start = (f32[4,24,128]{2,1,0:T(8,128)S(1)}, f32[4,24,128]{2,1,0:T(8,128)S(1)}, u32[]{:S(2)}, u32[]{:S(2)}) collective-permute-start(f32[4,24,128]{2,1,0:T(8,128)S(1)} %get-tuple-element.24), channel_id=1, source_target_pairs={{0,2},{2,0},{4,6},{6,4},{1,3},{3,1},{5,7},{7,5},{8,10},{10,8},{12,... | collective-permute-start | bytes 147464 | tf_op jit(solution)/shard_map/ppermute | solution.py:57
  4.8 1.5 %collective-permute-start.1 = (f32[4,24,128]{2,1,0:T(8,128)S(1)}, f32[4,24,128]{2,1,0:T(8,128)S(1)}, u32[]{:S(2)}, u32[]{:S(2)}) collective-permute-start(f32[4,24,128]{2,1,0:T(8,128)S(1)} %get-tuple-element.25), channel_id=1, source_target_pairs={{0,6},{2,4},{4,2},{6,0},{1,7},{3,5},{5,3},{7,1},{8,14},{10,12},{12... | collective-permute-start | bytes 147464 | tf_op jit(solution)/shard_map/ppermute | solution.py:57
  6.3 1.0 %copy-done = f32[127,3,256]{2,0,1:T(8,128)S(1)} copy-done((f32[127,3,256]{2,0,1:T(8,128)S(1)}, f32[127,3,256]{2,0,1:T(8,128)}, u32[]{:S(2)}) %copy-start) | copy-done | bytes 390168
  7.3 1.2 %shard_map.59 = (f32[32,3,128]{2,1,0:T(4,128)}, bf16[3,3,128,256]{3,2,1,0:T(8,128)(2,1)S(1)}) custom-call(f32[3,127,256]{2,1,0:T(8,128)S(1)} %bitcast.12), custom_call_target="tpu_custom_call" | custom-call | tf_op jit(solution)/shard_map/pallas_call | solution.py:456
  8.5 0.0 collective-permute-done.even_ref
  8.5 1.3 %collective-permute-done.1.odd_ref = f32[4,24,128]{2,1,0:T(8,128)S(1)} collective-permute-done((f32[4,24,128]{2,1,0:T(8,128)S(1)}, f32[4,24,128]{2,1,0:T(8,128)S(1)}, u32[]{:S(2)}, u32[]{:S(2)}) %collective-permute-start.1) | collective-permute-done | bytes 49184 | tf_op jit(solution)/shard_map/ppermute | solution.py:57
  9.8 0.1 shard_map.60
  9.9 1.6 %collective-permute-start.2 = (f32[4,56,128]{2,1,0:T(8,128)S(1)}, f32[4,56,128]{2,1,0:T(8,128)S(1)}, u32[]{:S(2)}, u32[]{:S(2)}) collective-permute-start(f32[4,56,128]{2,1,0:T(8,128)S(1)} %get-tuple-element.31), channel_id=1, source_target_pairs={{0,8},{8,0},{16,24},{24,16},{1,9},{9,1},{17,25},{25,17},{2,10},{10... | collective-permute-start | bytes 344072 | tf_op jit(solution)/shard_map/ppermute | solution.py:57
  11.5 2.5 %collective-permute-start.3 = (f32[4,56,128]{2,1,0:T(8,128)S(1)}, f32[4,56,128]{2,1,0:T(8,128)S(1)}, u32[]{:S(2)}, u32[]{:S(2)}) collective-permute-start(f32[4,56,128]{2,1,0:T(8,128)S(1)} %get-tuple-element.32), channel_id=1, source_target_pairs={{0,24},{8,16},{16,8},{24,0},{1,25},{9,17},{17,9},{25,1},{2,26},{10... | collective-permute-start | bytes 344072 | tf_op jit(solution)/shard_map/ppermute | solution.py:57
  14.0 2.7 %all-to-all-start = ((f32[32,3,128]{2,1,0:T(4,128)}), f32[32,3,128]{2,1,0:T(4,128)S(1)}, u32[]{:S(2)}, u32[]{:S(2)}) async-start(f32[32,3,128]{2,1,0:T(4,128)} %get-tuple-element.27), calls=%async_computation | async-start | bytes 131072 | tf_op jit(solution)/shard_map/all_to_all | solution.py:475
  16.7 1.8 %collective-permute-done.3.odd_ref = f32[4,56,128]{2,1,0:T(8,128)S(1)} collective-permute-done((f32[4,56,128]{2,1,0:T(8,128)S(1)}, f32[4,56,128]{2,1,0:T(8,128)S(1)}, u32[]{:S(2)}, u32[]{:S(2)}) %collective-permute-start.3) | collective-permute-done | bytes 114720 | tf_op jit(solution)/shard_map/ppermute | solution.py:57
  18.5 0.2 shard_map.61
  18.7 0.0 copy-start.1
  18.7 0.1 collective-permute-start.4
  18.8 0.3 copy-done.4
  19.2 0.5 %shard_map.62 = (f32[4,12,24,128]{3,2,1,0:T(8,128)S(1)}, s32[1,256]{1,0:T(1,128)S(1)}) custom-call(s32[4,128]{1,0:T(4,128)S(1)} %broadcast_in_dim.2.flags_ref, s32[1,256]{1,0:T(1,128)S(1)} %bitcast.16, f32[4,8,24,128]{3,2,1,0:T(8,128)S(1)} %bitcast.10, f32[4,3,24,128]{3,2,1,0:T(8,128)S(1)} %get-tuple-element.33.xlo_ref, ...), custom_call_target="tpu_custom_call" | custom-call | tf_op jit(solution)/shard_map/pallas_call | solution.py:488
  19.7 0.3 collective-permute-done.4.low_ref.high_ref
  20.0 1.9 %shard_map.63 = (f32[4,8,16,128]{3,2,1,0:T(8,128)S(1)}, f32[3,1,256]{2,1,0:T(1,128)S(1)}, f32[1,128]{1,0:T(1,128)S(1)}) custom-call(s32[4,128]{1,0:T(4,128)S(1)} %broadcast_in_dim.2.flags_ref, f32[4,8,24,128]{3,2,1,0:T(8,128)S(1)} %bitcast.11, f32[4,3,24,128]{3,2,1,0:T(8,128)S(1)} %get-tuple-element.33.xlo_ref, ...), custom_call_target="tpu_custom_call" | custom-call | tf_op jit(solution)/shard_map/pallas_call | solution.py:498
  21.9 2.1 %all-to-all-done.parts_ref = f32[32,3,128]{2,1,0:T(4,128)S(1)} async-done(((f32[32,3,128]{2,1,0:T(4,128)}), f32[32,3,128]{2,1,0:T(4,128)S(1)}, u32[]{:S(2)}, u32[]{:S(2)}) %all-to-all-start) | async-done | bytes 49184 | tf_op jit(solution)/shard_map/all_to_all | solution.py:475
  24.1 9.1 %all_to_all.10.got_ref = f32[32,4,128]{2,1,0:T(4,128)S(1)} all-to-all(f32[32,4,128]{2,1,0:T(4,128)S(1)} %shard_map.64), channel_id=1, replica_groups=mesh['gx'=4,'gy'=4,'gz'=2] {'gx','gy','gz'}, dimensions={0} | all-to-all | bytes 131072 | tf_op jit(solution)/shard_map/all_to_all | solution.py:512
  33.2 4.1 %shard_map.65 = (f32[3,128,256]{2,1,0:T(8,128)}, f32[128,128]{1,0:T(8,128)}, f32[4,8,16,128]{3,2,1,0:T(8,128)}) custom-call(f32[32,4,128]{2,1,0:T(4,128)S(1)} %all_to_all.10.got_ref, bf16[3,3,128,256]{3,2,1,0:T(8,128)(2,1)S(1)} %get-tuple-element.39.parts_ref, f32[3,1,256]{2,1,0:T(1,128)S(1)} %get-tuple-element.40.snap_ref, ...), custom_call_target="tpu_custom_call" | custom-call | tf_op jit(solution)/shard_map/pallas_call | solution.py:513
  (9 shorter events, 0.1 us)
Async XLA Ops:
  0.8 1.0 %copy-start.2 = (f32[4,8,16,128]{3,2,1,0:T(8,128)S(1)}, f32[4,8,16,128]{3,2,1,0:T(8,128)}, u32[]{:S(2)}) copy-start(f32[4,8,16,128]{3,2,1,0:T(8,128)} %param.3) | copy-start | bytes 786436
  1.8 8.0 %copy-start.3 = (f32[4,8,16,128]{3,2,1,0:T(8,128)S(1)}, f32[4,8,16,128]{3,2,1,0:T(8,128)}, u32[]{:S(2)}) copy-start(f32[4,8,16,128]{3,2,1,0:T(8,128)} %param.3) | copy-start | bytes 786436
  1.8 6.7 %collective-permute-start = (f32[4,24,128]{2,1,0:T(8,128)S(1)}, f32[4,24,128]{2,1,0:T(8,128)S(1)}, u32[]{:S(2)}, u32[]{:S(2)}) collective-permute-start(f32[4,24,128]{2,1,0:T(8,128)S(1)} %get-tuple-element.24), channel_id=1, source_target_pairs={{0,2},{2,0},{4,6},{6,4},{1,3},{3,1},{5,7},{7,5},{8,10},{10,8},{12,... | collective-permute-start | bytes 147464 | tf_op jit(solution)/shard_map/ppermute | solution.py:57
  4.8 5.0 %collective-permute-start.1 = (f32[4,24,128]{2,1,0:T(8,128)S(1)}, f32[4,24,128]{2,1,0:T(8,128)S(1)}, u32[]{:S(2)}, u32[]{:S(2)}) collective-permute-start(f32[4,24,128]{2,1,0:T(8,128)S(1)} %get-tuple-element.25), channel_id=1, source_target_pairs={{0,6},{2,4},{4,2},{6,0},{1,7},{3,5},{5,3},{7,1},{8,14},{10,12},{12... | collective-permute-start | bytes 147464 | tf_op jit(solution)/shard_map/ppermute | solution.py:57
  6.3 1.0 %copy-start = (f32[127,3,256]{2,0,1:T(8,128)S(1)}, f32[127,3,256]{2,0,1:T(8,128)}, u32[]{:S(2)}) copy-start(f32[127,3,256]{2,0,1:T(8,128)} %param.4) | copy-start | bytes 1170436
  9.9 6.8 %collective-permute-start.2 = (f32[4,56,128]{2,1,0:T(8,128)S(1)}, f32[4,56,128]{2,1,0:T(8,128)S(1)}, u32[]{:S(2)}, u32[]{:S(2)}) collective-permute-start(f32[4,56,128]{2,1,0:T(8,128)S(1)} %get-tuple-element.31), channel_id=1, source_target_pairs={{0,8},{8,0},{16,24},{24,16},{1,9},{9,1},{17,25},{25,17},{2,10},{10... | collective-permute-start | bytes 344072 | tf_op jit(solution)/shard_map/ppermute | solution.py:57
  11.5 7.0 %collective-permute-start.3 = (f32[4,56,128]{2,1,0:T(8,128)S(1)}, f32[4,56,128]{2,1,0:T(8,128)S(1)}, u32[]{:S(2)}, u32[]{:S(2)}) collective-permute-start(f32[4,56,128]{2,1,0:T(8,128)S(1)} %get-tuple-element.32), channel_id=1, source_target_pairs={{0,24},{8,16},{16,8},{24,0},{1,25},{9,17},{17,9},{25,1},{2,26},{10... | collective-permute-start | bytes 344072 | tf_op jit(solution)/shard_map/ppermute | solution.py:57
  14.0 10.1 %all-to-all-start = ((f32[32,3,128]{2,1,0:T(4,128)}), f32[32,3,128]{2,1,0:T(4,128)S(1)}, u32[]{:S(2)}, u32[]{:S(2)}) async-start(f32[32,3,128]{2,1,0:T(4,128)} %get-tuple-element.27), calls=%async_computation | async-start | bytes 131072 | tf_op jit(solution)/shard_map/all_to_all | solution.py:475
  18.5 0.7 %copy-start.4 = (s32[256]{0:T(256)S(1)}, s32[256]{0:T(256)}, u32[]{:S(2)}) copy-start(s32[256]{0:T(256)} %param.5) | copy-start | bytes 3076
  18.7 1.3 %copy-start.1 = (f32[127,3,256]{2,0,1:T(8,128)S(1)}, f32[127,3,256]{2,0,1:T(8,128)}, u32[]{:S(2)}) copy-start(f32[127,3,256]{2,0,1:T(8,128)} %param.4) | copy-start | bytes 1170436
  18.7 1.3 %collective-permute-start.4 = (f32[4,24,128]{2,1,0:T(8,128)S(1)}, f32[4,24,128]{2,1,0:T(8,128)S(1)}, u32[]{:S(2)}, u32[]{:S(2)}) collective-permute-start(f32[4,24,128]{2,1,0:T(8,128)S(1)} %get-tuple-element.36.own_ref), channel_id=1, source_target_pairs={{0,1},{1,0},{2,3},{3,2},{4,5},{5,4},{6,7},{7,6},{8,9},{9,8},{10,11... | collective-permute-start | bytes 147464 | tf_op jit(solution)/shard_map/ppermute | solution.py:485

commit v11 on v10

--- a/solution.py
+++ b/solution.py
@@ -57,7 +57,7 @@
     return lax.ppermute(block_even, axis, even), lax.ppermute(block_odd, axis, odd)
 
 
-LOWER_WALL, UPPER_WALL, ODD_Y, ODD_X = range(4)
+LOWER_WALL, UPPER_WALL, ODD_Y = range(3)
 
 
 def flag(flags_ref, which):
@@ -110,9 +110,9 @@
             odd_ref[f, planes * j : planes * j + planes] = jnp.where(odd, top, bottom)
 
 
-def walls_kernel(planes, flags_ref, flow_ref, even_ref, odd_ref, mid_ref, face_even_ref, face_odd_ref):
+def walls_kernel(planes, flags_ref, flow_ref, even_ref, odd_ref, mid_ref, first_ref, last_ref):
     fields, cells, nz = flow_ref.shape
-    odd_y, odd_x = flag(flags_ref, ODD_Y), flag(flags_ref, ODD_X)
+    odd_y = flag(flags_ref, ODD_Y)
     ny = cells // planes
     rows = ny + HALO
     sub = lax.broadcasted_iota(jnp.int32, (HALO, nz), 0)
@@ -132,14 +132,13 @@
                 value = jnp.where(odd_y, even_ref[f, part], odd_ref[f, part])
                 value = jnp.where(flag(flags_ref, LOWER_WALL), 0.0, value)
             mid_ref[f, pl.ds(ny + j, planes, stride=rows), :] = value
-        faces = []
-        for begin, near, next_one in ((0, 0, 1), (planes - DEPTH, planes - 1, planes - 2)):
+        for face_ref, begin, near, next_one in (
+            (first_ref, 0, 0, 1), (last_ref, planes - DEPTH, planes - 1, planes - 2)
+        ):
+            for k in range(DEPTH):
+                face_ref[f, ny * k : ny * k + ny] = flow_ref[f, ny * (begin + k) : ny * (begin + k) + ny]
             halos = [mid_ref[f, rows * i + ny : rows * i + rows] for i in (near, next_one)]
-            faces.append([flow_ref[f, ny * i : ny * i + ny] for i in range(begin, begin + DEPTH)] + [corner_rows(*halos, sub)])
-        for k, (first, last) in enumerate(zip(*faces)):
-            part = slice(ny * k, ny * k + first.shape[0])
-            face_even_ref[f, part] = jnp.where(odd_x, first, last)
-            face_odd_ref[f, part] = jnp.where(odd_x, last, first)
+            face_ref[f, ny * DEPTH : ny * DEPTH + HALO] = corner_rows(*halos, sub)
 
 
 def corner_rows(near, next_one, sub):
@@ -166,17 +165,14 @@
 GROUP = 8
 
 
-def pack_kernel(flags_ref, mid_ref, even_ref, odd_ref, packed_ref, xlo_ref, xhi_ref):
+def pack_kernel(mid_ref, low_ref, high_ref, packed_ref, xlo_ref, xhi_ref):
     fields, nx, rows, nz = mid_ref.shape
     ny = rows - HALO
-    odd = flag(flags_ref, ODD_X)
     lane = lax.broadcasted_iota(jnp.int32, (rows, nz), 1)
     sub = lax.broadcasted_iota(jnp.int32, (HALO, nz), 0)
     for f in range(fields):
-        for one_ref, other_ref, out_ref, order in (
-            (even_ref, odd_ref, xlo_ref, (2, 1, 0)), (odd_ref, even_ref, xhi_ref, (0, 1, 2))
-        ):
-            face = jnp.where(odd, one_ref[f], other_ref[f])
+        for face_ref, out_ref, order in ((low_ref, xlo_ref, (2, 1, 0)), (high_ref, xhi_ref, (0, 1, 2))):
+            face = face_ref[f]
             halo = corner_planes(face[ny * DEPTH :], sub)
             for k in range(DEPTH):
                 out_ref[f, k, 0:ny] = face[ny * k : ny * k + ny]
@@ -407,25 +403,29 @@
     blocks = tall // 8
     sub = lax.broadcasted_iota(jnp.int32, (8, 128), 0)
     panel = [work_ref[base + 8 * b : base + 8 * b + 8, :] for b in range(blocks)]
-    column = [
-        [jnp.broadcast_to(panel[b][:, base + k : base + k + 1], (8, 128)) for b in range(blocks)] for k in range(tall)
-    ]
     scale = [jnp.zeros((8, 128), jnp.float32) for _ in range(blocks)]
-    for j in range(tall):
-        mine, at = divmod(j, 8)
-        pivot = column[j][mine][at : at + 1, :]
-        inverse = 1.0 / pivot
-        scaled = {b: column[j][b] * inverse for b in range(mine, blocks)}
-        for k in range(j + 1, tall):
-            other, place = divmod(k, 8)
-            times = scaled[other][place : place + 1, :]
-            for b in range(other, blocks):
-                column[k][b] = column[k][b] - column[j][b] * times
-        scale[mine] = jnp.where(sub == at, lax.rsqrt(pivot), scale[mine])
-        pivot_row = panel[mine][at : at + 1, :] * jnp.concatenate([inverse, inverse], axis=1)
-        for b in range(mine, blocks):
-            times = jnp.where(sub > at, column[j][b], 0.0) if b == mine else column[j][b]
-            panel[b] = panel[b] - jnp.concatenate([times, times], axis=1) * pivot_row
+    half = tall // 2
+    for low in (0, half):
+        high = low + half
+        column = {
+            k: {b: jnp.broadcast_to(panel[b][:, base + k : base + k + 1], (8, 128)) for b in range(k // 8, blocks)}
+            for k in range(low, high)
+        }
+        for j in range(low, high):
+            mine, at = divmod(j, 8)
+            pivot = column[j][mine][at : at + 1, :]
+            inverse = 1.0 / pivot
+            scaled = {b: column[j][b] * inverse for b in range(mine, blocks)}
+            for k in range(j + 1, high):
+                other, place = divmod(k, 8)
+                times = scaled[other][place : place + 1, :]
+                for b in range(other, blocks):
+                    column[k][b] = column[k][b] - column[j][b] * times
+            scale[mine] = jnp.where(sub == at, lax.rsqrt(pivot), scale[mine])
+            pivot_row = panel[mine][at : at + 1, :]
+            for b in range(mine, blocks):
+                times = jnp.where(sub > at, scaled[b], 0.0) if b == mine else scaled[b]
+                panel[b] = panel[b] - jnp.concatenate([times, times], axis=1) * pivot_row
     for b in range(blocks):
         work_ref[base + 8 * b : base + 8 * b + 8, :] = panel[b] * jnp.concatenate([scale[b], scale[b]], axis=1)
 
@@ -446,7 +446,7 @@
     per = -(-3 * quarter // devices)
 
     place = lax.axis_index("gy")
-    flags = [place == 0, place == lax.axis_size("gy") - 1, place % 2 == 1, lax.axis_index("gx") % 2 == 1]
+    flags = [place == 0, place == lax.axis_size("gy") - 1, place % 2 == 1]
     flags = jnp.broadcast_to(jnp.stack(flags).astype(jnp.int32)[:, None], (len(flags), nz))
     strip = shape((fields, nx * DEPTH, nz))
     strips = call(
@@ -464,23 +464,23 @@
 
     rows = ny + HALO
     face = shape((fields, DEPTH * ny + HALO, nz))
-    mid, *faces = call(
+    mid, first, last = call(
         functools.partial(walls_kernel, nx),
         out_shape=(shape((fields, nx * rows, nz)), face, face),
         in_specs=[VMEM] * 4,
         out_specs=(VMEM,) * 3,
     )(flags, flat, y_even, y_odd)
     mid = mid.reshape(fields, nx, rows, nz)
-    x_even, x_odd = pairs(*faces, "gx")
+    low_face, high_face = neighbours(first, last, "gx")
     parts = lax.all_to_all(gram, ALL, 0, 0)
 
     beside = shape((fields, DEPTH, rows, nz))
     packed, xlo, xhi = call(
         pack_kernel,
         out_shape=(shape((fields, rows, nz)), beside, beside),
-        in_specs=[VMEM] * 4,
+        in_specs=[VMEM] * 3,
         out_specs=(VMEM,) * 3,
-    )(flags, mid, x_even, x_odd)
+    )(mid, low_face, high_face)
     if lax.axis_size("gz") == 2:
         low = high = lax.ppermute(packed, "gz", [(0, 1), (1, 0)])
     else:

time: 37.6 us -> 37.7 us (level)
    ppermute x0 -> x2, starting transfers between devices: none -> 3.88 us  [the longest x1 2.23 us: neighbours(): lax.ppermute(block_low, axis, backward)]
    ppermute x2 -> x1, starting transfers between devices: 3.97 us -> 1.49 us  [pairs(): lax.ppermute(block_odd, axis, odd)]
    ppermute x2 -> x1, waiting for transfers between devices: 3.07 us -> 1.26 us  [pairs(): lax.ppermute(block_odd, axis, odd)]
    ppermute x2 -> x1, starting transfers between devices: 4.65 us -> 3 us  [pairs(): lax.ppermute(block_even, axis, even)]
    all_to_all x1, waiting for transfers between devices: 2.15 us -> 3.22 us  [local(): parts = lax.all_to_all(gram, ALL, 0, 0)]
    ppermute x0 -> x2, waiting for transfers between devices: none -> 0.76 us  [the longest x1 0.38 us: neighbours(): lax.ppermute(block_high, axis, forward)]
    all_to_all x1, starting transfers between devices: 2.67 us -> 3.12 us  [local(): parts = lax.all_to_all(gram, ALL, 0, 0)]
  transfers between devices with their start and end apart: 6 -> 6, of which waited for: 4 -> 5; matrix products, arithmetic and copies ran while one was open for 0% -> 0% of each run, Pallas kernels for 10% -> 10%
where the time goes in v11:
time: 37.7 us; the launch traced here: 37.4 us
  starting transfers between devices  11.6 us (31%)
  blocking collectives  9.12 us (24%)
  Pallas kernels  7.99 us (21%)
  waiting for transfers between devices  5.58 us (15%)
  local copies, waits for them, and re-layouts  2.37 us (6%)
  between operations  0.71 us (2%)
    all_to_all x1, blocking collectives, local(): got = lax.all_to_all(send, ALL, 0, 0)  9.12 us
    pallas_call x1, Pallas kernels, local(): call(functools.partial(final_kernel, count), out_shape=(shape((comps, siz...  3.98 us
    all_to_all x1, waiting for transfers between devices, local(): parts = lax.all_to_all(gram, ALL, 0, 0)  3.22 us
    all_to_all x1, starting transfers between devices, local(): parts = lax.all_to_all(gram, ALL, 0, 0)  3.12 us
    ppermute x1, starting transfers between devices, pairs(): lax.ppermute(block_even, axis, even)  3 us
    unnamed x10, local copies, waits for them, and re-layouts  2.3 us
    ppermute x1, starting transfers between devices, neighbours(): lax.ppermute(block_low, axis, backward)  2.23 us
    pallas_call x1, Pallas kernels, local(): call(step_kernel, out_shape=(shape(flow.shape), shape((comps, 1, points))...  1.86 us
  transfers between devices with their start and end apart: 6, of which 5 were waited for; matrix products, arithmetic and copies ran while one was open for 0% of the time, Pallas kernels for 10%

profile of v11, /device:TPU:0, one launch (start us, length us, event | category | flops | bytes accessed | tf_op | source)
XLA Modules:
  0.0 37.4 jit_solution(9665074847775446892)
XLA Ops:
  0.6 0.1 add_convert_fusion
  0.7 0.1 broadcast_in_dim.2.flags_ref
  0.8 0.9 %copy-done.2 = f32[4,8,16,128]{3,2,1,0:T(8,128)S(1)} copy-done((f32[4,8,16,128]{3,2,1,0:T(8,128)S(1)}, f32[4,8,16,128]{3,2,1,0:T(8,128)}, u32[]{:S(2)}) %copy-start.2) | copy-done | bytes 262168
  1.8 3.0 %collective-permute-start = (f32[4,24,128]{2,1,0:T(8,128)S(1)}, f32[4,24,128]{2,1,0:T(8,128)S(1)}, u32[]{:S(2)}, u32[]{:S(2)}) collective-permute-start(f32[4,24,128]{2,1,0:T(8,128)S(1)} %get-tuple-element.24), channel_id=1, source_target_pairs={{0,2},{2,0},{4,6},{6,4},{1,3},{3,1},{5,7},{7,5},{8,10},{10,8},{12,... | collective-permute-start | bytes 147464 | tf_op jit(solution)/shard_map/ppermute | solution.py:57
  4.8 1.5 %collective-permute-start.1 = (f32[4,24,128]{2,1,0:T(8,128)S(1)}, f32[4,24,128]{2,1,0:T(8,128)S(1)}, u32[]{:S(2)}, u32[]{:S(2)}) collective-permute-start(f32[4,24,128]{2,1,0:T(8,128)S(1)} %get-tuple-element.25), channel_id=1, source_target_pairs={{0,6},{2,4},{4,2},{6,0},{1,7},{3,5},{5,3},{7,1},{8,14},{10,12},{12... | collective-permute-start | bytes 147464 | tf_op jit(solution)/shard_map/ppermute | solution.py:57
  6.3 1.0 %copy-done = f32[127,3,256]{2,0,1:T(8,128)S(1)} copy-done((f32[127,3,256]{2,0,1:T(8,128)S(1)}, f32[127,3,256]{2,0,1:T(8,128)}, u32[]{:S(2)}) %copy-start) | copy-done | bytes 390168
  7.3 1.2 %shard_map.59 = (f32[32,3,128]{2,1,0:T(4,128)}, bf16[3,3,128,256]{3,2,1,0:T(8,128)(2,1)S(1)}) custom-call(f32[3,127,256]{2,1,0:T(8,128)S(1)} %bitcast.11), custom_call_target="tpu_custom_call" | custom-call | tf_op jit(solution)/shard_map/pallas_call | solution.py:456
  8.5 1.3 %collective-permute-done.1.odd_ref = f32[4,24,128]{2,1,0:T(8,128)S(1)} collective-permute-done((f32[4,24,128]{2,1,0:T(8,128)S(1)}, f32[4,24,128]{2,1,0:T(8,128)S(1)}, u32[]{:S(2)}, u32[]{:S(2)}) %collective-permute-start.1) | collective-permute-done | bytes 49184 | tf_op jit(solution)/shard_map/ppermute | solution.py:57
  9.8 0.1 shard_map.60
  9.8 1.6 %collective-permute-start.2 = (f32[4,56,128]{2,1,0:T(8,128)S(1)}, f32[4,56,128]{2,1,0:T(8,128)S(1)}, u32[]{:S(2)}, u32[]{:S(2)}) collective-permute-start(f32[4,56,128]{2,1,0:T(8,128)S(1)} %get-tuple-element.31), channel_id=1, source_target_pairs={{0,8},{8,16},{16,24},{24,0},{1,9},{9,17},{17,25},{25,1},{2,10},{10... | collective-permute-start | bytes 344072 | tf_op jit(solution)/shard_map/ppermute | solution.py:50
  11.5 2.2 %collective-permute-start.3 = (f32[4,56,128]{2,1,0:T(8,128)S(1)}, f32[4,56,128]{2,1,0:T(8,128)S(1)}, u32[]{:S(2)}, u32[]{:S(2)}) collective-permute-start(f32[4,56,128]{2,1,0:T(8,128)S(1)} %get-tuple-element.32), channel_id=1, source_target_pairs={{8,0},{16,8},{24,16},{0,24},{9,1},{17,9},{25,17},{1,25},{10,2},{18... | collective-permute-start | bytes 344072 | tf_op jit(solution)/shard_map/ppermute | solution.py:50
  13.7 3.1 %all-to-all-start = ((f32[32,3,128]{2,1,0:T(4,128)}), f32[32,3,128]{2,1,0:T(4,128)S(1)}, u32[]{:S(2)}, u32[]{:S(2)}) async-start(f32[32,3,128]{2,1,0:T(4,128)} %get-tuple-element.27), calls=%async_computation | async-start | bytes 131072 | tf_op jit(solution)/shard_map/all_to_all | solution.py:475
  16.9 0.4 %collective-permute-done.2.low_ref = f32[4,56,128]{2,1,0:T(8,128)S(1)} collective-permute-done((f32[4,56,128]{2,1,0:T(8,128)S(1)}, f32[4,56,128]{2,1,0:T(8,128)S(1)}, u32[]{:S(2)}, u32[]{:S(2)}) %collective-permute-start.2) | collective-permute-done | bytes 114720 | tf_op jit(solution)/shard_map/ppermute | solution.py:50
  17.2 0.4 %collective-permute-done.3.high_ref = f32[4,56,128]{2,1,0:T(8,128)S(1)} collective-permute-done((f32[4,56,128]{2,1,0:T(8,128)S(1)}, f32[4,56,128]{2,1,0:T(8,128)S(1)}, u32[]{:S(2)}, u32[]{:S(2)}) %collective-permute-start.3) | collective-permute-done | bytes 114720 | tf_op jit(solution)/shard_map/ppermute | solution.py:50
  17.6 0.2 shard_map.61
  17.9 0.0 copy-start.1
  17.9 0.1 collective-permute-start.4
  18.0 0.3 copy-done.4
  18.3 0.5 %shard_map.62 = (f32[4,12,24,128]{3,2,1,0:T(8,128)S(1)}, s32[1,256]{1,0:T(1,128)S(1)}) custom-call(s32[3,128]{1,0:T(4,128)S(1)} %broadcast_in_dim.2.flags_ref, s32[1,256]{1,0:T(1,128)S(1)} %bitcast.15, f32[4,8,24,128]{3,2,1,0:T(8,128)S(1)} %bitcast.9, f32[4,3,24,128]{3,2,1,0:T(8,128)S(1)} %get-tuple-element.33.xlo_ref, ...), custom_call_target="tpu_custom_call" | custom-call | tf_op jit(solution)/shard_map/pallas_call | solution.py:488
  18.8 0.3 collective-permute-done.4.low_ref.high_ref
  19.2 1.9 %shard_map.63 = (f32[4,8,16,128]{3,2,1,0:T(8,128)S(1)}, f32[3,1,256]{2,1,0:T(1,128)S(1)}, f32[1,128]{1,0:T(1,128)S(1)}) custom-call(s32[3,128]{1,0:T(4,128)S(1)} %broadcast_in_dim.2.flags_ref, f32[4,8,24,128]{3,2,1,0:T(8,128)S(1)} %bitcast.10, f32[4,3,24,128]{3,2,1,0:T(8,128)S(1)} %get-tuple-element.33.xlo_ref, ...), custom_call_target="tpu_custom_call" | custom-call | tf_op jit(solution)/shard_map/pallas_call | solution.py:498
  21.0 3.2 %all-to-all-done.parts_ref = f32[32,3,128]{2,1,0:T(4,128)S(1)} async-done(((f32[32,3,128]{2,1,0:T(4,128)}), f32[32,3,128]{2,1,0:T(4,128)S(1)}, u32[]{:S(2)}, u32[]{:S(2)}) %all-to-all-start) | async-done | bytes 49184 | tf_op jit(solution)/shard_map/all_to_all | solution.py:475
  24.3 9.1 %all_to_all.10.got_ref = f32[32,4,128]{2,1,0:T(4,128)S(1)} all-to-all(f32[32,4,128]{2,1,0:T(4,128)S(1)} %shard_map.64), channel_id=1, replica_groups=mesh['gx'=4,'gy'=4,'gz'=2] {'gx','gy','gz'}, dimensions={0} | all-to-all | bytes 131072 | tf_op jit(solution)/shard_map/all_to_all | solution.py:512
  33.4 4.0 %shard_map.65 = (f32[3,128,256]{2,1,0:T(8,128)}, f32[128,128]{1,0:T(8,128)}, f32[4,8,16,128]{3,2,1,0:T(8,128)}) custom-call(f32[32,4,128]{2,1,0:T(4,128)S(1)} %all_to_all.10.got_ref, bf16[3,3,128,256]{3,2,1,0:T(8,128)(2,1)S(1)} %get-tuple-element.39.parts_ref, f32[3,1,256]{2,1,0:T(1,128)S(1)} %get-tuple-element.40.snap_ref, ...), custom_call_target="tpu_custom_call" | custom-call | tf_op jit(solution)/shard_map/pallas_call | solution.py:513
  (9 shorter events, 0.1 us)
Async XLA Ops:
  0.8 1.0 %copy-start.2 = (f32[4,8,16,128]{3,2,1,0:T(8,128)S(1)}, f32[4,8,16,128]{3,2,1,0:T(8,128)}, u32[]{:S(2)}) copy-start(f32[4,8,16,128]{3,2,1,0:T(8,128)} %param.3) | copy-start | bytes 786436
  1.7 8.0 %copy-start.3 = (f32[4,8,16,128]{3,2,1,0:T(8,128)S(1)}, f32[4,8,16,128]{3,2,1,0:T(8,128)}, u32[]{:S(2)}) copy-start(f32[4,8,16,128]{3,2,1,0:T(8,128)} %param.3) | copy-start | bytes 786436
  1.8 6.7 %collective-permute-start = (f32[4,24,128]{2,1,0:T(8,128)S(1)}, f32[4,24,128]{2,1,0:T(8,128)S(1)}, u32[]{:S(2)}, u32[]{:S(2)}) collective-permute-start(f32[4,24,128]{2,1,0:T(8,128)S(1)} %get-tuple-element.24), channel_id=1, source_target_pairs={{0,2},{2,0},{4,6},{6,4},{1,3},{3,1},{5,7},{7,5},{8,10},{10,8},{12,... | collective-permute-start | bytes 147464 | tf_op jit(solution)/shard_map/ppermute | solution.py:57
  4.8 5.0 %collective-permute-start.1 = (f32[4,24,128]{2,1,0:T(8,128)S(1)}, f32[4,24,128]{2,1,0:T(8,128)S(1)}, u32[]{:S(2)}, u32[]{:S(2)}) collective-permute-start(f32[4,24,128]{2,1,0:T(8,128)S(1)} %get-tuple-element.25), channel_id=1, source_target_pairs={{0,6},{2,4},{4,2},{6,0},{1,7},{3,5},{5,3},{7,1},{8,14},{10,12},{12... | collective-permute-start | bytes 147464 | tf_op jit(solution)/shard_map/ppermute | solution.py:57
  6.3 1.0 %copy-start = (f32[127,3,256]{2,0,1:T(8,128)S(1)}, f32[127,3,256]{2,0,1:T(8,128)}, u32[]{:S(2)}) copy-start(f32[127,3,256]{2,0,1:T(8,128)} %param.4) | copy-start | bytes 1170436
  9.8 7.4 %collective-permute-start.2 = (f32[4,56,128]{2,1,0:T(8,128)S(1)}, f32[4,56,128]{2,1,0:T(8,128)S(1)}, u32[]{:S(2)}, u32[]{:S(2)}) collective-permute-start(f32[4,56,128]{2,1,0:T(8,128)S(1)} %get-tuple-element.31), channel_id=1, source_target_pairs={{0,8},{8,16},{16,24},{24,0},{1,9},{9,17},{17,25},{25,1},{2,10},{10... | collective-permute-start | bytes 344072 | tf_op jit(solution)/shard_map/ppermute | solution.py:50
  11.5 6.1 %collective-permute-start.3 = (f32[4,56,128]{2,1,0:T(8,128)S(1)}, f32[4,56,128]{2,1,0:T(8,128)S(1)}, u32[]{:S(2)}, u32[]{:S(2)}) collective-permute-start(f32[4,56,128]{2,1,0:T(8,128)S(1)} %get-tuple-element.32), channel_id=1, source_target_pairs={{8,0},{16,8},{24,16},{0,24},{9,1},{17,9},{25,17},{1,25},{10,2},{18... | collective-permute-start | bytes 344072 | tf_op jit(solution)/shard_map/ppermute | solution.py:50
  13.7 10.5 %all-to-all-start = ((f32[32,3,128]{2,1,0:T(4,128)}), f32[32,3,128]{2,1,0:T(4,128)S(1)}, u32[]{:S(2)}, u32[]{:S(2)}) async-start(f32[32,3,128]{2,1,0:T(4,128)} %get-tuple-element.27), calls=%async_computation | async-start | bytes 131072 | tf_op jit(solution)/shard_map/all_to_all | solution.py:475
  17.6 0.7 %copy-start.4 = (s32[256]{0:T(256)S(1)}, s32[256]{0:T(256)}, u32[]{:S(2)}) copy-start(s32[256]{0:T(256)} %param.5) | copy-start | bytes 3076
  17.9 1.3 %copy-start.1 = (f32[127,3,256]{2,0,1:T(8,128)S(1)}, f32[127,3,256]{2,0,1:T(8,128)}, u32[]{:S(2)}) copy-start(f32[127,3,256]{2,0,1:T(8,128)} %param.4) | copy-start | bytes 1170436
  17.9 1.3 %collective-permute-start.4 = (f32[4,24,128]{2,1,0:T(8,128)S(1)}, f32[4,24,128]{2,1,0:T(8,128)S(1)}, u32[]{:S(2)}, u32[]{:S(2)}) collective-permute-start(f32[4,24,128]{2,1,0:T(8,128)S(1)} %get-tuple-element.36.own_ref), channel_id=1, source_target_pairs={{0,1},{1,0},{2,3},{3,2},{4,5},{5,4},{6,7},{7,6},{8,9},{9,8},{10,11... | collective-permute-start | bytes 147464 | tf_op jit(solution)/shard_map/ppermute | solution.py:485

commit v12 on v11

--- a/solution.py
+++ b/solution.py
@@ -50,11 +50,12 @@
     return lax.ppermute(block_high, axis, forward), lax.ppermute(block_low, axis, backward)
 
 
-def pairs(block_even, block_odd, axis):
+def pairs(block_odd, block_even, axis):
     count = lax.axis_size(axis)
     even = [(i, i + 1 - 2 * (i % 2)) for i in range(count)]
     odd = [(i, (i - 1 + 2 * (i % 2)) % count) for i in range(count)]
-    return lax.ppermute(block_even, axis, even), lax.ppermute(block_odd, axis, odd)
+    from_odd = lax.ppermute(block_odd, axis, odd)
+    return lax.ppermute(block_even, axis, even), from_odd
 
 
 LOWER_WALL, UPPER_WALL, ODD_Y = range(3)
@@ -99,7 +100,7 @@
 HALO = 2 * DEPTH + GAP
 
 
-def strips_kernel(planes, flags_ref, flow_ref, even_ref, odd_ref):
+def strips_kernel(planes, flags_ref, flow_ref, odd_ref, even_ref):
     ny = flow_ref.shape[1] // planes
     odd = flag(flags_ref, ODD_Y)
     for f in range(flow_ref.shape[0]):
@@ -110,7 +111,7 @@
             odd_ref[f, planes * j : planes * j + planes] = jnp.where(odd, top, bottom)
 
 
-def walls_kernel(planes, flags_ref, flow_ref, even_ref, odd_ref, mid_ref, first_ref, last_ref):
+def walls_kernel(planes, flags_ref, flow_ref, odd_ref, even_ref, mid_ref, first_ref, last_ref):
     fields, cells, nz = flow_ref.shape
     odd_y = flag(flags_ref, ODD_Y)
     ny = cells // planes
@@ -460,7 +461,7 @@
         out_specs=(VMEM, VMEM),
         scratch_shapes=[pltpu.VMEM((size, size), jnp.float32), pltpu.VMEM((devices * per, size), jnp.float32)],
     )(bricks)
-    y_even, y_odd, gram = lax.optimization_barrier((y_even, y_odd, gram))
+    y_odd, y_even, gram = lax.optimization_barrier((y_odd, y_even, gram))
 
     rows = ny + HALO
     face = shape((fields, DEPTH * ny + HALO, nz))
@@ -469,7 +470,7 @@
         out_shape=(shape((fields, nx * rows, nz)), face, face),
         in_specs=[VMEM] * 4,
         out_specs=(VMEM,) * 3,
-    )(flags, flat, y_even, y_odd)
+    )(flags, flat, y_odd, y_even)
     mid = mid.reshape(fields, nx, rows, nz)
     low_face, high_face = neighbours(first, last, "gx")
     parts = lax.all_to_all(gram, ALL, 0, 0)

time: 37.7 us -> 37.2 us (0.987)
  starting transfers between devices: 11.6 us -> 11 us
    all_to_all x1, waiting for transfers between devices: 3.22 us -> 2.55 us  [local(): parts = lax.all_to_all(gram, ALL, 0, 0)]
    ppermute x1, waiting for transfers between devices: 0.38 us -> 1.03 us  [neighbours(): lax.ppermute(block_high, axis, forward)]
    all_to_all x1, starting transfers between devices: 3.12 us -> 2.57 us  [local(): parts = lax.all_to_all(gram, ALL, 0, 0)]
  transfers between devices with their start and end apart: 6 -> 6, of which waited for: 5 -> 5; matrix products, arithmetic and copies ran while one was open for 0% -> 0% of each run, Pallas kernels for 10% -> 11%
where the time goes in v12:
time: 37.2 us; the launch traced here: 36.9 us
  starting transfers between devices  11 us (30%)
  blocking collectives  9.12 us (25%)
  Pallas kernels  7.99 us (21%)
  waiting for transfers between devices  5.63 us (15%)
  local copies, waits for them, and re-layouts  2.37 us (6%)
  between operations  0.71 us (2%)
    all_to_all x1, blocking collectives, local(): got = lax.all_to_all(send, ALL, 0, 0)  9.12 us
    pallas_call x1, Pallas kernels, local(): call(functools.partial(final_kernel, count), out_shape=(shape((comps, siz...  3.98 us
    ppermute x1, starting transfers between devices, pairs(): from_odd = lax.ppermute(block_odd, axis, odd)  3.96 us
    all_to_all x1, starting transfers between devices, local(): parts = lax.all_to_all(gram, ALL, 0, 0)  2.57 us
    all_to_all x1, waiting for transfers between devices, local(): parts = lax.all_to_all(gram, ALL, 0, 0)  2.55 us
    unnamed x10, local copies, waits for them, and re-layouts  2.3 us
    ppermute x1, starting transfers between devices, neighbours(): lax.ppermute(block_low, axis, backward)  2.25 us
    pallas_call x1, Pallas kernels, local(): call(step_kernel, out_shape=(shape(flow.shape), shape((comps, 1, points))...  1.87 us
  transfers between devices with their start and end apart: 6, of which 5 were waited for; matrix products, arithmetic and copies ran while one was open for 0% of the time, Pallas kernels for 11%

profile of v12, /device:TPU:0, one launch (start us, length us, event | category | flops | bytes accessed | tf_op | source)
XLA Modules:
  0.0 36.9 jit_solution(14373722518684993824)
XLA Ops:
  0.6 0.1 add_convert_fusion
  0.7 0.1 broadcast_in_dim.2.flags_ref
  0.8 0.9 %copy-done.2 = f32[4,8,16,128]{3,2,1,0:T(8,128)S(1)} copy-done((f32[4,8,16,128]{3,2,1,0:T(8,128)S(1)}, f32[4,8,16,128]{3,2,1,0:T(8,128)}, u32[]{:S(2)}) %copy-start.2) | copy-done | bytes 262168
  1.8 4.0 %collective-permute-start = (f32[4,24,128]{2,1,0:T(8,128)S(1)}, f32[4,24,128]{2,1,0:T(8,128)S(1)}, u32[]{:S(2)}, u32[]{:S(2)}) collective-permute-start(f32[4,24,128]{2,1,0:T(8,128)S(1)} %get-tuple-element.24), channel_id=1, source_target_pairs={{0,6},{2,4},{4,2},{6,0},{1,7},{3,5},{5,3},{7,1},{8,14},{10,12},{12... | collective-permute-start | bytes 147464 | tf_op jit(solution)/shard_map/ppermute | solution.py:57
  5.7 0.5 %collective-permute-start.1 = (f32[4,24,128]{2,1,0:T(8,128)S(1)}, f32[4,24,128]{2,1,0:T(8,128)S(1)}, u32[]{:S(2)}, u32[]{:S(2)}) collective-permute-start(f32[4,24,128]{2,1,0:T(8,128)S(1)} %get-tuple-element.25), channel_id=1, source_target_pairs={{0,2},{2,0},{4,6},{6,4},{1,3},{3,1},{5,7},{7,5},{8,10},{10,8},{12,... | collective-permute-start | bytes 147464 | tf_op jit(solution)/shard_map/ppermute | solution.py:58
  6.3 1.0 %copy-done = f32[127,3,256]{2,0,1:T(8,128)S(1)} copy-done((f32[127,3,256]{2,0,1:T(8,128)S(1)}, f32[127,3,256]{2,0,1:T(8,128)}, u32[]{:S(2)}) %copy-start) | copy-done | bytes 390168
  7.3 1.2 %shard_map.59 = (f32[32,3,128]{2,1,0:T(4,128)}, bf16[3,3,128,256]{3,2,1,0:T(8,128)(2,1)S(1)}) custom-call(f32[3,127,256]{2,1,0:T(8,128)S(1)} %bitcast.11), custom_call_target="tpu_custom_call" | custom-call | tf_op jit(solution)/shard_map/pallas_call | solution.py:457
  8.5 1.3 %collective-permute-done.1.even_ref = f32[4,24,128]{2,1,0:T(8,128)S(1)} collective-permute-done((f32[4,24,128]{2,1,0:T(8,128)S(1)}, f32[4,24,128]{2,1,0:T(8,128)S(1)}, u32[]{:S(2)}, u32[]{:S(2)}) %collective-permute-start.1) | collective-permute-done | bytes 49184 | tf_op jit(solution)/shard_map/ppermute | solution.py:58
  9.8 0.1 shard_map.60
  9.9 1.6 %collective-permute-start.2 = (f32[4,56,128]{2,1,0:T(8,128)S(1)}, f32[4,56,128]{2,1,0:T(8,128)S(1)}, u32[]{:S(2)}, u32[]{:S(2)}) collective-permute-start(f32[4,56,128]{2,1,0:T(8,128)S(1)} %get-tuple-element.31), channel_id=1, source_target_pairs={{0,8},{8,16},{16,24},{24,0},{1,9},{9,17},{17,25},{25,1},{2,10},{10... | collective-permute-start | bytes 344072 | tf_op jit(solution)/shard_map/ppermute | solution.py:50
  11.5 2.2 %collective-permute-start.3 = (f32[4,56,128]{2,1,0:T(8,128)S(1)}, f32[4,56,128]{2,1,0:T(8,128)S(1)}, u32[]{:S(2)}, u32[]{:S(2)}) collective-permute-start(f32[4,56,128]{2,1,0:T(8,128)S(1)} %get-tuple-element.32), channel_id=1, source_target_pairs={{8,0},{16,8},{24,16},{0,24},{9,1},{17,9},{25,17},{1,25},{10,2},{18... | collective-permute-start | bytes 344072 | tf_op jit(solution)/shard_map/ppermute | solution.py:50
  13.8 2.6 %all-to-all-start = ((f32[32,3,128]{2,1,0:T(4,128)}), f32[32,3,128]{2,1,0:T(4,128)S(1)}, u32[]{:S(2)}, u32[]{:S(2)}) async-start(f32[32,3,128]{2,1,0:T(4,128)} %get-tuple-element.27), calls=%async_computation | async-start | bytes 131072 | tf_op jit(solution)/shard_map/all_to_all | solution.py:476
  16.4 1.0 %collective-permute-done.2.low_ref = f32[4,56,128]{2,1,0:T(8,128)S(1)} collective-permute-done((f32[4,56,128]{2,1,0:T(8,128)S(1)}, f32[4,56,128]{2,1,0:T(8,128)S(1)}, u32[]{:S(2)}, u32[]{:S(2)}) %collective-permute-start.2) | collective-permute-done | bytes 114720 | tf_op jit(solution)/shard_map/ppermute | solution.py:50
  17.4 0.4 %collective-permute-done.3.high_ref = f32[4,56,128]{2,1,0:T(8,128)S(1)} collective-permute-done((f32[4,56,128]{2,1,0:T(8,128)S(1)}, f32[4,56,128]{2,1,0:T(8,128)S(1)}, u32[]{:S(2)}, u32[]{:S(2)}) %collective-permute-start.3) | collective-permute-done | bytes 114720 | tf_op jit(solution)/shard_map/ppermute | solution.py:50
  17.8 0.2 shard_map.61
  18.0 0.0 copy-start.1
  18.0 0.1 collective-permute-start.4
  18.1 0.3 copy-done.4
  18.5 0.5 %shard_map.62 = (f32[4,12,24,128]{3,2,1,0:T(8,128)S(1)}, s32[1,256]{1,0:T(1,128)S(1)}) custom-call(s32[3,128]{1,0:T(4,128)S(1)} %broadcast_in_dim.2.flags_ref, s32[1,256]{1,0:T(1,128)S(1)} %bitcast.15, f32[4,8,24,128]{3,2,1,0:T(8,128)S(1)} %bitcast.9, f32[4,3,24,128]{3,2,1,0:T(8,128)S(1)} %get-tuple-element.33.xlo_ref, ...), custom_call_target="tpu_custom_call" | custom-call | tf_op jit(solution)/shard_map/pallas_call | solution.py:489
  19.0 0.3 collective-permute-done.4.low_ref.high_ref
  19.3 1.9 %shard_map.63 = (f32[4,8,16,128]{3,2,1,0:T(8,128)S(1)}, f32[3,1,256]{2,1,0:T(1,128)S(1)}, f32[1,128]{1,0:T(1,128)S(1)}) custom-call(s32[3,128]{1,0:T(4,128)S(1)} %broadcast_in_dim.2.flags_ref, f32[4,8,24,128]{3,2,1,0:T(8,128)S(1)} %bitcast.10, f32[4,3,24,128]{3,2,1,0:T(8,128)S(1)} %get-tuple-element.33.xlo_ref, ...), custom_call_target="tpu_custom_call" | custom-call | tf_op jit(solution)/shard_map/pallas_call | solution.py:499
  21.2 2.6 %all-to-all-done.parts_ref = f32[32,3,128]{2,1,0:T(4,128)S(1)} async-done(((f32[32,3,128]{2,1,0:T(4,128)}), f32[32,3,128]{2,1,0:T(4,128)S(1)}, u32[]{:S(2)}, u32[]{:S(2)}) %all-to-all-start) | async-done | bytes 49184 | tf_op jit(solution)/shard_map/all_to_all | solution.py:476
  23.8 9.1 %all_to_all.10.got_ref = f32[32,4,128]{2,1,0:T(4,128)S(1)} all-to-all(f32[32,4,128]{2,1,0:T(4,128)S(1)} %shard_map.64), channel_id=1, replica_groups=mesh['gx'=4,'gy'=4,'gz'=2] {'gx','gy','gz'}, dimensions={0} | all-to-all | bytes 131072 | tf_op jit(solution)/shard_map/all_to_all | solution.py:513
  32.9 4.0 %shard_map.65 = (f32[3,128,256]{2,1,0:T(8,128)}, f32[128,128]{1,0:T(8,128)}, f32[4,8,16,128]{3,2,1,0:T(8,128)}) custom-call(f32[32,4,128]{2,1,0:T(4,128)S(1)} %all_to_all.10.got_ref, bf16[3,3,128,256]{3,2,1,0:T(8,128)(2,1)S(1)} %get-tuple-element.39.parts_ref, f32[3,1,256]{2,1,0:T(1,128)S(1)} %get-tuple-element.40.snap_ref, ...), custom_call_target="tpu_custom_call" | custom-call | tf_op jit(solution)/shard_map/pallas_call | solution.py:514
  (9 shorter events, 0.1 us)
Async XLA Ops:
  0.8 1.0 %copy-start.2 = (f32[4,8,16,128]{3,2,1,0:T(8,128)S(1)}, f32[4,8,16,128]{3,2,1,0:T(8,128)}, u32[]{:S(2)}) copy-start(f32[4,8,16,128]{3,2,1,0:T(8,128)} %param.3) | copy-start | bytes 786436
  1.7 8.1 %copy-start.3 = (f32[4,8,16,128]{3,2,1,0:T(8,128)S(1)}, f32[4,8,16,128]{3,2,1,0:T(8,128)}, u32[]{:S(2)}) copy-start(f32[4,8,16,128]{3,2,1,0:T(8,128)} %param.3) | copy-start | bytes 786436
  1.8 6.7 %collective-permute-start = (f32[4,24,128]{2,1,0:T(8,128)S(1)}, f32[4,24,128]{2,1,0:T(8,128)S(1)}, u32[]{:S(2)}, u32[]{:S(2)}) collective-permute-start(f32[4,24,128]{2,1,0:T(8,128)S(1)} %get-tuple-element.24), channel_id=1, source_target_pairs={{0,6},{2,4},{4,2},{6,0},{1,7},{3,5},{5,3},{7,1},{8,14},{10,12},{12... | collective-permute-start | bytes 147464 | tf_op jit(solution)/shard_map/ppermute | solution.py:57
  5.7 4.1 %collective-permute-start.1 = (f32[4,24,128]{2,1,0:T(8,128)S(1)}, f32[4,24,128]{2,1,0:T(8,128)S(1)}, u32[]{:S(2)}, u32[]{:S(2)}) collective-permute-start(f32[4,24,128]{2,1,0:T(8,128)S(1)} %get-tuple-element.25), channel_id=1, source_target_pairs={{0,2},{2,0},{4,6},{6,4},{1,3},{3,1},{5,7},{7,5},{8,10},{10,8},{12,... | collective-permute-start | bytes 147464 | tf_op jit(solution)/shard_map/ppermute | solution.py:58
  6.3 1.0 %copy-start = (f32[127,3,256]{2,0,1:T(8,128)S(1)}, f32[127,3,256]{2,0,1:T(8,128)}, u32[]{:S(2)}) copy-start(f32[127,3,256]{2,0,1:T(8,128)} %param.4) | copy-start | bytes 1170436
  9.9 7.5 %collective-permute-start.2 = (f32[4,56,128]{2,1,0:T(8,128)S(1)}, f32[4,56,128]{2,1,0:T(8,128)S(1)}, u32[]{:S(2)}, u32[]{:S(2)}) collective-permute-start(f32[4,56,128]{2,1,0:T(8,128)S(1)} %get-tuple-element.31), channel_id=1, source_target_pairs={{0,8},{8,16},{16,24},{24,0},{1,9},{9,17},{17,25},{25,1},{2,10},{10... | collective-permute-start | bytes 344072 | tf_op jit(solution)/shard_map/ppermute | solution.py:50
  11.5 6.2 %collective-permute-start.3 = (f32[4,56,128]{2,1,0:T(8,128)S(1)}, f32[4,56,128]{2,1,0:T(8,128)S(1)}, u32[]{:S(2)}, u32[]{:S(2)}) collective-permute-start(f32[4,56,128]{2,1,0:T(8,128)S(1)} %get-tuple-element.32), channel_id=1, source_target_pairs={{8,0},{16,8},{24,16},{0,24},{9,1},{17,9},{25,17},{1,25},{10,2},{18... | collective-permute-start | bytes 344072 | tf_op jit(solution)/shard_map/ppermute | solution.py:50
  13.8 10.0 %all-to-all-start = ((f32[32,3,128]{2,1,0:T(4,128)}), f32[32,3,128]{2,1,0:T(4,128)S(1)}, u32[]{:S(2)}, u32[]{:S(2)}) async-start(f32[32,3,128]{2,1,0:T(4,128)} %get-tuple-element.27), calls=%async_computation | async-start | bytes 131072 | tf_op jit(solution)/shard_map/all_to_all | solution.py:476
  17.8 0.7 %copy-start.4 = (s32[256]{0:T(256)S(1)}, s32[256]{0:T(256)}, u32[]{:S(2)}) copy-start(s32[256]{0:T(256)} %param.5) | copy-start | bytes 3076
  18.0 1.3 %copy-start.1 = (f32[127,3,256]{2,0,1:T(8,128)S(1)}, f32[127,3,256]{2,0,1:T(8,128)}, u32[]{:S(2)}) copy-start(f32[127,3,256]{2,0,1:T(8,128)} %param.4) | copy-start | bytes 1170436
  18.0 1.3 %collective-permute-start.4 = (f32[4,24,128]{2,1,0:T(8,128)S(1)}, f32[4,24,128]{2,1,0:T(8,128)S(1)}, u32[]{:S(2)}, u32[]{:S(2)}) collective-permute-start(f32[4,24,128]{2,1,0:T(8,128)S(1)} %get-tuple-element.36.own_ref), channel_id=1, source_target_pairs={{0,1},{1,0},{2,3},{3,2},{4,5},{5,4},{6,7},{7,6},{8,9},{9,8},{10,11... | collective-permute-start | bytes 147464 | tf_op jit(solution)/shard_map/ppermute | solution.py:486

commit v13 on v12

--- a/solution.py
+++ b/solution.py
@@ -12,7 +12,7 @@
 SOUND_SQ = 1.0
 DRIVING = 0.5
 
-ALL = ("gx", "gy", "gz")
+ALL = ("gz", "gy", "gx")
 DEPTH = 3
 EXACT = lax.Precision.HIGHEST
 VMEM = pl.BlockSpec(memory_space=pltpu.VMEM)
@@ -91,9 +91,10 @@
     packed_ref[...] = jnp.zeros_like(packed_ref)
     for k, value in enumerate(pack_upper(gram_ref[...], tall)):
         packed_ref[tall * k : tall * k + tall] = value
-    per = send_ref.shape[1]
+    per = send_ref.shape[1] - 1
+    empty = jnp.zeros((1, send_ref.shape[2]), jnp.float32)
     for d in range(send_ref.shape[0]):
-        send_ref[d] = packed_ref[per * d : per * d + per]
+        send_ref[d] = jnp.concatenate([packed_ref[per * d : per * d + per], empty], axis=0)
 
 
 GAP = 2
@@ -330,7 +331,7 @@
     total = parts_ref[0]
     for d in range(1, parts_ref.shape[0]):
         total = total + parts_ref[d]
-    block = jnp.concatenate([total, cross_ref[...]], axis=0)
+    block = jnp.concatenate([total[: total.shape[0] - 1], cross_ref[...]], axis=0)
     for d in range(send_ref.shape[0]):
         send_ref[d] = block
 
@@ -456,7 +457,7 @@
     y_even, y_odd = pairs(*strips, "gy")
     gram, basis_parts = call(
         gram_kernel,
-        out_shape=(shape((devices, per, size)), jax.ShapeDtypeStruct((3, comps, size, points), jnp.bfloat16)),
+        out_shape=(shape((devices, per + 1, size)), jax.ShapeDtypeStruct((3, comps, size, points), jnp.bfloat16)),
         in_specs=[VMEM],
         out_specs=(VMEM, VMEM),
         scratch_shapes=[pltpu.VMEM((size, size), jnp.float32), pltpu.VMEM((devices * per, size), jnp.float32)],

time: 37.2 us -> 37.1 us (level)
  no operation moved by 1% of the time
where the time goes in v13:
time: 37.1 us; the launch traced here: 36.8 us
  starting transfers between devices  11 us (30%)
  blocking collectives  9.11 us (25%)
  Pallas kernels  7.99 us (22%)
  waiting for transfers between devices  5.54 us (15%)
  local copies, waits for them, and re-layouts  2.37 us (6%)
  between operations  0.71 us (2%)
    all_to_all x1, blocking collectives, local(): got = lax.all_to_all(send, ALL, 0, 0)  9.11 us
    pallas_call x1, Pallas kernels, local(): call(functools.partial(final_kernel, count), out_shape=(shape((comps, siz...  3.98 us
    ppermute x1, starting transfers between devices, pairs(): from_odd = lax.ppermute(block_odd, axis, odd)  3.96 us
    all_to_all x1, starting transfers between devices, local(): parts = lax.all_to_all(gram, ALL, 0, 0)  2.57 us
    all_to_all x1, waiting for transfers between devices, local(): parts = lax.all_to_all(gram, ALL, 0, 0)  2.46 us
    unnamed x10, local copies, waits for them, and re-layouts  2.3 us
    ppermute x1, starting transfers between devices, neighbours(): lax.ppermute(block_low, axis, backward)  2.25 us
    pallas_call x1, Pallas kernels, local(): call(step_kernel, out_shape=(shape(flow.shape), shape((comps, 1, points))...  1.87 us
  transfers between devices with their start and end apart: 6, of which 5 were waited for; matrix products, arithmetic and copies ran while one was open for 0% of the time, Pallas kernels for 11%

profile of v13, /device:TPU:0, one launch (start us, length us, event | category | flops | bytes accessed | tf_op | source)
XLA Modules:
  0.0 36.8 jit_solution(15827202374884758366)
XLA Ops:
  0.6 0.1 add_convert_fusion
  0.7 0.1 broadcast_in_dim.2.flags_ref
  0.8 0.9 %copy-done.2 = f32[4,8,16,128]{3,2,1,0:T(8,128)S(1)} copy-done((f32[4,8,16,128]{3,2,1,0:T(8,128)S(1)}, f32[4,8,16,128]{3,2,1,0:T(8,128)}, u32[]{:S(2)}) %copy-start.2) | copy-done | bytes 262168
  1.8 4.0 %collective-permute-start = (f32[4,24,128]{2,1,0:T(8,128)S(1)}, f32[4,24,128]{2,1,0:T(8,128)S(1)}, u32[]{:S(2)}, u32[]{:S(2)}) collective-permute-start(f32[4,24,128]{2,1,0:T(8,128)S(1)} %get-tuple-element.24), channel_id=1, source_target_pairs={{0,6},{2,4},{4,2},{6,0},{1,7},{3,5},{5,3},{7,1},{8,14},{10,12},{12... | collective-permute-start | bytes 147464 | tf_op jit(solution)/shard_map/ppermute | solution.py:57
  5.7 0.5 %collective-permute-start.1 = (f32[4,24,128]{2,1,0:T(8,128)S(1)}, f32[4,24,128]{2,1,0:T(8,128)S(1)}, u32[]{:S(2)}, u32[]{:S(2)}) collective-permute-start(f32[4,24,128]{2,1,0:T(8,128)S(1)} %get-tuple-element.25), channel_id=1, source_target_pairs={{0,2},{2,0},{4,6},{6,4},{1,3},{3,1},{5,7},{7,5},{8,10},{10,8},{12,... | collective-permute-start | bytes 147464 | tf_op jit(solution)/shard_map/ppermute | solution.py:58
  6.3 1.0 %copy-done = f32[127,3,256]{2,0,1:T(8,128)S(1)} copy-done((f32[127,3,256]{2,0,1:T(8,128)S(1)}, f32[127,3,256]{2,0,1:T(8,128)}, u32[]{:S(2)}) %copy-start) | copy-done | bytes 390168
  7.3 1.2 %shard_map.59 = (f32[32,4,128]{2,1,0:T(4,128)}, bf16[3,3,128,256]{3,2,1,0:T(8,128)(2,1)S(1)}) custom-call(f32[3,127,256]{2,1,0:T(8,128)S(1)} %bitcast.11), custom_call_target="tpu_custom_call" | custom-call | tf_op jit(solution)/shard_map/pallas_call | solution.py:458
  8.5 1.3 %collective-permute-done.1.even_ref = f32[4,24,128]{2,1,0:T(8,128)S(1)} collective-permute-done((f32[4,24,128]{2,1,0:T(8,128)S(1)}, f32[4,24,128]{2,1,0:T(8,128)S(1)}, u32[]{:S(2)}, u32[]{:S(2)}) %collective-permute-start.1) | collective-permute-done | bytes 49184 | tf_op jit(solution)/shard_map/ppermute | solution.py:58
  9.8 0.1 shard_map.60
  9.9 1.6 %collective-permute-start.2 = (f32[4,56,128]{2,1,0:T(8,128)S(1)}, f32[4,56,128]{2,1,0:T(8,128)S(1)}, u32[]{:S(2)}, u32[]{:S(2)}) collective-permute-start(f32[4,56,128]{2,1,0:T(8,128)S(1)} %get-tuple-element.31), channel_id=1, source_target_pairs={{0,8},{8,16},{16,24},{24,0},{1,9},{9,17},{17,25},{25,1},{2,10},{10... | collective-permute-start | bytes 344072 | tf_op jit(solution)/shard_map/ppermute | solution.py:50
  11.5 2.2 %collective-permute-start.3 = (f32[4,56,128]{2,1,0:T(8,128)S(1)}, f32[4,56,128]{2,1,0:T(8,128)S(1)}, u32[]{:S(2)}, u32[]{:S(2)}) collective-permute-start(f32[4,56,128]{2,1,0:T(8,128)S(1)} %get-tuple-element.32), channel_id=1, source_target_pairs={{8,0},{16,8},{24,16},{0,24},{9,1},{17,9},{25,17},{1,25},{10,2},{18... | collective-permute-start | bytes 344072 | tf_op jit(solution)/shard_map/ppermute | solution.py:50
  13.8 2.6 %all-to-all-start = ((f32[32,4,128]{2,1,0:T(4,128)}), f32[32,4,128]{2,1,0:T(4,128)S(1)}, u32[]{:S(2)}, u32[]{:S(2)}) async-start(f32[32,4,128]{2,1,0:T(4,128)} %get-tuple-element.27), calls=%async_computation | async-start | bytes 131072 | tf_op jit(solution)/shard_map/all_to_all | solution.py:477
  16.4 1.0 %collective-permute-done.2.low_ref = f32[4,56,128]{2,1,0:T(8,128)S(1)} collective-permute-done((f32[4,56,128]{2,1,0:T(8,128)S(1)}, f32[4,56,128]{2,1,0:T(8,128)S(1)}, u32[]{:S(2)}, u32[]{:S(2)}) %collective-permute-start.2) | collective-permute-done | bytes 114720 | tf_op jit(solution)/shard_map/ppermute | solution.py:50
  17.4 0.4 %collective-permute-done.3.high_ref = f32[4,56,128]{2,1,0:T(8,128)S(1)} collective-permute-done((f32[4,56,128]{2,1,0:T(8,128)S(1)}, f32[4,56,128]{2,1,0:T(8,128)S(1)}, u32[]{:S(2)}, u32[]{:S(2)}) %collective-permute-start.3) | collective-permute-done | bytes 114720 | tf_op jit(solution)/shard_map/ppermute | solution.py:50
  17.8 0.2 shard_map.61
  18.0 0.0 copy-start.1
  18.0 0.1 collective-permute-start.4
  18.1 0.3 copy-done.4
  18.5 0.5 %shard_map.62 = (f32[4,12,24,128]{3,2,1,0:T(8,128)S(1)}, s32[1,256]{1,0:T(1,128)S(1)}) custom-call(s32[3,128]{1,0:T(4,128)S(1)} %broadcast_in_dim.2.flags_ref, s32[1,256]{1,0:T(1,128)S(1)} %bitcast.15, f32[4,8,24,128]{3,2,1,0:T(8,128)S(1)} %bitcast.9, f32[4,3,24,128]{3,2,1,0:T(8,128)S(1)} %get-tuple-element.33.xlo_ref, ...), custom_call_target="tpu_custom_call" | custom-call | tf_op jit(solution)/shard_map/pallas_call | solution.py:490
  19.0 0.3 collective-permute-done.4.low_ref.high_ref
  19.3 1.9 %shard_map.63 = (f32[4,8,16,128]{3,2,1,0:T(8,128)S(1)}, f32[3,1,256]{2,1,0:T(1,128)S(1)}, f32[1,128]{1,0:T(1,128)S(1)}) custom-call(s32[3,128]{1,0:T(4,128)S(1)} %broadcast_in_dim.2.flags_ref, f32[4,8,24,128]{3,2,1,0:T(8,128)S(1)} %bitcast.10, f32[4,3,24,128]{3,2,1,0:T(8,128)S(1)} %get-tuple-element.33.xlo_ref, ...), custom_call_target="tpu_custom_call" | custom-call | tf_op jit(solution)/shard_map/pallas_call | solution.py:500
  21.2 2.5 %all-to-all-done.parts_ref = f32[32,4,128]{2,1,0:T(4,128)S(1)} async-done(((f32[32,4,128]{2,1,0:T(4,128)}), f32[32,4,128]{2,1,0:T(4,128)S(1)}, u32[]{:S(2)}, u32[]{:S(2)}) %all-to-all-start) | async-done | bytes 65568 | tf_op jit(solution)/shard_map/all_to_all | solution.py:477
  23.7 9.1 %all_to_all.10.got_ref = f32[32,4,128]{2,1,0:T(4,128)S(1)} all-to-all(f32[32,4,128]{2,1,0:T(4,128)S(1)} %shard_map.64), channel_id=1, replica_groups=mesh['gx'=4,'gy'=4,'gz'=2] {'gz','gy','gx'}, dimensions={0} | all-to-all | bytes 131072 | tf_op jit(solution)/shard_map/all_to_all | solution.py:514
  32.8 4.0 %shard_map.65 = (f32[3,128,256]{2,1,0:T(8,128)}, f32[128,128]{1,0:T(8,128)}, f32[4,8,16,128]{3,2,1,0:T(8,128)}) custom-call(f32[32,4,128]{2,1,0:T(4,128)S(1)} %all_to_all.10.got_ref, bf16[3,3,128,256]{3,2,1,0:T(8,128)(2,1)S(1)} %get-tuple-element.39.parts_ref, f32[3,1,256]{2,1,0:T(1,128)S(1)} %get-tuple-element.40.snap_ref, ...), custom_call_target="tpu_custom_call" | custom-call | tf_op jit(solution)/shard_map/pallas_call | solution.py:515
  (9 shorter events, 0.1 us)
Async XLA Ops:
  0.8 1.0 %copy-start.2 = (f32[4,8,16,128]{3,2,1,0:T(8,128)S(1)}, f32[4,8,16,128]{3,2,1,0:T(8,128)}, u32[]{:S(2)}) copy-start(f32[4,8,16,128]{3,2,1,0:T(8,128)} %param.3) | copy-start | bytes 786436
  1.7 8.1 %copy-start.3 = (f32[4,8,16,128]{3,2,1,0:T(8,128)S(1)}, f32[4,8,16,128]{3,2,1,0:T(8,128)}, u32[]{:S(2)}) copy-start(f32[4,8,16,128]{3,2,1,0:T(8,128)} %param.3) | copy-start | bytes 786436
  1.8 6.7 %collective-permute-start = (f32[4,24,128]{2,1,0:T(8,128)S(1)}, f32[4,24,128]{2,1,0:T(8,128)S(1)}, u32[]{:S(2)}, u32[]{:S(2)}) collective-permute-start(f32[4,24,128]{2,1,0:T(8,128)S(1)} %get-tuple-element.24), channel_id=1, source_target_pairs={{0,6},{2,4},{4,2},{6,0},{1,7},{3,5},{5,3},{7,1},{8,14},{10,12},{12... | collective-permute-start | bytes 147464 | tf_op jit(solution)/shard_map/ppermute | solution.py:57
  5.7 4.1 %collective-permute-start.1 = (f32[4,24,128]{2,1,0:T(8,128)S(1)}, f32[4,24,128]{2,1,0:T(8,128)S(1)}, u32[]{:S(2)}, u32[]{:S(2)}) collective-permute-start(f32[4,24,128]{2,1,0:T(8,128)S(1)} %get-tuple-element.25), channel_id=1, source_target_pairs={{0,2},{2,0},{4,6},{6,4},{1,3},{3,1},{5,7},{7,5},{8,10},{10,8},{12,... | collective-permute-start | bytes 147464 | tf_op jit(solution)/shard_map/ppermute | solution.py:58
  6.3 1.0 %copy-start = (f32[127,3,256]{2,0,1:T(8,128)S(1)}, f32[127,3,256]{2,0,1:T(8,128)}, u32[]{:S(2)}) copy-start(f32[127,3,256]{2,0,1:T(8,128)} %param.4) | copy-start | bytes 1170436
  9.9 7.5 %collective-permute-start.2 = (f32[4,56,128]{2,1,0:T(8,128)S(1)}, f32[4,56,128]{2,1,0:T(8,128)S(1)}, u32[]{:S(2)}, u32[]{:S(2)}) collective-permute-start(f32[4,56,128]{2,1,0:T(8,128)S(1)} %get-tuple-element.31), channel_id=1, source_target_pairs={{0,8},{8,16},{16,24},{24,0},{1,9},{9,17},{17,25},{25,1},{2,10},{10... | collective-permute-start | bytes 344072 | tf_op jit(solution)/shard_map/ppermute | solution.py:50
  11.5 6.2 %collective-permute-start.3 = (f32[4,56,128]{2,1,0:T(8,128)S(1)}, f32[4,56,128]{2,1,0:T(8,128)S(1)}, u32[]{:S(2)}, u32[]{:S(2)}) collective-permute-start(f32[4,56,128]{2,1,0:T(8,128)S(1)} %get-tuple-element.32), channel_id=1, source_target_pairs={{8,0},{16,8},{24,16},{0,24},{9,1},{17,9},{25,17},{1,25},{10,2},{18... | collective-permute-start | bytes 344072 | tf_op jit(solution)/shard_map/ppermute | solution.py:50
  13.8 9.9 %all-to-all-start = ((f32[32,4,128]{2,1,0:T(4,128)}), f32[32,4,128]{2,1,0:T(4,128)S(1)}, u32[]{:S(2)}, u32[]{:S(2)}) async-start(f32[32,4,128]{2,1,0:T(4,128)} %get-tuple-element.27), calls=%async_computation | async-start | bytes 131072 | tf_op jit(solution)/shard_map/all_to_all | solution.py:477
  17.8 0.7 %copy-start.4 = (s32[256]{0:T(256)S(1)}, s32[256]{0:T(256)}, u32[]{:S(2)}) copy-start(s32[256]{0:T(256)} %param.5) | copy-start | bytes 3076
  18.0 1.3 %copy-start.1 = (f32[127,3,256]{2,0,1:T(8,128)S(1)}, f32[127,3,256]{2,0,1:T(8,128)}, u32[]{:S(2)}) copy-start(f32[127,3,256]{2,0,1:T(8,128)} %param.4) | copy-start | bytes 1170436
  18.0 1.3 %collective-permute-start.4 = (f32[4,24,128]{2,1,0:T(8,128)S(1)}, f32[4,24,128]{2,1,0:T(8,128)S(1)}, u32[]{:S(2)}, u32[]{:S(2)}) collective-permute-start(f32[4,24,128]{2,1,0:T(8,128)S(1)} %get-tuple-element.36.own_ref), channel_id=1, source_target_pairs={{0,1},{1,0},{2,3},{3,2},{4,5},{5,4},{6,7},{7,6},{8,9},{9,8},{10,11... | collective-permute-start | bytes 147464 | tf_op jit(solution)/shard_map/ppermute | solution.py:487

commit v14 on v13

--- a/solution.py
+++ b/solution.py
@@ -372,7 +372,7 @@
 
     for k in range(4):
         base = tall * k
-        eliminate(work_ref, base, tall)
+        eliminate(work_ref, base, tall, old[0] if k == 0 else None)
         done = work_ref[base : base + tall, :]
         if k < 3:
             change = dot_stacked(done[:, 0:size], done)
@@ -401,7 +401,7 @@
         copy.wait()
 
 
-def eliminate(work_ref, base, tall):
+def eliminate(work_ref, base, tall, early=None):
     blocks = tall // 8
     sub = lax.broadcasted_iota(jnp.int32, (8, 128), 0)
     panel = [work_ref[base + 8 * b : base + 8 * b + 8, :] for b in range(blocks)]
@@ -409,8 +409,9 @@
     half = tall // 2
     for low in (0, half):
         high = low + half
+        rows = panel if early is None or low else [early[8 * b : 8 * b + 8] for b in range(blocks)]
         column = {
-            k: {b: jnp.broadcast_to(panel[b][:, base + k : base + k + 1], (8, 128)) for b in range(k // 8, blocks)}
+            k: {b: jnp.broadcast_to(rows[b][:, base + k : base + k + 1], (8, 128)) for b in range(k // 8, blocks)}
             for k in range(low, high)
         }
         for j in range(low, high):

time: 37.1 us -> 36.9 us (level)
  no operation moved by 1% of the time
where the time goes in v14:
time: 36.9 us; the launch traced here: 36.7 us
  starting transfers between devices  11 us (30%)
  blocking collectives  9.11 us (25%)
  Pallas kernels  7.84 us (21%)
  waiting for transfers between devices  5.54 us (15%)
  local copies, waits for them, and re-layouts  2.37 us (6%)
  between operations  0.71 us (2%)
    all_to_all x1, blocking collectives, local(): got = lax.all_to_all(send, ALL, 0, 0)  9.11 us
    ppermute x1, starting transfers between devices, pairs(): from_odd = lax.ppermute(block_odd, axis, odd)  3.96 us
    pallas_call x1, Pallas kernels, local(): call(functools.partial(final_kernel, count), out_shape=(shape((comps, siz...  3.83 us
    all_to_all x1, starting transfers between devices, local(): parts = lax.all_to_all(gram, ALL, 0, 0)  2.57 us
    all_to_all x1, waiting for transfers between devices, local(): parts = lax.all_to_all(gram, ALL, 0, 0)  2.46 us
    unnamed x10, local copies, waits for them, and re-layouts  2.3 us
    ppermute x1, starting transfers between devices, neighbours(): lax.ppermute(block_low, axis, backward)  2.25 us
    pallas_call x1, Pallas kernels, local(): call(step_kernel, out_shape=(shape(flow.shape), shape((comps, 1, points))...  1.87 us
  transfers between devices with their start and end apart: 6, of which 5 were waited for; matrix products, arithmetic and copies ran while one was open for 0% of the time, Pallas kernels for 11%

profile of v14, /device:TPU:0, one launch (start us, length us, event | category | flops | bytes accessed | tf_op | source)
XLA Modules:
  0.0 36.7 jit_solution(4558839244716409653)
XLA Ops:
  0.6 0.1 add_convert_fusion
  0.7 0.1 broadcast_in_dim.2.flags_ref
  0.8 0.9 %copy-done.2 = f32[4,8,16,128]{3,2,1,0:T(8,128)S(1)} copy-done((f32[4,8,16,128]{3,2,1,0:T(8,128)S(1)}, f32[4,8,16,128]{3,2,1,0:T(8,128)}, u32[]{:S(2)}) %copy-start.2) | copy-done | bytes 262168
  1.8 4.0 %collective-permute-start = (f32[4,24,128]{2,1,0:T(8,128)S(1)}, f32[4,24,128]{2,1,0:T(8,128)S(1)}, u32[]{:S(2)}, u32[]{:S(2)}) collective-permute-start(f32[4,24,128]{2,1,0:T(8,128)S(1)} %get-tuple-element.24), channel_id=1, source_target_pairs={{0,6},{2,4},{4,2},{6,0},{1,7},{3,5},{5,3},{7,1},{8,14},{10,12},{12... | collective-permute-start | bytes 147464 | tf_op jit(solution)/shard_map/ppermute | solution.py:57
  5.7 0.5 %collective-permute-start.1 = (f32[4,24,128]{2,1,0:T(8,128)S(1)}, f32[4,24,128]{2,1,0:T(8,128)S(1)}, u32[]{:S(2)}, u32[]{:S(2)}) collective-permute-start(f32[4,24,128]{2,1,0:T(8,128)S(1)} %get-tuple-element.25), channel_id=1, source_target_pairs={{0,2},{2,0},{4,6},{6,4},{1,3},{3,1},{5,7},{7,5},{8,10},{10,8},{12,... | collective-permute-start | bytes 147464 | tf_op jit(solution)/shard_map/ppermute | solution.py:58
  6.3 1.0 %copy-done = f32[127,3,256]{2,0,1:T(8,128)S(1)} copy-done((f32[127,3,256]{2,0,1:T(8,128)S(1)}, f32[127,3,256]{2,0,1:T(8,128)}, u32[]{:S(2)}) %copy-start) | copy-done | bytes 390168
  7.3 1.2 %shard_map.59 = (f32[32,4,128]{2,1,0:T(4,128)}, bf16[3,3,128,256]{3,2,1,0:T(8,128)(2,1)S(1)}) custom-call(f32[3,127,256]{2,1,0:T(8,128)S(1)} %bitcast.11), custom_call_target="tpu_custom_call" | custom-call | tf_op jit(solution)/shard_map/pallas_call | solution.py:459
  8.5 1.3 %collective-permute-done.1.even_ref = f32[4,24,128]{2,1,0:T(8,128)S(1)} collective-permute-done((f32[4,24,128]{2,1,0:T(8,128)S(1)}, f32[4,24,128]{2,1,0:T(8,128)S(1)}, u32[]{:S(2)}, u32[]{:S(2)}) %collective-permute-start.1) | collective-permute-done | bytes 49184 | tf_op jit(solution)/shard_map/ppermute | solution.py:58
  9.8 0.1 shard_map.60
  9.9 1.6 %collective-permute-start.2 = (f32[4,56,128]{2,1,0:T(8,128)S(1)}, f32[4,56,128]{2,1,0:T(8,128)S(1)}, u32[]{:S(2)}, u32[]{:S(2)}) collective-permute-start(f32[4,56,128]{2,1,0:T(8,128)S(1)} %get-tuple-element.31), channel_id=1, source_target_pairs={{0,8},{8,16},{16,24},{24,0},{1,9},{9,17},{17,25},{25,1},{2,10},{10... | collective-permute-start | bytes 344072 | tf_op jit(solution)/shard_map/ppermute | solution.py:50
  11.5 2.2 %collective-permute-start.3 = (f32[4,56,128]{2,1,0:T(8,128)S(1)}, f32[4,56,128]{2,1,0:T(8,128)S(1)}, u32[]{:S(2)}, u32[]{:S(2)}) collective-permute-start(f32[4,56,128]{2,1,0:T(8,128)S(1)} %get-tuple-element.32), channel_id=1, source_target_pairs={{8,0},{16,8},{24,16},{0,24},{9,1},{17,9},{25,17},{1,25},{10,2},{18... | collective-permute-start | bytes 344072 | tf_op jit(solution)/shard_map/ppermute | solution.py:50
  13.8 2.6 %all-to-all-start = ((f32[32,4,128]{2,1,0:T(4,128)}), f32[32,4,128]{2,1,0:T(4,128)S(1)}, u32[]{:S(2)}, u32[]{:S(2)}) async-start(f32[32,4,128]{2,1,0:T(4,128)} %get-tuple-element.27), calls=%async_computation | async-start | bytes 131072 | tf_op jit(solution)/shard_map/all_to_all | solution.py:478
  16.4 1.0 %collective-permute-done.2.low_ref = f32[4,56,128]{2,1,0:T(8,128)S(1)} collective-permute-done((f32[4,56,128]{2,1,0:T(8,128)S(1)}, f32[4,56,128]{2,1,0:T(8,128)S(1)}, u32[]{:S(2)}, u32[]{:S(2)}) %collective-permute-start.2) | collective-permute-done | bytes 114720 | tf_op jit(solution)/shard_map/ppermute | solution.py:50
  17.4 0.4 %collective-permute-done.3.high_ref = f32[4,56,128]{2,1,0:T(8,128)S(1)} collective-permute-done((f32[4,56,128]{2,1,0:T(8,128)S(1)}, f32[4,56,128]{2,1,0:T(8,128)S(1)}, u32[]{:S(2)}, u32[]{:S(2)}) %collective-permute-start.3) | collective-permute-done | bytes 114720 | tf_op jit(solution)/shard_map/ppermute | solution.py:50
  17.8 0.2 shard_map.61
  18.0 0.0 copy-start.1
  18.0 0.1 collective-permute-start.4
  18.1 0.3 copy-done.4
  18.5 0.5 %shard_map.62 = (f32[4,12,24,128]{3,2,1,0:T(8,128)S(1)}, s32[1,256]{1,0:T(1,128)S(1)}) custom-call(s32[3,128]{1,0:T(4,128)S(1)} %broadcast_in_dim.2.flags_ref, s32[1,256]{1,0:T(1,128)S(1)} %bitcast.15, f32[4,8,24,128]{3,2,1,0:T(8,128)S(1)} %bitcast.9, f32[4,3,24,128]{3,2,1,0:T(8,128)S(1)} %get-tuple-element.33.xlo_ref, ...), custom_call_target="tpu_custom_call" | custom-call | tf_op jit(solution)/shard_map/pallas_call | solution.py:491
  19.0 0.3 collective-permute-done.4.low_ref.high_ref
  19.3 1.9 %shard_map.63 = (f32[4,8,16,128]{3,2,1,0:T(8,128)S(1)}, f32[3,1,256]{2,1,0:T(1,128)S(1)}, f32[1,128]{1,0:T(1,128)S(1)}) custom-call(s32[3,128]{1,0:T(4,128)S(1)} %broadcast_in_dim.2.flags_ref, f32[4,8,24,128]{3,2,1,0:T(8,128)S(1)} %bitcast.10, f32[4,3,24,128]{3,2,1,0:T(8,128)S(1)} %get-tuple-element.33.xlo_ref, ...), custom_call_target="tpu_custom_call" | custom-call | tf_op jit(solution)/shard_map/pallas_call | solution.py:501
  21.2 2.5 %all-to-all-done.parts_ref = f32[32,4,128]{2,1,0:T(4,128)S(1)} async-done(((f32[32,4,128]{2,1,0:T(4,128)}), f32[32,4,128]{2,1,0:T(4,128)S(1)}, u32[]{:S(2)}, u32[]{:S(2)}) %all-to-all-start) | async-done | bytes 65568 | tf_op jit(solution)/shard_map/all_to_all | solution.py:478
  23.7 9.1 %all_to_all.10.got_ref = f32[32,4,128]{2,1,0:T(4,128)S(1)} all-to-all(f32[32,4,128]{2,1,0:T(4,128)S(1)} %shard_map.64), channel_id=1, replica_groups=mesh['gx'=4,'gy'=4,'gz'=2] {'gz','gy','gx'}, dimensions={0} | all-to-all | bytes 131072 | tf_op jit(solution)/shard_map/all_to_all | solution.py:515
  32.8 3.8 %shard_map.65 = (f32[3,128,256]{2,1,0:T(8,128)}, f32[128,128]{1,0:T(8,128)}, f32[4,8,16,128]{3,2,1,0:T(8,128)}) custom-call(f32[32,4,128]{2,1,0:T(4,128)S(1)} %all_to_all.10.got_ref, bf16[3,3,128,256]{3,2,1,0:T(8,128)(2,1)S(1)} %get-tuple-element.39.parts_ref, f32[3,1,256]{2,1,0:T(1,128)S(1)} %get-tuple-element.40.snap_ref, ...), custom_call_target="tpu_custom_call" | custom-call | tf_op jit(solution)/shard_map/pallas_call | solution.py:516
  (9 shorter events, 0.1 us)
Async XLA Ops:
  0.8 1.0 %copy-start.2 = (f32[4,8,16,128]{3,2,1,0:T(8,128)S(1)}, f32[4,8,16,128]{3,2,1,0:T(8,128)}, u32[]{:S(2)}) copy-start(f32[4,8,16,128]{3,2,1,0:T(8,128)} %param.3) | copy-start | bytes 786436
  1.7 8.1 %copy-start.3 = (f32[4,8,16,128]{3,2,1,0:T(8,128)S(1)}, f32[4,8,16,128]{3,2,1,0:T(8,128)}, u32[]{:S(2)}) copy-start(f32[4,8,16,128]{3,2,1,0:T(8,128)} %param.3) | copy-start | bytes 786436
  1.8 6.7 %collective-permute-start = (f32[4,24,128]{2,1,0:T(8,128)S(1)}, f32[4,24,128]{2,1,0:T(8,128)S(1)}, u32[]{:S(2)}, u32[]{:S(2)}) collective-permute-start(f32[4,24,128]{2,1,0:T(8,128)S(1)} %get-tuple-element.24), channel_id=1, source_target_pairs={{0,6},{2,4},{4,2},{6,0},{1,7},{3,5},{5,3},{7,1},{8,14},{10,12},{12... | collective-permute-start | bytes 147464 | tf_op jit(solution)/shard_map/ppermute | solution.py:57
  5.7 4.1 %collective-permute-start.1 = (f32[4,24,128]{2,1,0:T(8,128)S(1)}, f32[4,24,128]{2,1,0:T(8,128)S(1)}, u32[]{:S(2)}, u32[]{:S(2)}) collective-permute-start(f32[4,24,128]{2,1,0:T(8,128)S(1)} %get-tuple-element.25), channel_id=1, source_target_pairs={{0,2},{2,0},{4,6},{6,4},{1,3},{3,1},{5,7},{7,5},{8,10},{10,8},{12,... | collective-permute-start | bytes 147464 | tf_op jit(solution)/shard_map/ppermute | solution.py:58
  6.3 1.0 %copy-start = (f32[127,3,256]{2,0,1:T(8,128)S(1)}, f32[127,3,256]{2,0,1:T(8,128)}, u32[]{:S(2)}) copy-start(f32[127,3,256]{2,0,1:T(8,128)} %param.4) | copy-start | bytes 1170436
  9.9 7.5 %collective-permute-start.2 = (f32[4,56,128]{2,1,0:T(8,128)S(1)}, f32[4,56,128]{2,1,0:T(8,128)S(1)}, u32[]{:S(2)}, u32[]{:S(2)}) collective-permute-start(f32[4,56,128]{2,1,0:T(8,128)S(1)} %get-tuple-element.31), channel_id=1, source_target_pairs={{0,8},{8,16},{16,24},{24,0},{1,9},{9,17},{17,25},{25,1},{2,10},{10... | collective-permute-start | bytes 344072 | tf_op jit(solution)/shard_map/ppermute | solution.py:50
  11.5 6.2 %collective-permute-start.3 = (f32[4,56,128]{2,1,0:T(8,128)S(1)}, f32[4,56,128]{2,1,0:T(8,128)S(1)}, u32[]{:S(2)}, u32[]{:S(2)}) collective-permute-start(f32[4,56,128]{2,1,0:T(8,128)S(1)} %get-tuple-element.32), channel_id=1, source_target_pairs={{8,0},{16,8},{24,16},{0,24},{9,1},{17,9},{25,17},{1,25},{10,2},{18... | collective-permute-start | bytes 344072 | tf_op jit(solution)/shard_map/ppermute | solution.py:50
  13.8 9.9 %all-to-all-start = ((f32[32,4,128]{2,1,0:T(4,128)}), f32[32,4,128]{2,1,0:T(4,128)S(1)}, u32[]{:S(2)}, u32[]{:S(2)}) async-start(f32[32,4,128]{2,1,0:T(4,128)} %get-tuple-element.27), calls=%async_computation | async-start | bytes 131072 | tf_op jit(solution)/shard_map/all_to_all | solution.py:478
  17.8 0.7 %copy-start.4 = (s32[256]{0:T(256)S(1)}, s32[256]{0:T(256)}, u32[]{:S(2)}) copy-start(s32[256]{0:T(256)} %param.5) | copy-start | bytes 3076
  18.0 1.3 %copy-start.1 = (f32[127,3,256]{2,0,1:T(8,128)S(1)}, f32[127,3,256]{2,0,1:T(8,128)}, u32[]{:S(2)}) copy-start(f32[127,3,256]{2,0,1:T(8,128)} %param.4) | copy-start | bytes 1170436
  18.0 1.3 %collective-permute-start.4 = (f32[4,24,128]{2,1,0:T(8,128)S(1)}, f32[4,24,128]{2,1,0:T(8,128)S(1)}, u32[]{:S(2)}, u32[]{:S(2)}) collective-permute-start(f32[4,24,128]{2,1,0:T(8,128)S(1)} %get-tuple-element.36.own_ref), channel_id=1, source_target_pairs={{0,1},{1,0},{2,3},{3,2},{4,5},{5,4},{6,7},{7,6},{8,9},{9,8},{10,11... | collective-permute-start | bytes 147464 | tf_op jit(solution)/shard_map/ppermute | solution.py:488

commit v15 on v14

--- a/solution.py
+++ b/solution.py
@@ -50,11 +50,15 @@
     return lax.ppermute(block_high, axis, forward), lax.ppermute(block_low, axis, backward)
 
 
-def pairs(block_odd, block_even, axis):
-    count = lax.axis_size(axis)
+def pairs(block_odd, block_even, axis, other):
+    count, width = lax.axis_size(axis), lax.axis_size(other)
     even = [(i, i + 1 - 2 * (i % 2)) for i in range(count)]
-    odd = [(i, (i - 1 + 2 * (i % 2)) % count) for i in range(count)]
-    from_odd = lax.ppermute(block_odd, axis, odd)
+    odd = []
+    for i in range(count):
+        for k in range(width):
+            to = (i, k + 1 - 2 * (k % 2)) if i in (0, count - 1) else (i - 1 + 2 * (i % 2), k)
+            odd.append((i * width + k, to[0] * width + to[1]))
+    from_odd = lax.ppermute(block_odd, (axis, other), odd)
     return lax.ppermute(block_even, axis, even), from_odd
 
 
@@ -455,7 +459,7 @@
     strips = call(
         functools.partial(strips_kernel, nx), out_shape=(strip, strip), in_specs=[VMEM] * 2, out_specs=(VMEM, VMEM)
     )(flags, flat)
-    y_even, y_odd = pairs(*strips, "gy")
+    y_even, y_odd = pairs(*strips, "gy", "gz")
     gram, basis_parts = call(
         gram_kernel,
         out_shape=(shape((devices, per + 1, size)), jax.ShapeDtypeStruct((3, comps, size, points), jnp.bfloat16)),

time: 36.9 us -> 36.6 us (level)
  waiting for transfers between devices: 5.54 us -> 4.59 us
  starting transfers between devices: 11 us -> 11.6 us
    ppermute x1, starting transfers between devices: 3.96 us -> 0.52 us  [pairs(): from_odd = lax.ppermute(block_odd, (axis, other), odd)]
    ppermute x1, starting transfers between devices: 0.54 us -> 3.98 us  [pairs(): return (lax.ppermute(block_even, axis, even), from_odd)]
    ppermute x1, waiting for transfers between devices: 1.32 us -> 0.35 us  [pairs(): return (lax.ppermute(block_even, axis, even), from_odd)]
    all_to_all x1, waiting for transfers between devices: 2.46 us -> 3.17 us  [local(): parts = lax.all_to_all(gram, ALL, 0, 0)]
    ppermute x1, waiting for transfers between devices: 1.03 us -> 0.35 us  [neighbours(): lax.ppermute(block_high, axis, forward)]
    all_to_all x1, starting transfers between devices: 2.57 us -> 3.18 us  [local(): parts = lax.all_to_all(gram, ALL, 0, 0)]
where the time goes in v15:
time: 36.6 us; the launch traced here: 36.3 us
  starting transfers between devices  11.6 us (32%)
  blocking collectives  9.12 us (25%)
  Pallas kernels  7.83 us (21%)
  waiting for transfers between devices  4.59 us (13%)
  local copies, waits for them, and re-layouts  2.37 us (6%)
  between operations  0.71 us (2%)
    all_to_all x1, blocking collectives, local(): got = lax.all_to_all(send, ALL, 0, 0)  9.12 us
    ppermute x1, starting transfers between devices, pairs(): return (lax.ppermute(block_even, axis, even), from_odd)  3.98 us
    pallas_call x1, Pallas kernels, local(): call(functools.partial(final_kernel, count), out_shape=(shape((comps, siz...  3.83 us
    all_to_all x1, starting transfers between devices, local(): parts = lax.all_to_all(gram, ALL, 0, 0)  3.18 us
    all_to_all x1, waiting for transfers between devices, local(): parts = lax.all_to_all(gram, ALL, 0, 0)  3.17 us
    unnamed x10, local copies, waits for them, and re-layouts  2.3 us
    ppermute x1, starting transfers between devices, neighbours(): lax.ppermute(block_low, axis, backward)  2.25 us
    pallas_call x1, Pallas kernels, local(): call(step_kernel, out_shape=(shape(flow.shape), shape((comps, 1, points))...  1.86 us
  transfers between devices with their start and end apart: 6, of which 5 were waited for; matrix products, arithmetic and copies ran while one was open for 0% of the time, Pallas kernels for 11%

profile of v15, /device:TPU:0, one launch (start us, length us, event | category | flops | bytes accessed | tf_op | source)
XLA Modules:
  0.0 36.3 jit_solution(14997435969828785784)
XLA Ops:
  0.6 0.1 add_convert_fusion
  0.7 0.1 broadcast_in_dim.2.flags_ref
  0.8 0.9 %copy-done.2 = f32[4,8,16,128]{3,2,1,0:T(8,128)S(1)} copy-done((f32[4,8,16,128]{3,2,1,0:T(8,128)S(1)}, f32[4,8,16,128]{3,2,1,0:T(8,128)}, u32[]{:S(2)}) %copy-start.2) | copy-done | bytes 262168
  1.8 0.5 %collective-permute-start = (f32[4,24,128]{2,1,0:T(8,128)S(1)}, f32[4,24,128]{2,1,0:T(8,128)S(1)}, u32[]{:S(2)}, u32[]{:S(2)}) collective-permute-start(f32[4,24,128]{2,1,0:T(8,128)S(1)} %get-tuple-element.24), channel_id=1, source_target_pairs={{0,1},{1,0},{2,4},{3,5},{4,2},{5,3},{6,7},{7,6},{8,9},{9,8},{10,12... | collective-permute-start | bytes 147464 | tf_op jit(solution)/shard_map/ppermute | solution.py:61
  2.3 4.0 %collective-permute-start.1 = (f32[4,24,128]{2,1,0:T(8,128)S(1)}, f32[4,24,128]{2,1,0:T(8,128)S(1)}, u32[]{:S(2)}, u32[]{:S(2)}) collective-permute-start(f32[4,24,128]{2,1,0:T(8,128)S(1)} %get-tuple-element.25), channel_id=1, source_target_pairs={{0,2},{2,0},{4,6},{6,4},{1,3},{3,1},{5,7},{7,5},{8,10},{10,8},{12,... | collective-permute-start | bytes 147464 | tf_op jit(solution)/shard_map/ppermute | solution.py:62
  6.3 1.0 %copy-done = f32[127,3,256]{2,0,1:T(8,128)S(1)} copy-done((f32[127,3,256]{2,0,1:T(8,128)S(1)}, f32[127,3,256]{2,0,1:T(8,128)}, u32[]{:S(2)}) %copy-start) | copy-done | bytes 390168
  7.3 1.2 %shard_map.59 = (f32[32,4,128]{2,1,0:T(4,128)}, bf16[3,3,128,256]{3,2,1,0:T(8,128)(2,1)S(1)}) custom-call(f32[3,127,256]{2,1,0:T(8,128)S(1)} %bitcast.11), custom_call_target="tpu_custom_call" | custom-call | tf_op jit(solution)/shard_map/pallas_call | solution.py:463
  8.5 0.4 collective-permute-done.1.even_ref
  8.9 0.1 shard_map.60
  8.9 1.6 %collective-permute-start.2 = (f32[4,56,128]{2,1,0:T(8,128)S(1)}, f32[4,56,128]{2,1,0:T(8,128)S(1)}, u32[]{:S(2)}, u32[]{:S(2)}) collective-permute-start(f32[4,56,128]{2,1,0:T(8,128)S(1)} %get-tuple-element.31), channel_id=1, source_target_pairs={{0,8},{8,16},{16,24},{24,0},{1,9},{9,17},{17,25},{25,1},{2,10},{10... | collective-permute-start | bytes 344072 | tf_op jit(solution)/shard_map/ppermute | solution.py:50
  10.6 2.2 %collective-permute-start.3 = (f32[4,56,128]{2,1,0:T(8,128)S(1)}, f32[4,56,128]{2,1,0:T(8,128)S(1)}, u32[]{:S(2)}, u32[]{:S(2)}) collective-permute-start(f32[4,56,128]{2,1,0:T(8,128)S(1)} %get-tuple-element.32), channel_id=1, source_target_pairs={{8,0},{16,8},{24,16},{0,24},{9,1},{17,9},{25,17},{1,25},{10,2},{18... | collective-permute-start | bytes 344072 | tf_op jit(solution)/shard_map/ppermute | solution.py:50
  12.8 3.2 %all-to-all-start = ((f32[32,4,128]{2,1,0:T(4,128)}), f32[32,4,128]{2,1,0:T(4,128)S(1)}, u32[]{:S(2)}, u32[]{:S(2)}) async-start(f32[32,4,128]{2,1,0:T(4,128)} %get-tuple-element.27), calls=%async_computation | async-start | bytes 131072 | tf_op jit(solution)/shard_map/all_to_all | solution.py:482
  16.0 0.3 collective-permute-done.2.low_ref
  16.3 0.4 %collective-permute-done.3.high_ref = f32[4,56,128]{2,1,0:T(8,128)S(1)} collective-permute-done((f32[4,56,128]{2,1,0:T(8,128)S(1)}, f32[4,56,128]{2,1,0:T(8,128)S(1)}, u32[]{:S(2)}, u32[]{:S(2)}) %collective-permute-start.3) | collective-permute-done | bytes 114720 | tf_op jit(solution)/shard_map/ppermute | solution.py:50
  16.7 0.2 shard_map.61
  17.0 0.0 copy-start.1
  17.0 0.1 collective-permute-start.4
  17.1 0.3 copy-done.4
  17.4 0.5 %shard_map.62 = (f32[4,12,24,128]{3,2,1,0:T(8,128)S(1)}, s32[1,256]{1,0:T(1,128)S(1)}) custom-call(s32[3,128]{1,0:T(4,128)S(1)} %broadcast_in_dim.2.flags_ref, s32[1,256]{1,0:T(1,128)S(1)} %bitcast.15, f32[4,8,24,128]{3,2,1,0:T(8,128)S(1)} %bitcast.9, f32[4,3,24,128]{3,2,1,0:T(8,128)S(1)} %get-tuple-element.33.xlo_ref, ...), custom_call_target="tpu_custom_call" | custom-call | tf_op jit(solution)/shard_map/pallas_call | solution.py:495
  17.9 0.3 collective-permute-done.4.low_ref.high_ref
  18.3 1.9 %shard_map.63 = (f32[4,8,16,128]{3,2,1,0:T(8,128)S(1)}, f32[3,1,256]{2,1,0:T(1,128)S(1)}, f32[1,128]{1,0:T(1,128)S(1)}) custom-call(s32[3,128]{1,0:T(4,128)S(1)} %broadcast_in_dim.2.flags_ref, f32[4,8,24,128]{3,2,1,0:T(8,128)S(1)} %bitcast.10, f32[4,3,24,128]{3,2,1,0:T(8,128)S(1)} %get-tuple-element.33.xlo_ref, ...), custom_call_target="tpu_custom_call" | custom-call | tf_op jit(solution)/shard_map/pallas_call | solution.py:505
  20.2 3.2 %all-to-all-done.parts_ref = f32[32,4,128]{2,1,0:T(4,128)S(1)} async-done(((f32[32,4,128]{2,1,0:T(4,128)}), f32[32,4,128]{2,1,0:T(4,128)S(1)}, u32[]{:S(2)}, u32[]{:S(2)}) %all-to-all-start) | async-done | bytes 65568 | tf_op jit(solution)/shard_map/all_to_all | solution.py:482
  23.4 9.1 %all_to_all.10.got_ref = f32[32,4,128]{2,1,0:T(4,128)S(1)} all-to-all(f32[32,4,128]{2,1,0:T(4,128)S(1)} %shard_map.64), channel_id=1, replica_groups=mesh['gx'=4,'gy'=4,'gz'=2] {'gz','gy','gx'}, dimensions={0} | all-to-all | bytes 131072 | tf_op jit(solution)/shard_map/all_to_all | solution.py:519
  32.5 3.8 %shard_map.65 = (f32[3,128,256]{2,1,0:T(8,128)}, f32[128,128]{1,0:T(8,128)}, f32[4,8,16,128]{3,2,1,0:T(8,128)}) custom-call(f32[32,4,128]{2,1,0:T(4,128)S(1)} %all_to_all.10.got_ref, bf16[3,3,128,256]{3,2,1,0:T(8,128)(2,1)S(1)} %get-tuple-element.39.parts_ref, f32[3,1,256]{2,1,0:T(1,128)S(1)} %get-tuple-element.40.snap_ref, ...), custom_call_target="tpu_custom_call" | custom-call | tf_op jit(solution)/shard_map/pallas_call | solution.py:520
  (9 shorter events, 0.1 us)
Async XLA Ops:
  0.8 1.0 %copy-start.2 = (f32[4,8,16,128]{3,2,1,0:T(8,128)S(1)}, f32[4,8,16,128]{3,2,1,0:T(8,128)}, u32[]{:S(2)}) copy-start(f32[4,8,16,128]{3,2,1,0:T(8,128)} %param.3) | copy-start | bytes 786436
  1.7 7.1 %copy-start.3 = (f32[4,8,16,128]{3,2,1,0:T(8,128)S(1)}, f32[4,8,16,128]{3,2,1,0:T(8,128)}, u32[]{:S(2)}) copy-start(f32[4,8,16,128]{3,2,1,0:T(8,128)} %param.3) | copy-start | bytes 786436
  1.8 6.7 %collective-permute-start = (f32[4,24,128]{2,1,0:T(8,128)S(1)}, f32[4,24,128]{2,1,0:T(8,128)S(1)}, u32[]{:S(2)}, u32[]{:S(2)}) collective-permute-start(f32[4,24,128]{2,1,0:T(8,128)S(1)} %get-tuple-element.24), channel_id=1, source_target_pairs={{0,1},{1,0},{2,4},{3,5},{4,2},{5,3},{6,7},{7,6},{8,9},{9,8},{10,12... | collective-permute-start | bytes 147464 | tf_op jit(solution)/shard_map/ppermute | solution.py:61
  2.3 6.6 %collective-permute-start.1 = (f32[4,24,128]{2,1,0:T(8,128)S(1)}, f32[4,24,128]{2,1,0:T(8,128)S(1)}, u32[]{:S(2)}, u32[]{:S(2)}) collective-permute-start(f32[4,24,128]{2,1,0:T(8,128)S(1)} %get-tuple-element.25), channel_id=1, source_target_pairs={{0,2},{2,0},{4,6},{6,4},{1,3},{3,1},{5,7},{7,5},{8,10},{10,8},{12,... | collective-permute-start | bytes 147464 | tf_op jit(solution)/shard_map/ppermute | solution.py:62
  6.3 1.0 %copy-start = (f32[127,3,256]{2,0,1:T(8,128)S(1)}, f32[127,3,256]{2,0,1:T(8,128)}, u32[]{:S(2)}) copy-start(f32[127,3,256]{2,0,1:T(8,128)} %param.4) | copy-start | bytes 1170436
  8.9 7.4 %collective-permute-start.2 = (f32[4,56,128]{2,1,0:T(8,128)S(1)}, f32[4,56,128]{2,1,0:T(8,128)S(1)}, u32[]{:S(2)}, u32[]{:S(2)}) collective-permute-start(f32[4,56,128]{2,1,0:T(8,128)S(1)} %get-tuple-element.31), channel_id=1, source_target_pairs={{0,8},{8,16},{16,24},{24,0},{1,9},{9,17},{17,25},{25,1},{2,10},{10... | collective-permute-start | bytes 344072 | tf_op jit(solution)/shard_map/ppermute | solution.py:50
  10.6 6.2 %collective-permute-start.3 = (f32[4,56,128]{2,1,0:T(8,128)S(1)}, f32[4,56,128]{2,1,0:T(8,128)S(1)}, u32[]{:S(2)}, u32[]{:S(2)}) collective-permute-start(f32[4,56,128]{2,1,0:T(8,128)S(1)} %get-tuple-element.32), channel_id=1, source_target_pairs={{8,0},{16,8},{24,16},{0,24},{9,1},{17,9},{25,17},{1,25},{10,2},{18... | collective-permute-start | bytes 344072 | tf_op jit(solution)/shard_map/ppermute | solution.py:50
  12.8 10.5 %all-to-all-start = ((f32[32,4,128]{2,1,0:T(4,128)}), f32[32,4,128]{2,1,0:T(4,128)S(1)}, u32[]{:S(2)}, u32[]{:S(2)}) async-start(f32[32,4,128]{2,1,0:T(4,128)} %get-tuple-element.27), calls=%async_computation | async-start | bytes 131072 | tf_op jit(solution)/shard_map/all_to_all | solution.py:482
  16.7 0.7 %copy-start.4 = (s32[256]{0:T(256)S(1)}, s32[256]{0:T(256)}, u32[]{:S(2)}) copy-start(s32[256]{0:T(256)} %param.5) | copy-start | bytes 3076
  17.0 1.3 %copy-start.1 = (f32[127,3,256]{2,0,1:T(8,128)S(1)}, f32[127,3,256]{2,0,1:T(8,128)}, u32[]{:S(2)}) copy-start(f32[127,3,256]{2,0,1:T(8,128)} %param.4) | copy-start | bytes 1170436
  17.0 1.3 %collective-permute-start.4 = (f32[4,24,128]{2,1,0:T(8,128)S(1)}, f32[4,24,128]{2,1,0:T(8,128)S(1)}, u32[]{:S(2)}, u32[]{:S(2)}) collective-permute-start(f32[4,24,128]{2,1,0:T(8,128)S(1)} %get-tuple-element.36.own_ref), channel_id=1, source_target_pairs={{0,1},{1,0},{2,3},{3,2},{4,5},{5,4},{6,7},{7,6},{8,9},{9,8},{10,11... | collective-permute-start | bytes 147464 | tf_op jit(solution)/shard_map/ppermute | solution.py:492

commit v16 on v15

--- a/solution.py
+++ b/solution.py
@@ -62,11 +62,16 @@
     return lax.ppermute(block_even, axis, even), from_odd
 
 
-LOWER_WALL, UPPER_WALL, ODD_Y = range(3)
-
-
-def flag(flags_ref, which):
-    return flags_ref[which : which + 1] == 1
+def at_lower_wall():
+    return lax.axis_index("gy") == 0
+
+
+def at_upper_wall():
+    return lax.axis_index("gy") == lax.axis_size("gy") - 1
+
+
+def odd_place():
+    return lax.axis_index("gy") % 2 == 1
 
 
 def pack_upper(rows, tall):
@@ -105,9 +110,9 @@
 HALO = 2 * DEPTH + GAP
 
 
-def strips_kernel(planes, flags_ref, flow_ref, odd_ref, even_ref):
+def strips_kernel(planes, flow_ref, odd_ref, even_ref):
     ny = flow_ref.shape[1] // planes
-    odd = flag(flags_ref, ODD_Y)
+    odd = odd_place()
     for f in range(flow_ref.shape[0]):
         for j in range(DEPTH):
             bottom = flow_ref[f, pl.ds(j, planes, stride=ny), :]
@@ -116,9 +121,9 @@
             odd_ref[f, planes * j : planes * j + planes] = jnp.where(odd, top, bottom)
 
 
-def walls_kernel(planes, flags_ref, flow_ref, odd_ref, even_ref, mid_ref, first_ref, last_ref):
+def walls_kernel(planes, flow_ref, odd_ref, even_ref, mid_ref, first_ref, last_ref):
     fields, cells, nz = flow_ref.shape
-    odd_y = flag(flags_ref, ODD_Y)
+    odd_y = odd_place()
     ny = cells // planes
     rows = ny + HALO
     sub = lax.broadcasted_iota(jnp.int32, (HALO, nz), 0)
@@ -131,12 +136,12 @@
             part = slice(planes * k, planes * k + planes)
             if j < DEPTH:
                 value = jnp.where(odd_y, odd_ref[f, part], even_ref[f, part])
-                value = jnp.where(flag(flags_ref, UPPER_WALL), 0.0, value)
+                value = jnp.where(at_upper_wall(), 0.0, value)
             elif j < DEPTH + GAP:
                 value = empty
             else:
                 value = jnp.where(odd_y, even_ref[f, part], odd_ref[f, part])
-                value = jnp.where(flag(flags_ref, LOWER_WALL), 0.0, value)
+                value = jnp.where(at_lower_wall(), 0.0, value)
             mid_ref[f, pl.ds(ny + j, planes, stride=rows), :] = value
         for face_ref, begin, near, next_one in (
             (first_ref, 0, 0, 1), (last_ref, planes - DEPTH, planes - 1, planes - 2)
@@ -215,10 +220,10 @@
     return out
 
 
-def beyond_walls(flags_ref, ny, shape):
+def beyond_walls(ny, shape):
     row = lax.broadcasted_iota(jnp.int32, shape, 0)
-    below = (row >= ny + DEPTH + GAP) & flag(flags_ref, LOWER_WALL)
-    above = (row >= ny) & (row < ny + DEPTH) & flag(flags_ref, UPPER_WALL)
+    below = (row >= ny + DEPTH + GAP) & at_lower_wall()
+    above = (row >= ny) & (row < ny + DEPTH) & at_upper_wall()
     return below | above
 
 
@@ -248,11 +253,11 @@
     return jnp.where(outside, 0.0, 0.75 * begin + 0.25 * (value + DT_STEP * rate))
 
 
-def first_kernel(flags_ref, sample_hbm, mid_ref, xlo_ref, xhi_ref, one_ref, sample_ref, sem):
+def first_kernel(sample_hbm, mid_ref, xlo_ref, xhi_ref, one_ref, sample_ref, sem):
     copy = pltpu.make_async_copy(sample_hbm, sample_ref, sem)
     copy.start()
     fields, nx, rows, nz = mid_ref.shape
-    outside = beyond_walls(flags_ref, rows - HALO, (rows, nz))
+    outside = beyond_walls(rows - HALO, (rows, nz))
     for i in range(1, nx + 2 * DEPTH - 1):
         centre, rate = plane_rates(functools.partial(plane_of, mid_ref, xlo_ref, xhi_ref), i, rows)
         for f in range(4):
@@ -261,7 +266,7 @@
 
 
 def step_kernel(
-    flags_ref, mid_ref, xlo_ref, xhi_ref, first_ref, own_ref, low_ref, high_ref, basis_ref, sample_ref,
+    mid_ref, xlo_ref, xhi_ref, first_ref, own_ref, low_ref, high_ref, basis_ref, sample_ref,
     flow_ref, snap_ref, cross_ref,
     one_ref, two_ref,
 ):
@@ -270,7 +275,7 @@
     modes = basis_ref.shape[1]
     planes = nx + 2 * DEPTH
     lane = lax.broadcasted_iota(jnp.int32, (rows, nz), 1)
-    outside = beyond_walls(flags_ref, ny, (rows, nz))
+    outside = beyond_walls(ny, (rows, nz))
     every = range(4)
     start = functools.partial(plane_of, mid_ref, xlo_ref, xhi_ref)
 
@@ -452,13 +457,10 @@
     quarter = size // 4
     per = -(-3 * quarter // devices)
 
-    place = lax.axis_index("gy")
-    flags = [place == 0, place == lax.axis_size("gy") - 1, place % 2 == 1]
-    flags = jnp.broadcast_to(jnp.stack(flags).astype(jnp.int32)[:, None], (len(flags), nz))
     strip = shape((fields, nx * DEPTH, nz))
     strips = call(
-        functools.partial(strips_kernel, nx), out_shape=(strip, strip), in_specs=[VMEM] * 2, out_specs=(VMEM, VMEM)
-    )(flags, flat)
+        functools.partial(strips_kernel, nx), out_shape=(strip, strip), in_specs=[VMEM], out_specs=(VMEM, VMEM)
+    )(flat)
     y_even, y_odd = pairs(*strips, "gy", "gz")
     gram, basis_parts = call(
         gram_kernel,
@@ -474,9 +476,9 @@
     mid, first, last = call(
         functools.partial(walls_kernel, nx),
         out_shape=(shape((fields, nx * rows, nz)), face, face),
-        in_specs=[VMEM] * 4,
+        in_specs=[VMEM] * 3,
         out_specs=(VMEM,) * 3,
-    )(flags, flat, y_odd, y_even)
+    )(flat, y_odd, y_even)
     mid = mid.reshape(fields, nx, rows, nz)
     low_face, high_face = neighbours(first, last, "gx")
     parts = lax.all_to_all(gram, ALL, 0, 0)
@@ -498,20 +500,20 @@
             shape((fields, nx + 2 * DEPTH - 2, rows, nz)),
             jax.ShapeDtypeStruct((1, points), sample.dtype),
         ),
-        in_specs=[VMEM, whole] + [VMEM] * 3,
+        in_specs=[whole] + [VMEM] * 3,
         out_specs=(VMEM, VMEM),
         scratch_shapes=[pltpu.SemaphoreType.DMA],
-    )(flags, sample.reshape(1, points), mid, xlo, xhi)
+    )(sample.reshape(1, points), mid, xlo, xhi)
     flow_new, snapshot, cross = call(
         step_kernel,
         out_shape=(shape(flow.shape), shape((comps, 1, points)), shape((1, size))),
-        in_specs=[VMEM] * 10,
+        in_specs=[VMEM] * 9,
         out_specs=(VMEM, VMEM, VMEM),
         scratch_shapes=[
             pltpu.VMEM((fields, nx + 2 * DEPTH - 2, rows, nz), jnp.float32),
             pltpu.VMEM((fields, nx + 2 * DEPTH - 4, rows, nz), jnp.float32),
         ],
-    )(flags, mid, xlo, xhi, begun, packed, low, high, bricks, cells)
+    )(mid, xlo, xhi, begun, packed, low, high, bricks, cells)
 
     send = call(
         merge_kernel, out_shape=shape((devices, per + 1, size)), in_specs=[VMEM] * 2, out_specs=VMEM

time: 36.6 us -> 36.4 us (level)
  no operation moved by 1% of the time
where the time goes in v16:
time: 36.4 us; the launch traced here: 36.1 us
  starting transfers between devices  11.6 us (32%)
  blocking collectives  9.12 us (25%)
  Pallas kernels  7.83 us (22%)
  waiting for transfers between devices  4.59 us (13%)
  local copies, waits for them, and re-layouts  2.29 us (6%)
  between operations  0.7 us (2%)
    all_to_all x1, blocking collectives, local(): got = lax.all_to_all(send, ALL, 0, 0)  9.12 us
    ppermute x1, starting transfers between devices, pairs(): return (lax.ppermute(block_even, axis, even), from_odd)  3.98 us
    pallas_call x1, Pallas kernels, local(): call(functools.partial(final_kernel, count), out_shape=(shape((comps, siz...  3.83 us
    all_to_all x1, starting transfers between devices, local(): parts = lax.all_to_all(gram, ALL, 0, 0)  3.18 us
    all_to_all x1, waiting for transfers between devices, local(): parts = lax.all_to_all(gram, ALL, 0, 0)  3.16 us
    unnamed x10, local copies, waits for them, and re-layouts  2.29 us
    ppermute x1, starting transfers between devices, neighbours(): lax.ppermute(block_low, axis, backward)  2.25 us
    pallas_call x1, Pallas kernels, local(): call(step_kernel, out_shape=(shape(flow.shape), shape((comps, 1, points))...  1.87 us
  transfers between devices with their start and end apart: 6, of which 5 were waited for; matrix products, arithmetic and copies ran while one was open for 0% of the time, Pallas kernels for 11%

profile of v16, /device:TPU:0, one launch (start us, length us, event | category | flops | bytes accessed | tf_op | source)
XLA Modules:
  0.0 36.1 jit_solution(11692938045158318273)
XLA Ops:
  0.6 0.9 %copy-done.2 = f32[4,8,16,128]{3,2,1,0:T(8,128)S(1)} copy-done((f32[4,8,16,128]{3,2,1,0:T(8,128)S(1)}, f32[4,8,16,128]{3,2,1,0:T(8,128)}, u32[]{:S(2)}) %copy-start.2) | copy-done | bytes 262168
  1.6 0.5 %collective-permute-start = (f32[4,24,128]{2,1,0:T(8,128)S(1)}, f32[4,24,128]{2,1,0:T(8,128)S(1)}, u32[]{:S(2)}, u32[]{:S(2)}) collective-permute-start(f32[4,24,128]{2,1,0:T(8,128)S(1)} %get-tuple-element.24), channel_id=1, source_target_pairs={{0,1},{1,0},{2,4},{3,5},{4,2},{5,3},{6,7},{7,6},{8,9},{9,8},{10,12... | collective-permute-start | bytes 147464 | tf_op jit(solution)/shard_map/ppermute | solution.py:61
  2.1 4.0 %collective-permute-start.1 = (f32[4,24,128]{2,1,0:T(8,128)S(1)}, f32[4,24,128]{2,1,0:T(8,128)S(1)}, u32[]{:S(2)}, u32[]{:S(2)}) collective-permute-start(f32[4,24,128]{2,1,0:T(8,128)S(1)} %get-tuple-element.25), channel_id=1, source_target_pairs={{0,2},{2,0},{4,6},{6,4},{1,3},{3,1},{5,7},{7,5},{8,10},{10,8},{12,... | collective-permute-start | bytes 147464 | tf_op jit(solution)/shard_map/ppermute | solution.py:62
  6.1 1.0 %copy-done = f32[127,3,256]{2,0,1:T(8,128)S(1)} copy-done((f32[127,3,256]{2,0,1:T(8,128)S(1)}, f32[127,3,256]{2,0,1:T(8,128)}, u32[]{:S(2)}) %copy-start) | copy-done | bytes 390168
  7.1 1.2 %shard_map.59 = (f32[32,4,128]{2,1,0:T(4,128)}, bf16[3,3,128,256]{3,2,1,0:T(8,128)(2,1)S(1)}) custom-call(f32[3,127,256]{2,1,0:T(8,128)S(1)} %bitcast.8), custom_call_target="tpu_custom_call" | custom-call | tf_op jit(solution)/shard_map/pallas_call | solution.py:465
  8.3 0.0 collective-permute-done.odd_ref
  8.4 0.4 collective-permute-done.1.even_ref
  8.7 0.1 shard_map.60
  8.8 1.6 %collective-permute-start.2 = (f32[4,56,128]{2,1,0:T(8,128)S(1)}, f32[4,56,128]{2,1,0:T(8,128)S(1)}, u32[]{:S(2)}, u32[]{:S(2)}) collective-permute-start(f32[4,56,128]{2,1,0:T(8,128)S(1)} %get-tuple-element.31), channel_id=1, source_target_pairs={{0,8},{8,16},{16,24},{24,0},{1,9},{9,17},{17,25},{25,1},{2,10},{10... | collective-permute-start | bytes 344072 | tf_op jit(solution)/shard_map/ppermute | solution.py:50
  10.4 2.2 %collective-permute-start.3 = (f32[4,56,128]{2,1,0:T(8,128)S(1)}, f32[4,56,128]{2,1,0:T(8,128)S(1)}, u32[]{:S(2)}, u32[]{:S(2)}) collective-permute-start(f32[4,56,128]{2,1,0:T(8,128)S(1)} %get-tuple-element.32), channel_id=1, source_target_pairs={{8,0},{16,8},{24,16},{0,24},{9,1},{17,9},{25,17},{1,25},{10,2},{18... | collective-permute-start | bytes 344072 | tf_op jit(solution)/shard_map/ppermute | solution.py:50
  12.6 3.2 %all-to-all-start = ((f32[32,4,128]{2,1,0:T(4,128)}), f32[32,4,128]{2,1,0:T(4,128)S(1)}, u32[]{:S(2)}, u32[]{:S(2)}) async-start(f32[32,4,128]{2,1,0:T(4,128)} %get-tuple-element.27), calls=%async_computation | async-start | bytes 131072 | tf_op jit(solution)/shard_map/all_to_all | solution.py:484
  15.8 0.3 collective-permute-done.2.low_ref
  16.2 0.4 %collective-permute-done.3.high_ref = f32[4,56,128]{2,1,0:T(8,128)S(1)} collective-permute-done((f32[4,56,128]{2,1,0:T(8,128)S(1)}, f32[4,56,128]{2,1,0:T(8,128)S(1)}, u32[]{:S(2)}, u32[]{:S(2)}) %collective-permute-start.3) | collective-permute-done | bytes 114720 | tf_op jit(solution)/shard_map/ppermute | solution.py:50
  16.6 0.2 shard_map.61
  16.8 0.0 copy-start.1
  16.8 0.1 collective-permute-start.4
  16.9 0.3 copy-done.4
  17.2 0.5 %shard_map.62 = (f32[4,12,24,128]{3,2,1,0:T(8,128)S(1)}, s32[1,256]{1,0:T(1,128)S(1)}) custom-call(s32[1,256]{1,0:T(1,128)S(1)} %bitcast.12, f32[4,8,24,128]{3,2,1,0:T(8,128)S(1)} %bitcast.6, f32[4,3,24,128]{3,2,1,0:T(8,128)S(1)} %get-tuple-element.33.xlo_ref, f32[4,3,24,128]{3,2,1,0:T(8,128)S(1)} %get-tuple-element.34.xhi_ref), custom_call_target="tpu_custom_call" | custom-call | tf_op jit(solution)/shard_map/pallas_call | solution.py:497
  17.8 0.3 collective-permute-done.4.low_ref.high_ref
  18.1 0.0 copy-done.1
  18.1 1.9 %shard_map.63 = (f32[4,8,16,128]{3,2,1,0:T(8,128)S(1)}, f32[3,1,256]{2,1,0:T(1,128)S(1)}, f32[1,128]{1,0:T(1,128)S(1)}) custom-call(f32[4,8,24,128]{3,2,1,0:T(8,128)S(1)} %bitcast.7, f32[4,3,24,128]{3,2,1,0:T(8,128)S(1)} %get-tuple-element.33.xlo_ref, f32[4,3,24,128]{3,2,1,0:T(8,128)S(1)} %get-tuple-element.34.xhi_ref, ...), custom_call_target="tpu_custom_call" | custom-call | tf_op jit(solution)/shard_map/pallas_call | solution.py:507
  20.0 3.2 %all-to-all-done.parts_ref = f32[32,4,128]{2,1,0:T(4,128)S(1)} async-done(((f32[32,4,128]{2,1,0:T(4,128)}), f32[32,4,128]{2,1,0:T(4,128)S(1)}, u32[]{:S(2)}, u32[]{:S(2)}) %all-to-all-start) | async-done | bytes 65568 | tf_op jit(solution)/shard_map/all_to_all | solution.py:484
  23.2 9.1 %all_to_all.10.got_ref = f32[32,4,128]{2,1,0:T(4,128)S(1)} all-to-all(f32[32,4,128]{2,1,0:T(4,128)S(1)} %shard_map.64), channel_id=1, replica_groups=mesh['gx'=4,'gy'=4,'gz'=2] {'gz','gy','gx'}, dimensions={0} | all-to-all | bytes 131072 | tf_op jit(solution)/shard_map/all_to_all | solution.py:521
  32.3 3.8 %shard_map.65 = (f32[3,128,256]{2,1,0:T(8,128)}, f32[128,128]{1,0:T(8,128)}, f32[4,8,16,128]{3,2,1,0:T(8,128)}) custom-call(f32[32,4,128]{2,1,0:T(4,128)S(1)} %all_to_all.10.got_ref, bf16[3,3,128,256]{3,2,1,0:T(8,128)(2,1)S(1)} %get-tuple-element.39.parts_ref, f32[3,1,256]{2,1,0:T(1,128)S(1)} %get-tuple-element.40.snap_ref, ...), custom_call_target="tpu_custom_call" | custom-call | tf_op jit(solution)/shard_map/pallas_call | solution.py:522
  (7 shorter events, 0.1 us)
Async XLA Ops:
  0.6 1.0 %copy-start.2 = (f32[4,8,16,128]{3,2,1,0:T(8,128)S(1)}, f32[4,8,16,128]{3,2,1,0:T(8,128)}, u32[]{:S(2)}) copy-start(f32[4,8,16,128]{3,2,1,0:T(8,128)} %param.3) | copy-start | bytes 786436
  1.6 7.1 %copy-start.3 = (f32[4,8,16,128]{3,2,1,0:T(8,128)S(1)}, f32[4,8,16,128]{3,2,1,0:T(8,128)}, u32[]{:S(2)}) copy-start(f32[4,8,16,128]{3,2,1,0:T(8,128)} %param.3) | copy-start | bytes 786436
  1.6 6.7 %collective-permute-start = (f32[4,24,128]{2,1,0:T(8,128)S(1)}, f32[4,24,128]{2,1,0:T(8,128)S(1)}, u32[]{:S(2)}, u32[]{:S(2)}) collective-permute-start(f32[4,24,128]{2,1,0:T(8,128)S(1)} %get-tuple-element.24), channel_id=1, source_target_pairs={{0,1},{1,0},{2,4},{3,5},{4,2},{5,3},{6,7},{7,6},{8,9},{9,8},{10,12... | collective-permute-start | bytes 147464 | tf_op jit(solution)/shard_map/ppermute | solution.py:61
  2.1 6.6 %collective-permute-start.1 = (f32[4,24,128]{2,1,0:T(8,128)S(1)}, f32[4,24,128]{2,1,0:T(8,128)S(1)}, u32[]{:S(2)}, u32[]{:S(2)}) collective-permute-start(f32[4,24,128]{2,1,0:T(8,128)S(1)} %get-tuple-element.25), channel_id=1, source_target_pairs={{0,2},{2,0},{4,6},{6,4},{1,3},{3,1},{5,7},{7,5},{8,10},{10,8},{12,... | collective-permute-start | bytes 147464 | tf_op jit(solution)/shard_map/ppermute | solution.py:62
  6.1 1.0 %copy-start = (f32[127,3,256]{2,0,1:T(8,128)S(1)}, f32[127,3,256]{2,0,1:T(8,128)}, u32[]{:S(2)}) copy-start(f32[127,3,256]{2,0,1:T(8,128)} %param.4) | copy-start | bytes 1170436
  8.8 7.4 %collective-permute-start.2 = (f32[4,56,128]{2,1,0:T(8,128)S(1)}, f32[4,56,128]{2,1,0:T(8,128)S(1)}, u32[]{:S(2)}, u32[]{:S(2)}) collective-permute-start(f32[4,56,128]{2,1,0:T(8,128)S(1)} %get-tuple-element.31), channel_id=1, source_target_pairs={{0,8},{8,16},{16,24},{24,0},{1,9},{9,17},{17,25},{25,1},{2,10},{10... | collective-permute-start | bytes 344072 | tf_op jit(solution)/shard_map/ppermute | solution.py:50
  10.4 6.2 %collective-permute-start.3 = (f32[4,56,128]{2,1,0:T(8,128)S(1)}, f32[4,56,128]{2,1,0:T(8,128)S(1)}, u32[]{:S(2)}, u32[]{:S(2)}) collective-permute-start(f32[4,56,128]{2,1,0:T(8,128)S(1)} %get-tuple-element.32), channel_id=1, source_target_pairs={{8,0},{16,8},{24,16},{0,24},{9,1},{17,9},{25,17},{1,25},{10,2},{18... | collective-permute-start | bytes 344072 | tf_op jit(solution)/shard_map/ppermute | solution.py:50
  12.6 10.5 %all-to-all-start = ((f32[32,4,128]{2,1,0:T(4,128)}), f32[32,4,128]{2,1,0:T(4,128)S(1)}, u32[]{:S(2)}, u32[]{:S(2)}) async-start(f32[32,4,128]{2,1,0:T(4,128)} %get-tuple-element.27), calls=%async_computation | async-start | bytes 131072 | tf_op jit(solution)/shard_map/all_to_all | solution.py:484
  16.6 0.7 %copy-start.4 = (s32[256]{0:T(256)S(1)}, s32[256]{0:T(256)}, u32[]{:S(2)}) copy-start(s32[256]{0:T(256)} %param.5) | copy-start | bytes 3076
  16.8 1.3 %copy-start.1 = (f32[127,3,256]{2,0,1:T(8,128)S(1)}, f32[127,3,256]{2,0,1:T(8,128)}, u32[]{:S(2)}) copy-start(f32[127,3,256]{2,0,1:T(8,128)} %param.4) | copy-start | bytes 1170436
  16.8 1.3 %collective-permute-start.4 = (f32[4,24,128]{2,1,0:T(8,128)S(1)}, f32[4,24,128]{2,1,0:T(8,128)S(1)}, u32[]{:S(2)}, u32[]{:S(2)}) collective-permute-start(f32[4,24,128]{2,1,0:T(8,128)S(1)} %get-tuple-element.36.own_ref), channel_id=1, source_target_pairs={{0,1},{1,0},{2,3},{3,2},{4,5},{5,4},{6,7},{7,6},{8,9},{9,8},{10,11... | collective-permute-start | bytes 147464 | tf_op jit(solution)/shard_map/ppermute | solution.py:494

commit v17 on v16

--- a/solution.py
+++ b/solution.py
@@ -387,9 +387,12 @@
             change = dot_stacked(done[:, 0:size], done)
             work_ref[base + tall : size, :] = work_ref[base + tall : size, :] - change[base + tall : size]
         factor_ref[base : base + tall, :] = jnp.where(lane >= row + base, done[:, 0:size], 0.0)
-        if k < 2:
+        if k == 3:
+            copies.append(pltpu.make_async_copy(factor_ref, factor_hbm, sems.at[1]))
+            copies[-1].start()
+        if k == 0:
             continue
-        begin, count_rows = (0, base + tall) if k == 2 else (base, tall)
+        begin, count_rows = (0, base + tall) if k == 1 else (base, tall)
         inverse = work_ref[begin : base + tall, size : 2 * size]
         pieces = jnp.concatenate(three_parts(inverse), axis=0)
         for c in range(comps):
@@ -402,10 +405,8 @@
                 value = value + inverse[:, size - 1 : size] * snap_ref[c]
             basis_out_ref[c, begin : base + tall, :] = value
         rows = (slice(None), pl.ds(begin, count_rows), slice(None))
-        copies.append(pltpu.make_async_copy(basis_out_ref.at[rows], basis_hbm.at[rows], sems.at[k]))
+        copies.append(pltpu.make_async_copy(basis_out_ref.at[rows], basis_hbm.at[rows], sems.at[1 + k]))
         copies[-1].start()
-    copies.append(pltpu.make_async_copy(factor_ref, factor_hbm, sems.at[1]))
-    copies[-1].start()
     for copy in copies:
         copy.wait()
 
@@ -529,7 +530,7 @@
             pltpu.VMEM((size, 2 * size), jnp.float32),
             pltpu.VMEM((comps, size, points), jnp.float32),
             pltpu.VMEM((size, size), jnp.float32),
-            pltpu.SemaphoreType.DMA((4,)),
+            pltpu.SemaphoreType.DMA((5,)),
         ],
     )(got, basis_parts, snapshot, flow_new)
     return flow_next, jnp.transpose(basis_next, (1, 0, 2)), factor

time: 36.4 us -> 36.3 us (level)
  no operation moved by 1% of the time
where the time goes in v17:
time: 36.3 us; the launch traced here: 36.1 us
  starting transfers between devices  11.6 us (32%)
  blocking collectives  9.12 us (25%)
  Pallas kernels  7.76 us (21%)
  waiting for transfers between devices  4.59 us (13%)
  local copies, waits for them, and re-layouts  2.29 us (6%)
  between operations  0.7 us (2%)
    all_to_all x1, blocking collectives, local(): got = lax.all_to_all(send, ALL, 0, 0)  9.12 us
    ppermute x1, starting transfers between devices, pairs(): return (lax.ppermute(block_even, axis, even), from_odd)  3.98 us
    pallas_call x1, Pallas kernels, local(): call(functools.partial(final_kernel, count), out_shape=(shape((comps, siz...  3.76 us
    all_to_all x1, starting transfers between devices, local(): parts = lax.all_to_all(gram, ALL, 0, 0)  3.18 us
    all_to_all x1, waiting for transfers between devices, local(): parts = lax.all_to_all(gram, ALL, 0, 0)  3.16 us
    unnamed x10, local copies, waits for them, and re-layouts  2.29 us
    ppermute x1, starting transfers between devices, neighbours(): lax.ppermute(block_low, axis, backward)  2.25 us
    pallas_call x1, Pallas kernels, local(): call(step_kernel, out_shape=(shape(flow.shape), shape((comps, 1, points))...  1.87 us
  transfers between devices with their start and end apart: 6, of which 5 were waited for; matrix products, arithmetic and copies ran while one was open for 0% of the time, Pallas kernels for 11%

profile of v17, /device:TPU:0, one launch (start us, length us, event | category | flops | bytes accessed | tf_op | source)
XLA Modules:
  0.0 36.1 jit_solution(7069924817449841710)
XLA Ops:
  0.6 0.9 %copy-done.2 = f32[4,8,16,128]{3,2,1,0:T(8,128)S(1)} copy-done((f32[4,8,16,128]{3,2,1,0:T(8,128)S(1)}, f32[4,8,16,128]{3,2,1,0:T(8,128)}, u32[]{:S(2)}) %copy-start.2) | copy-done | bytes 262168
  1.6 0.5 %collective-permute-start = (f32[4,24,128]{2,1,0:T(8,128)S(1)}, f32[4,24,128]{2,1,0:T(8,128)S(1)}, u32[]{:S(2)}, u32[]{:S(2)}) collective-permute-start(f32[4,24,128]{2,1,0:T(8,128)S(1)} %get-tuple-element.24), channel_id=1, source_target_pairs={{0,1},{1,0},{2,4},{3,5},{4,2},{5,3},{6,7},{7,6},{8,9},{9,8},{10,12... | collective-permute-start | bytes 147464 | tf_op jit(solution)/shard_map/ppermute | solution.py:61
  2.1 4.0 %collective-permute-start.1 = (f32[4,24,128]{2,1,0:T(8,128)S(1)}, f32[4,24,128]{2,1,0:T(8,128)S(1)}, u32[]{:S(2)}, u32[]{:S(2)}) collective-permute-start(f32[4,24,128]{2,1,0:T(8,128)S(1)} %get-tuple-element.25), channel_id=1, source_target_pairs={{0,2},{2,0},{4,6},{6,4},{1,3},{3,1},{5,7},{7,5},{8,10},{10,8},{12,... | collective-permute-start | bytes 147464 | tf_op jit(solution)/shard_map/ppermute | solution.py:62
  6.1 1.0 %copy-done = f32[127,3,256]{2,0,1:T(8,128)S(1)} copy-done((f32[127,3,256]{2,0,1:T(8,128)S(1)}, f32[127,3,256]{2,0,1:T(8,128)}, u32[]{:S(2)}) %copy-start) | copy-done | bytes 390168
  7.1 1.2 %shard_map.59 = (f32[32,4,128]{2,1,0:T(4,128)}, bf16[3,3,128,256]{3,2,1,0:T(8,128)(2,1)S(1)}) custom-call(f32[3,127,256]{2,1,0:T(8,128)S(1)} %bitcast.8), custom_call_target="tpu_custom_call" | custom-call | tf_op jit(solution)/shard_map/pallas_call | solution.py:466
  8.3 0.0 collective-permute-done.odd_ref
  8.4 0.4 collective-permute-done.1.even_ref
  8.7 0.1 shard_map.60
  8.8 1.6 %collective-permute-start.2 = (f32[4,56,128]{2,1,0:T(8,128)S(1)}, f32[4,56,128]{2,1,0:T(8,128)S(1)}, u32[]{:S(2)}, u32[]{:S(2)}) collective-permute-start(f32[4,56,128]{2,1,0:T(8,128)S(1)} %get-tuple-element.31), channel_id=1, source_target_pairs={{0,8},{8,16},{16,24},{24,0},{1,9},{9,17},{17,25},{25,1},{2,10},{10... | collective-permute-start | bytes 344072 | tf_op jit(solution)/shard_map/ppermute | solution.py:50
  10.4 2.2 %collective-permute-start.3 = (f32[4,56,128]{2,1,0:T(8,128)S(1)}, f32[4,56,128]{2,1,0:T(8,128)S(1)}, u32[]{:S(2)}, u32[]{:S(2)}) collective-permute-start(f32[4,56,128]{2,1,0:T(8,128)S(1)} %get-tuple-element.32), channel_id=1, source_target_pairs={{8,0},{16,8},{24,16},{0,24},{9,1},{17,9},{25,17},{1,25},{10,2},{18... | collective-permute-start | bytes 344072 | tf_op jit(solution)/shard_map/ppermute | solution.py:50
  12.6 3.2 %all-to-all-start = ((f32[32,4,128]{2,1,0:T(4,128)}), f32[32,4,128]{2,1,0:T(4,128)S(1)}, u32[]{:S(2)}, u32[]{:S(2)}) async-start(f32[32,4,128]{2,1,0:T(4,128)} %get-tuple-element.27), calls=%async_computation | async-start | bytes 131072 | tf_op jit(solution)/shard_map/all_to_all | solution.py:485
  15.8 0.3 collective-permute-done.2.low_ref
  16.2 0.4 %collective-permute-done.3.high_ref = f32[4,56,128]{2,1,0:T(8,128)S(1)} collective-permute-done((f32[4,56,128]{2,1,0:T(8,128)S(1)}, f32[4,56,128]{2,1,0:T(8,128)S(1)}, u32[]{:S(2)}, u32[]{:S(2)}) %collective-permute-start.3) | collective-permute-done | bytes 114720 | tf_op jit(solution)/shard_map/ppermute | solution.py:50
  16.6 0.2 shard_map.61
  16.8 0.0 copy-start.1
  16.8 0.1 collective-permute-start.4
  16.9 0.3 copy-done.4
  17.2 0.5 %shard_map.62 = (f32[4,12,24,128]{3,2,1,0:T(8,128)S(1)}, s32[1,256]{1,0:T(1,128)S(1)}) custom-call(s32[1,256]{1,0:T(1,128)S(1)} %bitcast.12, f32[4,8,24,128]{3,2,1,0:T(8,128)S(1)} %bitcast.6, f32[4,3,24,128]{3,2,1,0:T(8,128)S(1)} %get-tuple-element.33.xlo_ref, f32[4,3,24,128]{3,2,1,0:T(8,128)S(1)} %get-tuple-element.34.xhi_ref), custom_call_target="tpu_custom_call" | custom-call | tf_op jit(solution)/shard_map/pallas_call | solution.py:498
  17.8 0.3 collective-permute-done.4.low_ref.high_ref
  18.1 0.0 copy-done.1
  18.1 1.9 %shard_map.63 = (f32[4,8,16,128]{3,2,1,0:T(8,128)S(1)}, f32[3,1,256]{2,1,0:T(1,128)S(1)}, f32[1,128]{1,0:T(1,128)S(1)}) custom-call(f32[4,8,24,128]{3,2,1,0:T(8,128)S(1)} %bitcast.7, f32[4,3,24,128]{3,2,1,0:T(8,128)S(1)} %get-tuple-element.33.xlo_ref, f32[4,3,24,128]{3,2,1,0:T(8,128)S(1)} %get-tuple-element.34.xhi_ref, ...), custom_call_target="tpu_custom_call" | custom-call | tf_op jit(solution)/shard_map/pallas_call | solution.py:508
  20.0 3.2 %all-to-all-done.parts_ref = f32[32,4,128]{2,1,0:T(4,128)S(1)} async-done(((f32[32,4,128]{2,1,0:T(4,128)}), f32[32,4,128]{2,1,0:T(4,128)S(1)}, u32[]{:S(2)}, u32[]{:S(2)}) %all-to-all-start) | async-done | bytes 65568 | tf_op jit(solution)/shard_map/all_to_all | solution.py:485
  23.2 9.1 %all_to_all.10.got_ref = f32[32,4,128]{2,1,0:T(4,128)S(1)} all-to-all(f32[32,4,128]{2,1,0:T(4,128)S(1)} %shard_map.64), channel_id=1, replica_groups=mesh['gx'=4,'gy'=4,'gz'=2] {'gz','gy','gx'}, dimensions={0} | all-to-all | bytes 131072 | tf_op jit(solution)/shard_map/all_to_all | solution.py:522
  32.3 3.8 %shard_map.65 = (f32[3,128,256]{2,1,0:T(8,128)}, f32[128,128]{1,0:T(8,128)}, f32[4,8,16,128]{3,2,1,0:T(8,128)}) custom-call(f32[32,4,128]{2,1,0:T(4,128)S(1)} %all_to_all.10.got_ref, bf16[3,3,128,256]{3,2,1,0:T(8,128)(2,1)S(1)} %get-tuple-element.39.parts_ref, f32[3,1,256]{2,1,0:T(1,128)S(1)} %get-tuple-element.40.snap_ref, ...), custom_call_target="tpu_custom_call" | custom-call | tf_op jit(solution)/shard_map/pallas_call | solution.py:523
  (7 shorter events, 0.1 us)
Async XLA Ops:
  0.6 1.0 %copy-start.2 = (f32[4,8,16,128]{3,2,1,0:T(8,128)S(1)}, f32[4,8,16,128]{3,2,1,0:T(8,128)}, u32[]{:S(2)}) copy-start(f32[4,8,16,128]{3,2,1,0:T(8,128)} %param.3) | copy-start | bytes 786436
  1.6 7.1 %copy-start.3 = (f32[4,8,16,128]{3,2,1,0:T(8,128)S(1)}, f32[4,8,16,128]{3,2,1,0:T(8,128)}, u32[]{:S(2)}) copy-start(f32[4,8,16,128]{3,2,1,0:T(8,128)} %param.3) | copy-start | bytes 786436
  1.6 6.7 %collective-permute-start = (f32[4,24,128]{2,1,0:T(8,128)S(1)}, f32[4,24,128]{2,1,0:T(8,128)S(1)}, u32[]{:S(2)}, u32[]{:S(2)}) collective-permute-start(f32[4,24,128]{2,1,0:T(8,128)S(1)} %get-tuple-element.24), channel_id=1, source_target_pairs={{0,1},{1,0},{2,4},{3,5},{4,2},{5,3},{6,7},{7,6},{8,9},{9,8},{10,12... | collective-permute-start | bytes 147464 | tf_op jit(solution)/shard_map/ppermute | solution.py:61
  2.1 6.6 %collective-permute-start.1 = (f32[4,24,128]{2,1,0:T(8,128)S(1)}, f32[4,24,128]{2,1,0:T(8,128)S(1)}, u32[]{:S(2)}, u32[]{:S(2)}) collective-permute-start(f32[4,24,128]{2,1,0:T(8,128)S(1)} %get-tuple-element.25), channel_id=1, source_target_pairs={{0,2},{2,0},{4,6},{6,4},{1,3},{3,1},{5,7},{7,5},{8,10},{10,8},{12,... | collective-permute-start | bytes 147464 | tf_op jit(solution)/shard_map/ppermute | solution.py:62
  6.1 1.0 %copy-start = (f32[127,3,256]{2,0,1:T(8,128)S(1)}, f32[127,3,256]{2,0,1:T(8,128)}, u32[]{:S(2)}) copy-start(f32[127,3,256]{2,0,1:T(8,128)} %param.4) | copy-start | bytes 1170436
  8.8 7.4 %collective-permute-start.2 = (f32[4,56,128]{2,1,0:T(8,128)S(1)}, f32[4,56,128]{2,1,0:T(8,128)S(1)}, u32[]{:S(2)}, u32[]{:S(2)}) collective-permute-start(f32[4,56,128]{2,1,0:T(8,128)S(1)} %get-tuple-element.31), channel_id=1, source_target_pairs={{0,8},{8,16},{16,24},{24,0},{1,9},{9,17},{17,25},{25,1},{2,10},{10... | collective-permute-start | bytes 344072 | tf_op jit(solution)/shard_map/ppermute | solution.py:50
  10.4 6.2 %collective-permute-start.3 = (f32[4,56,128]{2,1,0:T(8,128)S(1)}, f32[4,56,128]{2,1,0:T(8,128)S(1)}, u32[]{:S(2)}, u32[]{:S(2)}) collective-permute-start(f32[4,56,128]{2,1,0:T(8,128)S(1)} %get-tuple-element.32), channel_id=1, source_target_pairs={{8,0},{16,8},{24,16},{0,24},{9,1},{17,9},{25,17},{1,25},{10,2},{18... | collective-permute-start | bytes 344072 | tf_op jit(solution)/shard_map/ppermute | solution.py:50
  12.6 10.5 %all-to-all-start = ((f32[32,4,128]{2,1,0:T(4,128)}), f32[32,4,128]{2,1,0:T(4,128)S(1)}, u32[]{:S(2)}, u32[]{:S(2)}) async-start(f32[32,4,128]{2,1,0:T(4,128)} %get-tuple-element.27), calls=%async_computation | async-start | bytes 131072 | tf_op jit(solution)/shard_map/all_to_all | solution.py:485
  16.6 0.7 %copy-start.4 = (s32[256]{0:T(256)S(1)}, s32[256]{0:T(256)}, u32[]{:S(2)}) copy-start(s32[256]{0:T(256)} %param.5) | copy-start | bytes 3076
  16.8 1.3 %copy-start.1 = (f32[127,3,256]{2,0,1:T(8,128)S(1)}, f32[127,3,256]{2,0,1:T(8,128)}, u32[]{:S(2)}) copy-start(f32[127,3,256]{2,0,1:T(8,128)} %param.4) | copy-start | bytes 1170436
  16.8 1.3 %collective-permute-start.4 = (f32[4,24,128]{2,1,0:T(8,128)S(1)}, f32[4,24,128]{2,1,0:T(8,128)S(1)}, u32[]{:S(2)}, u32[]{:S(2)}) collective-permute-start(f32[4,24,128]{2,1,0:T(8,128)S(1)} %get-tuple-element.36.own_ref), channel_id=1, source_target_pairs={{0,1},{1,0},{2,3},{3,2},{4,5},{5,4},{6,7},{7,6},{8,9},{9,8},{10,11... | collective-permute-start | bytes 147464 | tf_op jit(solution)/shard_map/ppermute | solution.py:495

commit v18 on v17

--- a/solution.py
+++ b/solution.py
@@ -110,10 +110,16 @@
 HALO = 2 * DEPTH + GAP
 
 
-def strips_kernel(planes, flow_ref, odd_ref, even_ref):
+def strips_kernel(planes, flow_hbm, odd_ref, even_ref, flow_ref, sems):
     ny = flow_ref.shape[1] // planes
     odd = odd_place()
-    for f in range(flow_ref.shape[0]):
+    copies = [
+        pltpu.make_async_copy(flow_hbm.at[f], flow_ref.at[f], sems.at[f]) for f in range(flow_ref.shape[0])
+    ]
+    for copy in copies:
+        copy.start()
+    for f, copy in enumerate(copies):
+        copy.wait()
         for j in range(DEPTH):
             bottom = flow_ref[f, pl.ds(j, planes, stride=ny), :]
             top = flow_ref[f, pl.ds(ny - DEPTH + j, planes, stride=ny), :]
@@ -460,8 +466,12 @@
 
     strip = shape((fields, nx * DEPTH, nz))
     strips = call(
-        functools.partial(strips_kernel, nx), out_shape=(strip, strip), in_specs=[VMEM], out_specs=(VMEM, VMEM)
-    )(flat)
+        functools.partial(strips_kernel, nx),
+        out_shape=(strip, strip),
+        in_specs=[whole],
+        out_specs=(VMEM, VMEM),
+        scratch_shapes=[pltpu.VMEM(flat.shape, jnp.float32), pltpu.SemaphoreType.DMA((fields,))],
+    )(pltpu.with_memory_space_constraint(flat, pltpu.HBM))
     y_even, y_odd = pairs(*strips, "gy", "gz")
     gram, basis_parts = call(
         gram_kernel,

time: 36.3 us -> 36.4 us (level)
  Pallas kernels: 7.76 us -> 8.74 us
  local copies, waits for them, and re-layouts: 2.29 us -> 1.35 us
    pallas_call x1, Pallas kernels: 0.04 us -> 1.02 us  [local(): call(functools.partial(strips_kernel, nx), out_shape=(strip, strip), in_s...]
    unnamed x10 -> x8, local copies, waits for them, and re-layouts: 2.29 us -> 1.35 us
where the time goes in v18:
time: 36.4 us; the launch traced here: 36.1 us
  starting transfers between devices  11.6 us (32%)
  blocking collectives  9.12 us (25%)
  Pallas kernels  8.74 us (24%)
  waiting for transfers between devices  4.59 us (13%)
  local copies, waits for them, and re-layouts  1.35 us (4%)
  between operations  0.71 us (2%)
    all_to_all x1, blocking collectives, local(): got = lax.all_to_all(send, ALL, 0, 0)  9.12 us
    ppermute x1, starting transfers between devices, pairs(): return (lax.ppermute(block_even, axis, even), from_odd)  3.98 us
    pallas_call x1, Pallas kernels, local(): call(functools.partial(final_kernel, count), out_shape=(shape((comps, siz...  3.76 us
    all_to_all x1, starting transfers between devices, local(): parts = lax.all_to_all(gram, ALL, 0, 0)  3.18 us
    all_to_all x1, waiting for transfers between devices, local(): parts = lax.all_to_all(gram, ALL, 0, 0)  3.16 us
    ppermute x1, starting transfers between devices, neighbours(): lax.ppermute(block_low, axis, backward)  2.25 us
    pallas_call x1, Pallas kernels, local(): call(step_kernel, out_shape=(shape(flow.shape), shape((comps, 1, points))...  1.86 us
    ppermute x1, starting transfers between devices, neighbours(): lax.ppermute(block_high, axis, forward)  1.63 us
  transfers between devices with their start and end apart: 6, of which 5 were waited for; matrix products, arithmetic and copies ran while one was open for 0% of the time, Pallas kernels for 11%

profile of v18, /device:TPU:0, one launch (start us, length us, event | category | flops | bytes accessed | tf_op | source)
XLA Modules:
  0.0 36.1 jit_solution(16029946198321187813)
XLA Ops:
  0.6 1.0 %shard_map.58 = (f32[4,24,128]{2,1,0:T(8,128)S(1)}, f32[4,24,128]{2,1,0:T(8,128)S(1)}) custom-call(f32[4,128,128]{2,1,0:T(8,128)} %bitcast.10), custom_call_target="tpu_custom_call" | custom-call | tf_op jit(solution)/shard_map/pallas_call | solution.py:468
  1.7 0.5 %collective-permute-start = (f32[4,24,128]{2,1,0:T(8,128)S(1)}, f32[4,24,128]{2,1,0:T(8,128)S(1)}, u32[]{:S(2)}, u32[]{:S(2)}) collective-permute-start(f32[4,24,128]{2,1,0:T(8,128)S(1)} %get-tuple-element.24), channel_id=1, source_target_pairs={{0,1},{1,0},{2,4},{3,5},{4,2},{5,3},{6,7},{7,6},{8,9},{9,8},{10,12... | collective-permute-start | bytes 147464 | tf_op jit(solution)/shard_map/ppermute | solution.py:61
  2.2 4.0 %collective-permute-start.1 = (f32[4,24,128]{2,1,0:T(8,128)S(1)}, f32[4,24,128]{2,1,0:T(8,128)S(1)}, u32[]{:S(2)}, u32[]{:S(2)}) collective-permute-start(f32[4,24,128]{2,1,0:T(8,128)S(1)} %get-tuple-element.25), channel_id=1, source_target_pairs={{0,2},{2,0},{4,6},{6,4},{1,3},{3,1},{5,7},{7,5},{8,10},{10,8},{12,... | collective-permute-start | bytes 147464 | tf_op jit(solution)/shard_map/ppermute | solution.py:62
  6.2 1.0 %copy-done = f32[127,3,256]{2,0,1:T(8,128)S(1)} copy-done((f32[127,3,256]{2,0,1:T(8,128)S(1)}, f32[127,3,256]{2,0,1:T(8,128)}, u32[]{:S(2)}) %copy-start) | copy-done | bytes 390168
  7.2 1.2 %shard_map.59 = (f32[32,4,128]{2,1,0:T(4,128)}, bf16[3,3,128,256]{3,2,1,0:T(8,128)(2,1)S(1)}) custom-call(f32[3,127,256]{2,1,0:T(8,128)S(1)} %bitcast.8), custom_call_target="tpu_custom_call" | custom-call | tf_op jit(solution)/shard_map/pallas_call | solution.py:476
  8.4 0.0 collective-permute-done.odd_ref
  8.4 0.4 collective-permute-done.1.even_ref
  8.8 0.0 copy-done.2
  8.8 0.1 shard_map.60
  8.8 1.6 %collective-permute-start.2 = (f32[4,56,128]{2,1,0:T(8,128)S(1)}, f32[4,56,128]{2,1,0:T(8,128)S(1)}, u32[]{:S(2)}, u32[]{:S(2)}) collective-permute-start(f32[4,56,128]{2,1,0:T(8,128)S(1)} %get-tuple-element.31), channel_id=1, source_target_pairs={{0,8},{8,16},{16,24},{24,0},{1,9},{9,17},{17,25},{25,1},{2,10},{10... | collective-permute-start | bytes 344072 | tf_op jit(solution)/shard_map/ppermute | solution.py:50
  10.4 2.2 %collective-permute-start.3 = (f32[4,56,128]{2,1,0:T(8,128)S(1)}, f32[4,56,128]{2,1,0:T(8,128)S(1)}, u32[]{:S(2)}, u32[]{:S(2)}) collective-permute-start(f32[4,56,128]{2,1,0:T(8,128)S(1)} %get-tuple-element.32), channel_id=1, source_target_pairs={{8,0},{16,8},{24,16},{0,24},{9,1},{17,9},{25,17},{1,25},{10,2},{18... | collective-permute-start | bytes 344072 | tf_op jit(solution)/shard_map/ppermute | solution.py:50
  12.7 3.2 %all-to-all-start = ((f32[32,4,128]{2,1,0:T(4,128)}), f32[32,4,128]{2,1,0:T(4,128)S(1)}, u32[]{:S(2)}, u32[]{:S(2)}) async-start(f32[32,4,128]{2,1,0:T(4,128)} %get-tuple-element.27), calls=%async_computation | async-start | bytes 131072 | tf_op jit(solution)/shard_map/all_to_all | solution.py:495
  15.9 0.3 collective-permute-done.2.low_ref
  16.2 0.4 %collective-permute-done.3.high_ref = f32[4,56,128]{2,1,0:T(8,128)S(1)} collective-permute-done((f32[4,56,128]{2,1,0:T(8,128)S(1)}, f32[4,56,128]{2,1,0:T(8,128)S(1)}, u32[]{:S(2)}, u32[]{:S(2)}) %collective-permute-start.3) | collective-permute-done | bytes 114720 | tf_op jit(solution)/shard_map/ppermute | solution.py:50
  16.6 0.2 shard_map.61
  16.9 0.0 copy-start.1
  16.9 0.1 collective-permute-start.4
  16.9 0.3 copy-done.3
  17.3 0.5 %shard_map.62 = (f32[4,12,24,128]{3,2,1,0:T(8,128)S(1)}, s32[1,256]{1,0:T(1,128)S(1)}) custom-call(s32[1,256]{1,0:T(1,128)S(1)} %bitcast.12, f32[4,8,24,128]{3,2,1,0:T(8,128)S(1)} %bitcast.6, f32[4,3,24,128]{3,2,1,0:T(8,128)S(1)} %get-tuple-element.33.xlo_ref, f32[4,3,24,128]{3,2,1,0:T(8,128)S(1)} %get-tuple-element.34.xhi_ref), custom_call_target="tpu_custom_call" | custom-call | tf_op jit(solution)/shard_map/pallas_call | solution.py:508
  17.8 0.3 collective-permute-done.4.low_ref.high_ref
  18.2 1.9 %shard_map.63 = (f32[4,8,16,128]{3,2,1,0:T(8,128)S(1)}, f32[3,1,256]{2,1,0:T(1,128)S(1)}, f32[1,128]{1,0:T(1,128)S(1)}) custom-call(f32[4,8,24,128]{3,2,1,0:T(8,128)S(1)} %bitcast.7, f32[4,3,24,128]{3,2,1,0:T(8,128)S(1)} %get-tuple-element.33.xlo_ref, f32[4,3,24,128]{3,2,1,0:T(8,128)S(1)} %get-tuple-element.34.xhi_ref, ...), custom_call_target="tpu_custom_call" | custom-call | tf_op jit(solution)/shard_map/pallas_call | solution.py:518
  20.0 3.2 %all-to-all-done.parts_ref = f32[32,4,128]{2,1,0:T(4,128)S(1)} async-done(((f32[32,4,128]{2,1,0:T(4,128)}), f32[32,4,128]{2,1,0:T(4,128)S(1)}, u32[]{:S(2)}, u32[]{:S(2)}) %all-to-all-start) | async-done | bytes 65568 | tf_op jit(solution)/shard_map/all_to_all | solution.py:495
  23.2 9.1 %all_to_all.10.got_ref = f32[32,4,128]{2,1,0:T(4,128)S(1)} all-to-all(f32[32,4,128]{2,1,0:T(4,128)S(1)} %shard_map.64), channel_id=1, replica_groups=mesh['gx'=4,'gy'=4,'gz'=2] {'gz','gy','gx'}, dimensions={0} | all-to-all | bytes 131072 | tf_op jit(solution)/shard_map/all_to_all | solution.py:532
  32.4 3.8 %shard_map.65 = (f32[3,128,256]{2,1,0:T(8,128)}, f32[128,128]{1,0:T(8,128)}, f32[4,8,16,128]{3,2,1,0:T(8,128)}) custom-call(f32[32,4,128]{2,1,0:T(4,128)S(1)} %all_to_all.10.got_ref, bf16[3,3,128,256]{3,2,1,0:T(8,128)(2,1)S(1)} %get-tuple-element.39.parts_ref, f32[3,1,256]{2,1,0:T(1,128)S(1)} %get-tuple-element.40.snap_ref, ...), custom_call_target="tpu_custom_call" | custom-call | tf_op jit(solution)/shard_map/pallas_call | solution.py:533
  (5 shorter events, 0.1 us)
Async XLA Ops:
  0.6 8.1 %copy-start.2 = (f32[4,8,16,128]{3,2,1,0:T(8,128)S(1)}, f32[4,8,16,128]{3,2,1,0:T(8,128)}, u32[]{:S(2)}) copy-start(f32[4,8,16,128]{3,2,1,0:T(8,128)} %param.3) | copy-start | bytes 786436
  1.7 6.7 %collective-permute-start = (f32[4,24,128]{2,1,0:T(8,128)S(1)}, f32[4,24,128]{2,1,0:T(8,128)S(1)}, u32[]{:S(2)}, u32[]{:S(2)}) collective-permute-start(f32[4,24,128]{2,1,0:T(8,128)S(1)} %get-tuple-element.24), channel_id=1, source_target_pairs={{0,1},{1,0},{2,4},{3,5},{4,2},{5,3},{6,7},{7,6},{8,9},{9,8},{10,12... | collective-permute-start | bytes 147464 | tf_op jit(solution)/shard_map/ppermute | solution.py:61
  2.2 6.6 %collective-permute-start.1 = (f32[4,24,128]{2,1,0:T(8,128)S(1)}, f32[4,24,128]{2,1,0:T(8,128)S(1)}, u32[]{:S(2)}, u32[]{:S(2)}) collective-permute-start(f32[4,24,128]{2,1,0:T(8,128)S(1)} %get-tuple-element.25), channel_id=1, source_target_pairs={{0,2},{2,0},{4,6},{6,4},{1,3},{3,1},{5,7},{7,5},{8,10},{10,8},{12,... | collective-permute-start | bytes 147464 | tf_op jit(solution)/shard_map/ppermute | solution.py:62
  6.2 1.0 %copy-start = (f32[127,3,256]{2,0,1:T(8,128)S(1)}, f32[127,3,256]{2,0,1:T(8,128)}, u32[]{:S(2)}) copy-start(f32[127,3,256]{2,0,1:T(8,128)} %param.4) | copy-start | bytes 1170436
  8.8 7.4 %collective-permute-start.2 = (f32[4,56,128]{2,1,0:T(8,128)S(1)}, f32[4,56,128]{2,1,0:T(8,128)S(1)}, u32[]{:S(2)}, u32[]{:S(2)}) collective-permute-start(f32[4,56,128]{2,1,0:T(8,128)S(1)} %get-tuple-element.31), channel_id=1, source_target_pairs={{0,8},{8,16},{16,24},{24,0},{1,9},{9,17},{17,25},{25,1},{2,10},{10... | collective-permute-start | bytes 344072 | tf_op jit(solution)/shard_map/ppermute | solution.py:50
  10.4 6.2 %collective-permute-start.3 = (f32[4,56,128]{2,1,0:T(8,128)S(1)}, f32[4,56,128]{2,1,0:T(8,128)S(1)}, u32[]{:S(2)}, u32[]{:S(2)}) collective-permute-start(f32[4,56,128]{2,1,0:T(8,128)S(1)} %get-tuple-element.32), channel_id=1, source_target_pairs={{8,0},{16,8},{24,16},{0,24},{9,1},{17,9},{25,17},{1,25},{10,2},{18... | collective-permute-start | bytes 344072 | tf_op jit(solution)/shard_map/ppermute | solution.py:50
  12.7 10.5 %all-to-all-start = ((f32[32,4,128]{2,1,0:T(4,128)}), f32[32,4,128]{2,1,0:T(4,128)S(1)}, u32[]{:S(2)}, u32[]{:S(2)}) async-start(f32[32,4,128]{2,1,0:T(4,128)} %get-tuple-element.27), calls=%async_computation | async-start | bytes 131072 | tf_op jit(solution)/shard_map/all_to_all | solution.py:495
  16.6 0.7 %copy-start.3 = (s32[256]{0:T(256)S(1)}, s32[256]{0:T(256)}, u32[]{:S(2)}) copy-start(s32[256]{0:T(256)} %param.5) | copy-start | bytes 3076
  16.9 1.3 %copy-start.1 = (f32[127,3,256]{2,0,1:T(8,128)S(1)}, f32[127,3,256]{2,0,1:T(8,128)}, u32[]{:S(2)}) copy-start(f32[127,3,256]{2,0,1:T(8,128)} %param.4) | copy-start | bytes 1170436
  16.9 1.3 %collective-permute-start.4 = (f32[4,24,128]{2,1,0:T(8,128)S(1)}, f32[4,24,128]{2,1,0:T(8,128)S(1)}, u32[]{:S(2)}, u32[]{:S(2)}) collective-permute-start(f32[4,24,128]{2,1,0:T(8,128)S(1)} %get-tuple-element.36.own_ref), channel_id=1, source_target_pairs={{0,1},{1,0},{2,3},{3,2},{4,5},{5,4},{6,7},{7,6},{8,9},{9,8},{10,11... | collective-permute-start | bytes 147464 | tf_op jit(solution)/shard_map/ppermute | solution.py:505

commit v19 on v17

--- a/solution.py
+++ b/solution.py
@@ -62,6 +62,14 @@
     return lax.ppermute(block_even, axis, even), from_odd
 
 
+def ring_pairs(block_odd, block_even, axis):
+    count = lax.axis_size(axis)
+    even = [(i, i + 1 - 2 * (i % 2)) for i in range(count)]
+    odd = [(i, (i - 1 + 2 * (i % 2)) % count) for i in range(count)]
+    from_odd = lax.ppermute(block_odd, axis, odd)
+    return lax.ppermute(block_even, axis, even), from_odd
+
+
 def at_lower_wall():
     return lax.axis_index("gy") == 0
 
@@ -70,8 +78,8 @@
     return lax.axis_index("gy") == lax.axis_size("gy") - 1
 
 
-def odd_place():
-    return lax.axis_index("gy") % 2 == 1
+def odd_place(axis="gy"):
+    return lax.axis_index(axis) % 2 == 1
 
 
 def pack_upper(rows, tall):
@@ -121,7 +129,7 @@
             odd_ref[f, planes * j : planes * j + planes] = jnp.where(odd, top, bottom)
 
 
-def walls_kernel(planes, flow_ref, odd_ref, even_ref, mid_ref, first_ref, last_ref):
+def walls_kernel(planes, flow_ref, odd_ref, even_ref, mid_ref, face_even_ref, face_odd_ref):
     fields, cells, nz = flow_ref.shape
     odd_y = odd_place()
     ny = cells // planes
@@ -143,13 +151,15 @@
                 value = jnp.where(odd_y, even_ref[f, part], odd_ref[f, part])
                 value = jnp.where(at_lower_wall(), 0.0, value)
             mid_ref[f, pl.ds(ny + j, planes, stride=rows), :] = value
-        for face_ref, begin, near, next_one in (
-            (first_ref, 0, 0, 1), (last_ref, planes - DEPTH, planes - 1, planes - 2)
-        ):
-            for k in range(DEPTH):
-                face_ref[f, ny * k : ny * k + ny] = flow_ref[f, ny * (begin + k) : ny * (begin + k) + ny]
+        faces = []
+        for begin, near, next_one in ((0, 0, 1), (planes - DEPTH, planes - 1, planes - 2)):
             halos = [mid_ref[f, rows * i + ny : rows * i + rows] for i in (near, next_one)]
-            face_ref[f, ny * DEPTH : ny * DEPTH + HALO] = corner_rows(*halos, sub)
+            own = [flow_ref[f, ny * i : ny * i + ny] for i in range(begin, begin + DEPTH)]
+            faces.append(own + [corner_rows(*halos, sub)])
+        for k, (first, last) in enumerate(zip(*faces)):
+            part = slice(ny * k, ny * k + first.shape[0])
+            face_even_ref[f, part] = jnp.where(odd_place("gx"), first, last)
+            face_odd_ref[f, part] = jnp.where(odd_place("gx"), last, first)
 
 
 def corner_rows(near, next_one, sub):
@@ -176,14 +186,16 @@
 GROUP = 8
 
 
-def pack_kernel(mid_ref, low_ref, high_ref, packed_ref, xlo_ref, xhi_ref):
+def pack_kernel(mid_ref, even_ref, odd_ref, packed_ref, xlo_ref, xhi_ref):
     fields, nx, rows, nz = mid_ref.shape
     ny = rows - HALO
     lane = lax.broadcasted_iota(jnp.int32, (rows, nz), 1)
     sub = lax.broadcasted_iota(jnp.int32, (HALO, nz), 0)
     for f in range(fields):
-        for face_ref, out_ref, order in ((low_ref, xlo_ref, (2, 1, 0)), (high_ref, xhi_ref, (0, 1, 2))):
-            face = face_ref[f]
+        for one_ref, other_ref, out_ref, order in (
+            (even_ref, odd_ref, xlo_ref, (2, 1, 0)), (odd_ref, even_ref, xhi_ref, (0, 1, 2))
+        ):
+            face = jnp.where(odd_place("gx"), one_ref[f], other_ref[f])
             halo = corner_planes(face[ny * DEPTH :], sub)
             for k in range(DEPTH):
                 out_ref[f, k, 0:ny] = face[ny * k : ny * k + ny]
@@ -474,14 +486,14 @@
 
     rows = ny + HALO
     face = shape((fields, DEPTH * ny + HALO, nz))
-    mid, first, last = call(
+    mid, face_even, face_odd = call(
         functools.partial(walls_kernel, nx),
         out_shape=(shape((fields, nx * rows, nz)), face, face),
         in_specs=[VMEM] * 3,
         out_specs=(VMEM,) * 3,
     )(flat, y_odd, y_even)
     mid = mid.reshape(fields, nx, rows, nz)
-    low_face, high_face = neighbours(first, last, "gx")
+    x_even, x_odd = ring_pairs(face_odd, face_even, "gx")
     parts = lax.all_to_all(gram, ALL, 0, 0)
 
     beside = shape((fields, DEPTH, rows, nz))
@@ -490,7 +502,7 @@
         out_shape=(shape((fields, rows, nz)), beside, beside),
         in_specs=[VMEM] * 3,
         out_specs=(VMEM,) * 3,
-    )(mid, low_face, high_face)
+    )(mid, x_even, x_odd)
     if lax.axis_size("gz") == 2:
         low = high = lax.ppermute(packed, "gz", [(0, 1), (1, 0)])
     else:

time: 36.3 us -> 36.1 us (level)
    all_to_all x1, waiting for transfers between devices: 3.16 us -> 2.1 us  [local(): parts = lax.all_to_all(gram, ALL, 0, 0)]
    ppermute x2, waiting for transfers between devices: 0.73 us -> 1.78 us  [the longest x1 1.78 us: ring_pairs(): from_odd = lax.ppermute(block_odd, axis, odd)]
    all_to_all x1, starting transfers between devices: 3.18 us -> 2.72 us  [local(): parts = lax.all_to_all(gram, ALL, 0, 0)]
  transfers between devices with their start and end apart: 6 -> 6, of which waited for: 5 -> 4; matrix products, arithmetic and copies ran while one was open for 0% -> 0% of each run, Pallas kernels for 11% -> 11%
where the time goes in v19:
time: 36.1 us; the launch traced here: 35.9 us
  starting transfers between devices  11.4 us (32%)
  blocking collectives  9.12 us (25%)
  Pallas kernels  7.76 us (21%)
  waiting for transfers between devices  4.58 us (13%)
  local copies, waits for them, and re-layouts  2.29 us (6%)
  between operations  0.71 us (2%)
    all_to_all x1, blocking collectives, local(): got = lax.all_to_all(send, ALL, 0, 0)  9.12 us
    ppermute x1, starting transfers between devices, pairs(): return (lax.ppermute(block_even, axis, even), from_odd)  3.98 us
    pallas_call x1, Pallas kernels, local(): call(functools.partial(final_kernel, count), out_shape=(shape((comps, siz...  3.76 us
    all_to_all x1, starting transfers between devices, local(): parts = lax.all_to_all(gram, ALL, 0, 0)  2.72 us
    ppermute x1, starting transfers between devices, ring_pairs(): from_odd = lax.ppermute(block_odd, axis, odd)  2.47 us
    unnamed x10, local copies, waits for them, and re-layouts  2.29 us
    all_to_all x1, waiting for transfers between devices, local(): parts = lax.all_to_all(gram, ALL, 0, 0)  2.1 us
    pallas_call x1, Pallas kernels, local(): call(step_kernel, out_shape=(shape(flow.shape), shape((comps, 1, points))...  1.87 us
  transfers between devices with their start and end apart: 6, of which 4 were waited for; matrix products, arithmetic and copies ran while one was open for 0% of the time, Pallas kernels for 11%

profile of v19, /device:TPU:0, one launch (start us, length us, event | category | flops | bytes accessed | tf_op | source)
XLA Modules:
  0.0 35.9 jit_solution(18282297270514833375)
XLA Ops:
  0.6 0.0 copy-start.2
  0.6 0.9 %copy-done.2 = f32[4,8,16,128]{3,2,1,0:T(8,128)S(1)} copy-done((f32[4,8,16,128]{3,2,1,0:T(8,128)S(1)}, f32[4,8,16,128]{3,2,1,0:T(8,128)}, u32[]{:S(2)}) %copy-start.2) | copy-done | bytes 262168
  1.6 0.5 %collective-permute-start = (f32[4,24,128]{2,1,0:T(8,128)S(1)}, f32[4,24,128]{2,1,0:T(8,128)S(1)}, u32[]{:S(2)}, u32[]{:S(2)}) collective-permute-start(f32[4,24,128]{2,1,0:T(8,128)S(1)} %get-tuple-element.24), channel_id=1, source_target_pairs={{0,1},{1,0},{2,4},{3,5},{4,2},{5,3},{6,7},{7,6},{8,9},{9,8},{10,12... | collective-permute-start | bytes 147464 | tf_op jit(solution)/shard_map/ppermute | solution.py:61
  2.1 4.0 %collective-permute-start.1 = (f32[4,24,128]{2,1,0:T(8,128)S(1)}, f32[4,24,128]{2,1,0:T(8,128)S(1)}, u32[]{:S(2)}, u32[]{:S(2)}) collective-permute-start(f32[4,24,128]{2,1,0:T(8,128)S(1)} %get-tuple-element.25), channel_id=1, source_target_pairs={{0,2},{2,0},{4,6},{6,4},{1,3},{3,1},{5,7},{7,5},{8,10},{10,8},{12,... | collective-permute-start | bytes 147464 | tf_op jit(solution)/shard_map/ppermute | solution.py:62
  6.1 1.0 %copy-done = f32[127,3,256]{2,0,1:T(8,128)S(1)} copy-done((f32[127,3,256]{2,0,1:T(8,128)S(1)}, f32[127,3,256]{2,0,1:T(8,128)}, u32[]{:S(2)}) %copy-start) | copy-done | bytes 390168
  7.1 1.2 %shard_map.59 = (f32[32,4,128]{2,1,0:T(4,128)}, bf16[3,3,128,256]{3,2,1,0:T(8,128)(2,1)S(1)}) custom-call(f32[3,127,256]{2,1,0:T(8,128)S(1)} %bitcast.8), custom_call_target="tpu_custom_call" | custom-call | tf_op jit(solution)/shard_map/pallas_call | solution.py:478
  8.3 0.0 collective-permute-done.odd_ref
  8.4 0.4 collective-permute-done.1.even_ref
  8.7 0.1 shard_map.60
  8.8 1.6 %collective-permute-start.2 = (f32[4,56,128]{2,1,0:T(8,128)S(1)}, f32[4,56,128]{2,1,0:T(8,128)S(1)}, u32[]{:S(2)}, u32[]{:S(2)}) collective-permute-start(f32[4,56,128]{2,1,0:T(8,128)S(1)} %get-tuple-element.31), channel_id=1, source_target_pairs={{0,8},{8,0},{16,24},{24,16},{1,9},{9,1},{17,25},{25,17},{2,10},{10... | collective-permute-start | bytes 344072 | tf_op jit(solution)/shard_map/ppermute | solution.py:70
  10.4 2.5 %collective-permute-start.3 = (f32[4,56,128]{2,1,0:T(8,128)S(1)}, f32[4,56,128]{2,1,0:T(8,128)S(1)}, u32[]{:S(2)}, u32[]{:S(2)}) collective-permute-start(f32[4,56,128]{2,1,0:T(8,128)S(1)} %get-tuple-element.32), channel_id=1, source_target_pairs={{0,24},{8,16},{16,8},{24,0},{1,25},{9,17},{17,9},{25,1},{2,26},{10... | collective-permute-start | bytes 344072 | tf_op jit(solution)/shard_map/ppermute | solution.py:69
  12.9 2.7 %all-to-all-start = ((f32[32,4,128]{2,1,0:T(4,128)}), f32[32,4,128]{2,1,0:T(4,128)S(1)}, u32[]{:S(2)}, u32[]{:S(2)}) async-start(f32[32,4,128]{2,1,0:T(4,128)} %get-tuple-element.27), calls=%async_computation | async-start | bytes 131072 | tf_op jit(solution)/shard_map/all_to_all | solution.py:497
  15.6 0.0 collective-permute-done.2.even_ref
  15.6 1.8 %collective-permute-done.3.odd_ref = f32[4,56,128]{2,1,0:T(8,128)S(1)} collective-permute-done((f32[4,56,128]{2,1,0:T(8,128)S(1)}, f32[4,56,128]{2,1,0:T(8,128)S(1)}, u32[]{:S(2)}, u32[]{:S(2)}) %collective-permute-start.3) | collective-permute-done | bytes 114720 | tf_op jit(solution)/shard_map/ppermute | solution.py:69
  17.4 0.2 shard_map.61
  17.7 0.0 copy-start.1
  17.7 0.1 collective-permute-start.4
  17.7 0.3 copy-done.4
  18.1 0.5 %shard_map.62 = (f32[4,12,24,128]{3,2,1,0:T(8,128)S(1)}, s32[1,256]{1,0:T(1,128)S(1)}) custom-call(s32[1,256]{1,0:T(1,128)S(1)} %bitcast.12, f32[4,8,24,128]{3,2,1,0:T(8,128)S(1)} %bitcast.6, f32[4,3,24,128]{3,2,1,0:T(8,128)S(1)} %get-tuple-element.33.xlo_ref, f32[4,3,24,128]{3,2,1,0:T(8,128)S(1)} %get-tuple-element.34.xhi_ref), custom_call_target="tpu_custom_call" | custom-call | tf_op jit(solution)/shard_map/pallas_call | solution.py:510
  18.6 0.3 collective-permute-done.4.low_ref.high_ref
  19.0 1.9 %shard_map.63 = (f32[4,8,16,128]{3,2,1,0:T(8,128)S(1)}, f32[3,1,256]{2,1,0:T(1,128)S(1)}, f32[1,128]{1,0:T(1,128)S(1)}) custom-call(f32[4,8,24,128]{3,2,1,0:T(8,128)S(1)} %bitcast.7, f32[4,3,24,128]{3,2,1,0:T(8,128)S(1)} %get-tuple-element.33.xlo_ref, f32[4,3,24,128]{3,2,1,0:T(8,128)S(1)} %get-tuple-element.34.xhi_ref, ...), custom_call_target="tpu_custom_call" | custom-call | tf_op jit(solution)/shard_map/pallas_call | solution.py:520
  20.8 2.1 %all-to-all-done.parts_ref = f32[32,4,128]{2,1,0:T(4,128)S(1)} async-done(((f32[32,4,128]{2,1,0:T(4,128)}), f32[32,4,128]{2,1,0:T(4,128)S(1)}, u32[]{:S(2)}, u32[]{:S(2)}) %all-to-all-start) | async-done | bytes 65568 | tf_op jit(solution)/shard_map/all_to_all | solution.py:497
  23.0 9.1 %all_to_all.10.got_ref = f32[32,4,128]{2,1,0:T(4,128)S(1)} all-to-all(f32[32,4,128]{2,1,0:T(4,128)S(1)} %shard_map.64), channel_id=1, replica_groups=mesh['gx'=4,'gy'=4,'gz'=2] {'gz','gy','gx'}, dimensions={0} | all-to-all | bytes 131072 | tf_op jit(solution)/shard_map/all_to_all | solution.py:534
  32.1 3.8 %shard_map.65 = (f32[3,128,256]{2,1,0:T(8,128)}, f32[128,128]{1,0:T(8,128)}, f32[4,8,16,128]{3,2,1,0:T(8,128)}) custom-call(f32[32,4,128]{2,1,0:T(4,128)S(1)} %all_to_all.10.got_ref, bf16[3,3,128,256]{3,2,1,0:T(8,128)(2,1)S(1)} %get-tuple-element.39.parts_ref, f32[3,1,256]{2,1,0:T(1,128)S(1)} %get-tuple-element.40.snap_ref, ...), custom_call_target="tpu_custom_call" | custom-call | tf_op jit(solution)/shard_map/pallas_call | solution.py:535
  (7 shorter events, 0.1 us)
Async XLA Ops:
  0.6 1.0 %copy-start.2 = (f32[4,8,16,128]{3,2,1,0:T(8,128)S(1)}, f32[4,8,16,128]{3,2,1,0:T(8,128)}, u32[]{:S(2)}) copy-start(f32[4,8,16,128]{3,2,1,0:T(8,128)} %param.3) | copy-start | bytes 786436
  1.6 7.1 %copy-start.3 = (f32[4,8,16,128]{3,2,1,0:T(8,128)S(1)}, f32[4,8,16,128]{3,2,1,0:T(8,128)}, u32[]{:S(2)}) copy-start(f32[4,8,16,128]{3,2,1,0:T(8,128)} %param.3) | copy-start | bytes 786436
  1.6 6.7 %collective-permute-start = (f32[4,24,128]{2,1,0:T(8,128)S(1)}, f32[4,24,128]{2,1,0:T(8,128)S(1)}, u32[]{:S(2)}, u32[]{:S(2)}) collective-permute-start(f32[4,24,128]{2,1,0:T(8,128)S(1)} %get-tuple-element.24), channel_id=1, source_target_pairs={{0,1},{1,0},{2,4},{3,5},{4,2},{5,3},{6,7},{7,6},{8,9},{9,8},{10,12... | collective-permute-start | bytes 147464 | tf_op jit(solution)/shard_map/ppermute | solution.py:61
  2.1 6.6 %collective-permute-start.1 = (f32[4,24,128]{2,1,0:T(8,128)S(1)}, f32[4,24,128]{2,1,0:T(8,128)S(1)}, u32[]{:S(2)}, u32[]{:S(2)}) collective-permute-start(f32[4,24,128]{2,1,0:T(8,128)S(1)} %get-tuple-element.25), channel_id=1, source_target_pairs={{0,2},{2,0},{4,6},{6,4},{1,3},{3,1},{5,7},{7,5},{8,10},{10,8},{12,... | collective-permute-start | bytes 147464 | tf_op jit(solution)/shard_map/ppermute | solution.py:62
  6.1 1.0 %copy-start = (f32[127,3,256]{2,0,1:T(8,128)S(1)}, f32[127,3,256]{2,0,1:T(8,128)}, u32[]{:S(2)}) copy-start(f32[127,3,256]{2,0,1:T(8,128)} %param.4) | copy-start | bytes 1170436
  8.8 6.8 %collective-permute-start.2 = (f32[4,56,128]{2,1,0:T(8,128)S(1)}, f32[4,56,128]{2,1,0:T(8,128)S(1)}, u32[]{:S(2)}, u32[]{:S(2)}) collective-permute-start(f32[4,56,128]{2,1,0:T(8,128)S(1)} %get-tuple-element.31), channel_id=1, source_target_pairs={{0,8},{8,0},{16,24},{24,16},{1,9},{9,1},{17,25},{25,17},{2,10},{10... | collective-permute-start | bytes 344072 | tf_op jit(solution)/shard_map/ppermute | solution.py:70
  10.4 7.0 %collective-permute-start.3 = (f32[4,56,128]{2,1,0:T(8,128)S(1)}, f32[4,56,128]{2,1,0:T(8,128)S(1)}, u32[]{:S(2)}, u32[]{:S(2)}) collective-permute-start(f32[4,56,128]{2,1,0:T(8,128)S(1)} %get-tuple-element.32), channel_id=1, source_target_pairs={{0,24},{8,16},{16,8},{24,0},{1,25},{9,17},{17,9},{25,1},{2,26},{10... | collective-permute-start | bytes 344072 | tf_op jit(solution)/shard_map/ppermute | solution.py:69
  12.9 10.1 %all-to-all-start = ((f32[32,4,128]{2,1,0:T(4,128)}), f32[32,4,128]{2,1,0:T(4,128)S(1)}, u32[]{:S(2)}, u32[]{:S(2)}) async-start(f32[32,4,128]{2,1,0:T(4,128)} %get-tuple-element.27), calls=%async_computation | async-start | bytes 131072 | tf_op jit(solution)/shard_map/all_to_all | solution.py:497
  17.4 0.7 %copy-start.4 = (s32[256]{0:T(256)S(1)}, s32[256]{0:T(256)}, u32[]{:S(2)}) copy-start(s32[256]{0:T(256)} %param.5) | copy-start | bytes 3076
  17.7 1.3 %copy-start.1 = (f32[127,3,256]{2,0,1:T(8,128)S(1)}, f32[127,3,256]{2,0,1:T(8,128)}, u32[]{:S(2)}) copy-start(f32[127,3,256]{2,0,1:T(8,128)} %param.4) | copy-start | bytes 1170436
  17.7 1.3 %collective-permute-start.4 = (f32[4,24,128]{2,1,0:T(8,128)S(1)}, f32[4,24,128]{2,1,0:T(8,128)S(1)}, u32[]{:S(2)}, u32[]{:S(2)}) collective-permute-start(f32[4,24,128]{2,1,0:T(8,128)S(1)} %get-tuple-element.36.own_ref), channel_id=1, source_target_pairs={{0,1},{1,0},{2,3},{3,2},{4,5},{5,4},{6,7},{7,6},{8,9},{9,8},{10,11... | collective-permute-start | bytes 147464 | tf_op jit(solution)/shard_map/ppermute | solution.py:507

commit v20 on v19

--- a/solution.py
+++ b/solution.py
@@ -93,11 +93,17 @@
     return [packed[0], packed[1], packed[2], pltpu.roll(packed[1], packed[1].shape[1] - tall, 1)]
 
 
-def gram_kernel(basis_ref, send_ref, parts_ref, gram_ref, packed_ref):
+def gram_kernel(basis_hbm, send_ref, parts_ref, gram_ref, packed_ref, basis_ref, sems):
     modes = basis_ref.shape[1]
+    copies = [
+        pltpu.make_async_copy(basis_hbm.at[c], basis_ref.at[c], sems.at[c]) for c in range(basis_ref.shape[0])
+    ]
+    for copy in copies:
+        copy.start()
     tall = gram_ref.shape[0] // 4
     total = jnp.zeros((modes, modes), jnp.float32)
     for c in range(basis_ref.shape[0]):
+        copies[c].wait()
         rows = basis_ref[c]
         total = total + dot(rows, rows, ((1,), (1,)))
         filled = jnp.concatenate([rows, jnp.zeros((1, rows.shape[1]), jnp.float32)], axis=0)
@@ -478,10 +484,13 @@
     gram, basis_parts = call(
         gram_kernel,
         out_shape=(shape((devices, per + 1, size)), jax.ShapeDtypeStruct((3, comps, size, points), jnp.bfloat16)),
-        in_specs=[VMEM],
+        in_specs=[whole],
         out_specs=(VMEM, VMEM),
-        scratch_shapes=[pltpu.VMEM((size, size), jnp.float32), pltpu.VMEM((devices * per, size), jnp.float32)],
-    )(bricks)
+        scratch_shapes=[pltpu.VMEM((size, size), jnp.float32), pltpu.VMEM((devices * per, size), jnp.float32),
+            pltpu.VMEM(bricks.shape, jnp.float32),
+            pltpu.SemaphoreType.DMA((comps,)),
+        ],
+    )(pltpu.with_memory_space_constraint(bricks, pltpu.HBM))
     y_odd, y_even, gram = lax.optimization_barrier((y_odd, y_even, gram))
 
     rows = ny + HALO

time: 36.1 us -> 36.1 us (level)
  Pallas kernels: 7.76 us -> 9.06 us
  local copies, waits for them, and re-layouts: 2.29 us -> 1.3 us
    pallas_call x1, Pallas kernels: 1.24 us -> 2.53 us  [local(): call(gram_kernel, out_shape=(shape((devices, per + 1, size)), jax.ShapeDt...]
    unnamed x10 -> x8, local copies, waits for them, and re-layouts: 2.29 us -> 1.3 us
  transfers between devices with their start and end apart: 6 -> 6, of which waited for: 4 -> 3; matrix products, arithmetic and copies ran while one was open for 0% -> 0% of each run, Pallas kernels for 11% -> 14%
where the time goes in v20:
time: 36.1 us; the launch traced here: 35.9 us
  starting transfers between devices  11.4 us (32%)
  blocking collectives  9.12 us (25%)
  Pallas kernels  9.06 us (25%)
  waiting for transfers between devices  4.27 us (12%)
  local copies, waits for them, and re-layouts  1.3 us (4%)
  between operations  0.73 us (2%)
    all_to_all x1, blocking collectives, local(): got = lax.all_to_all(send, ALL, 0, 0)  9.12 us
    ppermute x1, starting transfers between devices, pairs(): return (lax.ppermute(block_even, axis, even), from_odd)  3.98 us
    pallas_call x1, Pallas kernels, local(): call(functools.partial(final_kernel, count), out_shape=(shape((comps, siz...  3.76 us
    all_to_all x1, starting transfers between devices, local(): parts = lax.all_to_all(gram, ALL, 0, 0)  2.72 us
    pallas_call x1, Pallas kernels, local(): call(gram_kernel, out_shape=(shape((devices, per + 1, size)), jax.ShapeDt...  2.53 us
    ppermute x1, starting transfers between devices, ring_pairs(): from_odd = lax.ppermute(block_odd, axis, odd)  2.47 us
    ppermute x1, waiting for transfers between devices, ring_pairs(): from_odd = lax.ppermute(block_odd, axis, odd)  2.1 us
    pallas_call x1, Pallas kernels, local(): call(step_kernel, out_shape=(shape(flow.shape), shape((comps, 1, points))...  1.87 us
  transfers between devices with their start and end apart: 6, of which 3 were waited for; matrix products, arithmetic and copies ran while one was open for 0% of the time, Pallas kernels for 14%

profile of v20, /device:TPU:0, one launch (start us, length us, event | category | flops | bytes accessed | tf_op | source)
XLA Modules:
  0.0 35.9 jit_solution(11215853740518822289)
XLA Ops:
  0.6 0.0 copy-start.1
  0.6 0.9 %copy-done.1 = f32[4,8,16,128]{3,2,1,0:T(8,128)S(1)} copy-done((f32[4,8,16,128]{3,2,1,0:T(8,128)S(1)}, f32[4,8,16,128]{3,2,1,0:T(8,128)}, u32[]{:S(2)}) %copy-start.1) | copy-done | bytes 262168
  1.6 0.0 copy-start.2
  1.6 0.5 %collective-permute-start = (f32[4,24,128]{2,1,0:T(8,128)S(1)}, f32[4,24,128]{2,1,0:T(8,128)S(1)}, u32[]{:S(2)}, u32[]{:S(2)}) collective-permute-start(f32[4,24,128]{2,1,0:T(8,128)S(1)} %get-tuple-element.24), channel_id=1, source_target_pairs={{0,1},{1,0},{2,4},{3,5},{4,2},{5,3},{6,7},{7,6},{8,9},{9,8},{10,12... | collective-permute-start | bytes 147464 | tf_op jit(solution)/shard_map/ppermute | solution.py:61
  2.2 4.0 %collective-permute-start.1 = (f32[4,24,128]{2,1,0:T(8,128)S(1)}, f32[4,24,128]{2,1,0:T(8,128)S(1)}, u32[]{:S(2)}, u32[]{:S(2)}) collective-permute-start(f32[4,24,128]{2,1,0:T(8,128)S(1)} %get-tuple-element.25), channel_id=1, source_target_pairs={{0,2},{2,0},{4,6},{6,4},{1,3},{3,1},{5,7},{7,5},{8,10},{10,8},{12,... | collective-permute-start | bytes 147464 | tf_op jit(solution)/shard_map/ppermute | solution.py:62
  6.1 2.5 %shard_map.59 = (f32[32,4,128]{2,1,0:T(4,128)}, bf16[3,3,128,256]{3,2,1,0:T(8,128)(2,1)S(1)}) custom-call(f32[3,127,256]{2,1,0:T(8,128)} %bitcast.8), custom_call_target="tpu_custom_call" | custom-call | tf_op jit(solution)/shard_map/pallas_call | solution.py:484
  8.7 0.0 collective-permute-done.odd_ref
  8.7 0.0 collective-permute-done.1.even_ref
  8.7 0.1 shard_map.60
  8.8 1.6 %collective-permute-start.2 = (f32[4,56,128]{2,1,0:T(8,128)S(1)}, f32[4,56,128]{2,1,0:T(8,128)S(1)}, u32[]{:S(2)}, u32[]{:S(2)}) collective-permute-start(f32[4,56,128]{2,1,0:T(8,128)S(1)} %get-tuple-element.31), channel_id=1, source_target_pairs={{0,8},{8,0},{16,24},{24,16},{1,9},{9,1},{17,25},{25,17},{2,10},{10... | collective-permute-start | bytes 344072 | tf_op jit(solution)/shard_map/ppermute | solution.py:70
  10.4 2.5 %collective-permute-start.3 = (f32[4,56,128]{2,1,0:T(8,128)S(1)}, f32[4,56,128]{2,1,0:T(8,128)S(1)}, u32[]{:S(2)}, u32[]{:S(2)}) collective-permute-start(f32[4,56,128]{2,1,0:T(8,128)S(1)} %get-tuple-element.32), channel_id=1, source_target_pairs={{0,24},{8,16},{16,8},{24,0},{1,25},{9,17},{17,9},{25,1},{2,26},{10... | collective-permute-start | bytes 344072 | tf_op jit(solution)/shard_map/ppermute | solution.py:69
  12.9 2.7 %all-to-all-start = ((f32[32,4,128]{2,1,0:T(4,128)}), f32[32,4,128]{2,1,0:T(4,128)S(1)}, u32[]{:S(2)}, u32[]{:S(2)}) async-start(f32[32,4,128]{2,1,0:T(4,128)} %get-tuple-element.27), calls=%async_computation | async-start | bytes 131072 | tf_op jit(solution)/shard_map/all_to_all | solution.py:506
  15.6 0.0 collective-permute-done.2.even_ref
  15.6 2.1 %collective-permute-done.3.odd_ref = f32[4,56,128]{2,1,0:T(8,128)S(1)} collective-permute-done((f32[4,56,128]{2,1,0:T(8,128)S(1)}, f32[4,56,128]{2,1,0:T(8,128)S(1)}, u32[]{:S(2)}, u32[]{:S(2)}) %collective-permute-start.3) | collective-permute-done | bytes 114720 | tf_op jit(solution)/shard_map/ppermute | solution.py:69
  17.7 0.2 shard_map.61
  18.0 0.0 copy-start
  18.0 0.1 collective-permute-start.4
  18.1 0.3 copy-done.3
  18.4 0.5 %shard_map.62 = (f32[4,12,24,128]{3,2,1,0:T(8,128)S(1)}, s32[1,256]{1,0:T(1,128)S(1)}) custom-call(s32[1,256]{1,0:T(1,128)S(1)} %bitcast.12, f32[4,8,24,128]{3,2,1,0:T(8,128)S(1)} %bitcast.6, f32[4,3,24,128]{3,2,1,0:T(8,128)S(1)} %get-tuple-element.33.xlo_ref, f32[4,3,24,128]{3,2,1,0:T(8,128)S(1)} %get-tuple-element.34.xhi_ref), custom_call_target="tpu_custom_call" | custom-call | tf_op jit(solution)/shard_map/pallas_call | solution.py:519
  19.0 0.3 collective-permute-done.4.low_ref.high_ref
  19.3 1.9 %shard_map.63 = (f32[4,8,16,128]{3,2,1,0:T(8,128)S(1)}, f32[3,1,256]{2,1,0:T(1,128)S(1)}, f32[1,128]{1,0:T(1,128)S(1)}) custom-call(f32[4,8,24,128]{3,2,1,0:T(8,128)S(1)} %bitcast.7, f32[4,3,24,128]{3,2,1,0:T(8,128)S(1)} %get-tuple-element.33.xlo_ref, f32[4,3,24,128]{3,2,1,0:T(8,128)S(1)} %get-tuple-element.34.xhi_ref, ...), custom_call_target="tpu_custom_call" | custom-call | tf_op jit(solution)/shard_map/pallas_call | solution.py:529
  21.2 1.8 %all-to-all-done.parts_ref = f32[32,4,128]{2,1,0:T(4,128)S(1)} async-done(((f32[32,4,128]{2,1,0:T(4,128)}), f32[32,4,128]{2,1,0:T(4,128)S(1)}, u32[]{:S(2)}, u32[]{:S(2)}) %all-to-all-start) | async-done | bytes 65568 | tf_op jit(solution)/shard_map/all_to_all | solution.py:506
  23.0 9.1 %all_to_all.10.got_ref = f32[32,4,128]{2,1,0:T(4,128)S(1)} all-to-all(f32[32,4,128]{2,1,0:T(4,128)S(1)} %shard_map.64), channel_id=1, replica_groups=mesh['gx'=4,'gy'=4,'gz'=2] {'gz','gy','gx'}, dimensions={0} | all-to-all | bytes 131072 | tf_op jit(solution)/shard_map/all_to_all | solution.py:543
  32.1 3.8 %shard_map.65 = (f32[3,128,256]{2,1,0:T(8,128)}, f32[128,128]{1,0:T(8,128)}, f32[4,8,16,128]{3,2,1,0:T(8,128)}) custom-call(f32[32,4,128]{2,1,0:T(4,128)S(1)} %all_to_all.10.got_ref, bf16[3,3,128,256]{3,2,1,0:T(8,128)(2,1)S(1)} %get-tuple-element.39.parts_ref, f32[3,1,256]{2,1,0:T(1,128)S(1)} %get-tuple-element.40.snap_ref, ...), custom_call_target="tpu_custom_call" | custom-call | tf_op jit(solution)/shard_map/pallas_call | solution.py:544
  (5 shorter events, 0.1 us)
Async XLA Ops:
  0.6 1.0 %copy-start.1 = (f32[4,8,16,128]{3,2,1,0:T(8,128)S(1)}, f32[4,8,16,128]{3,2,1,0:T(8,128)}, u32[]{:S(2)}) copy-start(f32[4,8,16,128]{3,2,1,0:T(8,128)} %param.3) | copy-start | bytes 786436
  1.6 7.1 %copy-start.2 = (f32[4,8,16,128]{3,2,1,0:T(8,128)S(1)}, f32[4,8,16,128]{3,2,1,0:T(8,128)}, u32[]{:S(2)}) copy-start(f32[4,8,16,128]{3,2,1,0:T(8,128)} %param.3) | copy-start | bytes 786436
  1.6 7.0 %collective-permute-start = (f32[4,24,128]{2,1,0:T(8,128)S(1)}, f32[4,24,128]{2,1,0:T(8,128)S(1)}, u32[]{:S(2)}, u32[]{:S(2)}) collective-permute-start(f32[4,24,128]{2,1,0:T(8,128)S(1)} %get-tuple-element.24), channel_id=1, source_target_pairs={{0,1},{1,0},{2,4},{3,5},{4,2},{5,3},{6,7},{7,6},{8,9},{9,8},{10,12... | collective-permute-start | bytes 147464 | tf_op jit(solution)/shard_map/ppermute | solution.py:61
  2.2 6.6 %collective-permute-start.1 = (f32[4,24,128]{2,1,0:T(8,128)S(1)}, f32[4,24,128]{2,1,0:T(8,128)S(1)}, u32[]{:S(2)}, u32[]{:S(2)}) collective-permute-start(f32[4,24,128]{2,1,0:T(8,128)S(1)} %get-tuple-element.25), channel_id=1, source_target_pairs={{0,2},{2,0},{4,6},{6,4},{1,3},{3,1},{5,7},{7,5},{8,10},{10,8},{12,... | collective-permute-start | bytes 147464 | tf_op jit(solution)/shard_map/ppermute | solution.py:62
  8.8 6.8 %collective-permute-start.2 = (f32[4,56,128]{2,1,0:T(8,128)S(1)}, f32[4,56,128]{2,1,0:T(8,128)S(1)}, u32[]{:S(2)}, u32[]{:S(2)}) collective-permute-start(f32[4,56,128]{2,1,0:T(8,128)S(1)} %get-tuple-element.31), channel_id=1, source_target_pairs={{0,8},{8,0},{16,24},{24,16},{1,9},{9,1},{17,25},{25,17},{2,10},{10... | collective-permute-start | bytes 344072 | tf_op jit(solution)/shard_map/ppermute | solution.py:70
  10.4 7.3 %collective-permute-start.3 = (f32[4,56,128]{2,1,0:T(8,128)S(1)}, f32[4,56,128]{2,1,0:T(8,128)S(1)}, u32[]{:S(2)}, u32[]{:S(2)}) collective-permute-start(f32[4,56,128]{2,1,0:T(8,128)S(1)} %get-tuple-element.32), channel_id=1, source_target_pairs={{0,24},{8,16},{16,8},{24,0},{1,25},{9,17},{17,9},{25,1},{2,26},{10... | collective-permute-start | bytes 344072 | tf_op jit(solution)/shard_map/ppermute | solution.py:69
  12.9 10.1 %all-to-all-start = ((f32[32,4,128]{2,1,0:T(4,128)}), f32[32,4,128]{2,1,0:T(4,128)S(1)}, u32[]{:S(2)}, u32[]{:S(2)}) async-start(f32[32,4,128]{2,1,0:T(4,128)} %get-tuple-element.27), calls=%async_computation | async-start | bytes 131072 | tf_op jit(solution)/shard_map/all_to_all | solution.py:506
  17.7 0.7 %copy-start.3 = (s32[256]{0:T(256)S(1)}, s32[256]{0:T(256)}, u32[]{:S(2)}) copy-start(s32[256]{0:T(256)} %param.5) | copy-start | bytes 3076
  18.0 1.3 %copy-start = (f32[127,3,256]{2,0,1:T(8,128)S(1)}, f32[127,3,256]{2,0,1:T(8,128)}, u32[]{:S(2)}) copy-start(f32[127,3,256]{2,0,1:T(8,128)} %param.4) | copy-start | bytes 1170436
  18.0 1.3 %collective-permute-start.4 = (f32[4,24,128]{2,1,0:T(8,128)S(1)}, f32[4,24,128]{2,1,0:T(8,128)S(1)}, u32[]{:S(2)}, u32[]{:S(2)}) collective-permute-start(f32[4,24,128]{2,1,0:T(8,128)S(1)} %get-tuple-element.36.own_ref), channel_id=1, source_target_pairs={{0,1},{1,0},{2,3},{3,2},{4,5},{5,4},{6,7},{7,6},{8,9},{9,8},{10,11... | collective-permute-start | bytes 147464 | tf_op jit(solution)/shard_map/ppermute | solution.py:516
